TPU v7x, 32 devices: a whole 2x2x4 slice. The times are simulated.
32 devices in a mesh: gx: 4 (over y, x), gy: 8 (over z, core).
Axes of the slice: x: 2, y: 2, z: 4, core: 2. Of those that a mesh axis runs over, the one named last changes fastest.
Arguments:
- params: bfloat16 [128, 8, 32, 128], P(None, 'gx', 'gy'), may hold values from -6 to 6
- predicted: float32 [4, 8, 128, 128], P('gx', 'gy'), may hold values from -6 to 6
- measured_value: float32 [4, 8, 128], P('gx', 'gy'), may hold values from -6 to 6
- measurement_variance: float32 [4, 8, 128], P('gx', 'gy'), may hold values from 0.25 to 1
- observation_jitter: float32 [4, 8, 128, 128], P('gx', 'gy'), may hold values from -6 to 6
- obs_block: int32 [4, 8, 128], replicated, may hold values from 0 to 7
- taper_radius: int32 [8, 32], P('gx', 'gy'), may hold values from 1 to 2
- taper_pattern: int32 [8, 32, 25], P('gx', 'gy'), may hold values 0 or 1
Outputs:
- updated: bfloat16 [128, 8, 32, 128], P('gy', 'gx')
All inputs are finite; a program needn't handle non-finite values. No bound on the sum of `taper_pattern` on one device may be relied on, other than what follows from the above.
Results may differ from a plain program's by a relative error of at most 0.0039.
Values may be sent and summed in bfloat16 or wider, within the bound.
No kernel may reach another device: no remote copies, remote signals or barrier semaphores. Data moves between devices by JAX's collectives and lax.ppermute only.
A program may use at most 64 MiB of HBM per device.

v0:
```python
import jax
import jax.numpy as jnp
from jax import lax
from jax.sharding import PartitionSpec as P

CELLS = 128
BLK_X = 2
BLK_Y = 4
OBS_TILE = 128
PATTERN = 25


def with_halo(cells, sides, width):
    for axis, dim in sides:
        count = lax.axis_size(axis)
        ends = count - 1
        head = lax.slice_in_dim(cells, 0, width, axis=dim)
        tail = lax.slice_in_dim(cells, cells.shape[dim] - width, cells.shape[dim], axis=dim)
        cells = jnp.concatenate(
            [
                lax.ppermute(tail, axis, [(i, (i + 1) % count) for i in range(ends)]),
                cells,
                lax.ppermute(head, axis, [((i + 1) % count, i) for i in range(ends)]),
            ],
            axis=dim,
        )
    return cells


def tapers(radius, pattern, own_x, own_y, obs_x, obs_y):
    step_x = obs_x[None, :] - own_x[:, None]
    step_y = obs_y[None, :] - own_y[:, None]
    inside = (jnp.abs(step_x) <= 2) & (jnp.abs(step_y) <= 2)
    offset = (step_x + 2) * 5 + (step_y + 2)
    slots = jnp.arange(PATTERN, dtype=jnp.int32)
    picked = jnp.sum(jnp.where(offset[:, :, None] == slots, pattern[:, None, :], 0), axis=2)
    reach = (radius + 1).astype(jnp.float32)
    spread = (step_x * step_x + step_y * step_y).astype(jnp.float32)
    shaped = jnp.maximum(1.0 - spread / (reach * reach)[:, None], 0.0)
    return jnp.where(inside, picked.astype(jnp.float32), 0.0) * shaped


def obs_places(obs_map, tiles_x, tiles_y):
    place_x = tiles_x[:, None, None] * BLK_X + obs_map // BLK_Y
    place_y = tiles_y[None, :, None] * BLK_Y + obs_map % BLK_Y
    return (place_x.reshape(-1), place_y.reshape(-1))


def contribution(anomaly, d_set, z_set, obs_map, tiles_x, tiles_y, own_x, own_y, radius, pattern):
    members = anomaly.shape[0]
    blocks = own_x.shape[0]
    place_x, place_y = obs_places(obs_map, tiles_x, tiles_y)
    weights = tapers(radius, pattern, own_x, own_y, place_x, place_y) / (members - 1)
    cross = lax.dot_general(
        anomaly, d_set, (((0,), (2,)), ((), ())), preferred_element_type=jnp.float32
    )
    complete_extent = cross.shape
    gain = (
        (cross.reshape(blocks, -1, weights.shape[1]) * weights[:, None, :])
        .reshape(complete_extent)
        .astype(jnp.bfloat16)
    )
    return lax.dot_general(
        z_set, gain, (((0, 1, 3), (1, 2, 3)), ((), ())), preferred_element_type=jnp.float32
    )


def weigh(d_tile, observation_residual, variance, obs_map):
    members = d_tile.shape[0]
    gram = jnp.dot(d_tile.T, d_tile, preferred_element_type=jnp.float32) / (members - 1)
    same = obs_map[:, None] == obs_map[None, :]
    system = jnp.where(same, gram, 0.0) + jnp.diag(variance)
    factor = jnp.linalg.cholesky(system)
    solved = jax.scipy.linalg.cho_solve((factor, True), observation_residual.T)
    return solved.T.astype(jnp.bfloat16)


def per_device(
    params,
    predicted,
    measured_value,
    measurement_variance,
    observation_jitter,
    obs_block,
    taper_radius,
    taper_pattern,
):
    members = params.shape[0]
    blocks = BLK_X * BLK_Y
    tile_x = lax.axis_index("gx")
    tile_y = lax.axis_index("gy")
    block_mean = jnp.mean(params.astype(jnp.float32), axis=0, keepdims=True)
    anomaly = (
        (params.astype(jnp.float32) - block_mean)
        .astype(jnp.bfloat16)
        .reshape(members, blocks * CELLS)
    )
    prior_state = predicted[0, 0]
    predicted_deviation = (prior_state - jnp.mean(prior_state, axis=0, keepdims=True)).astype(
        jnp.bfloat16
    )
    observation_residual = (
        measured_value[0, 0][None, :]
        + jnp.sqrt(measurement_variance[0, 0])[None, :] * observation_jitter[0, 0]
        - prior_state
    )
    map_pad = jnp.pad(obs_block, ((1, 1), (1, 1), (0, 0)))
    near_map = lax.dynamic_slice(map_pad, (tile_x, tile_y, jnp.int32(0)), (3, 3, OBS_TILE))
    weighted = weigh(
        predicted_deviation, observation_residual, measurement_variance[0, 0], near_map[1, 1]
    )
    stacked = jnp.stack([predicted_deviation, weighted])[None, None]
    radius = taper_radius.reshape(blocks)
    pattern = taper_pattern.reshape(blocks, PATTERN)
    local_ids = jnp.arange(blocks, dtype=jnp.int32)
    own_x = tile_x * BLK_X + local_ids // BLK_Y
    own_y = tile_y * BLK_Y + local_ids % BLK_Y
    adjacent_everything = jnp.arange(3, dtype=jnp.int32) - 1
    centre_x = tile_x + adjacent_everything
    centre_y = tile_y + adjacent_everything
    near = with_halo(stacked, (("gx", 0), ("gy", 1)), 1)
    delta = contribution(
        anomaly,
        near[:, :, 0],
        near[:, :, 1],
        near_map,
        centre_x,
        centre_y,
        own_x,
        own_y,
        radius,
        pattern,
    )
    updated = (params.astype(jnp.float32) + delta.reshape(members, BLK_X, BLK_Y, CELLS)).astype(
        jnp.bfloat16
    )
    return lax.all_to_all(updated, "gy", split_axis=0, concat_axis=2, tiled=True)


def solution(mesh):
    placed = (
        P(None, "gx", "gy", None),
        P("gx", "gy", None, None),
        P("gx", "gy", None),
        P("gx", "gy", None),
        P("gx", "gy", None, None),
        P(),
        P("gx", "gy"),
        P("gx", "gy", None),
    )
    return jax.shard_map(
        per_device, mesh=mesh, in_specs=placed, out_specs=P("gy", "gx", None, None), check_vma=False
    )
```

profile of v0, /device:TPU:0, one launch (start us, length us, event | category | flops | bytes accessed | tf_op | source)
XLA Modules:
  0.0 71.0 jit_solution(15916581285482014969)
XLA Ops:
  0.0 0.0 copy-start
  0.0 0.7 bitcast_sqrt_fusion
  0.7 0.9 %copy.42 = f32[1,1,128,128]{2,3,1,0:T(8,128)S(1)} copy(f32[1,1,128,128]{3,2,1,0:T(8,128)} %param.9) | data formatting | bytes 131072 | tf_op args[1]
  1.6 0.9 %reduce_sum.27 = f32[128]{0:T(128)S(1)} reduce(f32[1,1,128,128]{3,2,1,0:T(8,128)} %param.9, f32[]{:T(128)} %constant.117.clone.1), dimensions={0,1,2}, to_apply=%region_0.0 | reduce | flops 16256 | bytes 66052 | tf_op jit(solution)/shard_map/reduce_sum | solution.py:99
  2.5 0.7 fusion.39
  3.2 0.1 broadcast_compare_fusion
  3.3 0.1 copy.46
  3.4 1.1 %compare_select_fusion = (f32[128,128]{0,1:T(8,128)S(1)}, f32[128,128]{0,1:T(8,128)S(1)}) fusion(s32[128]{0:T(128)S(1)} %fusion.39, f32[1,1,128,128]{3,2,1,0:T(8,128)} %param.9, f32[128]{0:T(128)S(1)} %broadcast_multiply_fusion.1), kind=kOutput, calls=%fused_computation.43 | convolution fusion | flops 4276224 | bytes 197632 | tf_op jit(solution)/shard_map/dot_general | solution.py:70
  4.6 0.1 fusion.13
  4.7 0.1 copy.45
  4.8 0.8 %fusion.12 = f32[128,128]{1,0:T(8,128)S(1)} fusion(pred[128,128]{1,0:T(8,128)(4,1)S(1)} %copy.46, f32[128,128]{0,1:T(8,128)S(1)} %get-tuple-element.8, f32[128,128]{1,0:T(8,128)S(1)} %copy.45, f32[128]{0:T(128)} %bitcast.76), kind=kLoop, calls=%fused_computation.32 | loop fusion | flops 147456 | bytes 213504 | tf_op jit(solution)/shard_map/jit(cholesky)/div | solution.py:73
  5.6 11.7 %cholesky.16 = f32[128,128]{1,0:T(8,128)S(1)} custom-call(f32[128,128]{1,0:T(8,128)S(1)} %fusion.12), custom_call_target="Cholesky" | custom-call | tf_op jit(solution)/shard_map/jit(cholesky)/cholesky | solution.py:73
  17.3 0.6 compare_reduce_fusion
  18.0 0.7 fusion.5
  18.6 9.8 %custom-call.10 = f32[1,128,128]{1,2,0:T(8,128)S(1)} custom-call(f32[1,128,128]{2,1,0:T(8,128)S(1)} %fusion.5), custom_call_target="InvertDiagBlocksLowerTriangular" | custom-call | tf_op jit(solution)/shard_map/jit(_cho_solve)/triangular_solve | solution.py:74
  28.5 1.2 %fusion.6 = f32[128,128]{1,0:T(8,128)S(1)} fusion(f32[1,128,128]{1,2,0:T(8,128)S(1)} %custom-call.10, f32[1,1,128,128]{3,2,1,0:T(8,128)} %param.9, f32[1,1,128,128]{3,2,1,0:T(8,128)} %param.12, f32[128]{0:T(128)S(1)} %bitcast_sqrt_fusion, f32[128]{0:T(128)} %bitcast.77), kind=kOutput, calls=%fused_computation.25 | convolution fusion | flops 25214976 | bytes 263168 | tf_op jit(solution)/shard_map/jit(_cho_solve)/triangular_solve | solution.py:74
  29.6 0.2 fusion.3
  29.9 1.3 %collective-permute-start.1 = (bf16[1,1,2,128,128]{3,4,2,1,0:T(8,128)(2,1)S(1)}, bf16[1,1,2,128,128]{3,4,2,1,0:T(8,128)(2,1)S(1)}, u32[]{:S(2)}, u32[]{:S(2)}) collective-permute-start(bf16[1,1,2,128,128]{3,4,2,1,0:T(8,128)(2,1)S(1)} %maximum_bitcast_fusion), channel_id=1, source_target_pairs={{8,0},{16,8},{24,16},{9,1},{17,9},{25,17},{10,2},{18,10},{26,18},{... | collective-permute-start | bytes 196616 | tf_op jit(solution)/shard_map/ppermute | solution.py:23
  31.2 5.5 %collective-permute-start = (bf16[1,1,2,128,128]{3,4,2,1,0:T(8,128)(2,1)S(1)}, bf16[1,1,2,128,128]{3,4,2,1,0:T(8,128)(2,1)S(1)}, u32[]{:S(2)}, u32[]{:S(2)}) collective-permute-start(bf16[1,1,2,128,128]{3,4,2,1,0:T(8,128)(2,1)S(1)} %maximum_bitcast_fusion), channel_id=1, source_target_pairs={{0,8},{8,16},{16,24},{1,9},{9,17},{17,25},{2,10},{10,18},{18,26},{... | collective-permute-start | bytes 196616 | tf_op jit(solution)/shard_map/ppermute | solution.py:21
  36.7 0.7 convert_multiply_fusion
  37.3 0.1 mul.91
  37.4 1.0 %convert_reduce_fusion = f32[2,4,128]{2,1,0:T(4,128)S(1)} fusion(bf16[128,2,4,128]{3,2,1,0:T(4,128)(2,1)} %param.8), kind=kLoop, calls=%fused_computation.11 | loop fusion | flops 261120 | bytes 266240 | tf_op jit(solution)/shard_map/reduce_sum | solution.py:92
  38.4 0.9 %fusion.34 = (s32[3,3,128]{2,1,0:T(4,128)S(1)}, s32[3,3,128]{2,1,0:T(4,128)S(1)}) fusion(s32[3]{0:T(128)S(1)} %get-tuple-element.12, s32[]{:T(128)S(6)} %select_n.68, s32[]{:T(128)S(6)} %select_n.69, s32[4,8,128]{2,1,0:T(8,128)} %param.13, s32[3]{0:T(128)S(1)} %get-tuple-element.11), kind=kLoop, calls=%fused_computation.68 | loop fusion | flops 32256 | bytes 25632 | tf_op jit(solution)/shard_map/add | solution.py:44
  39.3 0.8 %copy.48 = s32[8,25]{0,1:T(8,128)S(1)} copy(s32[8,25]{1,0:T(8,128)} %bitcast.75) | data formatting | bytes 1600 | tf_op jit(solution)/shard_map/jit(_where)/broadcast_in_dim | solution.py:36
  40.1 0.1 fusion.19
  40.1 0.2 select_reduce_fusion
  40.3 0.1 fusion.26
  40.4 0.0 collective-permute-done.1
  40.4 0.0 collective-permute-done
  40.5 1.3 %collective-permute-start.3 = (bf16[3,1,2,128,128]{3,4,2,1,0:T(8,128)(2,1)S(1)}, bf16[3,1,2,128,128]{3,4,2,1,0:T(8,128)(2,1)S(1)}, u32[]{:S(2)}, u32[]{:S(2)}) collective-permute-start(bf16[3,1,2,128,128]{3,4,2,1,0:T(8,128)(2,1)S(1)} %pad_maximum_fusion.1), channel_id=1, source_target_pairs={{1,0},{2,1},{3,2},{4,3},{5,4},{6,5},{7,6},{9,8},{10,9},{11,10},{12... | collective-permute-start | bytes 589832 | tf_op jit(solution)/shard_map/ppermute | solution.py:23
  41.8 3.0 %collective-permute-start.2 = (bf16[3,1,2,128,128]{3,4,2,1,0:T(8,128)(2,1)S(1)}, bf16[3,1,2,128,128]{3,4,2,1,0:T(8,128)(2,1)S(1)}, u32[]{:S(2)}, u32[]{:S(2)}) collective-permute-start(bf16[3,1,2,128,128]{3,4,2,1,0:T(8,128)(2,1)S(1)} %pad_maximum_fusion.1), channel_id=1, source_target_pairs={{0,1},{1,2},{2,3},{3,4},{4,5},{5,6},{6,7},{8,9},{9,10},{10,11},{11... | collective-permute-start | bytes 589832 | tf_op jit(solution)/shard_map/ppermute | solution.py:21
  44.8 0.0 copy-done
  44.8 0.1 fusion.4
  44.9 0.2 copy.47
  45.1 0.0 collective-permute-done.3
  45.1 0.8 %collective-permute-done.2 = bf16[3,1,2,128,128]{3,4,2,1,0:T(8,128)(2,1)S(1)} collective-permute-done((bf16[3,1,2,128,128]{3,4,2,1,0:T(8,128)(2,1)S(1)}, bf16[3,1,2,128,128]{3,4,2,1,0:T(8,128)(2,1)S(1)}, u32[]{:S(2)}, u32[]{:S(2)}) %collective-permute-start.2) | collective-permute-done | bytes 196640 | tf_op jit(solution)/shard_map/ppermute | solution.py:21
  45.9 0.1 pad_maximum_fusion
  46.0 0.8 %fusion = bf16[8,128,1152]{2,1,0:T(8,128)(2,1)S(1)} fusion(bf16[8,128,128]{2,1,0:T(8,128)(2,1)S(1)} %bitcast.73, bf16[1152,128,1]{1,0,2:T(8,128)(2,1)S(1)} %bitcast.72, f32[8,1152]{1,0:T(8,128)S(1)} %fusion.26), kind=kOutput, calls=%fused_computation.1 | convolution fusion | flops 304349184 | bytes 2953216 | tf_op jit(solution)/shard_map/dot_general | solution.py:54
  46.7 2.5 %copy.49 = bf16[8,128,1152]{1,2,0:T(8,128)(2,1)} copy(bf16[8,128,1152]{2,1,0:T(8,128)(2,1)S(1)} %fusion) | data formatting | bytes 4718592 | tf_op jit(solution)/shard_map/convert_element_type | solution.py:61
  49.3 2.2 %fusion.2 = bf16[128,2,4,128]{3,0,2,1:T(8,128)(2,1)S(1)} fusion(bf16[2,4,128,3,3,128]{2,5,4,3,1,0:T(8,128)(2,1)} %bitcast.71, bf16[3,3,2,128,128]{3,4,2,1,0:T(8,128)(2,1)S(1)} %pad_maximum_fusion, bf16[128,2,4,128]{3,2,1,0:T(4,128)(2,1)S(1)} %copy-done), kind=kOutput, calls=%fused_computation.4 | convolution fusion | flops 302383104 | bytes 3178496 | tf_op jit(solution)/shard_map/dot_general | solution.py:63
  51.5 0.2 copy.52
  51.7 18.5 %all_to_all.18 = bf16[128,2,4,128]{3,2,1,0:T(4,128)(2,1)S(1)} all-to-all(bf16[128,2,4,128]{3,2,1,0:T(4,128)(2,1)S(1)} %copy.52), channel_id=1, replica_groups=mesh['gx'=4,'gy'=8] {'gy'}, dimensions={0} | all-to-all | bytes 524288 | tf_op jit(solution)/shard_map/all_to_all | solution.py:137
  70.2 0.8 %copy.53 = bf16[16,2,8,4,128]{4,3,2,1,0:T(4,128)(2,1)} copy(bf16[16,2,8,4,128]{4,3,1,0,2:T(4,128)(2,1)S(1)} %bitcast.74) | data formatting | bytes 524288 | tf_op jit(solution)/shard_map/all_to_all | solution.py:137
  (10 shorter events, 0.1 us)
Async XLA Ops:
  0.0 44.8 %copy-start = (bf16[128,2,4,128]{3,2,1,0:T(4,128)(2,1)S(1)}, bf16[128,2,4,128]{3,2,1,0:T(4,128)(2,1)}, u32[]{:S(2)}) copy-start(bf16[128,2,4,128]{3,2,1,0:T(4,128)(2,1)} %param.8) | copy-start | bytes 786436
  29.9 10.6 %collective-permute-start.1 = (bf16[1,1,2,128,128]{3,4,2,1,0:T(8,128)(2,1)S(1)}, bf16[1,1,2,128,128]{3,4,2,1,0:T(8,128)(2,1)S(1)}, u32[]{:S(2)}, u32[]{:S(2)}) collective-permute-start(bf16[1,1,2,128,128]{3,4,2,1,0:T(8,128)(2,1)S(1)} %maximum_bitcast_fusion), channel_id=1, source_target_pairs={{8,0},{16,8},{24,16},{9,1},{17,9},{25,17},{10,2},{18,10},{26,18},{... | collective-permute-start | bytes 196616 | tf_op jit(solution)/shard_map/ppermute | solution.py:23
  31.2 9.3 %collective-permute-start = (bf16[1,1,2,128,128]{3,4,2,1,0:T(8,128)(2,1)S(1)}, bf16[1,1,2,128,128]{3,4,2,1,0:T(8,128)(2,1)S(1)}, u32[]{:S(2)}, u32[]{:S(2)}) collective-permute-start(bf16[1,1,2,128,128]{3,4,2,1,0:T(8,128)(2,1)S(1)} %maximum_bitcast_fusion), channel_id=1, source_target_pairs={{0,8},{8,16},{16,24},{1,9},{9,17},{17,25},{2,10},{10,18},{18,26},{... | collective-permute-start | bytes 196616 | tf_op jit(solution)/shard_map/ppermute | solution.py:21
  40.5 4.6 %collective-permute-start.3 = (bf16[3,1,2,128,128]{3,4,2,1,0:T(8,128)(2,1)S(1)}, bf16[3,1,2,128,128]{3,4,2,1,0:T(8,128)(2,1)S(1)}, u32[]{:S(2)}, u32[]{:S(2)}) collective-permute-start(bf16[3,1,2,128,128]{3,4,2,1,0:T(8,128)(2,1)S(1)} %pad_maximum_fusion.1), channel_id=1, source_target_pairs={{1,0},{2,1},{3,2},{4,3},{5,4},{6,5},{7,6},{9,8},{10,9},{11,10},{12... | collective-permute-start | bytes 589832 | tf_op jit(solution)/shard_map/ppermute | solution.py:23
  41.8 4.1 %collective-permute-start.2 = (bf16[3,1,2,128,128]{3,4,2,1,0:T(8,128)(2,1)S(1)}, bf16[3,1,2,128,128]{3,4,2,1,0:T(8,128)(2,1)S(1)}, u32[]{:S(2)}, u32[]{:S(2)}) collective-permute-start(bf16[3,1,2,128,128]{3,4,2,1,0:T(8,128)(2,1)S(1)} %pad_maximum_fusion.1), channel_id=1, source_target_pairs={{0,1},{1,2},{2,3},{3,4},{4,5},{5,6},{6,7},{8,9},{9,10},{10,11},{11... | collective-permute-start | bytes 589832 | tf_op jit(solution)/shard_map/ppermute | solution.py:21
where the time goes:
time: 71.6 us; the launch traced here: 71 us
  other arithmetic  27.8 us (39%)
  blocking collectives  18.5 us (26%)
  starting transfers between devices  11.1 us (16%)
  local copies, waits for them, and re-layouts  7.17 us (10%)
  matrix products  5.47 us (8%)
  waiting for transfers between devices  0.78 us (1%)
    all_to_all x1, blocking collectives, per_device(): lax.all_to_all(updated, 'gy', split_axis=0, concat_axis=2, tiled=True)  18.5 us
    another operation x3, other arithmetic, weigh(): factor = jnp.linalg.cholesky(system)  12.4 us
    another operation x2, other arithmetic, weigh(): solved = jax.scipy.linalg.cho_solve((factor, True), observation_residual.T)  10.5 us
    ppermute x2, starting transfers between devices, with_halo(): lax.ppermute(tail, axis, [(i, (i + 1) % count) for i in range(ends)])  8.52 us
    ppermute x2, starting transfers between devices, with_halo(): lax.ppermute(head, axis, [((i + 1) % count, i) for i in range(ends)])  2.58 us
    convert_element_type x1, local copies, waits for them, and re-layouts, contribution(): gain = (cross.reshape(blocks, -1, weights.shape[1]) * weights[:, None, :]...  2.51 us
    dot_general x1, matrix products, contribution(): lax.dot_general(z_set, gain, (((0, 1, 3), (1, 2, 3)), ((), ())), preferre...  2.2 us
  transfers between devices with their start and end apart: 4, of which 1 were waited for; matrix products, arithmetic and copies ran while one was open for 6% of the time, Pallas kernels for 0%

commit v1 on v0

v1 whole, which is shorter than its diff:
```python
import functools

import jax
import jax.numpy as jnp
from jax import lax
from jax.experimental import pallas as pl
from jax.experimental.pallas import tpu as pltpu
from jax.sharding import PartitionSpec as P

CELLS = 128
BLK_X = 2
BLK_Y = 4
BLOCKS = BLK_X * BLK_Y
OBS_TILE = 128
PATTERN = 25
SMALL = 32

F32 = jnp.float32
BF16 = jnp.bfloat16


def iota(shape, dim):
    return lax.broadcasted_iota(jnp.int32, shape, dim)


def split3(x):
    high = x.astype(BF16)
    rest = x - high.astype(F32)
    mid = rest.astype(BF16)
    low = (rest - mid.astype(F32)).astype(BF16)
    return high, mid, low


def dot(a, b, dims, precision=None):
    return lax.dot_general(a, b, ((dims[0], dims[1]), ((), ())), precision=precision, preferred_element_type=F32)


def sweep(rows, count, x_ref, idx_ref, rank, size):
    row = iota((rows, OBS_TILE), 0)
    exists = row < size

    def step(t):
        x = x_ref[0:rows, :]
        pivot_row = x_ref[pl.ds(t, 1), :]
        spread = jnp.broadcast_to(pivot_row, (rows, OBS_TILE))
        column = jnp.take_along_axis(spread, idx_ref[0:rows, :], axis=1, mode="promise_in_bounds")
        column = jnp.where(exists, column, 0.0)
        at = jnp.broadcast_to(idx_ref[pl.ds(t, 1), :], (8, OBS_TILE))
        pivot = jnp.take_along_axis(spread[0:8], at, axis=1, mode="promise_in_bounds")[0:1]
        pivot = jnp.where(t < size, pivot, 1.0)
        own = rank == t
        scaled = jnp.where(own, -1.0, pivot_row) / pivot
        at_row = row == t
        column = jnp.where(at_row, -1.0, column)
        x_ref[0:rows, :] = jnp.where(at_row | own, 0.0, x) - column * scaled

    def pair(k, carry):
        step(2 * k)
        step(2 * k + 1)
        return carry

    lax.fori_loop(0, (count + 1) // 2, pair, 0)


def weigh_kernel(pred_ref, mv_ref, var_ref, jit_ref, obs_ref, out_ref, x_ref, idx_ref, full_ref):
    members = pred_ref.shape[2]
    tile_x = lax.axis_index("gx")
    tile_y = lax.axis_index("gy")
    square = (OBS_TILE, OBS_TILE)
    pred = pred_ref[0, 0]
    var = var_ref[0]
    mean = jnp.sum(pred, axis=0, keepdims=True) / members
    deviation = (pred - mean).astype(BF16)
    out_ref[0] = deviation
    obs = obs_ref[tile_x, pl.ds(tile_y, 1), :]
    groups = (iota((BLOCKS, OBS_TILE), 0) == obs).astype(BF16)
    same = dot(groups, groups, ((0,), (0,)))
    gram = dot(deviation, deviation, ((0,), (0,))) / (members - 1)
    row, col = iota(square, 0), iota(square, 1)
    system = jnp.where(same > 0.5, gram, 0.0) + jnp.where(row == col, var, 0.0)
    size = jnp.sum(same, axis=0, keepdims=True)
    count = jnp.max(size).astype(jnp.int32)
    size = size.astype(jnp.int32)
    rank = jnp.sum(jnp.where(row < col, same, 0.0), axis=0, keepdims=True).astype(jnp.int32)
    place = row == rank
    hot = place.astype(BF16)
    high, mid, low = split3(system)
    x_ref[...] = (
        dot(hot, low, ((1,), (0,))) + dot(hot, mid, ((1,), (0,))) + dot(hot, high, ((1,), (0,)))
    )
    numbered = jnp.where(place, col, 0).astype(F32).astype(BF16)
    idx_ref[...] = dot(numbered, same.astype(BF16), ((1,), (0,))).astype(jnp.int32)

    def solve(rows):
        sweep(rows, count, x_ref, idx_ref, rank, size)
        high, mid, low = split3(x_ref[0:rows, :])
        taken = hot[0:rows]
        full = dot(taken, low, ((0,), (0,))) + dot(taken, mid, ((0,), (0,))) + dot(taken, high, ((0,), (0,)))
        full_ref[...] = jnp.where(same > 0.5, -full, 0.0)

    @pl.when(count <= SMALL)
    def _():
        solve(SMALL)

    @pl.when(count > SMALL)
    def _():
        solve(OBS_TILE)

    innovation = mv_ref[0] + jnp.sqrt(var) * jit_ref[0, 0] - pred
    weighted = dot(innovation, full_ref[...], ((1,), (0,)), lax.Precision.HIGHEST)
    out_ref[1] = weighted.astype(BF16)


def weigh(predicted, measured_value, measurement_variance, observation_jitter, obs_block):
    members = predicted.shape[2]
    return pl.pallas_call(
        weigh_kernel,
        out_shape=jax.ShapeDtypeStruct((2, members, OBS_TILE), BF16),
        in_specs=[pl.BlockSpec(memory_space=pltpu.VMEM)] * 5,
        out_specs=pl.BlockSpec(memory_space=pltpu.VMEM),
        scratch_shapes=[
            pltpu.VMEM((OBS_TILE, OBS_TILE), F32),
            pltpu.VMEM((OBS_TILE, OBS_TILE), jnp.int32),
            pltpu.VMEM((OBS_TILE, OBS_TILE), F32),
        ],
        compiler_params=pltpu.CompilerParams(vmem_limit_bytes=16 * 2**20),
        name="weigh",
    )(predicted, measured_value, measurement_variance, observation_jitter, obs_block)


def prepare_kernel(params_ref, radius_ref, pattern_ref, obs_ref, turned_ref, taper_ref):
    members = params_ref.shape[1]
    tile_x = lax.axis_index("gx")
    tile_y = lax.axis_index("gy")
    count_x, count_y = obs_ref.shape[0], obs_ref.shape[1]
    for b in range(BLOCKS):
        block = params_ref[b].astype(F32)
        mean = jnp.sum(block, axis=0, keepdims=True) / members
        anomaly = block - mean
        turned_ref[b] = anomaly.T.astype(BF16)

    shape = (BLOCKS, OBS_TILE)
    block = iota(shape, 0)
    radius = jnp.zeros(shape, jnp.int32)
    for b in range(BLOCKS):
        radius = jnp.where(block == b, radius_ref[b // BLK_Y, b % BLK_Y], radius)
    reach = (radius + 1).astype(F32)
    reach = reach * reach
    pattern = pattern_ref[...].astype(F32)
    slots = [jnp.broadcast_to(pattern[:, p : p + 1], shape) for p in range(PATTERN)]
    for dx in range(3):
        for dy in range(3):
            at_x, at_y = tile_x + (dx - 1), tile_y + (dy - 1)
            valid = (at_x >= 0) & (at_x < count_x) & (at_y >= 0) & (at_y < count_y)
            at_x = jnp.clip(at_x, 0, count_x - 1)
            at_y = jnp.clip(at_y, 0, count_y - 1)
            obs = obs_ref[at_x, pl.ds(at_y, 1), :]
            step_x = (dx - 1) * BLK_X + (obs >> 2) - (block >> 2)
            step_y = (dy - 1) * BLK_Y + (obs & 3) - (block & 3)
            inside = (jnp.abs(step_x) <= 2) & (jnp.abs(step_y) <= 2) & valid
            offset = (step_x + 2) * 5 + (step_y + 2)
            picked = jnp.zeros(shape, F32)
            for p in range(PATTERN):
                picked = jnp.where(offset == p, slots[p], picked)
            spread = (step_x * step_x + step_y * step_y).astype(F32)
            shaped = jnp.maximum(1.0 - spread / reach, 0.0)
            taper_ref[dx * 3 + dy] = jnp.where(inside, picked, 0.0) * shaped / (members - 1)


def prepare(by_block, taper_radius, taper_pattern, obs_block):
    members = by_block.shape[1]
    return pl.pallas_call(
        prepare_kernel,
        out_shape=(
            jax.ShapeDtypeStruct((BLOCKS, CELLS, members), BF16),
            jax.ShapeDtypeStruct((9, BLOCKS, OBS_TILE), F32),
        ),
        in_specs=[
            pl.BlockSpec(memory_space=pltpu.VMEM),
            pl.BlockSpec(memory_space=pltpu.SMEM),
            pl.BlockSpec(memory_space=pltpu.VMEM),
            pl.BlockSpec(memory_space=pltpu.VMEM),
        ],
        out_specs=(pl.BlockSpec(memory_space=pltpu.VMEM), pl.BlockSpec(memory_space=pltpu.VMEM)),
        compiler_params=pltpu.CompilerParams(vmem_limit_bytes=16 * 2**20),
        cost_estimate=pl.CostEstimate(flops=4_000_000, bytes_accessed=1_000_000, transcendentals=0),
        name="prepare",
    )(by_block, taper_radius, taper_pattern.reshape(BLOCKS, PATTERN), obs_block)


def update_kernel(params_ref, turned_ref, taper_ref, own_ref, low_ref, high_ref, out_ref):
    share = out_ref.shape[2]
    near = [ref.at[dx] for dx in range(3) for ref in (low_ref, own_ref, high_ref)]
    deviations = jnp.concatenate([tile[0] for tile in near], axis=1)
    weighted = jnp.concatenate([tile[1] for tile in near], axis=1)

    def one(b, carry):
        cross = dot(turned_ref[b], deviations, ((1,), (0,)))
        taper = jnp.concatenate([taper_ref[t, pl.ds(b, 1), :] for t in range(9)], axis=1)
        gain = (cross * taper).astype(BF16)
        delta = dot(weighted, gain, ((1,), (1,)))
        updated = (params_ref[b].astype(F32) + delta).astype(BF16)
        for d in range(out_ref.shape[0]):
            out_ref[d, b] = updated[d * share : (d + 1) * share]
        return carry

    lax.fori_loop(0, BLOCKS, one, 0, unroll=True)


def update(by_block, turned, taper, own, low, high, parts):
    members = by_block.shape[1]
    return pl.pallas_call(
        update_kernel,
        out_shape=jax.ShapeDtypeStruct((parts, BLOCKS, members // parts, CELLS), BF16),
        in_specs=[pl.BlockSpec(memory_space=pltpu.VMEM)] * 6,
        out_specs=pl.BlockSpec(memory_space=pltpu.VMEM),
        compiler_params=pltpu.CompilerParams(vmem_limit_bytes=40 * 2**20),
        name="update",
    )(by_block, turned, taper, own, low, high)


def neighbours(block, axis):
    count = lax.axis_size(axis)
    low = lax.ppermute(block, axis, [(i, i + 1) for i in range(count - 1)])
    high = lax.ppermute(block, axis, [(i + 1, i) for i in range(count - 1)])
    return low, high


def per_device(
    params,
    predicted,
    measured_value,
    measurement_variance,
    observation_jitter,
    obs_block,
    taper_radius,
    taper_pattern,
):
    members = params.shape[0]
    parts = lax.axis_size("gy")
    by_block = params.reshape(members, BLOCKS, CELLS).transpose(1, 0, 2)
    own = weigh(predicted, measured_value, measurement_variance, observation_jitter, obs_block)
    low_x, high_x = neighbours(own, "gx")
    turned, taper = prepare(by_block, taper_radius, taper_pattern, obs_block)
    column = jnp.stack([low_x, own, high_x])
    low, high = neighbours(column, "gy")
    updated = update(by_block, turned, taper, column, low, high, parts)
    arrived = lax.all_to_all(updated, "gy", split_axis=0, concat_axis=0, tiled=True)
    share = members // parts
    arrived = arrived.reshape(parts, BLK_X, BLK_Y, share, CELLS).transpose(3, 1, 0, 2, 4)
    return arrived.reshape(share, BLK_X, parts * BLK_Y, CELLS)


def solution(mesh):
    placed = (
        P(None, "gx", "gy", None),
        P("gx", "gy", None, None),
        P("gx", "gy", None),
        P("gx", "gy", None),
        P("gx", "gy", None, None),
        P(),
        P("gx", "gy"),
        P("gx", "gy", None),
    )
    return jax.shard_map(
        per_device, mesh=mesh, in_specs=placed, out_specs=P("gy", "gx", None, None), check_vma=False
    )
```

time: 71.6 us -> 43.5 us (0.61)
  the two profiles are of different devices: /device:TPU:0 before, /device:TPU:4 now
where the time goes in v1:
time: 43.5 us; the launch traced here: 43.1 us
  blocking collectives  17.2 us (40%)
  starting transfers between devices  10.2 us (23%)
  Pallas kernels  5.97 us (14%)
  local copies, waits for them, and re-layouts  5.24 us (12%)
  waiting for transfers between devices  4.38 us (10%)
    all_to_all x1, blocking collectives, per_device(): lax.all_to_all(updated, 'gy', split_axis=0, concat_axis=0, tiled=True)  17.2 us
    ppermute x2, starting transfers between devices, neighbours(): low = lax.ppermute(block, axis, [(i, i + 1) for i in range(count - 1)])  5.71 us
    ppermute x2, starting transfers between devices, neighbours(): high = lax.ppermute(block, axis, [(i + 1, i) for i in range(count - 1)])  4.46 us
    unnamed x17, local copies, waits for them, and re-layouts  4.42 us
    ppermute x2, waiting for transfers between devices, neighbours(): low = lax.ppermute(block, axis, [(i, i + 1) for i in range(count - 1)])  4.08 us
    pallas_call x1, Pallas kernels, weigh(): pl.pallas_call(weigh_kernel, out_shape=jax.ShapeDtypeStruct((2, members,...  3.03 us
    pallas_call x1, Pallas kernels, update(): pl.pallas_call(update_kernel, out_shape=jax.ShapeDtypeStruct((parts, BLOC...  2.1 us
  transfers between devices with their start and end apart: 4, of which 2 were waited for; matrix products, arithmetic and copies ran while one was open for 0% of the time, Pallas kernels for 2%

profile of v1, /device:TPU:4, one launch (start us, length us, event | category | flops | bytes accessed | tf_op | source)
XLA Modules:
  0.0 43.1 jit_solution(12210610404763535662)
XLA Ops:
  0.0 0.0 copy-start
  0.0 0.8 %copy-done = f32[1,1,128,128]{3,2,1,0:T(8,128)S(1)} copy-done((f32[1,1,128,128]{3,2,1,0:T(8,128)S(1)}, f32[1,1,128,128]{3,2,1,0:T(8,128)}, u32[]{:S(2)}) %copy-start) | copy-done | bytes 65560
  0.8 0.0 copy-start.1
  0.8 0.8 %copy-done.1 = f32[1,1,128,128]{3,2,1,0:T(8,128)S(1)} copy-done((f32[1,1,128,128]{3,2,1,0:T(8,128)S(1)}, f32[1,1,128,128]{3,2,1,0:T(8,128)}, u32[]{:S(2)}) %copy-start.1) | copy-done | bytes 65560
  1.7 0.0 copy-start.2
  1.7 0.7 %copy-done.2 = s32[4,8,128]{2,1,0:T(8,128)S(1)} copy-done((s32[4,8,128]{2,1,0:T(8,128)S(1)}, s32[4,8,128]{2,1,0:T(8,128)}, u32[]{:S(2)}) %copy-start.2) | copy-done | bytes 16408
  2.4 0.0 copy-start.5
  2.4 0.7 %copy-done.5 = f32[1,1,128]{2,1,0:T(1,128)S(1)} copy-done((f32[1,1,128]{2,1,0:T(1,128)S(1)}, f32[1,1,128]{2,1,0:T(1,128)}, u32[]{:S(2)}) %copy-start.5) | copy-done | bytes 536
  3.1 0.0 copy-start.6
  3.1 0.7 %copy-done.6 = f32[1,1,128]{2,1,0:T(1,128)S(1)} copy-done((f32[1,1,128]{2,1,0:T(1,128)S(1)}, f32[1,1,128]{2,1,0:T(1,128)}, u32[]{:S(2)}) %copy-start.6) | copy-done | bytes 536
  3.7 0.0 copy-start.7
  3.7 3.0 %weigh.1 = bf16[2,128,128]{2,1,0:T(8,128)(2,1)S(1)} custom-call(f32[1,1,128,128]{3,2,1,0:T(8,128)S(1)} %copy-done, f32[1,1,128]{2,1,0:T(1,128)S(1)} %copy-done.5, f32[1,1,128]{2,1,0:T(1,128)S(1)} %copy-done.6, f32[1,1,128,128]{3,2,1,0:T(8,128)S(1)} %copy-done.1, s32[4,8,128]{2,1,0:T(8,128)S(1)} %copy-done.2), custom_call_target="tpu_custom_call" | custom-call | tf_op jit(solution)/shard_map/weigh/pallas_call | solution.py:116
  6.8 3.2 %collective-permute-start.1 = (bf16[2,128,128]{2,1,0:T(8,128)(2,1)S(1)}, bf16[2,128,128]{2,1,0:T(8,128)(2,1)S(1)}, u32[]{:S(2)}, u32[]{:S(2)}) collective-permute-start(bf16[2,128,128]{2,1,0:T(8,128)(2,1)S(1)} %weigh.1), channel_id=1, source_target_pairs={{8,0},{16,8},{24,16},{9,1},{17,9},{25,17},{10,2},{18,10},{26,18},{... | collective-permute-start | bytes 196616 | tf_op jit(solution)/shard_map/ppermute | solution.py:225
  9.9 2.7 %collective-permute-start = (bf16[2,128,128]{2,1,0:T(8,128)(2,1)S(1)}, bf16[2,128,128]{2,1,0:T(8,128)(2,1)S(1)}, u32[]{:S(2)}, u32[]{:S(2)}) collective-permute-start(bf16[2,128,128]{2,1,0:T(8,128)(2,1)S(1)} %weigh.1), channel_id=1, source_target_pairs={{0,8},{8,16},{16,24},{1,9},{9,17},{17,25},{2,10},{10,18},{18,26},{... | collective-permute-start | bytes 196616 | tf_op jit(solution)/shard_map/ppermute | solution.py:224
  12.6 0.3 collective-permute-done.1
  12.9 4.1 %collective-permute-done = bf16[2,128,128]{2,1,0:T(8,128)(2,1)S(1)} collective-permute-done((bf16[2,128,128]{2,1,0:T(8,128)(2,1)S(1)}, bf16[2,128,128]{2,1,0:T(8,128)(2,1)S(1)}, u32[]{:S(2)}, u32[]{:S(2)}) %collective-permute-start) | collective-permute-done | bytes 65568 | tf_op jit(solution)/shard_map/ppermute | solution.py:224
  17.0 1.3 %collective-permute-start.3 = (bf16[3,2,128,128]{3,2,1,0:T(8,128)(2,1)S(1)}, bf16[3,2,128,128]{3,2,1,0:T(8,128)(2,1)S(1)}, u32[]{:S(2)}, u32[]{:S(2)}) collective-permute-start(bf16[3,2,128,128]{3,2,1,0:T(8,128)(2,1)S(1)} %pad_maximum_fusion.own_ref), channel_id=1, source_target_pairs={{1,0},{2,1},{3,2},{4,3},{5,4},{6,5},{7,6},{9,8},{10,9},{11,10},{12... | collective-permute-start | bytes 589832 | tf_op jit(solution)/shard_map/ppermute | solution.py:225
  18.3 3.0 %collective-permute-start.2 = (bf16[3,2,128,128]{3,2,1,0:T(8,128)(2,1)S(1)}, bf16[3,2,128,128]{3,2,1,0:T(8,128)(2,1)S(1)}, u32[]{:S(2)}, u32[]{:S(2)}) collective-permute-start(bf16[3,2,128,128]{3,2,1,0:T(8,128)(2,1)S(1)} %pad_maximum_fusion.own_ref), channel_id=1, source_target_pairs={{0,1},{1,2},{2,3},{3,4},{4,5},{5,6},{6,7},{8,9},{9,10},{10,11},{11... | collective-permute-start | bytes 589832 | tf_op jit(solution)/shard_map/ppermute | solution.py:224
  21.4 0.0 copy-done.7
  21.4 0.0 copy-start.3
  21.4 0.0 copy-start.4
  21.4 0.6 %copy-done.3 = s32[2,4,25]{2,1,0:T(4,128)S(1)} copy-done((s32[2,4,25]{2,1,0:T(4,128)S(1)}, s32[2,4,25]{2,1,0:T(4,128)}, u32[]{:S(2)}) %copy-start.3) | copy-done | bytes 824
  22.1 0.0 copy-done.4
  22.1 0.8 %prepare.1 = (bf16[8,128,128]{2,1,0:T(8,128)(2,1)S(1)}, f32[9,8,128]{2,1,0:T(8,128)S(1)}) custom-call(bf16[8,128,128]{2,1,0:T(8,128)(2,1)S(1)} %bitcast.11, s32[2,4]{1,0:T(2,128)S(1)} %copy-done.4, s32[8,25]{1,0:T(8,128)S(1)} %bitcast.14, s32[4,8,128]{2,1,0:T(8,128)S(1)} %copy-done.2), custom_call_target="tpu_custom_call" | custom-call | flops 4000000 | bytes 1000000 | tf_op jit(solution)/shard_map/prepare/pallas_call | solution.py:172
  23.0 0.0 collective-permute-done.3.high_ref
  23.0 0.0 collective-permute-done.2.low_ref
  23.0 2.1 %update.1 = bf16[8,8,16,128]{3,2,1,0:T(8,128)(2,1)S(1)} custom-call(bf16[8,128,128]{2,1,0:T(8,128)(2,1)S(1)} %bitcast.12, bf16[8,128,128]{2,1,0:T(8,128)(2,1)S(1)} %get-tuple-element.7.turned_ref, f32[9,8,128]{2,1,0:T(8,128)S(1)} %get-tuple-element.8.taper_ref, bf16[3,2,128,128]{3,2,1,0:T(8,128)(2,1)S(1)} %pad_maximum_fusion.own_ref, ...), custom_call_target="tpu_custom_call" | custom-call | tf_op jit(solution)/shard_map/update/pallas_call | solution.py:212
  25.1 17.2 %all_to_all.5 = bf16[8,8,16,128]{3,2,1,0:T(8,128)(2,1)S(1)} all-to-all(bf16[8,8,16,128]{3,2,1,0:T(8,128)(2,1)S(1)} %update.1), channel_id=1, replica_groups=mesh['gx'=4,'gy'=8] {'gy'}, dimensions={0} | all-to-all | bytes 524288 | tf_op jit(solution)/shard_map/all_to_all | solution.py:248
  42.3 0.8 %copy.10 = bf16[16,2,8,4,128]{4,3,2,1,0:T(4,128)(2,1)} copy(bf16[16,2,8,4,128]{4,0,3,1,2:T(8,128)(2,1)S(1)} %bitcast.15) | data formatting | bytes 524288 | tf_op jit(solution)/shard_map/transpose | solution.py:250
  (2 shorter events, 0.1 us)
Async XLA Ops:
  0.0 0.8 %copy-start = (f32[1,1,128,128]{3,2,1,0:T(8,128)S(1)}, f32[1,1,128,128]{3,2,1,0:T(8,128)}, u32[]{:S(2)}) copy-start(f32[1,1,128,128]{3,2,1,0:T(8,128)} %pred_ref.1) | copy-start | bytes 196612
  0.8 0.8 %copy-start.1 = (f32[1,1,128,128]{3,2,1,0:T(8,128)S(1)}, f32[1,1,128,128]{3,2,1,0:T(8,128)}, u32[]{:S(2)}) copy-start(f32[1,1,128,128]{3,2,1,0:T(8,128)} %jit_ref.1) | copy-start | bytes 196612
  1.7 0.7 %copy-start.2 = (s32[4,8,128]{2,1,0:T(8,128)S(1)}, s32[4,8,128]{2,1,0:T(8,128)}, u32[]{:S(2)}) copy-start(s32[4,8,128]{2,1,0:T(8,128)} %obs_ref.3) | copy-start | bytes 49156
  2.4 0.7 %copy-start.5 = (f32[1,1,128]{2,1,0:T(1,128)S(1)}, f32[1,1,128]{2,1,0:T(1,128)}, u32[]{:S(2)}) copy-start(f32[1,1,128]{2,1,0:T(1,128)} %mv_ref.1) | copy-start | bytes 1540
  3.1 0.7 %copy-start.6 = (f32[1,1,128]{2,1,0:T(1,128)S(1)}, f32[1,1,128]{2,1,0:T(1,128)}, u32[]{:S(2)}) copy-start(f32[1,1,128]{2,1,0:T(1,128)} %var_ref.1) | copy-start | bytes 1540
  3.7 17.7 %copy-start.7 = (bf16[128,2,4,128]{3,2,1,0:T(4,128)(2,1)S(1)}, bf16[128,2,4,128]{3,2,1,0:T(4,128)(2,1)}, u32[]{:S(2)}) copy-start(bf16[128,2,4,128]{3,2,1,0:T(4,128)(2,1)} %param.8) | copy-start | bytes 786436
  6.8 6.2 %collective-permute-start.1 = (bf16[2,128,128]{2,1,0:T(8,128)(2,1)S(1)}, bf16[2,128,128]{2,1,0:T(8,128)(2,1)S(1)}, u32[]{:S(2)}, u32[]{:S(2)}) collective-permute-start(bf16[2,128,128]{2,1,0:T(8,128)(2,1)S(1)} %weigh.1), channel_id=1, source_target_pairs={{8,0},{16,8},{24,16},{9,1},{17,9},{25,17},{10,2},{18,10},{26,18},{... | collective-permute-start | bytes 196616 | tf_op jit(solution)/shard_map/ppermute | solution.py:225
  9.9 7.1 %collective-permute-start = (bf16[2,128,128]{2,1,0:T(8,128)(2,1)S(1)}, bf16[2,128,128]{2,1,0:T(8,128)(2,1)S(1)}, u32[]{:S(2)}, u32[]{:S(2)}) collective-permute-start(bf16[2,128,128]{2,1,0:T(8,128)(2,1)S(1)} %weigh.1), channel_id=1, source_target_pairs={{0,8},{8,16},{16,24},{1,9},{9,17},{17,25},{2,10},{10,18},{18,26},{... | collective-permute-start | bytes 196616 | tf_op jit(solution)/shard_map/ppermute | solution.py:224
  17.0 5.9 %collective-permute-start.3 = (bf16[3,2,128,128]{3,2,1,0:T(8,128)(2,1)S(1)}, bf16[3,2,128,128]{3,2,1,0:T(8,128)(2,1)S(1)}, u32[]{:S(2)}, u32[]{:S(2)}) collective-permute-start(bf16[3,2,128,128]{3,2,1,0:T(8,128)(2,1)S(1)} %pad_maximum_fusion.own_ref), channel_id=1, source_target_pairs={{1,0},{2,1},{3,2},{4,3},{5,4},{6,5},{7,6},{9,8},{10,9},{11,10},{12... | collective-permute-start | bytes 589832 | tf_op jit(solution)/shard_map/ppermute | solution.py:225
  18.3 4.7 %collective-permute-start.2 = (bf16[3,2,128,128]{3,2,1,0:T(8,128)(2,1)S(1)}, bf16[3,2,128,128]{3,2,1,0:T(8,128)(2,1)S(1)}, u32[]{:S(2)}, u32[]{:S(2)}) collective-permute-start(bf16[3,2,128,128]{3,2,1,0:T(8,128)(2,1)S(1)} %pad_maximum_fusion.own_ref), channel_id=1, source_target_pairs={{0,1},{1,2},{2,3},{3,4},{4,5},{5,6},{6,7},{8,9},{9,10},{10,11},{11... | collective-permute-start | bytes 589832 | tf_op jit(solution)/shard_map/ppermute | solution.py:224
  21.4 0.7 %copy-start.3 = (s32[2,4,25]{2,1,0:T(4,128)S(1)}, s32[2,4,25]{2,1,0:T(4,128)}, u32[]{:S(2)}) copy-start(s32[2,4,25]{2,1,0:T(4,128)} %param.15) | copy-start | bytes 2404
  21.4 0.7 %copy-start.4 = (s32[2,4]{1,0:T(2,128)S(1)}, s32[2,4]{1,0:T(2,128)}, u32[]{:S(2)}) copy-start(s32[2,4]{1,0:T(2,128)} %radius_ref.1) | copy-start | bytes 100

commit v2 on v1

--- a/solution.py
+++ b/solution.py
@@ -14,6 +14,7 @@
 OBS_TILE = 128
 PATTERN = 25
 SMALL = 32
+EXTRA = 16
 
 F32 = jnp.float32
 BF16 = jnp.bfloat16
@@ -226,7 +227,141 @@
     return low, high
 
 
-def per_device(
+def deviate_kernel(pred_ref, radius_ref, pattern_ref, out_ref):
+    members = pred_ref.shape[2]
+    pred = pred_ref[0, 0]
+    mean = jnp.sum(pred, axis=0, keepdims=True) / members
+    out_ref[0:members] = (pred - mean).astype(BF16)
+    row, col = iota((EXTRA, OBS_TILE), 0), iota((EXTRA, OBS_TILE), 1)
+    extra = jnp.zeros((EXTRA, OBS_TILE), F32)
+    for b in range(BLOCKS):
+        extra = jnp.where((row == b) & (col == PATTERN), radius_ref[b // BLK_Y, b % BLK_Y].astype(F32), extra)
+    pattern = pattern_ref[...].astype(F32)
+    pattern = jnp.concatenate([pattern, jnp.zeros((BLOCKS, OBS_TILE - PATTERN), F32)], axis=1)
+    pattern = jnp.concatenate([pattern, jnp.zeros((EXTRA - BLOCKS, OBS_TILE), F32)], axis=0)
+    out_ref[members : members + EXTRA] = (extra + pattern).astype(BF16)
+
+
+def deviate(predicted, taper_radius, taper_pattern):
+    members = predicted.shape[2]
+    return pl.pallas_call(
+        deviate_kernel,
+        out_shape=jax.ShapeDtypeStruct((members + EXTRA, OBS_TILE), BF16),
+        in_specs=[
+            pl.BlockSpec(memory_space=pltpu.VMEM),
+            pl.BlockSpec(memory_space=pltpu.SMEM),
+            pl.BlockSpec(memory_space=pltpu.VMEM),
+        ],
+        out_specs=pl.BlockSpec(memory_space=pltpu.VMEM),
+        name="deviate",
+    )(predicted, taper_radius, taper_pattern.reshape(BLOCKS, PATTERN))
+
+
+def tapers_of(radius, pattern, tile_x, tile_y, obs_ref, members):
+    count_x, count_y = obs_ref.shape[0], obs_ref.shape[1]
+    shape = (BLOCKS, OBS_TILE)
+    block = iota(shape, 0)
+    reach = radius + 1.0
+    reach = reach * reach
+    slots = [jnp.broadcast_to(pattern[:, p : p + 1], shape) for p in range(PATTERN)]
+    found = []
+    for dx in range(3):
+        for dy in range(3):
+            at_x, at_y = tile_x + (dx - 1), tile_y + (dy - 1)
+            valid = (at_x >= 0) & (at_x < count_x) & (at_y >= 0) & (at_y < count_y)
+            at_x = jnp.clip(at_x, 0, count_x - 1)
+            at_y = jnp.clip(at_y, 0, count_y - 1)
+            obs = obs_ref[at_x, pl.ds(at_y, 1), :]
+            step_x = (dx - 1) * BLK_X + (obs >> 2) - (block >> 2)
+            step_y = (dy - 1) * BLK_Y + (obs & 3) - (block & 3)
+            inside = (jnp.abs(step_x) <= 2) & (jnp.abs(step_y) <= 2) & valid
+            offset = (step_x + 2) * 5 + (step_y + 2)
+            picked = jnp.zeros(shape, F32)
+            for p in range(PATTERN):
+                picked = jnp.where(offset == p, slots[p], picked)
+            spread = (step_x * step_x + step_y * step_y).astype(F32)
+            shaped = jnp.maximum(1.0 - spread / reach, 0.0)
+            found.append(jnp.where(inside, picked, 0.0) * shaped / (members - 1))
+    return found
+
+
+def regroup_kernel(params_ref, around_ref, weighted_ref, obs_ref, out_ref):
+    count_x, parts = obs_ref.shape[0], obs_ref.shape[1]
+    share = out_ref.shape[0]
+    rows = share * BLOCKS
+    members = share * parts
+    cells = members * BLOCKS
+    tile_x = lax.axis_index("gx")
+    mine = lax.axis_index("gy")
+    spread = (iota((members, cells), 1) // BLOCKS == iota((members, cells), 0)).astype(BF16)
+    diagonal = (iota((rows, cells), 0) % BLOCKS) == (iota((rows, cells), 1) % BLOCKS)
+    top = iota((share, BLOCKS, CELLS), 1) < BLK_Y
+    before = None
+    for s in range(parts):
+        wide = params_ref[s].astype(F32).reshape(members, BLOCKS, CELLS)
+        mean = jnp.sum(wide, axis=0, keepdims=True) / members
+        anomaly = (wide - mean).reshape(cells, CELLS).astype(BF16)
+        extra = around_ref[tile_x * parts + s, members : members + EXTRA].astype(F32)[0:BLOCKS]
+        tapers = tapers_of(extra[:, PATTERN : PATTERN + 1], extra, tile_x, s, obs_ref, members)
+        turned = jnp.zeros((rows, members), F32)
+        for t, (dx, dy) in enumerate([(dx, dy) for dx in (-1, 0, 1) for dy in (-1, 0, 1)]):
+            if not 0 <= s + dy < parts:
+                continue
+            tile = jnp.clip(tile_x + dx, 0, count_x - 1) * parts + s + dy
+            weighted = weighted_ref[tile].astype(F32)
+            scaled = weighted[:, None, :] * tapers[t][None]
+            scaled = scaled.reshape(rows, OBS_TILE).astype(BF16)
+            turned = turned + dot(scaled, around_ref[tile, 0:members], ((1,), (1,)))
+        wide_k = dot(turned.astype(BF16), spread, ((1,), (0,)))
+        wide_k = jnp.where(diagonal, wide_k, 0.0).astype(BF16)
+        delta = dot(wide_k, anomaly, ((1,), (0,)))
+        own = params_ref[s, pl.ds(pl.multiple_of(mine * rows, rows), rows), :].astype(F32)
+        now = (own + delta).reshape(share, BLOCKS, CELLS)
+        if s % 2 == 0:
+            before = now
+        else:
+            place = slice((s - 1) * BLK_Y, (s + 1) * BLK_Y)
+            out_ref[:, 0, place, :] = jnp.where(top, before, jnp.roll(now, BLK_Y, axis=1)).astype(BF16)
+            out_ref[:, 1, place, :] = jnp.where(top, jnp.roll(before, BLK_Y, axis=1), now).astype(BF16)
+
+
+def regroup(gathered, around, weighted, obs_block):
+    parts, cells, _ = gathered.shape
+    share = weighted.shape[1]
+    return pl.pallas_call(
+        regroup_kernel,
+        out_shape=jax.ShapeDtypeStruct((share, BLK_X, parts * BLK_Y, CELLS), BF16),
+        in_specs=[pl.BlockSpec(memory_space=pltpu.VMEM)] * 4,
+        out_specs=pl.BlockSpec(memory_space=pltpu.VMEM),
+        compiler_params=pltpu.CompilerParams(vmem_limit_bytes=40 * 2**20),
+        name="regroup",
+    )(gathered, around, weighted, obs_block)
+
+
+def gather_form(
+    params,
+    predicted,
+    measured_value,
+    measurement_variance,
+    observation_jitter,
+    obs_block,
+    taper_radius,
+    taper_pattern,
+):
+    members = params.shape[0]
+    tiles, parts = lax.axis_size("gx"), lax.axis_size("gy")
+    share = members // parts
+    gathered = lax.all_gather(params.reshape(members * BLOCKS, CELLS), "gy")
+    around = lax.all_gather(deviate(predicted, taper_radius, taper_pattern), ("gx", "gy"))
+    own = weigh(predicted, measured_value, measurement_variance, observation_jitter, obs_block)
+    sent = jnp.broadcast_to(own[1].reshape(1, parts, share, OBS_TILE), (tiles, parts, share, OBS_TILE))
+    weighted = lax.all_to_all(
+        sent.reshape(tiles * parts, share, OBS_TILE), ("gx", "gy"), split_axis=0, concat_axis=0, tiled=True
+    )
+    return regroup(gathered, around, weighted, obs_block)
+
+
+def halo_form(
     params,
     predicted,
     measured_value,
@@ -262,6 +397,7 @@
         P("gx", "gy"),
         P("gx", "gy", None),
     )
+    per_device = gather_form if mesh.shape["gy"] <= 8 else halo_form
     return jax.shard_map(
         per_device, mesh=mesh, in_specs=placed, out_specs=P("gy", "gx", None, None), check_vma=False
     )

time: 43.5 us -> 114 us (2.62)
  the two profiles are of different devices: /device:TPU:4 before, /device:TPU:0 now
where the time goes in v2:
time: 114 us
  waiting for transfers between devices  67.1 us (59%)
  blocking collectives  15.4 us (14%)
  between operations  13.4 us (12%)
  Pallas kernels  10.6 us (9%)
  local copies, waits for them, and re-layouts  7.3 us (6%)
    all_gather x1, waiting for transfers between devices, gather_form(): lax.all_gather(deviate(predicted, taper_radius, taper_pattern), ('gx', 'g...  36.7 us
    all_gather x1, waiting for transfers between devices, gather_form(): gathered = lax.all_gather(params.reshape(members * BLOCKS, CELLS), 'gy')  29.7 us
    all_to_all x1, blocking collectives, gather_form(): lax.all_to_all(sent.reshape(tiles * parts, share, OBS_TILE), ('gx', 'gy')...  15.4 us
    unnamed x16, local copies, waits for them, and re-layouts  7.28 us
    pallas_call x1, Pallas kernels, regroup(): pl.pallas_call(regroup_kernel, out_shape=jax.ShapeDtypeStruct((share, BLK...  6.4 us
    pallas_call x1, Pallas kernels, weigh(): pl.pallas_call(weigh_kernel, out_shape=jax.ShapeDtypeStruct((2, members,...  2.7 us
  transfers between devices with their start and end apart: 2, of which 2 were waited for; matrix products, arithmetic and copies ran while one was open for 0% of the time, Pallas kernels for 2%

profile of v2, /device:TPU:0, one launch (start us, length us, event | category | flops | bytes accessed | tf_op | source)
XLA Modules:
  0.0 113.8 jit_solution(2645421939954239833)
XLA Ops:
  6.5 0.0 all-gather.6.cloned.1.call-start
  6.5 1.5 %deviate.1 = bf16[144,128]{1,0:T(8,128)(2,1)} custom-call(f32[1,1,128,128]{3,2,1,0:T(8,128)} %pred_ref.3, s32[2,4]{1,0:T(2,128)} %radius_ref.1, s32[8,25]{1,0:T(8,128)} %bitcast.9), custom_call_target="tpu_custom_call" | custom-call | tf_op jit(solution)/shard_map/deviate/pallas_call | solution.py:247
  8.0 0.0 all-gather.6.cloned.1.call-update
  8.1 0.0 all-gather.4.cloned.1.call-start
  8.1 0.7 all-gather.4.cloned.1.call-update
  8.8 0.0 copy-start.2
  8.8 0.8 copy-done.2
  9.7 0.0 copy-start.3
  9.7 0.7 copy-done.3
  10.4 0.0 copy-start.5
  10.4 0.8 copy-done.5
  11.2 0.0 copy-start.6
  11.2 0.7 copy-done.6
  11.9 0.0 copy-start.7
  11.9 0.7 copy-done.7
  12.5 2.7 %weigh.1 = bf16[2,128,128]{2,1,0:T(8,128)(2,1)S(1)} custom-call(f32[1,1,128,128]{3,2,1,0:T(8,128)S(1)} %copy-done.2, f32[1,1,128]{2,1,0:T(1,128)S(1)} %copy-done.6, f32[1,1,128]{2,1,0:T(1,128)S(1)} %copy-done.7, f32[1,1,128,128]{3,2,1,0:T(8,128)S(1)} %copy-done.5, s32[4,8,128]{2,1,0:T(8,128)S(1)} %copy-done.3), custom_call_target="tpu_custom_call" | custom-call | tf_op jit(solution)/shard_map/weigh/pallas_call | solution.py:117
  15.3 15.4 %all_to_all.5.weighted_ref = bf16[32,16,128]{2,1,0:T(8,128)(2,1)S(1)} all-to-all(bf16[32,16,128]{2,1,0:T(8,128)(2,1)S(1)} %bitcast.6), channel_id=1, replica_groups=mesh['gx'=4,'gy'=8] {'gx','gy'}, dimensions={0} | all-to-all | bytes 262144 | tf_op jit(solution)/shard_map/all_to_all | solution.py:358
  30.6 36.7 %all-gather.6.cloned.1.call-done = bf16[4608,128]{1,0:T(8,128)(2,1)} async-done(((bf16[144,128]{1,0:T(8,128)(2,1)}), bf16[4608,128]{1,0:T(8,128)(2,1)}) %all-gather.6.cloned.1.call-update) | async-done | bytes 1179664 | tf_op jit(solution)/shard_map/all_gather | solution.py:355
  67.3 29.7 %all-gather.4.cloned.1.call-done.params_ref = bf16[8,1024,128]{2,1,0:T(8,128)(2,1)} async-done(((bf16[1,1024,128]{2,1,0:T(8,128)(2,1)}), bf16[8,1024,128]{2,1,0:T(8,128)(2,1)}) %all-gather.4.cloned.1.call-update) | async-done | bytes 2097168 | tf_op jit(solution)/shard_map/all_gather | solution.py:354
  97.0 0.0 copy-start
  97.0 1.6 %copy-done = bf16[8,1024,128]{2,1,0:T(8,128)(2,1)S(1)} copy-done((bf16[8,1024,128]{2,1,0:T(8,128)(2,1)S(1)}, bf16[8,1024,128]{2,1,0:T(8,128)(2,1)}, u32[]{:S(2)}) %copy-start) | copy-done | bytes 2097176
  98.6 0.0 copy-start.1
  98.6 1.3 %copy-done.1 = bf16[4608,128]{1,0:T(8,128)(2,1)S(1)} copy-done((bf16[4608,128]{1,0:T(8,128)(2,1)S(1)}, bf16[4608,128]{1,0:T(8,128)(2,1)}, u32[]{:S(2)}) %copy-start.1) | copy-done | bytes 1179672
  99.9 0.0 copy-start.4
  99.9 0.7 copy-done.4
  100.6 6.4 %regroup.1 = bf16[16,2,32,128]{3,2,1,0:T(8,128)(2,1)} custom-call(bf16[8,1024,128]{2,1,0:T(8,128)(2,1)S(1)} %copy-done, bf16[32,144,128]{2,1,0:T(8,128)(2,1)S(1)} %bitcast.5, bf16[32,16,128]{2,1,0:T(8,128)(2,1)S(1)} %all_to_all.5.weighted_ref, s32[4,8,128]{2,1,0:T(8,128)S(1)} %copy-done.4), custom_call_target="tpu_custom_call" | custom-call | tf_op jit(solution)/shard_map/regroup/pallas_call | solution.py:331
  (2 shorter events, 0.0 us)
Async XLA Ops:
  6.5 60.8 %all-gather.6.cloned.1.call-start = ((), (), s32[]{:S(2)}) async-start(), calls=%async_computation.2 | async-start | bytes 1216512 | tf_op jit(solution)/shard_map/all_gather | solution.py:355
  8.1 88.9 %all-gather.4.cloned.1.call-start = ((), (), s32[]{:S(2)}) async-start(), calls=%async_computation.1 | async-start | bytes 2359296 | tf_op jit(solution)/shard_map/all_gather | solution.py:354
  8.8 0.8 copy-start.2
  9.7 0.7 copy-start.3
  10.4 0.8 copy-start.5
  11.2 0.7 copy-start.6
  11.9 0.7 copy-start.7
  97.0 1.6 %copy-start = (bf16[8,1024,128]{2,1,0:T(8,128)(2,1)S(1)}, bf16[8,1024,128]{2,1,0:T(8,128)(2,1)}, u32[]{:S(2)}) copy-start(bf16[8,1024,128]{2,1,0:T(8,128)(2,1)} %all-gather.4.cloned.1.call-done.params_ref) | copy-start | bytes 6291460
  98.6 1.3 %copy-start.1 = (bf16[4608,128]{1,0:T(8,128)(2,1)S(1)}, bf16[4608,128]{1,0:T(8,128)(2,1)}, u32[]{:S(2)}) copy-start(bf16[4608,128]{1,0:T(8,128)(2,1)} %all-gather.6.cloned.1.call-done) | copy-start | bytes 3538948
  99.9 0.7 copy-start.4
Sparse Core Ops, SparseCore 0:
  10.4 56.9 all-gather.5
  68.9 28.0 all-gather.3

commit v3 on v1

--- a/solution.py
+++ b/solution.py
@@ -62,17 +62,41 @@
     lax.fori_loop(0, (count + 1) // 2, pair, 0)
 
 
-def weigh_kernel(pred_ref, mv_ref, var_ref, jit_ref, obs_ref, out_ref, x_ref, idx_ref, full_ref):
-    members = pred_ref.shape[2]
+def in_hbm(*arrays):
+    return [pltpu.with_memory_space_constraint(array, pltpu.HBM) for array in arrays]
+
+
+def fetch(pairs, sems):
+    copies = [pltpu.make_async_copy(src, dst, sems.at[k]) for k, (src, dst) in enumerate(pairs)]
+    for copy in copies:
+        copy.start()
+    return copies
+
+
+def weigh_kernel(
+    pred_hbm, mv_hbm, var_hbm, jit_hbm, obs_hbm, out_ref,
+    pred_ref, mv_ref, var_ref, jit_ref, obs_ref, x_ref, idx_ref, full_ref, sems,
+):
+    members = pred_ref.shape[0]
     tile_x = lax.axis_index("gx")
     tile_y = lax.axis_index("gy")
     square = (OBS_TILE, OBS_TILE)
-    pred = pred_ref[0, 0]
-    var = var_ref[0]
+    pairs = [
+        (pred_hbm.at[0, 0], pred_ref),
+        (obs_hbm.at[tile_x], obs_ref),
+        (var_hbm.at[0], var_ref),
+        (mv_hbm.at[0], mv_ref),
+        (jit_hbm.at[0, 0], jit_ref),
+    ]
+    copies = fetch(pairs, sems)
+    for copy in copies[:3]:
+        copy.wait()
+    pred = pred_ref[...]
+    var = var_ref[...]
     mean = jnp.sum(pred, axis=0, keepdims=True) / members
     deviation = (pred - mean).astype(BF16)
     out_ref[0] = deviation
-    obs = obs_ref[tile_x, pl.ds(tile_y, 1), :]
+    obs = obs_ref[pl.ds(tile_y, 1), :]
     groups = (iota((BLOCKS, OBS_TILE), 0) == obs).astype(BF16)
     same = dot(groups, groups, ((0,), (0,)))
     gram = dot(deviation, deviation, ((0,), (0,))) / (members - 1)
@@ -106,7 +130,9 @@
     def _():
         solve(OBS_TILE)
 
-    innovation = mv_ref[0] + jnp.sqrt(var) * jit_ref[0, 0] - pred
+    for copy in copies[3:]:
+        copy.wait()
+    innovation = mv_ref[...] + jnp.sqrt(var) * jit_ref[...] - pred
     weighted = dot(innovation, full_ref[...], ((1,), (0,)), lax.Precision.HIGHEST)
     out_ref[1] = weighted.astype(BF16)
 
@@ -116,29 +142,45 @@
     return pl.pallas_call(
         weigh_kernel,
         out_shape=jax.ShapeDtypeStruct((2, members, OBS_TILE), BF16),
-        in_specs=[pl.BlockSpec(memory_space=pltpu.VMEM)] * 5,
+        in_specs=[pl.BlockSpec(memory_space=pltpu.HBM)] * 5,
         out_specs=pl.BlockSpec(memory_space=pltpu.VMEM),
         scratch_shapes=[
+            pltpu.VMEM((members, OBS_TILE), F32),
+            pltpu.VMEM((1, OBS_TILE), F32),
+            pltpu.VMEM((1, OBS_TILE), F32),
+            pltpu.VMEM((members, OBS_TILE), F32),
+            pltpu.VMEM((obs_block.shape[1], OBS_TILE), jnp.int32),
             pltpu.VMEM((OBS_TILE, OBS_TILE), F32),
             pltpu.VMEM((OBS_TILE, OBS_TILE), jnp.int32),
             pltpu.VMEM((OBS_TILE, OBS_TILE), F32),
+            pltpu.SemaphoreType.DMA((5,)),
         ],
         compiler_params=pltpu.CompilerParams(vmem_limit_bytes=16 * 2**20),
         name="weigh",
-    )(predicted, measured_value, measurement_variance, observation_jitter, obs_block)
-
-
-def prepare_kernel(params_ref, radius_ref, pattern_ref, obs_ref, turned_ref, taper_ref):
+    )(*in_hbm(predicted, measured_value, measurement_variance, observation_jitter, obs_block))
+
+
+def offsets(place):
+    even = 1 - 2 * (place & 1)
+    return 0, even, -even
+
+
+def prepare_kernel(
+    params_ref, radius_hbm, pattern_hbm, obs_hbm, turned_ref, taper_ref, radius_ref, pattern_ref, obs_ref, sems
+):
     members = params_ref.shape[1]
     tile_x = lax.axis_index("gx")
     tile_y = lax.axis_index("gy")
     count_x, count_y = obs_ref.shape[0], obs_ref.shape[1]
+    copies = fetch([(radius_hbm, radius_ref), (pattern_hbm, pattern_ref), (obs_hbm, obs_ref)], sems)
     for b in range(BLOCKS):
         block = params_ref[b].astype(F32)
         mean = jnp.sum(block, axis=0, keepdims=True) / members
         anomaly = block - mean
         turned_ref[b] = anomaly.T.astype(BF16)
 
+    for copy in copies:
+        copy.wait()
     shape = (BLOCKS, OBS_TILE)
     block = iota(shape, 0)
     radius = jnp.zeros(shape, jnp.int32)
@@ -146,17 +188,17 @@
         radius = jnp.where(block == b, radius_ref[b // BLK_Y, b % BLK_Y], radius)
     reach = (radius + 1).astype(F32)
     reach = reach * reach
-    pattern = pattern_ref[...].astype(F32)
+    pattern = jnp.concatenate([pattern_ref[i] for i in range(BLK_X)], axis=0).astype(F32)
     slots = [jnp.broadcast_to(pattern[:, p : p + 1], shape) for p in range(PATTERN)]
-    for dx in range(3):
-        for dy in range(3):
-            at_x, at_y = tile_x + (dx - 1), tile_y + (dy - 1)
+    for ix, dx in enumerate(offsets(tile_x)):
+        for iy, dy in enumerate(offsets(tile_y)):
+            at_x, at_y = tile_x + dx, tile_y + dy
             valid = (at_x >= 0) & (at_x < count_x) & (at_y >= 0) & (at_y < count_y)
             at_x = jnp.clip(at_x, 0, count_x - 1)
             at_y = jnp.clip(at_y, 0, count_y - 1)
             obs = obs_ref[at_x, pl.ds(at_y, 1), :]
-            step_x = (dx - 1) * BLK_X + (obs >> 2) - (block >> 2)
-            step_y = (dy - 1) * BLK_Y + (obs & 3) - (block & 3)
+            step_x = dx * BLK_X + (obs >> 2) - (block >> 2)
+            step_y = dy * BLK_Y + (obs & 3) - (block & 3)
             inside = (jnp.abs(step_x) <= 2) & (jnp.abs(step_y) <= 2) & valid
             offset = (step_x + 2) * 5 + (step_y + 2)
             picked = jnp.zeros(shape, F32)
@@ -164,7 +206,7 @@
                 picked = jnp.where(offset == p, slots[p], picked)
             spread = (step_x * step_x + step_y * step_y).astype(F32)
             shaped = jnp.maximum(1.0 - spread / reach, 0.0)
-            taper_ref[dx * 3 + dy] = jnp.where(inside, picked, 0.0) * shaped / (members - 1)
+            taper_ref[ix * 3 + iy] = jnp.where(inside, picked, 0.0) * shaped / (members - 1)
 
 
 def prepare(by_block, taper_radius, taper_pattern, obs_block):
@@ -175,22 +217,23 @@
             jax.ShapeDtypeStruct((BLOCKS, CELLS, members), BF16),
             jax.ShapeDtypeStruct((9, BLOCKS, OBS_TILE), F32),
         ),
-        in_specs=[
-            pl.BlockSpec(memory_space=pltpu.VMEM),
-            pl.BlockSpec(memory_space=pltpu.SMEM),
-            pl.BlockSpec(memory_space=pltpu.VMEM),
-            pl.BlockSpec(memory_space=pltpu.VMEM),
+        in_specs=[pl.BlockSpec(memory_space=pltpu.VMEM)] + [pl.BlockSpec(memory_space=pltpu.HBM)] * 3,
+        out_specs=(pl.BlockSpec(memory_space=pltpu.VMEM), pl.BlockSpec(memory_space=pltpu.VMEM)),
+        scratch_shapes=[
+            pltpu.SMEM(taper_radius.shape, jnp.int32),
+            pltpu.VMEM(taper_pattern.shape, jnp.int32),
+            pltpu.VMEM(obs_block.shape, jnp.int32),
+            pltpu.SemaphoreType.DMA((3,)),
         ],
-        out_specs=(pl.BlockSpec(memory_space=pltpu.VMEM), pl.BlockSpec(memory_space=pltpu.VMEM)),
         compiler_params=pltpu.CompilerParams(vmem_limit_bytes=16 * 2**20),
         cost_estimate=pl.CostEstimate(flops=4_000_000, bytes_accessed=1_000_000, transcendentals=0),
         name="prepare",
-    )(by_block, taper_radius, taper_pattern.reshape(BLOCKS, PATTERN), obs_block)
-
-
-def update_kernel(params_ref, turned_ref, taper_ref, own_ref, low_ref, high_ref, out_ref):
+    )(by_block, *in_hbm(taper_radius, taper_pattern, obs_block))
+
+
+def update_kernel(params_ref, turned_ref, taper_ref, own_ref, even_ref, odd_ref, out_ref):
     share = out_ref.shape[2]
-    near = [ref.at[dx] for dx in range(3) for ref in (low_ref, own_ref, high_ref)]
+    near = [ref.at[ix] for ix in range(3) for ref in (own_ref, even_ref, odd_ref)]
     deviations = jnp.concatenate([tile[0] for tile in near], axis=1)
     weighted = jnp.concatenate([tile[1] for tile in near], axis=1)
 
@@ -207,7 +250,7 @@
     lax.fori_loop(0, BLOCKS, one, 0, unroll=True)
 
 
-def update(by_block, turned, taper, own, low, high, parts):
+def update(by_block, turned, taper, own, even, odd, parts):
     members = by_block.shape[1]
     return pl.pallas_call(
         update_kernel,
@@ -216,14 +259,16 @@
         out_specs=pl.BlockSpec(memory_space=pltpu.VMEM),
         compiler_params=pltpu.CompilerParams(vmem_limit_bytes=40 * 2**20),
         name="update",
-    )(by_block, turned, taper, own, low, high)
-
-
-def neighbours(block, axis):
+    )(by_block, turned, taper, own, even, odd)
+
+
+def swaps(block, axis):
     count = lax.axis_size(axis)
-    low = lax.ppermute(block, axis, [(i, i + 1) for i in range(count - 1)])
-    high = lax.ppermute(block, axis, [(i + 1, i) for i in range(count - 1)])
-    return low, high
+    found = []
+    for first in (0, 1):
+        pairs = [(i, i + 1) for i in range(first, count - 1, 2)]
+        found.append(lax.ppermute(block, axis, pairs + [(b, a) for a, b in pairs]))
+    return found
 
 
 def per_device(
@@ -240,11 +285,12 @@
     parts = lax.axis_size("gy")
     by_block = params.reshape(members, BLOCKS, CELLS).transpose(1, 0, 2)
     own = weigh(predicted, measured_value, measurement_variance, observation_jitter, obs_block)
-    low_x, high_x = neighbours(own, "gx")
+    even, odd = swaps(own, "gx")
     turned, taper = prepare(by_block, taper_radius, taper_pattern, obs_block)
-    column = jnp.stack([low_x, own, high_x])
-    low, high = neighbours(column, "gy")
-    updated = update(by_block, turned, taper, column, low, high, parts)
+    column = jnp.stack([own, even, odd])
+    column, turned, taper = lax.optimization_barrier((column, turned, taper))
+    even, odd = swaps(column, "gy")
+    updated = update(by_block, turned, taper, column, even, odd, parts)
     arrived = lax.all_to_all(updated, "gy", split_axis=0, concat_axis=0, tiled=True)
     share = members // parts
     arrived = arrived.reshape(parts, BLK_X, BLK_Y, share, CELLS).transpose(3, 1, 0, 2, 4)

time: 43.5 us -> 37.8 us (0.87)
  the two profiles are of different devices: /device:TPU:4 before, /device:TPU:0 now
where the time goes in v3:
time: 37.8 us; the launch traced here: 37.6 us
  blocking collectives  16.6 us (44%)
  starting transfers between devices  10.6 us (28%)
  Pallas kernels  6.47 us (17%)
  waiting for transfers between devices  2.04 us (5%)
  local copies, waits for them, and re-layouts  1.81 us (5%)
    all_to_all x1, blocking collectives, per_device(): lax.all_to_all(updated, 'gy', split_axis=0, concat_axis=0, tiled=True)  16.6 us
    ppermute x4, starting transfers between devices, swaps(): found.append(lax.ppermute(block, axis, pairs + [(b, a) for a, b in pairs]))  10.6 us
    pallas_call x1, Pallas kernels, weigh(): pl.pallas_call(weigh_kernel, out_shape=jax.ShapeDtypeStruct((2, members,...  3.4 us
    pallas_call x1, Pallas kernels, update(): pl.pallas_call(update_kernel, out_shape=jax.ShapeDtypeStruct((parts, BLOC...  2.09 us
    ppermute x4, waiting for transfers between devices, swaps(): found.append(lax.ppermute(block, axis, pairs + [(b, a) for a, b in pairs]))  2.04 us
    unnamed x1, local copies, waits for them, and re-layouts  0.99 us
    pallas_call x1, Pallas kernels, prepare(): pl.pallas_call(prepare_kernel, out_shape=(jax.ShapeDtypeStruct((BLOCKS, C...  0.97 us
    transpose x1, local copies, waits for them, and re-layouts, per_device(): arrived.reshape(parts, BLK_X, BLK_Y, share, CELLS).transpose(3, 1, 0, 2, 4)  0.82 us
  transfers between devices with their start and end apart: 4, of which 2 were waited for; matrix products, arithmetic and copies ran while one was open for 3% of the time, Pallas kernels for 3%

profile of v3, /device:TPU:0, one launch (start us, length us, event | category | flops | bytes accessed | tf_op | source)
XLA Modules:
  0.0 37.6 jit_solution(14039411222683191093)
XLA Ops:
  0.0 3.4 %weigh.1 = bf16[2,128,128]{2,1,0:T(8,128)(2,1)S(1)} custom-call(f32[1,1,128,128]{3,2,1,0:T(8,128)} %pred_hbm.1, f32[1,1,128]{2,1,0:T(1,128)} %mv_hbm.1, f32[1,1,128]{2,1,0:T(1,128)} %var_hbm.1, f32[1,1,128,128]{3,2,1,0:T(8,128)} %jit_hbm.1, s32[4,8,128]{2,1,0:T(8,128)} %obs_hbm.3), custom_call_target="tpu_custom_call" | custom-call | tf_op jit(solution)/shard_map/weigh/pallas_call | solution.py:142
  3.4 0.7 %collective-permute-start.1 = (bf16[2,128,128]{2,1,0:T(8,128)(2,1)S(1)}, bf16[2,128,128]{2,1,0:T(8,128)(2,1)S(1)}, u32[]{:S(2)}, u32[]{:S(2)}) collective-permute-start(bf16[2,128,128]{2,1,0:T(8,128)(2,1)S(1)} %weigh.1), channel_id=1, source_target_pairs={{8,16},{16,8},{9,17},{17,9},{10,18},{18,10},{11,19},{19,11},{12,20... | collective-permute-start | bytes 196616 | tf_op jit(solution)/shard_map/ppermute | solution.py:270
  4.1 5.9 %collective-permute-start = (bf16[2,128,128]{2,1,0:T(8,128)(2,1)S(1)}, bf16[2,128,128]{2,1,0:T(8,128)(2,1)S(1)}, u32[]{:S(2)}, u32[]{:S(2)}) collective-permute-start(bf16[2,128,128]{2,1,0:T(8,128)(2,1)S(1)} %weigh.1), channel_id=1, source_target_pairs={{0,8},{16,24},{8,0},{24,16},{1,9},{17,25},{9,1},{25,17},{2,10},{18... | collective-permute-start | bytes 196616 | tf_op jit(solution)/shard_map/ppermute | solution.py:270
  10.0 1.0 %copy.9 = bf16[128,2,4,128]{3,0,2,1:T(8,128)(2,1)S(1)} copy(bf16[128,2,4,128]{3,2,1,0:T(4,128)(2,1)} %param.8) | data formatting | bytes 524288 | tf_op args[0]
  11.0 1.0 %prepare.1 = (bf16[8,128,128]{2,1,0:T(8,128)(2,1)S(1)}, f32[9,8,128]{2,1,0:T(8,128)S(1)}) custom-call(bf16[8,128,128]{2,1,0:T(8,128)(2,1)S(1)} %bitcast.10, s32[2,4]{1,0:T(2,128)} %radius_hbm.1, s32[2,4,25]{2,1,0:T(4,128)} %pattern_hbm.1, s32[4,8,128]{2,1,0:T(8,128)} %obs_hbm.3), custom_call_target="tpu_custom_call" | custom-call | flops 4000000 | bytes 1000000 | tf_op jit(solution)/shard_map/prepare/pallas_call | solution.py:214
  12.0 0.0 collective-permute-done.1
  12.0 1.0 %collective-permute-done = bf16[2,128,128]{2,1,0:T(8,128)(2,1)S(1)} collective-permute-done((bf16[2,128,128]{2,1,0:T(8,128)(2,1)S(1)}, bf16[2,128,128]{2,1,0:T(8,128)(2,1)S(1)}, u32[]{:S(2)}, u32[]{:S(2)}) %collective-permute-start) | collective-permute-done | bytes 65568 | tf_op jit(solution)/shard_map/ppermute | solution.py:270
  13.0 0.7 %collective-permute-start.3 = (bf16[3,2,128,128]{3,2,1,0:T(8,128)(2,1)S(1)}, bf16[3,2,128,128]{3,2,1,0:T(8,128)(2,1)S(1)}, u32[]{:S(2)}, u32[]{:S(2)}) collective-permute-start(bf16[3,2,128,128]{3,2,1,0:T(8,128)(2,1)S(1)} %pad_maximum_fusion.own_ref), channel_id=1, source_target_pairs={{1,2},{3,4},{5,6},{2,1},{4,3},{6,5},{9,10},{11,12},{13,14},{10,9},... | collective-permute-start | bytes 589832 | tf_op jit(solution)/shard_map/ppermute | solution.py:270
  13.7 3.3 %collective-permute-start.2 = (bf16[3,2,128,128]{3,2,1,0:T(8,128)(2,1)S(1)}, bf16[3,2,128,128]{3,2,1,0:T(8,128)(2,1)S(1)}, u32[]{:S(2)}, u32[]{:S(2)}) collective-permute-start(bf16[3,2,128,128]{3,2,1,0:T(8,128)(2,1)S(1)} %pad_maximum_fusion.own_ref), channel_id=1, source_target_pairs={{0,1},{2,3},{4,5},{6,7},{1,0},{3,2},{5,4},{7,6},{8,9},{10,11},{12,... | collective-permute-start | bytes 589832 | tf_op jit(solution)/shard_map/ppermute | solution.py:270
  17.0 0.0 collective-permute-done.3.odd_ref
  17.0 1.1 %collective-permute-done.2.even_ref = bf16[3,2,128,128]{3,2,1,0:T(8,128)(2,1)S(1)} collective-permute-done((bf16[3,2,128,128]{3,2,1,0:T(8,128)(2,1)S(1)}, bf16[3,2,128,128]{3,2,1,0:T(8,128)(2,1)S(1)}, u32[]{:S(2)}, u32[]{:S(2)}) %collective-permute-start.2) | collective-permute-done | bytes 196640 | tf_op jit(solution)/shard_map/ppermute | solution.py:270
  18.1 2.1 %update.1 = bf16[8,8,16,128]{3,2,1,0:T(8,128)(2,1)S(1)} custom-call(bf16[8,128,128]{2,1,0:T(8,128)(2,1)S(1)} %bitcast.11, bf16[8,128,128]{2,1,0:T(8,128)(2,1)S(1)} %get-tuple-element.12.turned_ref, f32[9,8,128]{2,1,0:T(8,128)S(1)} %get-tuple-element.13.taper_ref, bf16[3,2,128,128]{3,2,1,0:T(8,128)(2,1)S(1)} %pad_maximum_fusion.own_ref, ...), custom_call_target="tpu_custom_call" | custom-call | tf_op jit(solution)/shard_map/update/pallas_call | solution.py:255
  20.2 16.6 %all_to_all.5 = bf16[8,8,16,128]{3,2,1,0:T(8,128)(2,1)S(1)} all-to-all(bf16[8,8,16,128]{3,2,1,0:T(8,128)(2,1)S(1)} %update.1), channel_id=1, replica_groups=mesh['gx'=4,'gy'=8] {'gy'}, dimensions={0} | all-to-all | bytes 524288 | tf_op jit(solution)/shard_map/all_to_all | solution.py:294
  36.7 0.8 %copy.10 = bf16[16,2,8,4,128]{4,3,2,1,0:T(4,128)(2,1)} copy(bf16[16,2,8,4,128]{4,0,3,1,2:T(8,128)(2,1)S(1)} %bitcast.13) | data formatting | bytes 524288 | tf_op jit(solution)/shard_map/transpose | solution.py:296
  (1 shorter events, 0.0 us)
Async XLA Ops:
  3.4 8.6 %collective-permute-start.1 = (bf16[2,128,128]{2,1,0:T(8,128)(2,1)S(1)}, bf16[2,128,128]{2,1,0:T(8,128)(2,1)S(1)}, u32[]{:S(2)}, u32[]{:S(2)}) collective-permute-start(bf16[2,128,128]{2,1,0:T(8,128)(2,1)S(1)} %weigh.1), channel_id=1, source_target_pairs={{8,16},{16,8},{9,17},{17,9},{10,18},{18,10},{11,19},{19,11},{12,20... | collective-permute-start | bytes 196616 | tf_op jit(solution)/shard_map/ppermute | solution.py:270
  4.1 8.9 %collective-permute-start = (bf16[2,128,128]{2,1,0:T(8,128)(2,1)S(1)}, bf16[2,128,128]{2,1,0:T(8,128)(2,1)S(1)}, u32[]{:S(2)}, u32[]{:S(2)}) collective-permute-start(bf16[2,128,128]{2,1,0:T(8,128)(2,1)S(1)} %weigh.1), channel_id=1, source_target_pairs={{0,8},{16,24},{8,0},{24,16},{1,9},{17,25},{9,1},{25,17},{2,10},{18... | collective-permute-start | bytes 196616 | tf_op jit(solution)/shard_map/ppermute | solution.py:270
  13.0 4.0 %collective-permute-start.3 = (bf16[3,2,128,128]{3,2,1,0:T(8,128)(2,1)S(1)}, bf16[3,2,128,128]{3,2,1,0:T(8,128)(2,1)S(1)}, u32[]{:S(2)}, u32[]{:S(2)}) collective-permute-start(bf16[3,2,128,128]{3,2,1,0:T(8,128)(2,1)S(1)} %pad_maximum_fusion.own_ref), channel_id=1, source_target_pairs={{1,2},{3,4},{5,6},{2,1},{4,3},{6,5},{9,10},{11,12},{13,14},{10,9},... | collective-permute-start | bytes 589832 | tf_op jit(solution)/shard_map/ppermute | solution.py:270
  13.7 4.4 %collective-permute-start.2 = (bf16[3,2,128,128]{3,2,1,0:T(8,128)(2,1)S(1)}, bf16[3,2,128,128]{3,2,1,0:T(8,128)(2,1)S(1)}, u32[]{:S(2)}, u32[]{:S(2)}) collective-permute-start(bf16[3,2,128,128]{3,2,1,0:T(8,128)(2,1)S(1)} %pad_maximum_fusion.own_ref), channel_id=1, source_target_pairs={{0,1},{2,3},{4,5},{6,7},{1,0},{3,2},{5,4},{7,6},{8,9},{10,11},{12,... | collective-permute-start | bytes 589832 | tf_op jit(solution)/shard_map/ppermute | solution.py:270

commit v4 on v3

--- a/solution.py
+++ b/solution.py
@@ -39,27 +39,39 @@
     row = iota((rows, OBS_TILE), 0)
     exists = row < size
 
-    def step(t):
-        x = x_ref[0:rows, :]
-        pivot_row = x_ref[pl.ds(t, 1), :]
-        spread = jnp.broadcast_to(pivot_row, (rows, OBS_TILE))
-        column = jnp.take_along_axis(spread, idx_ref[0:rows, :], axis=1, mode="promise_in_bounds")
-        column = jnp.where(exists, column, 0.0)
-        at = jnp.broadcast_to(idx_ref[pl.ds(t, 1), :], (8, OBS_TILE))
-        pivot = jnp.take_along_axis(spread[0:8], at, axis=1, mode="promise_in_bounds")[0:1]
-        pivot = jnp.where(t < size, pivot, 1.0)
-        own = rank == t
-        scaled = jnp.where(own, -1.0, pivot_row) / pivot
-        at_row = row == t
-        column = jnp.where(at_row, -1.0, column)
-        x_ref[0:rows, :] = jnp.where(at_row | own, 0.0, x) - column * scaled
-
-    def pair(k, carry):
-        step(2 * k)
-        step(2 * k + 1)
-        return carry
-
-    lax.fori_loop(0, (count + 1) // 2, pair, 0)
+    def taken(spread, indices):
+        return jnp.take_along_axis(spread, indices, axis=1, mode="promise_in_bounds")
+
+    def step(k, carry):
+        t = 2 * k
+        u = t + 1
+        row_t, row_u = x_ref[pl.ds(t, 1), :], x_ref[pl.ds(u, 1), :]
+        spread_t = jnp.broadcast_to(row_t, (rows, OBS_TILE))
+        spread_u = jnp.broadcast_to(row_u, (rows, OBS_TILE))
+        at_t = jnp.broadcast_to(idx_ref[pl.ds(t, 1), :], (8, OBS_TILE))
+        at_u = jnp.broadcast_to(idx_ref[pl.ds(u, 1), :], (8, OBS_TILE))
+        has_t, has_u = t < size, u < size
+        a = jnp.where(has_t, taken(spread_t[0:8], at_t)[0:1], 1.0)
+        b = jnp.where(has_u, taken(spread_t[0:8], at_u)[0:1], 0.0)
+        d = jnp.where(has_u, taken(spread_u[0:8], at_u)[0:1], 1.0)
+        scale = 1.0 / (a * d - b * b)
+        own_t, own_u = rank == t, rank == u
+        own = own_t | own_u
+        head_t = jnp.where(own, jnp.where(own_t, -1.0, 0.0), row_t)
+        head_u = jnp.where(own, jnp.where(own_u, -1.0, 0.0), row_u)
+        scaled_t = (d * head_t - b * head_u) * scale
+        scaled_u = (a * head_u - b * head_t) * scale
+        column_t = jnp.where(exists, taken(spread_t, idx_ref[0:rows, :]), 0.0)
+        column_u = jnp.where(exists, taken(spread_u, idx_ref[0:rows, :]), 0.0)
+        on_t, on_u = row == t, row == u
+        on = on_t | on_u
+        column_t = jnp.where(on, jnp.where(on_t, -1.0, 0.0), column_t)
+        column_u = jnp.where(on, jnp.where(on_u, -1.0, 0.0), column_u)
+        x = jnp.where(on | own, 0.0, x_ref[0:rows, :])
+        x_ref[0:rows, :] = x - column_t * scaled_t - column_u * scaled_u
+        return carry
+
+    lax.fori_loop(0, (count + 1) // 2, step, 0)
 
 
 def in_hbm(*arrays):
@@ -160,9 +172,9 @@
     )(*in_hbm(predicted, measured_value, measurement_variance, observation_jitter, obs_block))
 
 
-def offsets(place):
+def offset(which, place):
     even = 1 - 2 * (place & 1)
-    return 0, even, -even
+    return jnp.where(which == 0, 0, jnp.where(which == 1, even, -even))
 
 
 def prepare_kernel(
@@ -173,12 +185,14 @@
     tile_y = lax.axis_index("gy")
     count_x, count_y = obs_ref.shape[0], obs_ref.shape[1]
     copies = fetch([(radius_hbm, radius_ref), (pattern_hbm, pattern_ref), (obs_hbm, obs_ref)], sems)
-    for b in range(BLOCKS):
+
+    def turn(b, carry):
         block = params_ref[b].astype(F32)
         mean = jnp.sum(block, axis=0, keepdims=True) / members
-        anomaly = block - mean
-        turned_ref[b] = anomaly.T.astype(BF16)
-
+        turned_ref[b] = (block - mean).T.astype(BF16)
+        return carry
+
+    lax.fori_loop(0, BLOCKS, turn, 0)
     for copy in copies:
         copy.wait()
     shape = (BLOCKS, OBS_TILE)
@@ -190,23 +204,28 @@
     reach = reach * reach
     pattern = jnp.concatenate([pattern_ref[i] for i in range(BLK_X)], axis=0).astype(F32)
     slots = [jnp.broadcast_to(pattern[:, p : p + 1], shape) for p in range(PATTERN)]
-    for ix, dx in enumerate(offsets(tile_x)):
-        for iy, dy in enumerate(offsets(tile_y)):
-            at_x, at_y = tile_x + dx, tile_y + dy
-            valid = (at_x >= 0) & (at_x < count_x) & (at_y >= 0) & (at_y < count_y)
-            at_x = jnp.clip(at_x, 0, count_x - 1)
-            at_y = jnp.clip(at_y, 0, count_y - 1)
-            obs = obs_ref[at_x, pl.ds(at_y, 1), :]
-            step_x = dx * BLK_X + (obs >> 2) - (block >> 2)
-            step_y = dy * BLK_Y + (obs & 3) - (block & 3)
-            inside = (jnp.abs(step_x) <= 2) & (jnp.abs(step_y) <= 2) & valid
-            offset = (step_x + 2) * 5 + (step_y + 2)
-            picked = jnp.zeros(shape, F32)
-            for p in range(PATTERN):
-                picked = jnp.where(offset == p, slots[p], picked)
-            spread = (step_x * step_x + step_y * step_y).astype(F32)
-            shaped = jnp.maximum(1.0 - spread / reach, 0.0)
-            taper_ref[ix * 3 + iy] = jnp.where(inside, picked, 0.0) * shaped / (members - 1)
+
+    def tile(t, carry):
+        iy, ix = t // 3, t % 3
+        dx, dy = offset(ix, tile_x), offset(iy, tile_y)
+        at_x, at_y = tile_x + dx, tile_y + dy
+        valid = (at_x >= 0) & (at_x < count_x) & (at_y >= 0) & (at_y < count_y)
+        at_x = jnp.clip(at_x, 0, count_x - 1)
+        at_y = jnp.clip(at_y, 0, count_y - 1)
+        obs = obs_ref[at_x, pl.ds(at_y, 1), :]
+        step_x = dx * BLK_X + (obs >> 2) - (block >> 2)
+        step_y = dy * BLK_Y + (obs & 3) - (block & 3)
+        inside = (jnp.abs(step_x) <= 2) & (jnp.abs(step_y) <= 2) & valid
+        slot = (step_x + 2) * 5 + (step_y + 2)
+        picked = jnp.zeros(shape, F32)
+        for p in range(PATTERN):
+            picked = jnp.where(slot == p, slots[p], picked)
+        spread = (step_x * step_x + step_y * step_y).astype(F32)
+        shaped = jnp.maximum(1.0 - spread / reach, 0.0)
+        taper_ref[iy, ix] = jnp.where(inside, picked, 0.0) * shaped / (members - 1)
+        return carry
+
+    lax.fori_loop(0, 9, tile, 0)
 
 
 def prepare(by_block, taper_radius, taper_pattern, obs_block):
@@ -215,7 +234,7 @@
         prepare_kernel,
         out_shape=(
             jax.ShapeDtypeStruct((BLOCKS, CELLS, members), BF16),
-            jax.ShapeDtypeStruct((9, BLOCKS, OBS_TILE), F32),
+            jax.ShapeDtypeStruct((3, 3, BLOCKS, OBS_TILE), F32),
         ),
         in_specs=[pl.BlockSpec(memory_space=pltpu.VMEM)] + [pl.BlockSpec(memory_space=pltpu.HBM)] * 3,
         out_specs=(pl.BlockSpec(memory_space=pltpu.VMEM), pl.BlockSpec(memory_space=pltpu.VMEM)),
@@ -231,44 +250,89 @@
     )(by_block, *in_hbm(taper_radius, taper_pattern, obs_block))
 
 
-def update_kernel(params_ref, turned_ref, taper_ref, own_ref, even_ref, odd_ref, out_ref):
+def moved(b, which, turned_ref, taper_ref, column_ref):
+    cross = dot(turned_ref[b], column_ref[0], ((1,), (0,)))
+    taper = jnp.concatenate([taper_ref[which, ix, pl.ds(b, 1), :] for ix in range(3)], axis=1)
+    gain = (cross * taper).astype(BF16)
+    return dot(column_ref[1], gain, ((1,), (1,)))
+
+
+def block_of(k, side, tile_y):
+    first = 2 * ((tile_y & 1) ^ 1 ^ side)
+    return (k >> 1) * BLK_Y + first + (k & 1)
+
+
+def put(out_ref, b, updated):
     share = out_ref.shape[2]
-    near = [ref.at[ix] for ix in range(3) for ref in (own_ref, even_ref, odd_ref)]
-    deviations = jnp.concatenate([tile[0] for tile in near], axis=1)
-    weighted = jnp.concatenate([tile[1] for tile in near], axis=1)
-
-    def one(b, carry):
-        cross = dot(turned_ref[b], deviations, ((1,), (0,)))
-        taper = jnp.concatenate([taper_ref[t, pl.ds(b, 1), :] for t in range(9)], axis=1)
-        gain = (cross * taper).astype(BF16)
-        delta = dot(weighted, gain, ((1,), (1,)))
-        updated = (params_ref[b].astype(F32) + delta).astype(BF16)
-        for d in range(out_ref.shape[0]):
-            out_ref[d, b] = updated[d * share : (d + 1) * share]
-        return carry
-
-    lax.fori_loop(0, BLOCKS, one, 0, unroll=True)
-
-
-def update(by_block, turned, taper, own, even, odd, parts):
+    for d in range(out_ref.shape[0]):
+        out_ref[d, b] = updated[d * share : (d + 1) * share]
+
+
+def near_kernel(params_ref, turned_ref, taper_ref, own_ref, even_ref, out_ref, part_ref):
+    tile_y = lax.axis_index("gy")
+
+    def finish(k, carry):
+        b = block_of(k, 0, tile_y)
+        delta = moved(b, 0, turned_ref, taper_ref, own_ref) + moved(b, 1, turned_ref, taper_ref, even_ref)
+        put(out_ref, b, (params_ref[b].astype(F32) + delta).astype(BF16))
+        return carry
+
+    def begin(k, carry):
+        b = block_of(k, 1, tile_y)
+        part_ref[k] = params_ref[b].astype(F32) + moved(b, 0, turned_ref, taper_ref, own_ref)
+        return carry
+
+    lax.fori_loop(0, BLOCKS // 2, finish, 0)
+    lax.fori_loop(0, BLOCKS // 2, begin, 0)
+
+
+def far_kernel(turned_ref, taper_ref, odd_ref, part_ref, done_ref, out_ref):
+    del done_ref
+    tile_y = lax.axis_index("gy")
+
+    def finish(k, carry):
+        b = block_of(k, 1, tile_y)
+        put(out_ref, b, (part_ref[k] + moved(b, 2, turned_ref, taper_ref, odd_ref)).astype(BF16))
+        return carry
+
+    lax.fori_loop(0, BLOCKS // 2, finish, 0)
+
+
+VMEM = pl.BlockSpec(memory_space=pltpu.VMEM)
+
+
+def update_near(by_block, turned, taper, own, even, parts):
     members = by_block.shape[1]
     return pl.pallas_call(
-        update_kernel,
-        out_shape=jax.ShapeDtypeStruct((parts, BLOCKS, members // parts, CELLS), BF16),
-        in_specs=[pl.BlockSpec(memory_space=pltpu.VMEM)] * 6,
-        out_specs=pl.BlockSpec(memory_space=pltpu.VMEM),
-        compiler_params=pltpu.CompilerParams(vmem_limit_bytes=40 * 2**20),
-        name="update",
-    )(by_block, turned, taper, own, even, odd)
-
-
-def swaps(block, axis):
-    count = lax.axis_size(axis)
-    found = []
-    for first in (0, 1):
-        pairs = [(i, i + 1) for i in range(first, count - 1, 2)]
-        found.append(lax.ppermute(block, axis, pairs + [(b, a) for a, b in pairs]))
-    return found
+        near_kernel,
+        out_shape=(
+            jax.ShapeDtypeStruct((parts, BLOCKS, members // parts, CELLS), BF16),
+            jax.ShapeDtypeStruct((BLOCKS // 2, members, CELLS), F32),
+        ),
+        in_specs=[VMEM] * 5,
+        out_specs=(VMEM, VMEM),
+        compiler_params=pltpu.CompilerParams(vmem_limit_bytes=24 * 2**20),
+        cost_estimate=pl.CostEstimate(flops=400_000_000, bytes_accessed=2_000_000, transcendentals=0),
+        name="near",
+    )(by_block, turned, taper, own, even)
+
+
+def update_far(turned, taper, odd, part, done):
+    return pl.pallas_call(
+        far_kernel,
+        out_shape=jax.ShapeDtypeStruct(done.shape, BF16),
+        in_specs=[VMEM] * 4 + [pl.BlockSpec(memory_space=pl.ANY)],
+        out_specs=VMEM,
+        input_output_aliases={4: 0},
+        compiler_params=pltpu.CompilerParams(vmem_limit_bytes=24 * 2**20),
+        cost_estimate=pl.CostEstimate(flops=100_000_000, bytes_accessed=1_000_000, transcendentals=0),
+        name="far",
+    )(turned, taper, odd, part, done)
+
+
+def swap(block, axis, first):
+    pairs = [(i, i + 1) for i in range(first, lax.axis_size(axis) - 1, 2)]
+    return lax.ppermute(block, axis, pairs + [(b, a) for a, b in pairs])
 
 
 def per_device(
@@ -285,12 +349,15 @@
     parts = lax.axis_size("gy")
     by_block = params.reshape(members, BLOCKS, CELLS).transpose(1, 0, 2)
     own = weigh(predicted, measured_value, measurement_variance, observation_jitter, obs_block)
-    even, odd = swaps(own, "gx")
+    even = swap(own, "gx", 0)
+    odd = swap(own, "gx", 1)
     turned, taper = prepare(by_block, taper_radius, taper_pattern, obs_block)
-    column = jnp.stack([own, even, odd])
+    column = jnp.concatenate([own, even, odd], axis=2)
     column, turned, taper = lax.optimization_barrier((column, turned, taper))
-    even, odd = swaps(column, "gy")
-    updated = update(by_block, turned, taper, column, even, odd, parts)
+    odd = swap(column, "gy", 1)
+    even = swap(column, "gy", 0)
+    done, part = update_near(by_block, turned, taper, column, even, parts)
+    updated = update_far(turned, taper, odd, part, done)
     arrived = lax.all_to_all(updated, "gy", split_axis=0, concat_axis=0, tiled=True)
     share = members // parts
     arrived = arrived.reshape(parts, BLK_X, BLK_Y, share, CELLS).transpose(3, 1, 0, 2, 4)

time: 37.8 us -> 36.3 us (0.960)
  starting transfers between devices: 10.6 us -> 6.94 us
  Pallas kernels: 6.47 us -> 8.81 us
  waiting for transfers between devices: 2.04 us -> 1.33 us
  blocking collectives: 16.6 us -> 17 us
    ppermute x4, starting transfers between devices: 10.6 us -> 6.94 us  [swap(): return lax.ppermute(block, axis, pairs + [(b, a) for a, b in pairs])]
    pallas_call x1 -> x2, Pallas kernels: 2.09 us -> 4.27 us  [the longest x1 2.92 us: update_near(): pl.pallas_call(near_kernel, out_shape=(jax.ShapeDtypeStruct((parts, BLOCK...]
    ppermute x4, waiting for transfers between devices: 2.04 us -> 1.33 us  [swap(): return lax.ppermute(block, axis, pairs + [(b, a) for a, b in pairs])]
    pallas_call x1, Pallas kernels: 0.97 us -> 1.54 us  [prepare(): pl.pallas_call(prepare_kernel, out_shape=(jax.ShapeDtypeStruct((BLOCKS, C...]
    all_to_all x1, blocking collectives: 16.6 us -> 17 us  [per_device(): lax.all_to_all(updated, 'gy', split_axis=0, concat_axis=0, tiled=True)]
    pallas_call x1, Pallas kernels: 3.4 us -> 3.01 us  [weigh(): pl.pallas_call(weigh_kernel, out_shape=jax.ShapeDtypeStruct((2, members,...]
  transfers between devices with their start and end apart: 4 -> 4, of which waited for: 2 -> 2; matrix products, arithmetic and copies ran while one was open for 3% -> 3% of each run, Pallas kernels for 3% -> 12%
where the time goes in v4:
time: 36.3 us; the launch traced here: 36 us
  blocking collectives  17 us (47%)
  Pallas kernels  8.81 us (24%)
  starting transfers between devices  6.94 us (19%)
  local copies, waits for them, and re-layouts  1.81 us (5%)
  waiting for transfers between devices  1.33 us (4%)
    all_to_all x1, blocking collectives, per_device(): lax.all_to_all(updated, 'gy', split_axis=0, concat_axis=0, tiled=True)  17 us
    ppermute x4, starting transfers between devices, swap(): return lax.ppermute(block, axis, pairs + [(b, a) for a, b in pairs])  6.94 us
    pallas_call x1, Pallas kernels, weigh(): pl.pallas_call(weigh_kernel, out_shape=jax.ShapeDtypeStruct((2, members,...  3.01 us
    pallas_call x1, Pallas kernels, update_near(): pl.pallas_call(near_kernel, out_shape=(jax.ShapeDtypeStruct((parts, BLOCK...  2.92 us
    pallas_call x1, Pallas kernels, prepare(): pl.pallas_call(prepare_kernel, out_shape=(jax.ShapeDtypeStruct((BLOCKS, C...  1.54 us
    pallas_call x1, Pallas kernels, update_far(): pl.pallas_call(far_kernel, out_shape=jax.ShapeDtypeStruct(done.shape, BF1...  1.35 us
    ppermute x4, waiting for transfers between devices, swap(): return lax.ppermute(block, axis, pairs + [(b, a) for a, b in pairs])  1.33 us
    unnamed x1, local copies, waits for them, and re-layouts  0.99 us
  transfers between devices with their start and end apart: 4, of which 2 were waited for; matrix products, arithmetic and copies ran while one was open for 3% of the time, Pallas kernels for 12%

profile of v4, /device:TPU:0, one launch (start us, length us, event | category | flops | bytes accessed | tf_op | source)
XLA Modules:
  0.0 36.0 jit_solution(7308844852996946601)
XLA Ops:
  0.0 3.0 %weigh.1 = bf16[2,128,128]{2,1,0:T(8,128)(2,1)S(1)} custom-call(f32[1,1,128,128]{3,2,1,0:T(8,128)} %pred_hbm.1, f32[1,1,128]{2,1,0:T(1,128)} %mv_hbm.1, f32[1,1,128]{2,1,0:T(1,128)} %var_hbm.1, f32[1,1,128,128]{3,2,1,0:T(8,128)} %jit_hbm.1, s32[4,8,128]{2,1,0:T(8,128)} %obs_hbm.3), custom_call_target="tpu_custom_call" | custom-call | tf_op jit(solution)/shard_map/weigh/pallas_call | solution.py:154
  3.0 0.7 %collective-permute-start.1 = (bf16[2,128,128]{2,1,0:T(8,128)(2,1)S(1)}, bf16[2,128,128]{2,1,0:T(8,128)(2,1)S(1)}, u32[]{:S(2)}, u32[]{:S(2)}) collective-permute-start(bf16[2,128,128]{2,1,0:T(8,128)(2,1)S(1)} %weigh.1), channel_id=1, source_target_pairs={{8,16},{16,8},{9,17},{17,9},{10,18},{18,10},{11,19},{19,11},{12,20... | collective-permute-start | bytes 196616 | tf_op jit(solution)/shard_map/ppermute | solution.py:335
  3.7 5.5 %collective-permute-start = (bf16[2,128,128]{2,1,0:T(8,128)(2,1)S(1)}, bf16[2,128,128]{2,1,0:T(8,128)(2,1)S(1)}, u32[]{:S(2)}, u32[]{:S(2)}) collective-permute-start(bf16[2,128,128]{2,1,0:T(8,128)(2,1)S(1)} %weigh.1), channel_id=1, source_target_pairs={{0,8},{16,24},{8,0},{24,16},{1,9},{17,25},{9,1},{25,17},{2,10},{18... | collective-permute-start | bytes 196616 | tf_op jit(solution)/shard_map/ppermute | solution.py:335
  9.2 1.0 %copy.10 = bf16[128,2,4,128]{3,0,2,1:T(8,128)(2,1)S(1)} copy(bf16[128,2,4,128]{3,2,1,0:T(4,128)(2,1)} %param.8) | data formatting | bytes 524288 | tf_op args[0]
  10.2 1.5 %prepare.1 = (bf16[8,128,128]{2,1,0:T(8,128)(2,1)S(1)}, f32[3,3,8,128]{3,2,1,0:T(8,128)S(1)}) custom-call(bf16[8,128,128]{2,1,0:T(8,128)(2,1)S(1)} %bitcast.7, s32[2,4]{1,0:T(2,128)} %radius_hbm.1, s32[2,4,25]{2,1,0:T(4,128)} %pattern_hbm.1, s32[4,8,128]{2,1,0:T(8,128)} %obs_hbm.3), custom_call_target="tpu_custom_call" | custom-call | flops 4000000 | bytes 1000000 | tf_op jit(solution)/shard_map/prepare/pallas_call | solution.py:233
  11.8 0.0 collective-permute-done.1
  11.8 0.6 %collective-permute-done = bf16[2,128,128]{2,1,0:T(8,128)(2,1)S(1)} collective-permute-done((bf16[2,128,128]{2,1,0:T(8,128)(2,1)S(1)}, bf16[2,128,128]{2,1,0:T(8,128)(2,1)S(1)}, u32[]{:S(2)}, u32[]{:S(2)}) %collective-permute-start) | collective-permute-done | bytes 65568 | tf_op jit(solution)/shard_map/ppermute | solution.py:335
  12.4 0.1 collective-permute-start.3
  12.5 0.7 %collective-permute-start.2 = (bf16[2,128,384]{2,1,0:T(8,128)(2,1)S(1)}, bf16[2,128,384]{2,1,0:T(8,128)(2,1)S(1)}, u32[]{:S(2)}, u32[]{:S(2)}) collective-permute-start(bf16[2,128,384]{2,1,0:T(8,128)(2,1)S(1)} %pad_maximum_fusion.own_ref), channel_id=1, source_target_pairs={{1,2},{3,4},{5,6},{2,1},{4,3},{6,5},{9,10},{11,12},{13,14},{10,9},... | collective-permute-start | bytes 589832 | tf_op jit(solution)/shard_map/ppermute | solution.py:335
  13.1 0.7 %collective-permute-done.3.even_ref = bf16[2,128,384]{2,1,0:T(8,128)(2,1)S(1)} collective-permute-done((bf16[2,128,384]{2,1,0:T(8,128)(2,1)S(1)}, bf16[2,128,384]{2,1,0:T(8,128)(2,1)S(1)}, u32[]{:S(2)}, u32[]{:S(2)}) %collective-permute-start.3) | collective-permute-done | bytes 196640 | tf_op jit(solution)/shard_map/ppermute | solution.py:335
  13.9 2.9 %near.1 = (bf16[8,8,16,128]{3,2,1,0:T(8,128)(2,1)S(1)}, f32[4,128,128]{2,1,0:T(8,128)S(1)}) custom-call(bf16[8,128,128]{2,1,0:T(8,128)(2,1)S(1)} %bitcast.8, bf16[8,128,128]{2,1,0:T(8,128)(2,1)S(1)} %get-tuple-element.14.turned_ref, f32[3,3,8,128]{3,2,1,0:T(8,128)S(1)} %get-tuple-element.15.taper_ref, bf16[2,128,384]{2,1,0:T(8,128)(2,1)S(1)} %pad_maximum_fusion.own_ref, ...), custom_call_target="tpu_custom_call" | custom-call | flops 400000000 | bytes 2000000 | tf_op jit(solution)/shard_map/near/pallas_call | solution.py:306
  16.8 0.0 collective-permute-done.2.odd_ref
  16.8 1.3 %far.1 = bf16[8,8,16,128]{3,2,1,0:T(8,128)(2,1)S(1)} custom-call(bf16[8,128,128]{2,1,0:T(8,128)(2,1)S(1)} %get-tuple-element.14.turned_ref, f32[3,3,8,128]{3,2,1,0:T(8,128)S(1)} %get-tuple-element.15.taper_ref, bf16[2,128,384]{2,1,0:T(8,128)(2,1)S(1)} %collective-permute-done.2.odd_ref, ...), custom_call_target="tpu_custom_call", output_to_operand_aliasing={{}: (4, {})} | custom-call | flops 100000000 | bytes 1000000 | tf_op jit(solution)/shard_map/far/pallas_call | solution.py:321
  18.2 17.0 %all_to_all.5 = bf16[8,8,16,128]{3,2,1,0:T(8,128)(2,1)S(1)} all-to-all(bf16[8,8,16,128]{3,2,1,0:T(8,128)(2,1)S(1)} %far.1), channel_id=1, replica_groups=mesh['gx'=4,'gy'=8] {'gy'}, dimensions={0} | all-to-all | bytes 524288 | tf_op jit(solution)/shard_map/all_to_all | solution.py:361
  35.2 0.8 %copy.11 = bf16[16,2,8,4,128]{4,3,2,1,0:T(4,128)(2,1)} copy(bf16[16,2,8,4,128]{4,0,3,1,2:T(8,128)(2,1)S(1)} %bitcast.9) | data formatting | bytes 524288 | tf_op jit(solution)/shard_map/transpose | solution.py:363
  (1 shorter events, 0.0 us)
Async XLA Ops:
  3.0 8.7 %collective-permute-start.1 = (bf16[2,128,128]{2,1,0:T(8,128)(2,1)S(1)}, bf16[2,128,128]{2,1,0:T(8,128)(2,1)S(1)}, u32[]{:S(2)}, u32[]{:S(2)}) collective-permute-start(bf16[2,128,128]{2,1,0:T(8,128)(2,1)S(1)} %weigh.1), channel_id=1, source_target_pairs={{8,16},{16,8},{9,17},{17,9},{10,18},{18,10},{11,19},{19,11},{12,20... | collective-permute-start | bytes 196616 | tf_op jit(solution)/shard_map/ppermute | solution.py:335
  3.7 8.7 %collective-permute-start = (bf16[2,128,128]{2,1,0:T(8,128)(2,1)S(1)}, bf16[2,128,128]{2,1,0:T(8,128)(2,1)S(1)}, u32[]{:S(2)}, u32[]{:S(2)}) collective-permute-start(bf16[2,128,128]{2,1,0:T(8,128)(2,1)S(1)} %weigh.1), channel_id=1, source_target_pairs={{0,8},{16,24},{8,0},{24,16},{1,9},{17,25},{9,1},{25,17},{2,10},{18... | collective-permute-start | bytes 196616 | tf_op jit(solution)/shard_map/ppermute | solution.py:335
  12.4 1.5 %collective-permute-start.3 = (bf16[2,128,384]{2,1,0:T(8,128)(2,1)S(1)}, bf16[2,128,384]{2,1,0:T(8,128)(2,1)S(1)}, u32[]{:S(2)}, u32[]{:S(2)}) collective-permute-start(bf16[2,128,384]{2,1,0:T(8,128)(2,1)S(1)} %pad_maximum_fusion.own_ref), channel_id=1, source_target_pairs={{0,1},{2,3},{4,5},{6,7},{1,0},{3,2},{5,4},{7,6},{8,9},{10,11},{12,... | collective-permute-start | bytes 589832 | tf_op jit(solution)/shard_map/ppermute | solution.py:335
  12.5 4.4 %collective-permute-start.2 = (bf16[2,128,384]{2,1,0:T(8,128)(2,1)S(1)}, bf16[2,128,384]{2,1,0:T(8,128)(2,1)S(1)}, u32[]{:S(2)}, u32[]{:S(2)}) collective-permute-start(bf16[2,128,384]{2,1,0:T(8,128)(2,1)S(1)} %pad_maximum_fusion.own_ref), channel_id=1, source_target_pairs={{1,2},{3,4},{5,6},{2,1},{4,3},{6,5},{9,10},{11,12},{13,14},{10,9},... | collective-permute-start | bytes 589832 | tf_op jit(solution)/shard_map/ppermute | solution.py:335

commit v5 on v4

--- a/solution.py
+++ b/solution.py
@@ -54,13 +54,14 @@
         a = jnp.where(has_t, taken(spread_t[0:8], at_t)[0:1], 1.0)
         b = jnp.where(has_u, taken(spread_t[0:8], at_u)[0:1], 0.0)
         d = jnp.where(has_u, taken(spread_u[0:8], at_u)[0:1], 1.0)
-        scale = 1.0 / (a * d - b * b)
         own_t, own_u = rank == t, rank == u
         own = own_t | own_u
         head_t = jnp.where(own, jnp.where(own_t, -1.0, 0.0), row_t)
         head_u = jnp.where(own, jnp.where(own_u, -1.0, 0.0), row_u)
-        scaled_t = (d * head_t - b * head_u) * scale
-        scaled_u = (a * head_u - b * head_t) * scale
+        inverse = 1.0 / a
+        factor = b * inverse
+        scaled_u = (head_u - factor * head_t) / (d - b * factor)
+        scaled_t = head_t * inverse - factor * scaled_u
         column_t = jnp.where(exists, taken(spread_t, idx_ref[0:rows, :]), 0.0)
         column_u = jnp.where(exists, taken(spread_u, idx_ref[0:rows, :]), 0.0)
         on_t, on_u = row == t, row == u
@@ -174,7 +175,7 @@
 
 def offset(which, place):
     even = 1 - 2 * (place & 1)
-    return jnp.where(which == 0, 0, jnp.where(which == 1, even, -even))
+    return (0, even, -even)[which]
 
 
 def prepare_kernel(
@@ -186,13 +187,10 @@
     count_x, count_y = obs_ref.shape[0], obs_ref.shape[1]
     copies = fetch([(radius_hbm, radius_ref), (pattern_hbm, pattern_ref), (obs_hbm, obs_ref)], sems)
 
-    def turn(b, carry):
+    for b in range(BLOCKS):
         block = params_ref[b].astype(F32)
         mean = jnp.sum(block, axis=0, keepdims=True) / members
         turned_ref[b] = (block - mean).T.astype(BF16)
-        return carry
-
-    lax.fori_loop(0, BLOCKS, turn, 0)
     for copy in copies:
         copy.wait()
     shape = (BLOCKS, OBS_TILE)
@@ -205,7 +203,7 @@
     pattern = jnp.concatenate([pattern_ref[i] for i in range(BLK_X)], axis=0).astype(F32)
     slots = [jnp.broadcast_to(pattern[:, p : p + 1], shape) for p in range(PATTERN)]
 
-    def tile(t, carry):
+    for t in range(9):
         iy, ix = t // 3, t % 3
         dx, dy = offset(ix, tile_x), offset(iy, tile_y)
         at_x, at_y = tile_x + dx, tile_y + dy
@@ -223,9 +221,6 @@
         spread = (step_x * step_x + step_y * step_y).astype(F32)
         shaped = jnp.maximum(1.0 - spread / reach, 0.0)
         taper_ref[iy, ix] = jnp.where(inside, picked, 0.0) * shaped / (members - 1)
-        return carry
-
-    lax.fori_loop(0, 9, tile, 0)
 
 
 def prepare(by_block, taper_radius, taper_pattern, obs_block):
@@ -250,11 +245,12 @@
     )(by_block, *in_hbm(taper_radius, taper_pattern, obs_block))
 
 
-def moved(b, which, turned_ref, taper_ref, column_ref):
-    cross = dot(turned_ref[b], column_ref[0], ((1,), (0,)))
-    taper = jnp.concatenate([taper_ref[which, ix, pl.ds(b, 1), :] for ix in range(3)], axis=1)
+def moved(b, which, turned_ref, taper_ref, tiles_ref):
+    cross = dot(turned_ref[b], tiles_ref[0], ((1,), (0,)))
+    count = tiles_ref.shape[2] // OBS_TILE
+    taper = jnp.concatenate([taper_ref[which, k, pl.ds(b, 1), :] for k in range(count)], axis=1)
     gain = (cross * taper).astype(BF16)
-    return dot(column_ref[1], gain, ((1,), (1,)))
+    return dot(tiles_ref[1], gain, ((1,), (1,)))
 
 
 def block_of(k, side, tile_y):
@@ -271,31 +267,21 @@
 def near_kernel(params_ref, turned_ref, taper_ref, own_ref, even_ref, out_ref, part_ref):
     tile_y = lax.axis_index("gy")
 
-    def finish(k, carry):
+    for k in range(BLOCKS // 2):
         b = block_of(k, 0, tile_y)
         delta = moved(b, 0, turned_ref, taper_ref, own_ref) + moved(b, 1, turned_ref, taper_ref, even_ref)
         put(out_ref, b, (params_ref[b].astype(F32) + delta).astype(BF16))
-        return carry
-
-    def begin(k, carry):
+    for k in range(BLOCKS // 2):
         b = block_of(k, 1, tile_y)
         part_ref[k] = params_ref[b].astype(F32) + moved(b, 0, turned_ref, taper_ref, own_ref)
-        return carry
-
-    lax.fori_loop(0, BLOCKS // 2, finish, 0)
-    lax.fori_loop(0, BLOCKS // 2, begin, 0)
 
 
 def far_kernel(turned_ref, taper_ref, odd_ref, part_ref, done_ref, out_ref):
     del done_ref
     tile_y = lax.axis_index("gy")
-
-    def finish(k, carry):
+    for k in range(BLOCKS // 2):
         b = block_of(k, 1, tile_y)
         put(out_ref, b, (part_ref[k] + moved(b, 2, turned_ref, taper_ref, odd_ref)).astype(BF16))
-        return carry
-
-    lax.fori_loop(0, BLOCKS // 2, finish, 0)
 
 
 VMEM = pl.BlockSpec(memory_space=pltpu.VMEM)

time: 36.3 us -> 36.1 us (level)
  Pallas kernels: 8.81 us -> 6.56 us
  blocking collectives: 17 us -> 18.3 us
  waiting for transfers between devices: 1.33 us -> 1.8 us
    all_to_all x1, blocking collectives: 17 us -> 18.3 us  [per_device(): lax.all_to_all(updated, 'gy', split_axis=0, concat_axis=0, tiled=True)]
    pallas_call x1, Pallas kernels: 2.92 us -> 1.89 us  [update_near(): pl.pallas_call(near_kernel, out_shape=(jax.ShapeDtypeStruct((parts, BLOCK...]
    pallas_call x1, Pallas kernels: 1.54 us -> 0.97 us  [prepare(): pl.pallas_call(prepare_kernel, out_shape=(jax.ShapeDtypeStruct((BLOCKS, C...]
    ppermute x4, waiting for transfers between devices: 1.33 us -> 1.8 us  [swap(): return lax.ppermute(block, axis, pairs + [(b, a) for a, b in pairs])]
    pallas_call x1, Pallas kernels: 1.35 us -> 0.89 us  [update_far(): pl.pallas_call(far_kernel, out_shape=jax.ShapeDtypeStruct(done.shape, BF1...]
  transfers between devices with their start and end apart: 4 -> 4, of which waited for: 2 -> 2; matrix products, arithmetic and copies ran while one was open for 3% -> 3% of each run, Pallas kernels for 12% -> 8%
where the time goes in v5:
time: 36.1 us; the launch traced here: 35.8 us
  blocking collectives  18.3 us (51%)
  starting transfers between devices  7.25 us (20%)
  Pallas kernels  6.56 us (18%)
  local copies, waits for them, and re-layouts  1.81 us (5%)
  waiting for transfers between devices  1.8 us (5%)
    all_to_all x1, blocking collectives, per_device(): lax.all_to_all(updated, 'gy', split_axis=0, concat_axis=0, tiled=True)  18.3 us
    ppermute x4, starting transfers between devices, swap(): return lax.ppermute(block, axis, pairs + [(b, a) for a, b in pairs])  7.25 us
    pallas_call x1, Pallas kernels, weigh(): pl.pallas_call(weigh_kernel, out_shape=jax.ShapeDtypeStruct((2, members,...  2.81 us
    pallas_call x1, Pallas kernels, update_near(): pl.pallas_call(near_kernel, out_shape=(jax.ShapeDtypeStruct((parts, BLOCK...  1.89 us
    ppermute x4, waiting for transfers between devices, swap(): return lax.ppermute(block, axis, pairs + [(b, a) for a, b in pairs])  1.8 us
    unnamed x1, local copies, waits for them, and re-layouts  0.99 us
    pallas_call x1, Pallas kernels, prepare(): pl.pallas_call(prepare_kernel, out_shape=(jax.ShapeDtypeStruct((BLOCKS, C...  0.97 us
    pallas_call x1, Pallas kernels, update_far(): pl.pallas_call(far_kernel, out_shape=jax.ShapeDtypeStruct(done.shape, BF1...  0.89 us
  transfers between devices with their start and end apart: 4, of which 2 were waited for; matrix products, arithmetic and copies ran while one was open for 3% of the time, Pallas kernels for 8%

profile of v5, /device:TPU:0, one launch (start us, length us, event | category | flops | bytes accessed | tf_op | source)
XLA Modules:
  0.0 35.8 jit_solution(11508353475585529021)
XLA Ops:
  0.0 2.8 %weigh.1 = bf16[2,128,128]{2,1,0:T(8,128)(2,1)S(1)} custom-call(f32[1,1,128,128]{3,2,1,0:T(8,128)} %pred_hbm.1, f32[1,1,128]{2,1,0:T(1,128)} %mv_hbm.1, f32[1,1,128]{2,1,0:T(1,128)} %var_hbm.1, f32[1,1,128,128]{3,2,1,0:T(8,128)} %jit_hbm.1, s32[4,8,128]{2,1,0:T(8,128)} %obs_hbm.3), custom_call_target="tpu_custom_call" | custom-call | tf_op jit(solution)/shard_map/weigh/pallas_call | solution.py:155
  2.8 0.7 %collective-permute-start.1 = (bf16[2,128,128]{2,1,0:T(8,128)(2,1)S(1)}, bf16[2,128,128]{2,1,0:T(8,128)(2,1)S(1)}, u32[]{:S(2)}, u32[]{:S(2)}) collective-permute-start(bf16[2,128,128]{2,1,0:T(8,128)(2,1)S(1)} %weigh.1), channel_id=1, source_target_pairs={{8,16},{16,8},{9,17},{17,9},{10,18},{18,10},{11,19},{19,11},{12,20... | collective-permute-start | bytes 196616 | tf_op jit(solution)/shard_map/ppermute | solution.py:321
  3.5 5.8 %collective-permute-start = (bf16[2,128,128]{2,1,0:T(8,128)(2,1)S(1)}, bf16[2,128,128]{2,1,0:T(8,128)(2,1)S(1)}, u32[]{:S(2)}, u32[]{:S(2)}) collective-permute-start(bf16[2,128,128]{2,1,0:T(8,128)(2,1)S(1)} %weigh.1), channel_id=1, source_target_pairs={{0,8},{16,24},{8,0},{24,16},{1,9},{17,25},{9,1},{25,17},{2,10},{18... | collective-permute-start | bytes 196616 | tf_op jit(solution)/shard_map/ppermute | solution.py:321
  9.3 1.0 %copy.10 = bf16[128,2,4,128]{3,0,2,1:T(8,128)(2,1)S(1)} copy(bf16[128,2,4,128]{3,2,1,0:T(4,128)(2,1)} %param.8) | data formatting | bytes 524288 | tf_op args[0]
  10.3 1.0 %prepare.1 = (bf16[8,128,128]{2,1,0:T(8,128)(2,1)S(1)}, f32[3,3,8,128]{3,2,1,0:T(8,128)S(1)}) custom-call(bf16[8,128,128]{2,1,0:T(8,128)(2,1)S(1)} %bitcast.7, s32[2,4]{1,0:T(2,128)} %radius_hbm.1, s32[2,4,25]{2,1,0:T(4,128)} %pattern_hbm.1, s32[4,8,128]{2,1,0:T(8,128)} %obs_hbm.3), custom_call_target="tpu_custom_call" | custom-call | flops 4000000 | bytes 1000000 | tf_op jit(solution)/shard_map/prepare/pallas_call | solution.py:228
  11.3 0.0 collective-permute-done.1
  11.3 1.0 %collective-permute-done = bf16[2,128,128]{2,1,0:T(8,128)(2,1)S(1)} collective-permute-done((bf16[2,128,128]{2,1,0:T(8,128)(2,1)S(1)}, bf16[2,128,128]{2,1,0:T(8,128)(2,1)S(1)}, u32[]{:S(2)}, u32[]{:S(2)}) %collective-permute-start) | collective-permute-done | bytes 65568 | tf_op jit(solution)/shard_map/ppermute | solution.py:321
  12.4 0.1 collective-permute-start.3
  12.5 0.7 %collective-permute-start.2 = (bf16[2,128,384]{2,1,0:T(8,128)(2,1)S(1)}, bf16[2,128,384]{2,1,0:T(8,128)(2,1)S(1)}, u32[]{:S(2)}, u32[]{:S(2)}) collective-permute-start(bf16[2,128,384]{2,1,0:T(8,128)(2,1)S(1)} %pad_maximum_fusion.own_ref), channel_id=1, source_target_pairs={{1,2},{3,4},{5,6},{2,1},{4,3},{6,5},{9,10},{11,12},{13,14},{10,9},... | collective-permute-start | bytes 589832 | tf_op jit(solution)/shard_map/ppermute | solution.py:321
  13.1 0.7 %collective-permute-done.3.even_ref = bf16[2,128,384]{2,1,0:T(8,128)(2,1)S(1)} collective-permute-done((bf16[2,128,384]{2,1,0:T(8,128)(2,1)S(1)}, bf16[2,128,384]{2,1,0:T(8,128)(2,1)S(1)}, u32[]{:S(2)}, u32[]{:S(2)}) %collective-permute-start.3) | collective-permute-done | bytes 196640 | tf_op jit(solution)/shard_map/ppermute | solution.py:321
  13.9 1.9 %near.1 = (bf16[8,8,16,128]{3,2,1,0:T(8,128)(2,1)S(1)}, f32[4,128,128]{2,1,0:T(8,128)S(1)}) custom-call(bf16[8,128,128]{2,1,0:T(8,128)(2,1)S(1)} %bitcast.8, bf16[8,128,128]{2,1,0:T(8,128)(2,1)S(1)} %get-tuple-element.14.turned_ref, f32[3,3,8,128]{3,2,1,0:T(8,128)S(1)} %get-tuple-element.15.taper_ref, bf16[2,128,384]{2,1,0:T(8,128)(2,1)S(1)} %pad_maximum_fusion.own_ref, ...), custom_call_target="tpu_custom_call" | custom-call | flops 400000000 | bytes 2000000 | tf_op jit(solution)/shard_map/near/pallas_call | solution.py:292
  15.8 0.0 collective-permute-done.2.odd_ref
  15.8 0.9 %far.1 = bf16[8,8,16,128]{3,2,1,0:T(8,128)(2,1)S(1)} custom-call(bf16[8,128,128]{2,1,0:T(8,128)(2,1)S(1)} %get-tuple-element.14.turned_ref, f32[3,3,8,128]{3,2,1,0:T(8,128)S(1)} %get-tuple-element.15.taper_ref, bf16[2,128,384]{2,1,0:T(8,128)(2,1)S(1)} %collective-permute-done.2.odd_ref, ...), custom_call_target="tpu_custom_call", output_to_operand_aliasing={{}: (4, {})} | custom-call | flops 100000000 | bytes 1000000 | tf_op jit(solution)/shard_map/far/pallas_call | solution.py:307
  16.7 18.3 %all_to_all.5 = bf16[8,8,16,128]{3,2,1,0:T(8,128)(2,1)S(1)} all-to-all(bf16[8,8,16,128]{3,2,1,0:T(8,128)(2,1)S(1)} %far.1), channel_id=1, replica_groups=mesh['gx'=4,'gy'=8] {'gy'}, dimensions={0} | all-to-all | bytes 524288 | tf_op jit(solution)/shard_map/all_to_all | solution.py:347
  35.0 0.8 %copy.11 = bf16[16,2,8,4,128]{4,3,2,1,0:T(4,128)(2,1)} copy(bf16[16,2,8,4,128]{4,0,3,1,2:T(8,128)(2,1)S(1)} %bitcast.9) | data formatting | bytes 524288 | tf_op jit(solution)/shard_map/transpose | solution.py:349
  (1 shorter events, 0.0 us)
Async XLA Ops:
  2.8 8.5 %collective-permute-start.1 = (bf16[2,128,128]{2,1,0:T(8,128)(2,1)S(1)}, bf16[2,128,128]{2,1,0:T(8,128)(2,1)S(1)}, u32[]{:S(2)}, u32[]{:S(2)}) collective-permute-start(bf16[2,128,128]{2,1,0:T(8,128)(2,1)S(1)} %weigh.1), channel_id=1, source_target_pairs={{8,16},{16,8},{9,17},{17,9},{10,18},{18,10},{11,19},{19,11},{12,20... | collective-permute-start | bytes 196616 | tf_op jit(solution)/shard_map/ppermute | solution.py:321
  3.5 8.9 %collective-permute-start = (bf16[2,128,128]{2,1,0:T(8,128)(2,1)S(1)}, bf16[2,128,128]{2,1,0:T(8,128)(2,1)S(1)}, u32[]{:S(2)}, u32[]{:S(2)}) collective-permute-start(bf16[2,128,128]{2,1,0:T(8,128)(2,1)S(1)} %weigh.1), channel_id=1, source_target_pairs={{0,8},{16,24},{8,0},{24,16},{1,9},{17,25},{9,1},{25,17},{2,10},{18... | collective-permute-start | bytes 196616 | tf_op jit(solution)/shard_map/ppermute | solution.py:321
  12.4 1.5 %collective-permute-start.3 = (bf16[2,128,384]{2,1,0:T(8,128)(2,1)S(1)}, bf16[2,128,384]{2,1,0:T(8,128)(2,1)S(1)}, u32[]{:S(2)}, u32[]{:S(2)}) collective-permute-start(bf16[2,128,384]{2,1,0:T(8,128)(2,1)S(1)} %pad_maximum_fusion.own_ref), channel_id=1, source_target_pairs={{0,1},{2,3},{4,5},{6,7},{1,0},{3,2},{5,4},{7,6},{8,9},{10,11},{12,... | collective-permute-start | bytes 589832 | tf_op jit(solution)/shard_map/ppermute | solution.py:321
  12.5 3.3 %collective-permute-start.2 = (bf16[2,128,384]{2,1,0:T(8,128)(2,1)S(1)}, bf16[2,128,384]{2,1,0:T(8,128)(2,1)S(1)}, u32[]{:S(2)}, u32[]{:S(2)}) collective-permute-start(bf16[2,128,384]{2,1,0:T(8,128)(2,1)S(1)} %pad_maximum_fusion.own_ref), channel_id=1, source_target_pairs={{1,2},{3,4},{5,6},{2,1},{4,3},{6,5},{9,10},{11,12},{13,14},{10,9},... | collective-permute-start | bytes 589832 | tf_op jit(solution)/shard_map/ppermute | solution.py:321

commit v6 on v5

--- a/solution.py
+++ b/solution.py
@@ -317,8 +317,11 @@
 
 
 def swap(block, axis, first):
-    pairs = [(i, i + 1) for i in range(first, lax.axis_size(axis) - 1, 2)]
-    return lax.ppermute(block, axis, pairs + [(b, a) for a, b in pairs])
+    count = lax.axis_size(axis)
+    pairs = [(i, i + 1) for i in range(first, count - 1, 2)]
+    paired = {i for pair in pairs for i in pair}
+    alone = [(i, i) for i in range(count) if i not in paired]
+    return lax.ppermute(block, axis, pairs + [(b, a) for a, b in pairs] + alone)
 
 
 def per_device(
@@ -340,8 +343,8 @@
     turned, taper = prepare(by_block, taper_radius, taper_pattern, obs_block)
     column = jnp.concatenate([own, even, odd], axis=2)
     column, turned, taper = lax.optimization_barrier((column, turned, taper))
+    even = swap(column, "gy", 0)
     odd = swap(column, "gy", 1)
-    even = swap(column, "gy", 0)
     done, part = update_near(by_block, turned, taper, column, even, parts)
     updated = update_far(turned, taper, odd, part, done)
     arrived = lax.all_to_all(updated, "gy", split_axis=0, concat_axis=0, tiled=True)

time: 36.1 us -> 36 us (level)
  no operation moved by 1% of the time
where the time goes in v6:
time: 36 us; the launch traced here: 35.7 us
  blocking collectives  18.3 us (51%)
  starting transfers between devices  7.25 us (20%)
  Pallas kernels  6.56 us (18%)
  local copies, waits for them, and re-layouts  1.81 us (5%)
  waiting for transfers between devices  1.7 us (5%)
    all_to_all x1, blocking collectives, per_device(): lax.all_to_all(updated, 'gy', split_axis=0, concat_axis=0, tiled=True)  18.3 us
    ppermute x4, starting transfers between devices, swap(): return lax.ppermute(block, axis, pairs + [(b, a) for a, b in pairs] + alone)  7.25 us
    pallas_call x1, Pallas kernels, weigh(): pl.pallas_call(weigh_kernel, out_shape=jax.ShapeDtypeStruct((2, members,...  2.81 us
    pallas_call x1, Pallas kernels, update_near(): pl.pallas_call(near_kernel, out_shape=(jax.ShapeDtypeStruct((parts, BLOCK...  1.89 us
    ppermute x4, waiting for transfers between devices, swap(): return lax.ppermute(block, axis, pairs + [(b, a) for a, b in pairs] + alone)  1.7 us
    unnamed x1, local copies, waits for them, and re-layouts  0.99 us
    pallas_call x1, Pallas kernels, prepare(): pl.pallas_call(prepare_kernel, out_shape=(jax.ShapeDtypeStruct((BLOCKS, C...  0.97 us
    pallas_call x1, Pallas kernels, update_far(): pl.pallas_call(far_kernel, out_shape=jax.ShapeDtypeStruct(done.shape, BF1...  0.89 us
  transfers between devices with their start and end apart: 4, of which 2 were waited for; matrix products, arithmetic and copies ran while one was open for 3% of the time, Pallas kernels for 8%

profile of v6, /device:TPU:0, one launch (start us, length us, event | category | flops | bytes accessed | tf_op | source)
XLA Modules:
  0.0 35.7 jit_solution(3394434066630249627)
XLA Ops:
  0.0 2.8 %weigh.1 = bf16[2,128,128]{2,1,0:T(8,128)(2,1)S(1)} custom-call(f32[1,1,128,128]{3,2,1,0:T(8,128)} %pred_hbm.1, f32[1,1,128]{2,1,0:T(1,128)} %mv_hbm.1, f32[1,1,128]{2,1,0:T(1,128)} %var_hbm.1, f32[1,1,128,128]{3,2,1,0:T(8,128)} %jit_hbm.1, s32[4,8,128]{2,1,0:T(8,128)} %obs_hbm.3), custom_call_target="tpu_custom_call" | custom-call | tf_op jit(solution)/shard_map/weigh/pallas_call | solution.py:155
  2.8 0.7 %collective-permute-start.1 = (bf16[2,128,128]{2,1,0:T(8,128)(2,1)S(1)}, bf16[2,128,128]{2,1,0:T(8,128)(2,1)S(1)}, u32[]{:S(2)}, u32[]{:S(2)}) collective-permute-start(bf16[2,128,128]{2,1,0:T(8,128)(2,1)S(1)} %weigh.1), channel_id=1, source_target_pairs={{8,16},{16,8},{0,0},{24,24},{9,17},{17,9},{1,1},{25,25},{10,18},{1... | collective-permute-start | bytes 196616 | tf_op jit(solution)/shard_map/ppermute | solution.py:324
  3.5 5.8 %collective-permute-start = (bf16[2,128,128]{2,1,0:T(8,128)(2,1)S(1)}, bf16[2,128,128]{2,1,0:T(8,128)(2,1)S(1)}, u32[]{:S(2)}, u32[]{:S(2)}) collective-permute-start(bf16[2,128,128]{2,1,0:T(8,128)(2,1)S(1)} %weigh.1), channel_id=1, source_target_pairs={{0,8},{16,24},{8,0},{24,16},{1,9},{17,25},{9,1},{25,17},{2,10},{18... | collective-permute-start | bytes 196616 | tf_op jit(solution)/shard_map/ppermute | solution.py:324
  9.3 1.0 %copy.10 = bf16[128,2,4,128]{3,0,2,1:T(8,128)(2,1)S(1)} copy(bf16[128,2,4,128]{3,2,1,0:T(4,128)(2,1)} %param.8) | data formatting | bytes 524288 | tf_op args[0]
  10.3 1.0 %prepare.1 = (bf16[8,128,128]{2,1,0:T(8,128)(2,1)S(1)}, f32[3,3,8,128]{3,2,1,0:T(8,128)S(1)}) custom-call(bf16[8,128,128]{2,1,0:T(8,128)(2,1)S(1)} %bitcast.7, s32[2,4]{1,0:T(2,128)} %radius_hbm.1, s32[2,4,25]{2,1,0:T(4,128)} %pattern_hbm.1, s32[4,8,128]{2,1,0:T(8,128)} %obs_hbm.3), custom_call_target="tpu_custom_call" | custom-call | flops 4000000 | bytes 1000000 | tf_op jit(solution)/shard_map/prepare/pallas_call | solution.py:228
  11.3 0.0 collective-permute-done.1
  11.3 0.9 %collective-permute-done = bf16[2,128,128]{2,1,0:T(8,128)(2,1)S(1)} collective-permute-done((bf16[2,128,128]{2,1,0:T(8,128)(2,1)S(1)}, bf16[2,128,128]{2,1,0:T(8,128)(2,1)S(1)}, u32[]{:S(2)}, u32[]{:S(2)}) %collective-permute-start) | collective-permute-done | bytes 65568 | tf_op jit(solution)/shard_map/ppermute | solution.py:324
  12.3 0.1 collective-permute-start.3
  12.4 0.7 %collective-permute-start.2 = (bf16[2,128,384]{2,1,0:T(8,128)(2,1)S(1)}, bf16[2,128,384]{2,1,0:T(8,128)(2,1)S(1)}, u32[]{:S(2)}, u32[]{:S(2)}) collective-permute-start(bf16[2,128,384]{2,1,0:T(8,128)(2,1)S(1)} %pad_maximum_fusion.own_ref), channel_id=1, source_target_pairs={{1,2},{3,4},{5,6},{2,1},{4,3},{6,5},{0,0},{7,7},{9,10},{11,12},{13... | collective-permute-start | bytes 589832 | tf_op jit(solution)/shard_map/ppermute | solution.py:324
  13.0 0.7 %collective-permute-done.3.even_ref = bf16[2,128,384]{2,1,0:T(8,128)(2,1)S(1)} collective-permute-done((bf16[2,128,384]{2,1,0:T(8,128)(2,1)S(1)}, bf16[2,128,384]{2,1,0:T(8,128)(2,1)S(1)}, u32[]{:S(2)}, u32[]{:S(2)}) %collective-permute-start.3) | collective-permute-done | bytes 196640 | tf_op jit(solution)/shard_map/ppermute | solution.py:324
  13.8 1.9 %near.1 = (bf16[8,8,16,128]{3,2,1,0:T(8,128)(2,1)S(1)}, f32[4,128,128]{2,1,0:T(8,128)S(1)}) custom-call(bf16[8,128,128]{2,1,0:T(8,128)(2,1)S(1)} %bitcast.8, bf16[8,128,128]{2,1,0:T(8,128)(2,1)S(1)} %get-tuple-element.14.turned_ref, f32[3,3,8,128]{3,2,1,0:T(8,128)S(1)} %get-tuple-element.15.taper_ref, bf16[2,128,384]{2,1,0:T(8,128)(2,1)S(1)} %pad_maximum_fusion.own_ref, ...), custom_call_target="tpu_custom_call" | custom-call | flops 400000000 | bytes 2000000 | tf_op jit(solution)/shard_map/near/pallas_call | solution.py:292
  15.7 0.0 collective-permute-done.2.odd_ref
  15.7 0.9 %far.1 = bf16[8,8,16,128]{3,2,1,0:T(8,128)(2,1)S(1)} custom-call(bf16[8,128,128]{2,1,0:T(8,128)(2,1)S(1)} %get-tuple-element.14.turned_ref, f32[3,3,8,128]{3,2,1,0:T(8,128)S(1)} %get-tuple-element.15.taper_ref, bf16[2,128,384]{2,1,0:T(8,128)(2,1)S(1)} %collective-permute-done.2.odd_ref, ...), custom_call_target="tpu_custom_call", output_to_operand_aliasing={{}: (4, {})} | custom-call | flops 100000000 | bytes 1000000 | tf_op jit(solution)/shard_map/far/pallas_call | solution.py:307
  16.6 18.3 %all_to_all.5 = bf16[8,8,16,128]{3,2,1,0:T(8,128)(2,1)S(1)} all-to-all(bf16[8,8,16,128]{3,2,1,0:T(8,128)(2,1)S(1)} %far.1), channel_id=1, replica_groups=mesh['gx'=4,'gy'=8] {'gy'}, dimensions={0} | all-to-all | bytes 524288 | tf_op jit(solution)/shard_map/all_to_all | solution.py:350
  34.9 0.8 %copy.11 = bf16[16,2,8,4,128]{4,3,2,1,0:T(4,128)(2,1)} copy(bf16[16,2,8,4,128]{4,0,3,1,2:T(8,128)(2,1)S(1)} %bitcast.9) | data formatting | bytes 524288 | tf_op jit(solution)/shard_map/transpose | solution.py:352
  (1 shorter events, 0.0 us)
Async XLA Ops:
  2.8 8.5 %collective-permute-start.1 = (bf16[2,128,128]{2,1,0:T(8,128)(2,1)S(1)}, bf16[2,128,128]{2,1,0:T(8,128)(2,1)S(1)}, u32[]{:S(2)}, u32[]{:S(2)}) collective-permute-start(bf16[2,128,128]{2,1,0:T(8,128)(2,1)S(1)} %weigh.1), channel_id=1, source_target_pairs={{8,16},{16,8},{0,0},{24,24},{9,17},{17,9},{1,1},{25,25},{10,18},{1... | collective-permute-start | bytes 196616 | tf_op jit(solution)/shard_map/ppermute | solution.py:324
  3.5 8.8 %collective-permute-start = (bf16[2,128,128]{2,1,0:T(8,128)(2,1)S(1)}, bf16[2,128,128]{2,1,0:T(8,128)(2,1)S(1)}, u32[]{:S(2)}, u32[]{:S(2)}) collective-permute-start(bf16[2,128,128]{2,1,0:T(8,128)(2,1)S(1)} %weigh.1), channel_id=1, source_target_pairs={{0,8},{16,24},{8,0},{24,16},{1,9},{17,25},{9,1},{25,17},{2,10},{18... | collective-permute-start | bytes 196616 | tf_op jit(solution)/shard_map/ppermute | solution.py:324
  12.3 1.5 %collective-permute-start.3 = (bf16[2,128,384]{2,1,0:T(8,128)(2,1)S(1)}, bf16[2,128,384]{2,1,0:T(8,128)(2,1)S(1)}, u32[]{:S(2)}, u32[]{:S(2)}) collective-permute-start(bf16[2,128,384]{2,1,0:T(8,128)(2,1)S(1)} %pad_maximum_fusion.own_ref), channel_id=1, source_target_pairs={{0,1},{2,3},{4,5},{6,7},{1,0},{3,2},{5,4},{7,6},{8,9},{10,11},{12,... | collective-permute-start | bytes 589832 | tf_op jit(solution)/shard_map/ppermute | solution.py:324
  12.4 3.3 %collective-permute-start.2 = (bf16[2,128,384]{2,1,0:T(8,128)(2,1)S(1)}, bf16[2,128,384]{2,1,0:T(8,128)(2,1)S(1)}, u32[]{:S(2)}, u32[]{:S(2)}) collective-permute-start(bf16[2,128,384]{2,1,0:T(8,128)(2,1)S(1)} %pad_maximum_fusion.own_ref), channel_id=1, source_target_pairs={{1,2},{3,4},{5,6},{2,1},{4,3},{6,5},{0,0},{7,7},{9,10},{11,12},{13... | collective-permute-start | bytes 589832 | tf_op jit(solution)/shard_map/ppermute | solution.py:324

commit v7 on v5

--- a/solution.py
+++ b/solution.py
@@ -316,8 +316,11 @@
     )(turned, taper, odd, part, done)
 
 
-def swap(block, axis, first):
-    pairs = [(i, i + 1) for i in range(first, lax.axis_size(axis) - 1, 2)]
+def swap(block, axis, first, close=False):
+    count = lax.axis_size(axis)
+    pairs = [(i, i + 1) for i in range(first, count - 1, 2)]
+    if close:
+        pairs.append((count - 1, 0))
     return lax.ppermute(block, axis, pairs + [(b, a) for a, b in pairs])
 
 
@@ -336,7 +339,7 @@
     by_block = params.reshape(members, BLOCKS, CELLS).transpose(1, 0, 2)
     own = weigh(predicted, measured_value, measurement_variance, observation_jitter, obs_block)
     even = swap(own, "gx", 0)
-    odd = swap(own, "gx", 1)
+    odd = swap(own, "gx", 1, close=True)
     turned, taper = prepare(by_block, taper_radius, taper_pattern, obs_block)
     column = jnp.concatenate([own, even, odd], axis=2)
     column, turned, taper = lax.optimization_barrier((column, turned, taper))

time: 36.1 us -> 34.6 us (0.958)
  starting transfers between devices: 7.25 us -> 5.55 us
  waiting for transfers between devices: 1.8 us -> 2.2 us
    ppermute x4, starting transfers between devices: 7.25 us -> 5.55 us  [swap(): return lax.ppermute(block, axis, pairs + [(b, a) for a, b in pairs])]
    ppermute x4, waiting for transfers between devices: 1.8 us -> 2.2 us  [swap(): return lax.ppermute(block, axis, pairs + [(b, a) for a, b in pairs])]
where the time goes in v7:
time: 34.6 us; the launch traced here: 34.3 us
  blocking collectives  18.2 us (53%)
  Pallas kernels  6.46 us (19%)
  starting transfers between devices  5.55 us (16%)
  waiting for transfers between devices  2.2 us (6%)
  local copies, waits for them, and re-layouts  1.81 us (5%)
    all_to_all x1, blocking collectives, per_device(): lax.all_to_all(updated, 'gy', split_axis=0, concat_axis=0, tiled=True)  18.2 us
    ppermute x4, starting transfers between devices, swap(): return lax.ppermute(block, axis, pairs + [(b, a) for a, b in pairs])  5.55 us
    pallas_call x1, Pallas kernels, weigh(): pl.pallas_call(weigh_kernel, out_shape=jax.ShapeDtypeStruct((2, members,...  2.71 us
    ppermute x4, waiting for transfers between devices, swap(): return lax.ppermute(block, axis, pairs + [(b, a) for a, b in pairs])  2.2 us
    pallas_call x1, Pallas kernels, update_near(): pl.pallas_call(near_kernel, out_shape=(jax.ShapeDtypeStruct((parts, BLOCK...  1.89 us
    unnamed x1, local copies, waits for them, and re-layouts  0.99 us
    pallas_call x1, Pallas kernels, prepare(): pl.pallas_call(prepare_kernel, out_shape=(jax.ShapeDtypeStruct((BLOCKS, C...  0.97 us
    pallas_call x1, Pallas kernels, update_far(): pl.pallas_call(far_kernel, out_shape=jax.ShapeDtypeStruct(done.shape, BF1...  0.89 us
  transfers between devices with their start and end apart: 4, of which 2 were waited for; matrix products, arithmetic and copies ran while one was open for 3% of the time, Pallas kernels for 8%

profile of v7, /device:TPU:0, one launch (start us, length us, event | category | flops | bytes accessed | tf_op | source)
XLA Modules:
  0.0 34.3 jit_solution(15424929084950659568)
XLA Ops:
  0.0 2.7 %weigh.1 = bf16[2,128,128]{2,1,0:T(8,128)(2,1)S(1)} custom-call(f32[1,1,128,128]{3,2,1,0:T(8,128)} %pred_hbm.1, f32[1,1,128]{2,1,0:T(1,128)} %mv_hbm.1, f32[1,1,128]{2,1,0:T(1,128)} %var_hbm.1, f32[1,1,128,128]{3,2,1,0:T(8,128)} %jit_hbm.1, s32[4,8,128]{2,1,0:T(8,128)} %obs_hbm.3), custom_call_target="tpu_custom_call" | custom-call | tf_op jit(solution)/shard_map/weigh/pallas_call | solution.py:155
  2.7 4.0 %collective-permute-start.1 = (bf16[2,128,128]{2,1,0:T(8,128)(2,1)S(1)}, bf16[2,128,128]{2,1,0:T(8,128)(2,1)S(1)}, u32[]{:S(2)}, u32[]{:S(2)}) collective-permute-start(bf16[2,128,128]{2,1,0:T(8,128)(2,1)S(1)} %weigh.1), channel_id=1, source_target_pairs={{8,16},{24,0},{16,8},{0,24},{9,17},{25,1},{17,9},{1,25},{10,18},{2... | collective-permute-start | bytes 196616 | tf_op jit(solution)/shard_map/ppermute | solution.py:324
  6.7 0.8 %collective-permute-start = (bf16[2,128,128]{2,1,0:T(8,128)(2,1)S(1)}, bf16[2,128,128]{2,1,0:T(8,128)(2,1)S(1)}, u32[]{:S(2)}, u32[]{:S(2)}) collective-permute-start(bf16[2,128,128]{2,1,0:T(8,128)(2,1)S(1)} %weigh.1), channel_id=1, source_target_pairs={{0,8},{16,24},{8,0},{24,16},{1,9},{17,25},{9,1},{25,17},{2,10},{18... | collective-permute-start | bytes 196616 | tf_op jit(solution)/shard_map/ppermute | solution.py:324
  7.5 1.0 %copy.10 = bf16[128,2,4,128]{3,0,2,1:T(8,128)(2,1)S(1)} copy(bf16[128,2,4,128]{3,2,1,0:T(4,128)(2,1)} %param.8) | data formatting | bytes 524288 | tf_op args[0]
  8.5 1.0 %prepare.1 = (bf16[8,128,128]{2,1,0:T(8,128)(2,1)S(1)}, f32[3,3,8,128]{3,2,1,0:T(8,128)S(1)}) custom-call(bf16[8,128,128]{2,1,0:T(8,128)(2,1)S(1)} %bitcast.7, s32[2,4]{1,0:T(2,128)} %radius_hbm.1, s32[2,4,25]{2,1,0:T(4,128)} %pattern_hbm.1, s32[4,8,128]{2,1,0:T(8,128)} %obs_hbm.3), custom_call_target="tpu_custom_call" | custom-call | flops 4000000 | bytes 1000000 | tf_op jit(solution)/shard_map/prepare/pallas_call | solution.py:228
  9.5 0.0 collective-permute-done.1
  9.5 1.4 %collective-permute-done = bf16[2,128,128]{2,1,0:T(8,128)(2,1)S(1)} collective-permute-done((bf16[2,128,128]{2,1,0:T(8,128)(2,1)S(1)}, bf16[2,128,128]{2,1,0:T(8,128)(2,1)S(1)}, u32[]{:S(2)}, u32[]{:S(2)}) %collective-permute-start) | collective-permute-done | bytes 65568 | tf_op jit(solution)/shard_map/ppermute | solution.py:324
  11.0 0.1 collective-permute-start.3
  11.1 0.7 %collective-permute-start.2 = (bf16[2,128,384]{2,1,0:T(8,128)(2,1)S(1)}, bf16[2,128,384]{2,1,0:T(8,128)(2,1)S(1)}, u32[]{:S(2)}, u32[]{:S(2)}) collective-permute-start(bf16[2,128,384]{2,1,0:T(8,128)(2,1)S(1)} %pad_maximum_fusion.own_ref), channel_id=1, source_target_pairs={{1,2},{3,4},{5,6},{2,1},{4,3},{6,5},{9,10},{11,12},{13,14},{10,9},... | collective-permute-start | bytes 589832 | tf_op jit(solution)/shard_map/ppermute | solution.py:324
  11.7 0.7 %collective-permute-done.3.even_ref = bf16[2,128,384]{2,1,0:T(8,128)(2,1)S(1)} collective-permute-done((bf16[2,128,384]{2,1,0:T(8,128)(2,1)S(1)}, bf16[2,128,384]{2,1,0:T(8,128)(2,1)S(1)}, u32[]{:S(2)}, u32[]{:S(2)}) %collective-permute-start.3) | collective-permute-done | bytes 196640 | tf_op jit(solution)/shard_map/ppermute | solution.py:324
  12.5 1.9 %near.1 = (bf16[8,8,16,128]{3,2,1,0:T(8,128)(2,1)S(1)}, f32[4,128,128]{2,1,0:T(8,128)S(1)}) custom-call(bf16[8,128,128]{2,1,0:T(8,128)(2,1)S(1)} %bitcast.8, bf16[8,128,128]{2,1,0:T(8,128)(2,1)S(1)} %get-tuple-element.14.turned_ref, f32[3,3,8,128]{3,2,1,0:T(8,128)S(1)} %get-tuple-element.15.taper_ref, bf16[2,128,384]{2,1,0:T(8,128)(2,1)S(1)} %pad_maximum_fusion.own_ref, ...), custom_call_target="tpu_custom_call" | custom-call | flops 400000000 | bytes 2000000 | tf_op jit(solution)/shard_map/near/pallas_call | solution.py:292
  14.4 0.0 collective-permute-done.2.odd_ref
  14.4 0.9 %far.1 = bf16[8,8,16,128]{3,2,1,0:T(8,128)(2,1)S(1)} custom-call(bf16[8,128,128]{2,1,0:T(8,128)(2,1)S(1)} %get-tuple-element.14.turned_ref, f32[3,3,8,128]{3,2,1,0:T(8,128)S(1)} %get-tuple-element.15.taper_ref, bf16[2,128,384]{2,1,0:T(8,128)(2,1)S(1)} %collective-permute-done.2.odd_ref, ...), custom_call_target="tpu_custom_call", output_to_operand_aliasing={{}: (4, {})} | custom-call | flops 100000000 | bytes 1000000 | tf_op jit(solution)/shard_map/far/pallas_call | solution.py:307
  15.3 18.2 %all_to_all.5 = bf16[8,8,16,128]{3,2,1,0:T(8,128)(2,1)S(1)} all-to-all(bf16[8,8,16,128]{3,2,1,0:T(8,128)(2,1)S(1)} %far.1), channel_id=1, replica_groups=mesh['gx'=4,'gy'=8] {'gy'}, dimensions={0} | all-to-all | bytes 524288 | tf_op jit(solution)/shard_map/all_to_all | solution.py:350
  33.5 0.8 %copy.11 = bf16[16,2,8,4,128]{4,3,2,1,0:T(4,128)(2,1)} copy(bf16[16,2,8,4,128]{4,0,3,1,2:T(8,128)(2,1)S(1)} %bitcast.9) | data formatting | bytes 524288 | tf_op jit(solution)/shard_map/transpose | solution.py:352
  (1 shorter events, 0.0 us)
Async XLA Ops:
  2.7 6.8 %collective-permute-start.1 = (bf16[2,128,128]{2,1,0:T(8,128)(2,1)S(1)}, bf16[2,128,128]{2,1,0:T(8,128)(2,1)S(1)}, u32[]{:S(2)}, u32[]{:S(2)}) collective-permute-start(bf16[2,128,128]{2,1,0:T(8,128)(2,1)S(1)} %weigh.1), channel_id=1, source_target_pairs={{8,16},{24,0},{16,8},{0,24},{9,17},{25,1},{17,9},{1,25},{10,18},{2... | collective-permute-start | bytes 196616 | tf_op jit(solution)/shard_map/ppermute | solution.py:324
  6.7 4.3 %collective-permute-start = (bf16[2,128,128]{2,1,0:T(8,128)(2,1)S(1)}, bf16[2,128,128]{2,1,0:T(8,128)(2,1)S(1)}, u32[]{:S(2)}, u32[]{:S(2)}) collective-permute-start(bf16[2,128,128]{2,1,0:T(8,128)(2,1)S(1)} %weigh.1), channel_id=1, source_target_pairs={{0,8},{16,24},{8,0},{24,16},{1,9},{17,25},{9,1},{25,17},{2,10},{18... | collective-permute-start | bytes 196616 | tf_op jit(solution)/shard_map/ppermute | solution.py:324
  11.0 1.5 %collective-permute-start.3 = (bf16[2,128,384]{2,1,0:T(8,128)(2,1)S(1)}, bf16[2,128,384]{2,1,0:T(8,128)(2,1)S(1)}, u32[]{:S(2)}, u32[]{:S(2)}) collective-permute-start(bf16[2,128,384]{2,1,0:T(8,128)(2,1)S(1)} %pad_maximum_fusion.own_ref), channel_id=1, source_target_pairs={{0,1},{2,3},{4,5},{6,7},{1,0},{3,2},{5,4},{7,6},{8,9},{10,11},{12,... | collective-permute-start | bytes 589832 | tf_op jit(solution)/shard_map/ppermute | solution.py:324
  11.1 3.3 %collective-permute-start.2 = (bf16[2,128,384]{2,1,0:T(8,128)(2,1)S(1)}, bf16[2,128,384]{2,1,0:T(8,128)(2,1)S(1)}, u32[]{:S(2)}, u32[]{:S(2)}) collective-permute-start(bf16[2,128,384]{2,1,0:T(8,128)(2,1)S(1)} %pad_maximum_fusion.own_ref), channel_id=1, source_target_pairs={{1,2},{3,4},{5,6},{2,1},{4,3},{6,5},{9,10},{11,12},{13,14},{10,9},... | collective-permute-start | bytes 589832 | tf_op jit(solution)/shard_map/ppermute | solution.py:324

commit v8 on v7

--- a/solution.py
+++ b/solution.py
@@ -245,10 +245,10 @@
     )(by_block, *in_hbm(taper_radius, taper_pattern, obs_block))
 
 
-def moved(b, which, turned_ref, taper_ref, tiles_ref):
+def moved(b, which, first, turned_ref, taper_ref, tiles_ref):
     cross = dot(turned_ref[b], tiles_ref[0], ((1,), (0,)))
     count = tiles_ref.shape[2] // OBS_TILE
-    taper = jnp.concatenate([taper_ref[which, k, pl.ds(b, 1), :] for k in range(count)], axis=1)
+    taper = jnp.concatenate([taper_ref[which, first + k, pl.ds(b, 1), :] for k in range(count)], axis=1)
     gain = (cross * taper).astype(BF16)
     return dot(tiles_ref[1], gain, ((1,), (1,)))
 
@@ -269,19 +269,20 @@
 
     for k in range(BLOCKS // 2):
         b = block_of(k, 0, tile_y)
-        delta = moved(b, 0, turned_ref, taper_ref, own_ref) + moved(b, 1, turned_ref, taper_ref, even_ref)
+        delta = moved(b, 0, 0, turned_ref, taper_ref, own_ref) + moved(b, 1, 0, turned_ref, taper_ref, even_ref)
         put(out_ref, b, (params_ref[b].astype(F32) + delta).astype(BF16))
     for k in range(BLOCKS // 2):
         b = block_of(k, 1, tile_y)
-        part_ref[k] = params_ref[b].astype(F32) + moved(b, 0, turned_ref, taper_ref, own_ref)
-
-
-def far_kernel(turned_ref, taper_ref, odd_ref, part_ref, done_ref, out_ref):
+        part_ref[k] = params_ref[b].astype(F32) + moved(b, 0, 0, turned_ref, taper_ref, own_ref)
+
+
+def far_kernel(turned_ref, taper_ref, odd_ref, beside_ref, part_ref, done_ref, out_ref):
     del done_ref
     tile_y = lax.axis_index("gy")
     for k in range(BLOCKS // 2):
         b = block_of(k, 1, tile_y)
-        put(out_ref, b, (part_ref[k] + moved(b, 2, turned_ref, taper_ref, odd_ref)).astype(BF16))
+        delta = moved(b, 2, 0, turned_ref, taper_ref, odd_ref) + moved(b, 2, 1, turned_ref, taper_ref, beside_ref)
+        put(out_ref, b, (part_ref[k] + delta).astype(BF16))
 
 
 VMEM = pl.BlockSpec(memory_space=pltpu.VMEM)
@@ -303,17 +304,17 @@
     )(by_block, turned, taper, own, even)
 
 
-def update_far(turned, taper, odd, part, done):
+def update_far(turned, taper, odd, beside, part, done):
     return pl.pallas_call(
         far_kernel,
         out_shape=jax.ShapeDtypeStruct(done.shape, BF16),
-        in_specs=[VMEM] * 4 + [pl.BlockSpec(memory_space=pl.ANY)],
+        in_specs=[VMEM] * 5 + [pl.BlockSpec(memory_space=pl.ANY)],
         out_specs=VMEM,
-        input_output_aliases={4: 0},
+        input_output_aliases={5: 0},
         compiler_params=pltpu.CompilerParams(vmem_limit_bytes=24 * 2**20),
         cost_estimate=pl.CostEstimate(flops=100_000_000, bytes_accessed=1_000_000, transcendentals=0),
         name="far",
-    )(turned, taper, odd, part, done)
+    )(turned, taper, odd, beside, part, done)
 
 
 def swap(block, axis, first, close=False):
@@ -338,15 +339,18 @@
     parts = lax.axis_size("gy")
     by_block = params.reshape(members, BLOCKS, CELLS).transpose(1, 0, 2)
     own = weigh(predicted, measured_value, measurement_variance, observation_jitter, obs_block)
+    sent, by_block = lax.optimization_barrier((own, by_block))
+    across = swap(sent, "gy", 1)
     even = swap(own, "gx", 0)
     odd = swap(own, "gx", 1, close=True)
     turned, taper = prepare(by_block, taper_radius, taper_pattern, obs_block)
+    even, odd, across, turned, taper = lax.optimization_barrier((even, odd, across, turned, taper))
+    beside = jnp.concatenate([even, odd], axis=2)
     column = jnp.concatenate([own, even, odd], axis=2)
-    column, turned, taper = lax.optimization_barrier((column, turned, taper))
-    odd = swap(column, "gy", 1)
+    across_beside = swap(beside, "gy", 1)
     even = swap(column, "gy", 0)
     done, part = update_near(by_block, turned, taper, column, even, parts)
-    updated = update_far(turned, taper, odd, part, done)
+    updated = update_far(turned, taper, across, across_beside, part, done)
     arrived = lax.all_to_all(updated, "gy", split_axis=0, concat_axis=0, tiled=True)
     share = members // parts
     arrived = arrived.reshape(parts, BLK_X, BLK_Y, share, CELLS).transpose(3, 1, 0, 2, 4)

time: 34.6 us -> 36.7 us (1.061)
  starting transfers between devices: 5.55 us -> 8.98 us
  waiting for transfers between devices: 2.2 us -> 1.38 us
  blocking collectives: 18.2 us -> 17.6 us
    ppermute x4 -> x5, starting transfers between devices: 5.55 us -> 8.98 us  [swap(): return lax.ppermute(block, axis, pairs + [(b, a) for a, b in pairs])]
    ppermute x4 -> x5, waiting for transfers between devices: 2.2 us -> 1.38 us  [swap(): return lax.ppermute(block, axis, pairs + [(b, a) for a, b in pairs])]
    all_to_all x1, blocking collectives: 18.2 us -> 17.6 us  [per_device(): lax.all_to_all(updated, 'gy', split_axis=0, concat_axis=0, tiled=True)]
  transfers between devices with their start and end apart: 4 -> 5, of which waited for: 2 -> 2; matrix products, arithmetic and copies ran while one was open for 3% -> 3% of each run, Pallas kernels for 8% -> 8%
where the time goes in v8:
time: 36.7 us; the launch traced here: 36.4 us
  blocking collectives  17.6 us (48%)
  starting transfers between devices  8.98 us (24%)
  Pallas kernels  6.48 us (18%)
  local copies, waits for them, and re-layouts  1.81 us (5%)
  waiting for transfers between devices  1.38 us (4%)
    all_to_all x1, blocking collectives, per_device(): lax.all_to_all(updated, 'gy', split_axis=0, concat_axis=0, tiled=True)  17.6 us
    ppermute x5, starting transfers between devices, swap(): return lax.ppermute(block, axis, pairs + [(b, a) for a, b in pairs])  8.98 us
    pallas_call x1, Pallas kernels, weigh(): pl.pallas_call(weigh_kernel, out_shape=jax.ShapeDtypeStruct((2, members,...  2.71 us
    pallas_call x1, Pallas kernels, update_near(): pl.pallas_call(near_kernel, out_shape=(jax.ShapeDtypeStruct((parts, BLOCK...  1.9 us
    ppermute x5, waiting for transfers between devices, swap(): return lax.ppermute(block, axis, pairs + [(b, a) for a, b in pairs])  1.38 us
    unnamed x1, local copies, waits for them, and re-layouts  0.99 us
    pallas_call x1, Pallas kernels, prepare(): pl.pallas_call(prepare_kernel, out_shape=(jax.ShapeDtypeStruct((BLOCKS, C...  0.97 us
    pallas_call x1, Pallas kernels, update_far(): pl.pallas_call(far_kernel, out_shape=jax.ShapeDtypeStruct(done.shape, BF1...  0.91 us
  transfers between devices with their start and end apart: 5, of which 2 were waited for; matrix products, arithmetic and copies ran while one was open for 3% of the time, Pallas kernels for 8%

profile of v8, /device:TPU:0, one launch (start us, length us, event | category | flops | bytes accessed | tf_op | source)
XLA Modules:
  0.0 36.4 jit_solution(5695742432144027395)
XLA Ops:
  0.0 2.7 %weigh.1 = bf16[2,128,128]{2,1,0:T(8,128)(2,1)S(1)} custom-call(f32[1,1,128,128]{3,2,1,0:T(8,128)} %pred_hbm.1, f32[1,1,128]{2,1,0:T(1,128)} %mv_hbm.1, f32[1,1,128]{2,1,0:T(1,128)} %var_hbm.1, f32[1,1,128,128]{3,2,1,0:T(8,128)} %jit_hbm.1, s32[4,8,128]{2,1,0:T(8,128)} %obs_hbm.3), custom_call_target="tpu_custom_call" | custom-call | tf_op jit(solution)/shard_map/weigh/pallas_call | solution.py:155
  2.7 4.1 %collective-permute-start.1 = (bf16[2,128,128]{2,1,0:T(8,128)(2,1)S(1)}, bf16[2,128,128]{2,1,0:T(8,128)(2,1)S(1)}, u32[]{:S(2)}, u32[]{:S(2)}) collective-permute-start(bf16[2,128,128]{2,1,0:T(8,128)(2,1)S(1)} %weigh.1), channel_id=1, source_target_pairs={{8,16},{24,0},{16,8},{0,24},{9,17},{25,1},{17,9},{1,25},{10,18},{2... | collective-permute-start | bytes 196616 | tf_op jit(solution)/shard_map/ppermute | solution.py:325
  6.8 0.6 %collective-permute-start = (bf16[2,128,128]{2,1,0:T(8,128)(2,1)S(1)}, bf16[2,128,128]{2,1,0:T(8,128)(2,1)S(1)}, u32[]{:S(2)}, u32[]{:S(2)}) collective-permute-start(bf16[2,128,128]{2,1,0:T(8,128)(2,1)S(1)} %weigh.1), channel_id=1, source_target_pairs={{0,8},{16,24},{8,0},{24,16},{1,9},{17,25},{9,1},{25,17},{2,10},{18... | collective-permute-start | bytes 196616 | tf_op jit(solution)/shard_map/ppermute | solution.py:325
  7.4 1.0 %copy.10 = bf16[128,2,4,128]{3,0,2,1:T(8,128)(2,1)S(1)} copy(bf16[128,2,4,128]{3,2,1,0:T(4,128)(2,1)} %param.8) | data formatting | bytes 524288 | tf_op args[0]
  8.4 0.7 %collective-permute-start.2 = (bf16[2,128,128]{2,1,0:T(8,128)(2,1)S(1)}, bf16[2,128,128]{2,1,0:T(8,128)(2,1)S(1)}, u32[]{:S(2)}, u32[]{:S(2)}) collective-permute-start(bf16[2,128,128]{2,1,0:T(8,128)(2,1)S(1)} %weigh.1), channel_id=1, source_target_pairs={{1,2},{3,4},{5,6},{2,1},{4,3},{6,5},{9,10},{11,12},{13,14},{10,9},... | collective-permute-start | bytes 196616 | tf_op jit(solution)/shard_map/ppermute | solution.py:325
  9.1 1.0 %prepare.1 = (bf16[8,128,128]{2,1,0:T(8,128)(2,1)S(1)}, f32[3,3,8,128]{3,2,1,0:T(8,128)S(1)}) custom-call(bf16[8,128,128]{2,1,0:T(8,128)(2,1)S(1)} %bitcast.7, s32[2,4]{1,0:T(2,128)} %radius_hbm.1, s32[2,4,25]{2,1,0:T(4,128)} %pattern_hbm.1, s32[4,8,128]{2,1,0:T(8,128)} %obs_hbm.3), custom_call_target="tpu_custom_call" | custom-call | flops 4000000 | bytes 1000000 | tf_op jit(solution)/shard_map/prepare/pallas_call | solution.py:228
  10.1 0.0 collective-permute-done.1
  10.1 1.0 %collective-permute-done = bf16[2,128,128]{2,1,0:T(8,128)(2,1)S(1)} collective-permute-done((bf16[2,128,128]{2,1,0:T(8,128)(2,1)S(1)}, bf16[2,128,128]{2,1,0:T(8,128)(2,1)S(1)}, u32[]{:S(2)}, u32[]{:S(2)}) %collective-permute-start) | collective-permute-done | bytes 65568 | tf_op jit(solution)/shard_map/ppermute | solution.py:325
  11.1 0.0 collective-permute-done.2.odd_ref
  11.1 3.0 %collective-permute-start.4 = (bf16[2,128,384]{2,1,0:T(8,128)(2,1)S(1)}, bf16[2,128,384]{2,1,0:T(8,128)(2,1)S(1)}, u32[]{:S(2)}, u32[]{:S(2)}) collective-permute-start(bf16[2,128,384]{2,1,0:T(8,128)(2,1)S(1)} %pad_maximum_fusion.own_ref), channel_id=1, source_target_pairs={{0,1},{2,3},{4,5},{6,7},{1,0},{3,2},{5,4},{7,6},{8,9},{10,11},{12,... | collective-permute-start | bytes 589832 | tf_op jit(solution)/shard_map/ppermute | solution.py:325
  14.1 0.7 %collective-permute-start.3 = (bf16[2,128,256]{2,1,0:T(8,128)(2,1)S(1)}, bf16[2,128,256]{2,1,0:T(8,128)(2,1)S(1)}, u32[]{:S(2)}, u32[]{:S(2)}) collective-permute-start(bf16[2,128,256]{2,1,0:T(8,128)(2,1)S(1)} %pad_maximum_fusion.1), channel_id=1, source_target_pairs={{1,2},{3,4},{5,6},{2,1},{4,3},{6,5},{9,10},{11,12},{13,14},{10,9},... | collective-permute-start | bytes 393224 | tf_op jit(solution)/shard_map/ppermute | solution.py:325
  14.7 0.4 %collective-permute-done.4.even_ref = bf16[2,128,384]{2,1,0:T(8,128)(2,1)S(1)} collective-permute-done((bf16[2,128,384]{2,1,0:T(8,128)(2,1)S(1)}, bf16[2,128,384]{2,1,0:T(8,128)(2,1)S(1)}, u32[]{:S(2)}, u32[]{:S(2)}) %collective-permute-start.4) | collective-permute-done | bytes 196640 | tf_op jit(solution)/shard_map/ppermute | solution.py:325
  15.1 1.9 %near.1 = (bf16[8,8,16,128]{3,2,1,0:T(8,128)(2,1)S(1)}, f32[4,128,128]{2,1,0:T(8,128)S(1)}) custom-call(bf16[8,128,128]{2,1,0:T(8,128)(2,1)S(1)} %bitcast.8, bf16[8,128,128]{2,1,0:T(8,128)(2,1)S(1)} %get-tuple-element.20.turned_ref, f32[3,3,8,128]{3,2,1,0:T(8,128)S(1)} %get-tuple-element.21.taper_ref, bf16[2,128,384]{2,1,0:T(8,128)(2,1)S(1)} %pad_maximum_fusion.own_ref, ...), custom_call_target="tpu_custom_call" | custom-call | flops 400000000 | bytes 2000000 | tf_op jit(solution)/shard_map/near/pallas_call | solution.py:293
  17.0 0.0 collective-permute-done.3.beside_ref
  17.0 0.9 %far.1 = bf16[8,8,16,128]{3,2,1,0:T(8,128)(2,1)S(1)} custom-call(bf16[8,128,128]{2,1,0:T(8,128)(2,1)S(1)} %get-tuple-element.20.turned_ref, f32[3,3,8,128]{3,2,1,0:T(8,128)S(1)} %get-tuple-element.21.taper_ref, bf16[2,128,128]{2,1,0:T(8,128)(2,1)S(1)} %collective-permute-done.2.odd_ref, ...), custom_call_target="tpu_custom_call", output_to_operand_aliasing={{}: (5, {})} | custom-call | flops 100000000 | bytes 1000000 | tf_op jit(solution)/shard_map/far/pallas_call | solution.py:308
  17.9 17.6 %all_to_all.5 = bf16[8,8,16,128]{3,2,1,0:T(8,128)(2,1)S(1)} all-to-all(bf16[8,8,16,128]{3,2,1,0:T(8,128)(2,1)S(1)} %far.1), channel_id=1, replica_groups=mesh['gx'=4,'gy'=8] {'gy'}, dimensions={0} | all-to-all | bytes 524288 | tf_op jit(solution)/shard_map/all_to_all | solution.py:354
  35.5 0.8 %copy.11 = bf16[16,2,8,4,128]{4,3,2,1,0:T(4,128)(2,1)} copy(bf16[16,2,8,4,128]{4,0,3,1,2:T(8,128)(2,1)S(1)} %bitcast.9) | data formatting | bytes 524288 | tf_op jit(solution)/shard_map/transpose | solution.py:356
  (2 shorter events, 0.1 us)
Async XLA Ops:
  2.7 7.3 %collective-permute-start.1 = (bf16[2,128,128]{2,1,0:T(8,128)(2,1)S(1)}, bf16[2,128,128]{2,1,0:T(8,128)(2,1)S(1)}, u32[]{:S(2)}, u32[]{:S(2)}) collective-permute-start(bf16[2,128,128]{2,1,0:T(8,128)(2,1)S(1)} %weigh.1), channel_id=1, source_target_pairs={{8,16},{24,0},{16,8},{0,24},{9,17},{25,1},{17,9},{1,25},{10,18},{2... | collective-permute-start | bytes 196616 | tf_op jit(solution)/shard_map/ppermute | solution.py:325
  6.8 4.3 %collective-permute-start = (bf16[2,128,128]{2,1,0:T(8,128)(2,1)S(1)}, bf16[2,128,128]{2,1,0:T(8,128)(2,1)S(1)}, u32[]{:S(2)}, u32[]{:S(2)}) collective-permute-start(bf16[2,128,128]{2,1,0:T(8,128)(2,1)S(1)} %weigh.1), channel_id=1, source_target_pairs={{0,8},{16,24},{8,0},{24,16},{1,9},{17,25},{9,1},{25,17},{2,10},{18... | collective-permute-start | bytes 196616 | tf_op jit(solution)/shard_map/ppermute | solution.py:325
  8.4 2.7 %collective-permute-start.2 = (bf16[2,128,128]{2,1,0:T(8,128)(2,1)S(1)}, bf16[2,128,128]{2,1,0:T(8,128)(2,1)S(1)}, u32[]{:S(2)}, u32[]{:S(2)}) collective-permute-start(bf16[2,128,128]{2,1,0:T(8,128)(2,1)S(1)} %weigh.1), channel_id=1, source_target_pairs={{1,2},{3,4},{5,6},{2,1},{4,3},{6,5},{9,10},{11,12},{13,14},{10,9},... | collective-permute-start | bytes 196616 | tf_op jit(solution)/shard_map/ppermute | solution.py:325
  11.1 4.0 %collective-permute-start.4 = (bf16[2,128,384]{2,1,0:T(8,128)(2,1)S(1)}, bf16[2,128,384]{2,1,0:T(8,128)(2,1)S(1)}, u32[]{:S(2)}, u32[]{:S(2)}) collective-permute-start(bf16[2,128,384]{2,1,0:T(8,128)(2,1)S(1)} %pad_maximum_fusion.own_ref), channel_id=1, source_target_pairs={{0,1},{2,3},{4,5},{6,7},{1,0},{3,2},{5,4},{7,6},{8,9},{10,11},{12,... | collective-permute-start | bytes 589832 | tf_op jit(solution)/shard_map/ppermute | solution.py:325
  14.1 3.0 %collective-permute-start.3 = (bf16[2,128,256]{2,1,0:T(8,128)(2,1)S(1)}, bf16[2,128,256]{2,1,0:T(8,128)(2,1)S(1)}, u32[]{:S(2)}, u32[]{:S(2)}) collective-permute-start(bf16[2,128,256]{2,1,0:T(8,128)(2,1)S(1)} %pad_maximum_fusion.1), channel_id=1, source_target_pairs={{1,2},{3,4},{5,6},{2,1},{4,3},{6,5},{9,10},{11,12},{13,14},{10,9},... | collective-permute-start | bytes 393224 | tf_op jit(solution)/shard_map/ppermute | solution.py:325

commit v9 on v7

--- a/solution.py
+++ b/solution.py
@@ -11,6 +11,7 @@
 BLK_X = 2
 BLK_Y = 4
 BLOCKS = BLK_X * BLK_Y
+SIDE = BLOCKS // 2
 OBS_TILE = 128
 PATTERN = 25
 SMALL = 32
@@ -87,7 +88,7 @@
 
 
 def weigh_kernel(
-    pred_hbm, mv_hbm, var_hbm, jit_hbm, obs_hbm, out_ref,
+    pred_hbm, mv_hbm, var_hbm, jit_hbm, obs_hbm, params_hbm, out_ref, params_ref,
     pred_ref, mv_ref, var_ref, jit_ref, obs_ref, x_ref, idx_ref, full_ref, sems,
 ):
     members = pred_ref.shape[0]
@@ -100,6 +101,7 @@
         (var_hbm.at[0], var_ref),
         (mv_hbm.at[0], mv_ref),
         (jit_hbm.at[0, 0], jit_ref),
+        (params_hbm, params_ref),
     ]
     copies = fetch(pairs, sems)
     for copy in copies[:3]:
@@ -150,13 +152,13 @@
     out_ref[1] = weighted.astype(BF16)
 
 
-def weigh(predicted, measured_value, measurement_variance, observation_jitter, obs_block):
+def weigh(predicted, measured_value, measurement_variance, observation_jitter, obs_block, params):
     members = predicted.shape[2]
     return pl.pallas_call(
         weigh_kernel,
-        out_shape=jax.ShapeDtypeStruct((2, members, OBS_TILE), BF16),
-        in_specs=[pl.BlockSpec(memory_space=pltpu.HBM)] * 5,
-        out_specs=pl.BlockSpec(memory_space=pltpu.VMEM),
+        out_shape=(jax.ShapeDtypeStruct((2, members, OBS_TILE), BF16), jax.ShapeDtypeStruct(params.shape, BF16)),
+        in_specs=[pl.BlockSpec(memory_space=pltpu.HBM)] * 6,
+        out_specs=(pl.BlockSpec(memory_space=pltpu.VMEM), pl.BlockSpec(memory_space=pltpu.VMEM)),
         scratch_shapes=[
             pltpu.VMEM((members, OBS_TILE), F32),
             pltpu.VMEM((1, OBS_TILE), F32),
@@ -166,11 +168,11 @@
             pltpu.VMEM((OBS_TILE, OBS_TILE), F32),
             pltpu.VMEM((OBS_TILE, OBS_TILE), jnp.int32),
             pltpu.VMEM((OBS_TILE, OBS_TILE), F32),
-            pltpu.SemaphoreType.DMA((5,)),
+            pltpu.SemaphoreType.DMA((6,)),
         ],
         compiler_params=pltpu.CompilerParams(vmem_limit_bytes=16 * 2**20),
         name="weigh",
-    )(*in_hbm(predicted, measured_value, measurement_variance, observation_jitter, obs_block))
+    )(*in_hbm(predicted, measured_value, measurement_variance, observation_jitter, obs_block, params))
 
 
 def offset(which, place):
@@ -179,7 +181,8 @@
 
 
 def prepare_kernel(
-    params_ref, radius_hbm, pattern_hbm, obs_hbm, turned_ref, taper_ref, radius_ref, pattern_ref, obs_ref, sems
+    params_ref, radius_hbm, pattern_hbm, obs_hbm, turned_ref, taper_ref, message_ref,
+    radius_ref, pattern_ref, obs_ref, sems,
 ):
     members = params_ref.shape[1]
     tile_x = lax.axis_index("gx")
@@ -203,6 +206,7 @@
     pattern = jnp.concatenate([pattern_ref[i] for i in range(BLK_X)], axis=0).astype(F32)
     slots = [jnp.broadcast_to(pattern[:, p : p + 1], shape) for p in range(PATTERN)]
 
+    reached = []
     for t in range(9):
         iy, ix = t // 3, t % 3
         dx, dy = offset(ix, tile_x), offset(iy, tile_y)
@@ -220,7 +224,21 @@
             picked = jnp.where(slot == p, slots[p], picked)
         spread = (step_x * step_x + step_y * step_y).astype(F32)
         shaped = jnp.maximum(1.0 - spread / reach, 0.0)
-        taper_ref[iy, ix] = jnp.where(inside, picked, 0.0) * shaped / (members - 1)
+        taper = jnp.where(inside, picked, 0.0) * shaped / (members - 1)
+        taper_ref[iy, ix] = taper
+        if iy == 2:
+            lower = jnp.concatenate([taper[0:2], taper[4:6]], axis=0)
+            upper = jnp.concatenate([taper[2:4], taper[6:8]], axis=0)
+            reached.append(jnp.where(first_of(1, tile_y) == 0, lower, upper))
+    for k in range(SIDE):
+        message_ref[k * CELLS : (k + 1) * CELLS] = turned_ref[block_of(k, 1, tile_y)]
+    tapers = jnp.concatenate(reached + [jnp.zeros((SIDE, OBS_TILE), F32)], axis=0)
+    high = tapers.astype(BF16)
+    low = (tapers - high.astype(F32)).astype(BF16)
+    message_ref[SIDE * CELLS : SIDE * CELLS + 16, 0:OBS_TILE] = high
+    message_ref[SIDE * CELLS + 16 : SIDE * CELLS + 32, 0:OBS_TILE] = low
+    if members > OBS_TILE:
+        message_ref[SIDE * CELLS : SIDE * CELLS + 32, OBS_TILE:members] = jnp.zeros((32, members - OBS_TILE), BF16)
 
 
 def prepare(by_block, taper_radius, taper_pattern, obs_block):
@@ -230,9 +248,10 @@
         out_shape=(
             jax.ShapeDtypeStruct((BLOCKS, CELLS, members), BF16),
             jax.ShapeDtypeStruct((3, 3, BLOCKS, OBS_TILE), F32),
+            jax.ShapeDtypeStruct((SIDE * CELLS + 32, members), BF16),
         ),
         in_specs=[pl.BlockSpec(memory_space=pltpu.VMEM)] + [pl.BlockSpec(memory_space=pltpu.HBM)] * 3,
-        out_specs=(pl.BlockSpec(memory_space=pltpu.VMEM), pl.BlockSpec(memory_space=pltpu.VMEM)),
+        out_specs=(pl.BlockSpec(memory_space=pltpu.VMEM),) * 3,
         scratch_shapes=[
             pltpu.SMEM(taper_radius.shape, jnp.int32),
             pltpu.VMEM(taper_pattern.shape, jnp.int32),
@@ -245,17 +264,23 @@
     )(by_block, *in_hbm(taper_radius, taper_pattern, obs_block))
 
 
-def moved(b, which, turned_ref, taper_ref, tiles_ref):
-    cross = dot(turned_ref[b], tiles_ref[0], ((1,), (0,)))
-    count = tiles_ref.shape[2] // OBS_TILE
-    taper = jnp.concatenate([taper_ref[which, k, pl.ds(b, 1), :] for k in range(count)], axis=1)
+def gained(turned, taper, column_ref):
+    cross = dot(turned, column_ref[0], ((1,), (0,)))
     gain = (cross * taper).astype(BF16)
-    return dot(tiles_ref[1], gain, ((1,), (1,)))
+    return dot(column_ref[1], gain, ((1,), (1,)))
+
+
+def moved(b, which, turned_ref, taper_ref, column_ref):
+    taper = jnp.concatenate([taper_ref[which, ix, pl.ds(b, 1), :] for ix in range(3)], axis=1)
+    return gained(turned_ref[b], taper, column_ref)
+
+
+def first_of(side, tile_y):
+    return 2 * ((tile_y & 1) ^ 1 ^ side)
 
 
 def block_of(k, side, tile_y):
-    first = 2 * ((tile_y & 1) ^ 1 ^ side)
-    return (k >> 1) * BLK_Y + first + (k & 1)
+    return (k >> 1) * BLK_Y + first_of(side, tile_y) + (k & 1)
 
 
 def put(out_ref, b, updated):
@@ -264,56 +289,121 @@
         out_ref[d, b] = updated[d * share : (d + 1) * share]
 
 
-def near_kernel(params_ref, turned_ref, taper_ref, own_ref, even_ref, out_ref, part_ref):
+def own_kernel(params_ref, turned_ref, taper_ref, own_ref, out_ref, part_ref):
     tile_y = lax.axis_index("gy")
-
-    for k in range(BLOCKS // 2):
+    for k in range(SIDE):
         b = block_of(k, 0, tile_y)
-        delta = moved(b, 0, turned_ref, taper_ref, own_ref) + moved(b, 1, turned_ref, taper_ref, even_ref)
-        put(out_ref, b, (params_ref[b].astype(F32) + delta).astype(BF16))
-    for k in range(BLOCKS // 2):
+        part_ref[k] = params_ref[b].astype(F32) + moved(b, 0, turned_ref, taper_ref, own_ref)
+    for k in range(SIDE):
         b = block_of(k, 1, tile_y)
-        part_ref[k] = params_ref[b].astype(F32) + moved(b, 0, turned_ref, taper_ref, own_ref)
-
-
-def far_kernel(turned_ref, taper_ref, odd_ref, part_ref, done_ref, out_ref):
+        put(out_ref, b, (params_ref[b].astype(F32) + moved(b, 0, turned_ref, taper_ref, own_ref)).astype(BF16))
+
+
+def even_kernel(turned_ref, taper_ref, even_ref, part_ref, done_ref, out_ref):
     del done_ref
     tile_y = lax.axis_index("gy")
-    for k in range(BLOCKS // 2):
-        b = block_of(k, 1, tile_y)
-        put(out_ref, b, (part_ref[k] + moved(b, 2, turned_ref, taper_ref, odd_ref)).astype(BF16))
+    for k in range(SIDE):
+        b = block_of(k, 0, tile_y)
+        put(out_ref, b, (part_ref[k] + moved(b, 1, turned_ref, taper_ref, even_ref)).astype(BF16))
+
+
+def odd_kernel(message_ref, own_ref, done_ref, out_ref):
+    del done_ref
+    end = SIDE * CELLS
+    tapers = message_ref[end : end + 16, 0:OBS_TILE].astype(F32) + message_ref[end + 16 : end + 32, 0:OBS_TILE].astype(F32)
+    for k in range(SIDE):
+        taper = jnp.concatenate([tapers[ix * SIDE + k : ix * SIDE + k + 1] for ix in range(3)], axis=1)
+        put(out_ref, BLOCKS + k, gained(message_ref[k * CELLS : (k + 1) * CELLS], taper, own_ref).astype(BF16))
+
+
+def gather_kernel(arrived_ref, out_hbm, rows_ref, out_ref, sems):
+    parts, _, share, _ = arrived_ref.shape
+    line = parts * BLK_Y
+    for s in range(parts):
+        pair = s - 1 if s % 2 == 0 else s + 1
+        first = 2 * (s % 2)
+        for b in range(BLOCKS):
+            x, y = b // BLK_Y, b % BLK_Y
+            value = arrived_ref[s, b].astype(F32)
+            if first <= y < first + 2 and 0 <= pair < parts:
+                value = value + arrived_ref[pair, BLOCKS + x * 2 + y - first].astype(F32)
+            rows_ref[pl.ds(x * line + s * BLK_Y + y, share, stride=BLK_X * line), :] = value
+    pieces = sems.shape[0]
+    step = rows_ref.shape[0] // pieces
+    copies = []
+    for p in range(pieces):
+        place = slice(p * step, (p + 1) * step)
+        out_ref[place] = rows_ref[place].astype(BF16)
+        copies.append(pltpu.make_async_copy(out_ref.at[pl.ds(p * step, step)], out_hbm.at[pl.ds(p * step, step)], sems.at[p]))
+        copies[-1].start()
+    for copy in copies:
+        copy.wait()
 
 
 VMEM = pl.BlockSpec(memory_space=pltpu.VMEM)
-
-
-def update_near(by_block, turned, taper, own, even, parts):
+LONG = pl.CostEstimate(flops=4_000_000_000, bytes_accessed=10_000_000, transcendentals=0)
+LIMIT = pltpu.CompilerParams(vmem_limit_bytes=24 * 2**20)
+
+
+def update_own(by_block, turned, taper, own, parts):
     members = by_block.shape[1]
     return pl.pallas_call(
-        near_kernel,
+        own_kernel,
         out_shape=(
-            jax.ShapeDtypeStruct((parts, BLOCKS, members // parts, CELLS), BF16),
-            jax.ShapeDtypeStruct((BLOCKS // 2, members, CELLS), F32),
+            jax.ShapeDtypeStruct((parts, BLOCKS + SIDE, members // parts, CELLS), BF16),
+            jax.ShapeDtypeStruct((SIDE, members, CELLS), F32),
         ),
-        in_specs=[VMEM] * 5,
+        in_specs=[VMEM] * 4,
         out_specs=(VMEM, VMEM),
-        compiler_params=pltpu.CompilerParams(vmem_limit_bytes=24 * 2**20),
-        cost_estimate=pl.CostEstimate(flops=400_000_000, bytes_accessed=2_000_000, transcendentals=0),
-        name="near",
-    )(by_block, turned, taper, own, even)
-
-
-def update_far(turned, taper, odd, part, done):
+        compiler_params=LIMIT,
+        cost_estimate=LONG,
+        name="own",
+    )(by_block, turned, taper, own)
+
+
+def update_even(turned, taper, even, part, done):
     return pl.pallas_call(
-        far_kernel,
+        even_kernel,
         out_shape=jax.ShapeDtypeStruct(done.shape, BF16),
         in_specs=[VMEM] * 4 + [pl.BlockSpec(memory_space=pl.ANY)],
         out_specs=VMEM,
         input_output_aliases={4: 0},
-        compiler_params=pltpu.CompilerParams(vmem_limit_bytes=24 * 2**20),
-        cost_estimate=pl.CostEstimate(flops=100_000_000, bytes_accessed=1_000_000, transcendentals=0),
-        name="far",
-    )(turned, taper, odd, part, done)
+        compiler_params=LIMIT,
+        cost_estimate=LONG,
+        name="even",
+    )(turned, taper, even, part, done)
+
+
+def update_odd(message, own, done):
+    return pl.pallas_call(
+        odd_kernel,
+        out_shape=jax.ShapeDtypeStruct(done.shape, BF16),
+        in_specs=[VMEM] * 2 + [pl.BlockSpec(memory_space=pl.ANY)],
+        out_specs=VMEM,
+        input_output_aliases={2: 0},
+        compiler_params=LIMIT,
+        cost_estimate=LONG,
+        name="odd",
+    )(message, own, done)
+
+
+def gather(arrived):
+    parts, _, share, _ = arrived.shape
+    rows = share * BLOCKS * parts
+    out = pl.pallas_call(
+        gather_kernel,
+        out_shape=jax.ShapeDtypeStruct((rows, CELLS), BF16),
+        in_specs=[VMEM],
+        out_specs=pl.BlockSpec(memory_space=pl.ANY),
+        scratch_shapes=[
+            pltpu.VMEM((rows, CELLS), F32),
+            pltpu.VMEM((rows, CELLS), BF16),
+            pltpu.SemaphoreType.DMA((4,)),
+        ],
+        compiler_params=LIMIT,
+        name="gather",
+    )(arrived)
+    return out.reshape(share, BLK_X, parts * BLK_Y, CELLS)
 
 
 def swap(block, axis, first, close=False):
@@ -336,21 +426,21 @@
 ):
     members = params.shape[0]
     parts = lax.axis_size("gy")
+    own, params = weigh(
+        predicted, measured_value, measurement_variance, observation_jitter, obs_block, params
+    )
     by_block = params.reshape(members, BLOCKS, CELLS).transpose(1, 0, 2)
-    own = weigh(predicted, measured_value, measurement_variance, observation_jitter, obs_block)
     even = swap(own, "gx", 0)
     odd = swap(own, "gx", 1, close=True)
-    turned, taper = prepare(by_block, taper_radius, taper_pattern, obs_block)
+    turned, taper, message = prepare(by_block, taper_radius, taper_pattern, obs_block)
+    message = swap(message, "gy", 1)
     column = jnp.concatenate([own, even, odd], axis=2)
     column, turned, taper = lax.optimization_barrier((column, turned, taper))
-    odd = swap(column, "gy", 1)
     even = swap(column, "gy", 0)
-    done, part = update_near(by_block, turned, taper, column, even, parts)
-    updated = update_far(turned, taper, odd, part, done)
-    arrived = lax.all_to_all(updated, "gy", split_axis=0, concat_axis=0, tiled=True)
-    share = members // parts
-    arrived = arrived.reshape(parts, BLK_X, BLK_Y, share, CELLS).transpose(3, 1, 0, 2, 4)
-    return arrived.reshape(share, BLK_X, parts * BLK_Y, CELLS)
+    done, part = update_own(by_block, turned, taper, column, parts)
+    done = update_even(turned, taper, even, part, done)
+    done = update_odd(message, column, done)
+    return gather(lax.all_to_all(done, "gy", split_axis=0, concat_axis=0, tiled=True))
 
 
 def solution(mesh):

time: 34.6 us -> 34.3 us (level)
  Pallas kernels: 6.46 us -> 8.7 us
  local copies, waits for them, and re-layouts: 1.81 us -> 0.04 us
  blocking collectives: 18.2 us -> 17.4 us
    pallas_call x3 -> x5, Pallas kernels: 5.49 us -> 7.72 us  [the longest x1 3.13 us: weigh(): pl.pallas_call(weigh_kernel, out_shape=(jax.ShapeDtypeStruct((2, members,...]
    unnamed x1 -> x0, local copies, waits for them, and re-layouts: 0.99 us -> none
    transpose x1 -> x0, local copies, waits for them, and re-layouts: 0.82 us -> none  [per_device(): arrived.reshape(parts, BLK_X, BLK_Y, share, CELLS).transpose(3, 1, 0, 2, 4)]
    all_to_all x1, blocking collectives: 18.2 us -> 17.4 us  [per_device(): lax.all_to_all(done, 'gy', split_axis=0, concat_axis=0, tiled=True)]
  transfers between devices with their start and end apart: 4 -> 4, of which waited for: 2 -> 2; matrix products, arithmetic and copies ran while one was open for 3% -> 0% of each run, Pallas kernels for 8% -> 10%
where the time goes in v9:
time: 34.3 us; the launch traced here: 34 us
  blocking collectives  17.4 us (51%)
  Pallas kernels  8.7 us (25%)
  starting transfers between devices  5.44 us (16%)
  waiting for transfers between devices  2.34 us (7%)
    all_to_all x1, blocking collectives, per_device(): lax.all_to_all(done, 'gy', split_axis=0, concat_axis=0, tiled=True)  17.4 us
    ppermute x4, starting transfers between devices, swap(): return lax.ppermute(block, axis, pairs + [(b, a) for a, b in pairs])  5.44 us
    pallas_call x1, Pallas kernels, weigh(): pl.pallas_call(weigh_kernel, out_shape=(jax.ShapeDtypeStruct((2, members,...  3.13 us
    ppermute x4, waiting for transfers between devices, swap(): return lax.ppermute(block, axis, pairs + [(b, a) for a, b in pairs])  2.34 us
    pallas_call x1, Pallas kernels, update_own(): pl.pallas_call(own_kernel, out_shape=(jax.ShapeDtypeStruct((parts, BLOCKS...  1.64 us
    pallas_call x1, Pallas kernels, gather(): pl.pallas_call(gather_kernel, out_shape=jax.ShapeDtypeStruct((rows, CELLS...  1.17 us
    pallas_call x1, Pallas kernels, prepare(): pl.pallas_call(prepare_kernel, out_shape=(jax.ShapeDtypeStruct((BLOCKS, C...  0.98 us
    pallas_call x1, Pallas kernels, update_even(): pl.pallas_call(even_kernel, out_shape=jax.ShapeDtypeStruct(done.shape, BF...  0.89 us
  transfers between devices with their start and end apart: 4, of which 2 were waited for; matrix products, arithmetic and copies ran while one was open for 0% of the time, Pallas kernels for 10%

profile of v9, /device:TPU:0, one launch (start us, length us, event | category | flops | bytes accessed | tf_op | source)
XLA Modules:
  0.0 34.0 jit_solution(4823305946629086306)
XLA Ops:
  0.0 3.1 %weigh.1 = (bf16[2,128,128]{2,1,0:T(8,128)(2,1)S(1)}, bf16[128,2,4,128]{3,2,1,0:T(4,128)(2,1)S(1)}) custom-call(f32[1,1,128,128]{3,2,1,0:T(8,128)} %pred_hbm.1, f32[1,1,128]{2,1,0:T(1,128)} %mv_hbm.1, f32[1,1,128]{2,1,0:T(1,128)} %var_hbm.1, f32[1,1,128,128]{3,2,1,0:T(8,128)} %jit_hbm.1, s32[4,8,128]{2,1,0:T(8,128)} %obs_hbm.3, ...), custom_call_target="tpu_custom_call" | custom-call | tf_op jit(solution)/shard_map/weigh/pallas_call | solution.py:157
  3.1 3.9 %collective-permute-start.2 = (bf16[2,128,128]{2,1,0:T(8,128)(2,1)S(1)}, bf16[2,128,128]{2,1,0:T(8,128)(2,1)S(1)}, u32[]{:S(2)}, u32[]{:S(2)}) collective-permute-start(bf16[2,128,128]{2,1,0:T(8,128)(2,1)S(1)} %get-tuple-element.17), channel_id=1, source_target_pairs={{8,16},{24,0},{16,8},{0,24},{9,17},{25,1},{17,9},{1,25},{10,18},{2... | collective-permute-start | bytes 196616 | tf_op jit(solution)/shard_map/ppermute | solution.py:414
  7.0 0.2 collective-permute-start.1
  7.3 1.0 %prepare.1 = (bf16[8,128,128]{2,1,0:T(8,128)(2,1)S(1)}, f32[3,3,8,128]{3,2,1,0:T(8,128)S(1)}, bf16[544,128]{1,0:T(8,128)(2,1)S(1)}) custom-call(bf16[8,128,128]{2,1,0:T(8,128)(2,1)S(1)} %bitcast.4, s32[2,4]{1,0:T(2,128)} %radius_hbm.1, s32[2,4,25]{2,1,0:T(4,128)} %pattern_hbm.1, s32[4,8,128]{2,1,0:T(8,128)} %obs_hbm.3), custom_call_target="tpu_custom_call" | custom-call | flops 4000000 | bytes 1000000 | tf_op jit(solution)/shard_map/prepare/pallas_call | solution.py:246
  8.3 0.7 %collective-permute-start = (bf16[544,128]{1,0:T(8,128)(2,1)S(1)}, bf16[544,128]{1,0:T(8,128)(2,1)S(1)}, u32[]{:S(2)}, u32[]{:S(2)}) collective-permute-start(bf16[544,128]{1,0:T(8,128)(2,1)S(1)} %get-tuple-element.16), channel_id=1, source_target_pairs={{1,2},{3,4},{5,6},{2,1},{4,3},{6,5},{9,10},{11,12},{13,14},{10,9},... | collective-permute-start | bytes 417800 | tf_op jit(solution)/shard_map/ppermute | solution.py:414
  8.9 0.8 %collective-permute-done.2 = bf16[2,128,128]{2,1,0:T(8,128)(2,1)S(1)} collective-permute-done((bf16[2,128,128]{2,1,0:T(8,128)(2,1)S(1)}, bf16[2,128,128]{2,1,0:T(8,128)(2,1)S(1)}, u32[]{:S(2)}, u32[]{:S(2)}) %collective-permute-start.2) | collective-permute-done | bytes 65568 | tf_op jit(solution)/shard_map/ppermute | solution.py:414
  9.7 1.6 %collective-permute-done.1 = bf16[2,128,128]{2,1,0:T(8,128)(2,1)S(1)} collective-permute-done((bf16[2,128,128]{2,1,0:T(8,128)(2,1)S(1)}, bf16[2,128,128]{2,1,0:T(8,128)(2,1)S(1)}, u32[]{:S(2)}, u32[]{:S(2)}) %collective-permute-start.1) | collective-permute-done | bytes 65568 | tf_op jit(solution)/shard_map/ppermute | solution.py:414
  11.3 0.7 %collective-permute-start.3 = (bf16[2,128,384]{2,1,0:T(8,128)(2,1)S(1)}, bf16[2,128,384]{2,1,0:T(8,128)(2,1)S(1)}, u32[]{:S(2)}, u32[]{:S(2)}) collective-permute-start(bf16[2,128,384]{2,1,0:T(8,128)(2,1)S(1)} %pad_maximum_fusion.own_ref), channel_id=1, source_target_pairs={{0,1},{2,3},{4,5},{6,7},{1,0},{3,2},{5,4},{7,6},{8,9},{10,11},{12,... | collective-permute-start | bytes 589832 | tf_op jit(solution)/shard_map/ppermute | solution.py:414
  12.0 1.6 %own.1 = (bf16[8,12,16,128]{3,2,1,0:T(8,128)(2,1)S(1)}, f32[4,128,128]{2,1,0:T(8,128)S(1)}) custom-call(bf16[8,128,128]{2,1,0:T(8,128)(2,1)S(1)} %bitcast.5, bf16[8,128,128]{2,1,0:T(8,128)(2,1)S(1)} %get-tuple-element.21.turned_ref, f32[3,3,8,128]{3,2,1,0:T(8,128)S(1)} %get-tuple-element.22.taper_ref, bf16[2,128,384]{2,1,0:T(8,128)(2,1)S(1)} %pad_maximum_fusion.own_ref), custom_call_target="tpu_custom_call" | custom-call | flops 4000000000 | bytes 10000000 | tf_op jit(solution)/shard_map/own/pallas_call | solution.py:350
  13.6 0.0 collective-permute-done.3.even_ref
  13.6 0.9 %even.1.done_ref = bf16[8,12,16,128]{3,2,1,0:T(8,128)(2,1)S(1)} custom-call(bf16[8,128,128]{2,1,0:T(8,128)(2,1)S(1)} %get-tuple-element.21.turned_ref, f32[3,3,8,128]{3,2,1,0:T(8,128)S(1)} %get-tuple-element.22.taper_ref, bf16[2,128,384]{2,1,0:T(8,128)(2,1)S(1)} %collective-permute-done.3.even_ref, ...), custom_call_target="tpu_custom_call", output_to_operand_aliasing={{}: (4, {})} | custom-call | flops 4000000000 | bytes 10000000 | tf_op jit(solution)/shard_map/even/pallas_call | solution.py:365
  14.5 0.0 collective-permute-done.message_ref
  14.6 0.9 %odd.1 = bf16[8,12,16,128]{3,2,1,0:T(8,128)(2,1)S(1)} custom-call(bf16[544,128]{1,0:T(8,128)(2,1)S(1)} %collective-permute-done.message_ref, bf16[2,128,384]{2,1,0:T(8,128)(2,1)S(1)} %pad_maximum_fusion.own_ref, bf16[8,12,16,128]{3,2,1,0:T(8,128)(2,1)S(1)} %even.1.done_ref), custom_call_target="tpu_custom_call", output_to_operand_aliasing={{}: (2, {})} | custom-call | flops 4000000000 | bytes 10000000 | tf_op jit(solution)/shard_map/odd/pallas_call | solution.py:378
  15.4 17.4 %all_to_all.5.arrived_ref = bf16[8,12,16,128]{3,2,1,0:T(8,128)(2,1)S(1)} all-to-all(bf16[8,12,16,128]{3,2,1,0:T(8,128)(2,1)S(1)} %odd.1), channel_id=1, replica_groups=mesh['gx'=4,'gy'=8] {'gy'}, dimensions={0} | all-to-all | bytes 786432 | tf_op jit(solution)/shard_map/all_to_all | solution.py:443
  32.8 1.2 %gather.1 = bf16[1024,128]{1,0:T(8,128)(2,1)} custom-call(bf16[8,12,16,128]{3,2,1,0:T(8,128)(2,1)S(1)} %all_to_all.5.arrived_ref), custom_call_target="tpu_custom_call" | custom-call | tf_op jit(solution)/shard_map/gather/pallas_call | solution.py:393
  (2 shorter events, 0.1 us)
Async XLA Ops:
  3.1 6.6 %collective-permute-start.2 = (bf16[2,128,128]{2,1,0:T(8,128)(2,1)S(1)}, bf16[2,128,128]{2,1,0:T(8,128)(2,1)S(1)}, u32[]{:S(2)}, u32[]{:S(2)}) collective-permute-start(bf16[2,128,128]{2,1,0:T(8,128)(2,1)S(1)} %get-tuple-element.17), channel_id=1, source_target_pairs={{8,16},{24,0},{16,8},{0,24},{9,17},{25,1},{17,9},{1,25},{10,18},{2... | collective-permute-start | bytes 196616 | tf_op jit(solution)/shard_map/ppermute | solution.py:414
  7.0 4.3 %collective-permute-start.1 = (bf16[2,128,128]{2,1,0:T(8,128)(2,1)S(1)}, bf16[2,128,128]{2,1,0:T(8,128)(2,1)S(1)}, u32[]{:S(2)}, u32[]{:S(2)}) collective-permute-start(bf16[2,128,128]{2,1,0:T(8,128)(2,1)S(1)} %get-tuple-element.17), channel_id=1, source_target_pairs={{0,8},{16,24},{8,0},{24,16},{1,9},{17,25},{9,1},{25,17},{2,10},{18... | collective-permute-start | bytes 196616 | tf_op jit(solution)/shard_map/ppermute | solution.py:414
  8.3 6.3 %collective-permute-start = (bf16[544,128]{1,0:T(8,128)(2,1)S(1)}, bf16[544,128]{1,0:T(8,128)(2,1)S(1)}, u32[]{:S(2)}, u32[]{:S(2)}) collective-permute-start(bf16[544,128]{1,0:T(8,128)(2,1)S(1)} %get-tuple-element.16), channel_id=1, source_target_pairs={{1,2},{3,4},{5,6},{2,1},{4,3},{6,5},{9,10},{11,12},{13,14},{10,9},... | collective-permute-start | bytes 417800 | tf_op jit(solution)/shard_map/ppermute | solution.py:414
  11.3 2.3 %collective-permute-start.3 = (bf16[2,128,384]{2,1,0:T(8,128)(2,1)S(1)}, bf16[2,128,384]{2,1,0:T(8,128)(2,1)S(1)}, u32[]{:S(2)}, u32[]{:S(2)}) collective-permute-start(bf16[2,128,384]{2,1,0:T(8,128)(2,1)S(1)} %pad_maximum_fusion.own_ref), channel_id=1, source_target_pairs={{0,1},{2,3},{4,5},{6,7},{1,0},{3,2},{5,4},{7,6},{8,9},{10,11},{12,... | collective-permute-start | bytes 589832 | tf_op jit(solution)/shard_map/ppermute | solution.py:414

commit v10 on v7

--- a/solution.py
+++ b/solution.py
@@ -11,6 +11,7 @@
 BLK_X = 2
 BLK_Y = 4
 BLOCKS = BLK_X * BLK_Y
+SIDE = BLOCKS // 2
 OBS_TILE = 128
 PATTERN = 25
 SMALL = 32
@@ -87,7 +88,7 @@
 
 
 def weigh_kernel(
-    pred_hbm, mv_hbm, var_hbm, jit_hbm, obs_hbm, out_ref,
+    pred_hbm, mv_hbm, var_hbm, jit_hbm, obs_hbm, params_hbm, out_ref, params_ref,
     pred_ref, mv_ref, var_ref, jit_ref, obs_ref, x_ref, idx_ref, full_ref, sems,
 ):
     members = pred_ref.shape[0]
@@ -100,6 +101,7 @@
         (var_hbm.at[0], var_ref),
         (mv_hbm.at[0], mv_ref),
         (jit_hbm.at[0, 0], jit_ref),
+        (params_hbm, params_ref),
     ]
     copies = fetch(pairs, sems)
     for copy in copies[:3]:
@@ -150,13 +152,13 @@
     out_ref[1] = weighted.astype(BF16)
 
 
-def weigh(predicted, measured_value, measurement_variance, observation_jitter, obs_block):
+def weigh(predicted, measured_value, measurement_variance, observation_jitter, obs_block, params):
     members = predicted.shape[2]
     return pl.pallas_call(
         weigh_kernel,
-        out_shape=jax.ShapeDtypeStruct((2, members, OBS_TILE), BF16),
-        in_specs=[pl.BlockSpec(memory_space=pltpu.HBM)] * 5,
-        out_specs=pl.BlockSpec(memory_space=pltpu.VMEM),
+        out_shape=(jax.ShapeDtypeStruct((2, members, OBS_TILE), BF16), jax.ShapeDtypeStruct(params.shape, BF16)),
+        in_specs=[pl.BlockSpec(memory_space=pltpu.HBM)] * 6,
+        out_specs=(pl.BlockSpec(memory_space=pltpu.VMEM), pl.BlockSpec(memory_space=pltpu.VMEM)),
         scratch_shapes=[
             pltpu.VMEM((members, OBS_TILE), F32),
             pltpu.VMEM((1, OBS_TILE), F32),
@@ -166,11 +168,11 @@
             pltpu.VMEM((OBS_TILE, OBS_TILE), F32),
             pltpu.VMEM((OBS_TILE, OBS_TILE), jnp.int32),
             pltpu.VMEM((OBS_TILE, OBS_TILE), F32),
-            pltpu.SemaphoreType.DMA((5,)),
+            pltpu.SemaphoreType.DMA((6,)),
         ],
         compiler_params=pltpu.CompilerParams(vmem_limit_bytes=16 * 2**20),
         name="weigh",
-    )(*in_hbm(predicted, measured_value, measurement_variance, observation_jitter, obs_block))
+    )(*in_hbm(predicted, measured_value, measurement_variance, observation_jitter, obs_block, params))
 
 
 def offset(which, place):
@@ -253,67 +255,161 @@
     return dot(tiles_ref[1], gain, ((1,), (1,)))
 
 
+def first_of(side, tile_y):
+    return 2 * ((tile_y & 1) ^ 1 ^ side)
+
+
 def block_of(k, side, tile_y):
-    first = 2 * ((tile_y & 1) ^ 1 ^ side)
-    return (k >> 1) * BLK_Y + first + (k & 1)
-
-
-def put(out_ref, b, updated):
-    share = out_ref.shape[2]
-    for d in range(out_ref.shape[0]):
-        out_ref[d, b] = updated[d * share : (d + 1) * share]
-
-
-def near_kernel(params_ref, turned_ref, taper_ref, own_ref, even_ref, out_ref, part_ref):
+    return (k >> 1) * BLK_Y + first_of(side, tile_y) + (k & 1)
+
+
+def target(chip, r, chips):
+    return chip ^ r if chips & (chips - 1) == 0 else (chip + r) % chips
+
+
+def source(chip, r, chips):
+    return chip ^ r if chips & (chips - 1) == 0 else (chip + chips - r) % chips
+
+
+def put(piece_refs, rows_ref, k, updated):
+    chips, share = len(piece_refs), piece_refs[0].shape[2]
+    mine = lax.axis_index("gy")
+    rows_ref[k] = updated
+    for r, ref in enumerate(piece_refs):
+        for flip in (0, 1):
+            owner = 2 * target(mine >> 1, r, chips) + ((mine & 1) ^ flip)
+            ref[flip, k] = rows_ref[k, pl.ds(pl.multiple_of(owner * share, share), share), :]
+
+
+def near_kernel(params_ref, turned_ref, taper_ref, own_ref, even_ref, part_ref, *refs):
+    piece_refs, rows_ref = refs[:-1], refs[-1]
     tile_y = lax.axis_index("gy")
-
-    for k in range(BLOCKS // 2):
+    for k in range(SIDE):
         b = block_of(k, 0, tile_y)
         delta = moved(b, 0, turned_ref, taper_ref, own_ref) + moved(b, 1, turned_ref, taper_ref, even_ref)
-        put(out_ref, b, (params_ref[b].astype(F32) + delta).astype(BF16))
-    for k in range(BLOCKS // 2):
+        put(piece_refs, rows_ref, k, (params_ref[b].astype(F32) + delta).astype(BF16))
+    for k in range(SIDE):
         b = block_of(k, 1, tile_y)
         part_ref[k] = params_ref[b].astype(F32) + moved(b, 0, turned_ref, taper_ref, own_ref)
 
 
-def far_kernel(turned_ref, taper_ref, odd_ref, part_ref, done_ref, out_ref):
-    del done_ref
+def far_kernel(turned_ref, taper_ref, odd_ref, part_ref, near_ref, *refs):
+    both_ref, rows_ref = refs[1], refs[-1]
+    piece_refs = (refs[0], both_ref.at[1], *refs[2:-1])
+    both_ref[0] = near_ref[...]
     tile_y = lax.axis_index("gy")
-    for k in range(BLOCKS // 2):
+    for k in range(SIDE):
         b = block_of(k, 1, tile_y)
-        put(out_ref, b, (part_ref[k] + moved(b, 2, turned_ref, taper_ref, odd_ref)).astype(BF16))
+        put(piece_refs, rows_ref, k, (part_ref[k] + moved(b, 2, turned_ref, taper_ref, odd_ref)).astype(BF16))
+
+
+def sorted_pieces(refs):
+    both_ref, rest = refs[0], refs[1:]
+    near, far = rest[: len(rest) // 2], rest[len(rest) // 2 :]
+    return [(near[0], both_ref.at[0], *near[1:]), (far[0], both_ref.at[1], *far[1:])]
+
+
+def pack_kernel(*refs):
+    out_ref = refs[-1]
+    for side, pieces in enumerate(sorted_pieces(refs[:-1])):
+        for r, piece in enumerate(pieces):
+            out_ref[side, r] = piece[1]
+
+
+def gather_kernel(even_ref, *refs):
+    out_hbm, rows_ref, out_ref, sems = refs[-4:]
+    pieces = sorted_pieces(refs[:-4])
+    chips, share = even_ref.shape[1], even_ref.shape[3]
+    mine = lax.axis_index("gy")
+    chip, core = mine >> 1, mine & 1
+    line = 2 * chips * BLK_Y
+    for r in range(chips):
+        for flip in (0, 1):
+            other = core ^ flip
+            tile = 2 * source(chip, r, chips) + other
+            for side in (0, 1):
+                for k in range(SIDE):
+                    piece = even_ref[side, r, k] if flip else pieces[side][r][0, k]
+                    start = (k >> 1) * line + tile * BLK_Y + first_of(side, other) + (k & 1)
+                    rows_ref[pl.ds(start, share, stride=BLK_X * line), :] = piece.astype(F32)
+    pieces = sems.shape[0]
+    step = rows_ref.shape[0] // pieces
+    copies = []
+    for p in range(pieces):
+        place = slice(p * step, (p + 1) * step)
+        out_ref[place] = rows_ref[place].astype(BF16)
+        copies.append(pltpu.make_async_copy(out_ref.at[pl.ds(p * step, step)], out_hbm.at[pl.ds(p * step, step)], sems.at[p]))
+        copies[-1].start()
+    for copy in copies:
+        copy.wait()
 
 
 VMEM = pl.BlockSpec(memory_space=pltpu.VMEM)
+LONG = pl.CostEstimate(flops=4_000_000_000, bytes_accessed=10_000_000, transcendentals=0)
+LIMIT = pltpu.CompilerParams(vmem_limit_bytes=24 * 2**20)
 
 
 def update_near(by_block, turned, taper, own, even, parts):
     members = by_block.shape[1]
+    pieces = [jax.ShapeDtypeStruct((2, SIDE, members // parts, CELLS), BF16)] * (parts // 2)
     return pl.pallas_call(
         near_kernel,
-        out_shape=(
-            jax.ShapeDtypeStruct((parts, BLOCKS, members // parts, CELLS), BF16),
-            jax.ShapeDtypeStruct((BLOCKS // 2, members, CELLS), F32),
-        ),
+        out_shape=(jax.ShapeDtypeStruct((SIDE, members, CELLS), F32), *pieces),
         in_specs=[VMEM] * 5,
-        out_specs=(VMEM, VMEM),
-        compiler_params=pltpu.CompilerParams(vmem_limit_bytes=24 * 2**20),
-        cost_estimate=pl.CostEstimate(flops=400_000_000, bytes_accessed=2_000_000, transcendentals=0),
+        out_specs=(VMEM,) * (1 + len(pieces)),
+        scratch_shapes=[pltpu.VMEM((SIDE, members, CELLS), BF16)],
+        compiler_params=LIMIT,
+        cost_estimate=LONG,
         name="near",
     )(by_block, turned, taper, own, even)
 
 
-def update_far(turned, taper, odd, part, done):
+def update_far(turned, taper, odd, part, near):
+    members = part.shape[1]
+    parts = members // near[0].shape[2]
+    piece = jax.ShapeDtypeStruct(near[0].shape, BF16)
+    shapes = (piece, jax.ShapeDtypeStruct((2, *piece.shape), BF16)) + (piece,) * (parts // 2 - 2)
     return pl.pallas_call(
         far_kernel,
-        out_shape=jax.ShapeDtypeStruct(done.shape, BF16),
-        in_specs=[VMEM] * 4 + [pl.BlockSpec(memory_space=pl.ANY)],
+        out_shape=shapes,
+        in_specs=[VMEM] * 5,
+        out_specs=(VMEM,) * len(shapes),
+        scratch_shapes=[pltpu.VMEM((SIDE, members, CELLS), BF16)],
+        compiler_params=LIMIT,
+        cost_estimate=LONG,
+        name="far",
+    )(turned, taper, odd, part, near[1])
+
+
+def pack(pieces):
+    chips = len(pieces) // 2 + 1
+    return pl.pallas_call(
+        pack_kernel,
+        out_shape=jax.ShapeDtypeStruct((2, chips, *pieces[1].shape[1:]), BF16),
+        in_specs=[VMEM] * len(pieces),
         out_specs=VMEM,
-        input_output_aliases={4: 0},
-        compiler_params=pltpu.CompilerParams(vmem_limit_bytes=24 * 2**20),
-        cost_estimate=pl.CostEstimate(flops=100_000_000, bytes_accessed=1_000_000, transcendentals=0),
-        name="far",
-    )(turned, taper, odd, part, done)
+        compiler_params=LIMIT,
+        name="pack",
+    )(*pieces)
+
+
+def gather(even, pieces):
+    _, chips, _, share, _ = even.shape
+    rows = share * BLOCKS * 2 * chips
+    out = pl.pallas_call(
+        gather_kernel,
+        out_shape=jax.ShapeDtypeStruct((rows, CELLS), BF16),
+        in_specs=[VMEM] * (1 + len(pieces)),
+        out_specs=pl.BlockSpec(memory_space=pl.ANY),
+        scratch_shapes=[
+            pltpu.VMEM((rows, CELLS), F32),
+            pltpu.VMEM((rows, CELLS), BF16),
+            pltpu.SemaphoreType.DMA((4,)),
+        ],
+        compiler_params=LIMIT,
+        name="gather",
+    )(even, *pieces)
+    return out.reshape(share, BLK_X, 2 * chips * BLK_Y, CELLS)
 
 
 def swap(block, axis, first, close=False):
@@ -322,6 +418,12 @@
     if close:
         pairs.append((count - 1, 0))
     return lax.ppermute(block, axis, pairs + [(b, a) for a, b in pairs])
+
+
+def hop(piece, r):
+    count = lax.axis_size("gy")
+    pairs = [(i, 2 * target(i // 2, r, count // 2) + i % 2) for i in range(count)]
+    return lax.ppermute(piece, "gy", pairs)
 
 
 def per_device(
@@ -336,21 +438,30 @@
 ):
     members = params.shape[0]
     parts = lax.axis_size("gy")
+    own, params = weigh(
+        predicted, measured_value, measurement_variance, observation_jitter, obs_block, params
+    )
     by_block = params.reshape(members, BLOCKS, CELLS).transpose(1, 0, 2)
-    own = weigh(predicted, measured_value, measurement_variance, observation_jitter, obs_block)
     even = swap(own, "gx", 0)
     odd = swap(own, "gx", 1, close=True)
     turned, taper = prepare(by_block, taper_radius, taper_pattern, obs_block)
     column = jnp.concatenate([own, even, odd], axis=2)
     column, turned, taper = lax.optimization_barrier((column, turned, taper))
+    even = swap(column, "gy", 0)
     odd = swap(column, "gy", 1)
-    even = swap(column, "gy", 0)
-    done, part = update_near(by_block, turned, taper, column, even, parts)
-    updated = update_far(turned, taper, odd, part, done)
-    arrived = lax.all_to_all(updated, "gy", split_axis=0, concat_axis=0, tiled=True)
-    share = members // parts
-    arrived = arrived.reshape(parts, BLK_X, BLK_Y, share, CELLS).transpose(3, 1, 0, 2, 4)
-    return arrived.reshape(share, BLK_X, parts * BLK_Y, CELLS)
+    part, *near = update_near(by_block, turned, taper, column, even, parts)
+    rounds = range(parts // 2 - 1, 1, -1)
+    near_hops = [hop(near[r], r) for r in rounds]
+    far_own, both, *far = update_far(turned, taper, odd, part, near)
+    far_hops = []
+    for k, r in enumerate(rounds):
+        far_hops.append(hop(far[r - 2], r))
+        if k + 1 < len(rounds):
+            far[r - 3], near_hops[k] = lax.optimization_barrier((far[r - 3], near_hops[k]))
+        else:
+            both, near_hops[k] = lax.optimization_barrier((both, near_hops[k]))
+    pieces = [hop(both, 1), near[0], *near_hops[::-1], far_own, *far_hops[::-1]]
+    return gather(swap(pack(pieces), "gy", 0), pieces)
 
 
 def solution(mesh):

time: 34.6 us -> 32.4 us (0.936)
  blocking collectives: 18.2 us -> 0 us
  starting transfers between devices: 5.55 us -> 15.1 us
  waiting for transfers between devices: 2.2 us -> 8.93 us
  local copies, waits for them, and re-layouts: 1.81 us -> 0.04 us
  Pallas kernels: 6.46 us -> 7.85 us
    all_to_all x1 -> x0, blocking collectives: 18.2 us -> none  [per_device(): lax.all_to_all(updated, 'gy', split_axis=0, concat_axis=0, tiled=True)]
    ppermute x0 -> x5, starting transfers between devices: none -> 9.66 us  [hop(): return lax.ppermute(piece, 'gy', pairs)]
    ppermute x0 -> x5, waiting for transfers between devices: none -> 4.26 us  [hop(): return lax.ppermute(piece, 'gy', pairs)]
    ppermute x4 -> x5, waiting for transfers between devices: 2.2 us -> 4.68 us  [swap(): return lax.ppermute(block, axis, pairs + [(b, a) for a, b in pairs])]
    pallas_call x3 -> x5, Pallas kernels: 5.49 us -> 6.88 us  [the longest x1 2.92 us: weigh(): pl.pallas_call(weigh_kernel, out_shape=(jax.ShapeDtypeStruct((2, members,...]
    unnamed x1 -> x0, local copies, waits for them, and re-layouts: 0.99 us -> none
    transpose x1 -> x0, local copies, waits for them, and re-layouts: 0.82 us -> none  [per_device(): arrived.reshape(parts, BLK_X, BLK_Y, share, CELLS).transpose(3, 1, 0, 2, 4)]
    ppermute x4 -> x5, starting transfers between devices: 5.55 us -> 5.42 us  [swap(): return lax.ppermute(block, axis, pairs + [(b, a) for a, b in pairs])]
  transfers between devices with their start and end apart: 4 -> 10, of which waited for: 2 -> 6; matrix products, arithmetic and copies ran while one was open for 3% -> 0% of each run, Pallas kernels for 8% -> 12%
where the time goes in v10:
time: 32.4 us; the launch traced here: 32 us
  starting transfers between devices  15.1 us (47%)
  waiting for transfers between devices  8.93 us (28%)
  Pallas kernels  7.85 us (24%)
    ppermute x5, starting transfers between devices, hop(): return lax.ppermute(piece, 'gy', pairs)  9.66 us
    ppermute x5, starting transfers between devices, swap(): return lax.ppermute(block, axis, pairs + [(b, a) for a, b in pairs])  5.42 us
    ppermute x5, waiting for transfers between devices, swap(): return lax.ppermute(block, axis, pairs + [(b, a) for a, b in pairs])  4.68 us
    ppermute x5, waiting for transfers between devices, hop(): return lax.ppermute(piece, 'gy', pairs)  4.26 us
    pallas_call x1, Pallas kernels, weigh(): pl.pallas_call(weigh_kernel, out_shape=(jax.ShapeDtypeStruct((2, members,...  2.92 us
    pallas_call x1, Pallas kernels, update_near(): pl.pallas_call(near_kernel, out_shape=(jax.ShapeDtypeStruct((SIDE, member...  1.9 us
    pallas_call x1, Pallas kernels, gather(): pl.pallas_call(gather_kernel, out_shape=jax.ShapeDtypeStruct((rows, CELLS...  1.15 us
    pallas_call x1, Pallas kernels, prepare(): pl.pallas_call(prepare_kernel, out_shape=(jax.ShapeDtypeStruct((BLOCKS, C...  0.97 us
  transfers between devices with their start and end apart: 10, of which 6 were waited for; matrix products, arithmetic and copies ran while one was open for 0% of the time, Pallas kernels for 12%

profile of v10, /device:TPU:0, one launch (start us, length us, event | category | flops | bytes accessed | tf_op | source)
XLA Modules:
  0.0 32.0 jit_solution(11862996983252175251)
XLA Ops:
  0.0 2.9 %weigh.1 = (bf16[2,128,128]{2,1,0:T(8,128)(2,1)S(1)}, bf16[128,2,4,128]{3,2,1,0:T(4,128)(2,1)S(1)}) custom-call(f32[1,1,128,128]{3,2,1,0:T(8,128)} %pred_hbm.1, f32[1,1,128]{2,1,0:T(1,128)} %mv_hbm.1, f32[1,1,128]{2,1,0:T(1,128)} %var_hbm.1, f32[1,1,128,128]{3,2,1,0:T(8,128)} %jit_hbm.1, s32[4,8,128]{2,1,0:T(8,128)} %obs_hbm.3, ...), custom_call_target="tpu_custom_call" | custom-call | tf_op jit(solution)/shard_map/weigh/pallas_call | solution.py:157
  2.9 3.9 %collective-permute-start.1 = (bf16[2,128,128]{2,1,0:T(8,128)(2,1)S(1)}, bf16[2,128,128]{2,1,0:T(8,128)(2,1)S(1)}, u32[]{:S(2)}, u32[]{:S(2)}) collective-permute-start(bf16[2,128,128]{2,1,0:T(8,128)(2,1)S(1)} %get-tuple-element.25), channel_id=1, source_target_pairs={{8,16},{24,0},{16,8},{0,24},{9,17},{25,1},{17,9},{1,25},{10,18},{2... | collective-permute-start | bytes 196616 | tf_op jit(solution)/shard_map/ppermute | solution.py:420
  6.8 0.7 %collective-permute-start = (bf16[2,128,128]{2,1,0:T(8,128)(2,1)S(1)}, bf16[2,128,128]{2,1,0:T(8,128)(2,1)S(1)}, u32[]{:S(2)}, u32[]{:S(2)}) collective-permute-start(bf16[2,128,128]{2,1,0:T(8,128)(2,1)S(1)} %get-tuple-element.25), channel_id=1, source_target_pairs={{0,8},{16,24},{8,0},{24,16},{1,9},{17,25},{9,1},{25,17},{2,10},{18... | collective-permute-start | bytes 196616 | tf_op jit(solution)/shard_map/ppermute | solution.py:420
  7.6 1.0 %prepare.1 = (bf16[8,128,128]{2,1,0:T(8,128)(2,1)S(1)}, f32[3,3,8,128]{3,2,1,0:T(8,128)S(1)}) custom-call(bf16[8,128,128]{2,1,0:T(8,128)(2,1)S(1)} %bitcast.4, s32[2,4]{1,0:T(2,128)} %radius_hbm.1, s32[2,4,25]{2,1,0:T(4,128)} %pattern_hbm.1, s32[4,8,128]{2,1,0:T(8,128)} %obs_hbm.3), custom_call_target="tpu_custom_call" | custom-call | flops 4000000 | bytes 1000000 | tf_op jit(solution)/shard_map/prepare/pallas_call | solution.py:230
  8.5 0.7 %collective-permute-done.1 = bf16[2,128,128]{2,1,0:T(8,128)(2,1)S(1)} collective-permute-done((bf16[2,128,128]{2,1,0:T(8,128)(2,1)S(1)}, bf16[2,128,128]{2,1,0:T(8,128)(2,1)S(1)}, u32[]{:S(2)}, u32[]{:S(2)}) %collective-permute-start.1) | collective-permute-done | bytes 65568 | tf_op jit(solution)/shard_map/ppermute | solution.py:420
  9.3 1.9 %collective-permute-done = bf16[2,128,128]{2,1,0:T(8,128)(2,1)S(1)} collective-permute-done((bf16[2,128,128]{2,1,0:T(8,128)(2,1)S(1)}, bf16[2,128,128]{2,1,0:T(8,128)(2,1)S(1)}, u32[]{:S(2)}, u32[]{:S(2)}) %collective-permute-start) | collective-permute-done | bytes 65568 | tf_op jit(solution)/shard_map/ppermute | solution.py:420
  11.2 0.1 collective-permute-start.3
  11.3 0.7 %collective-permute-start.2 = (bf16[2,128,384]{2,1,0:T(8,128)(2,1)S(1)}, bf16[2,128,384]{2,1,0:T(8,128)(2,1)S(1)}, u32[]{:S(2)}, u32[]{:S(2)}) collective-permute-start(bf16[2,128,384]{2,1,0:T(8,128)(2,1)S(1)} %pad_maximum_fusion.own_ref), channel_id=1, source_target_pairs={{1,2},{3,4},{5,6},{2,1},{4,3},{6,5},{9,10},{11,12},{13,14},{10,9},... | collective-permute-start | bytes 589832 | tf_op jit(solution)/shard_map/ppermute | solution.py:420
  11.9 0.7 %collective-permute-done.3.even_ref = bf16[2,128,384]{2,1,0:T(8,128)(2,1)S(1)} collective-permute-done((bf16[2,128,384]{2,1,0:T(8,128)(2,1)S(1)}, bf16[2,128,384]{2,1,0:T(8,128)(2,1)S(1)}, u32[]{:S(2)}, u32[]{:S(2)}) %collective-permute-start.3) | collective-permute-done | bytes 196640 | tf_op jit(solution)/shard_map/ppermute | solution.py:420
  12.7 1.9 %near.1 = (f32[4,128,128]{2,1,0:T(8,128)S(1)}, bf16[2,4,16,128]{3,2,1,0:T(8,128)(2,1)S(1)}, bf16[2,4,16,128]{3,2,1,0:T(8,128)(2,1)S(1)}, bf16[2,4,16,128]{3,2,1,0:T(8,128)(2,1)S(1)}, bf16[2,4,16,128]{3,2,1,0:T(8,128)(2,1)S(1)}) custom-call(bf16[8,128,128]{2,1,0:T(8,128)(2,1)S(1)} %bitcast.5, bf16[8,128,128]{2,1,0:T(8,128)(2,1)S(1)} %get-tuple-element.29.turned_ref, ...), custom_call_target="tpu_custom_call" | custom-call | flops 4000000000 | bytes 10000000 | tf_op jit(solution)/shard_map/near/pallas_call | solution.py:355
  14.6 3.6 %collective-permute-start.4 = (bf16[2,4,16,128]{3,2,1,0:T(8,128)(2,1)S(1)}, bf16[2,4,16,128]{3,2,1,0:T(8,128)(2,1)S(1)}, u32[]{:S(2)}, u32[]{:S(2)}) collective-permute-start(bf16[2,4,16,128]{3,2,1,0:T(8,128)(2,1)S(1)} %get-tuple-element.35), channel_id=1, source_target_pairs={{0,4},{1,5},{2,6},{3,7},{4,0},{5,1},{6,2},{7,3},{8,12},{9,13},{10,... | collective-permute-start | bytes 98312 | tf_op jit(solution)/shard_map/ppermute | solution.py:426
  18.2 1.4 %collective-permute-start.6 = (bf16[2,4,16,128]{3,2,1,0:T(8,128)(2,1)S(1)}, bf16[2,4,16,128]{3,2,1,0:T(8,128)(2,1)S(1)}, u32[]{:S(2)}, u32[]{:S(2)}) collective-permute-start(bf16[2,4,16,128]{3,2,1,0:T(8,128)(2,1)S(1)} %get-tuple-element.40), channel_id=1, source_target_pairs={{0,6},{1,7},{2,4},{3,5},{4,2},{5,3},{6,0},{7,1},{8,14},{9,15},{10,... | collective-permute-start | bytes 98312 | tf_op jit(solution)/shard_map/ppermute | solution.py:426
  19.6 0.0 collective-permute-done.2.odd_ref
  19.6 0.9 %far.1 = (bf16[2,4,16,128]{3,2,1,0:T(8,128)(2,1)S(1)}, bf16[2,2,4,16,128]{4,3,2,1,0:T(8,128)(2,1)S(1)}, bf16[2,4,16,128]{3,2,1,0:T(8,128)(2,1)S(1)}, bf16[2,4,16,128]{3,2,1,0:T(8,128)(2,1)S(1)}) custom-call(bf16[8,128,128]{2,1,0:T(8,128)(2,1)S(1)} %get-tuple-element.29.turned_ref, f32[3,3,8,128]{3,2,1,0:T(8,128)S(1)} %get-tuple-element.30.taper_ref, ...), custom_call_target="tpu_custom_call" | custom-call | flops 4000000000 | bytes 10000000 | tf_op jit(solution)/shard_map/far/pallas_call | solution.py:372
  20.5 0.0 collective-permute-done.4.refs_2_
  20.6 1.6 %collective-permute-start.5 = (bf16[2,2,4,16,128]{4,3,2,1,0:T(8,128)(2,1)S(1)}, bf16[2,2,4,16,128]{4,3,2,1,0:T(8,128)(2,1)S(1)}, u32[]{:S(2)}, u32[]{:S(2)}) collective-permute-start(bf16[2,2,4,16,128]{4,3,2,1,0:T(8,128)(2,1)S(1)} %get-tuple-element.36), channel_id=1, source_target_pairs={{0,2},{1,3},{2,0},{3,1},{4,6},{5,7},{6,4},{7,5},{8,10},{9,11},{10,... | collective-permute-start | bytes 196616 | tf_op jit(solution)/shard_map/ppermute | solution.py:426
  22.1 2.5 %collective-permute-start.8 = (bf16[2,4,16,128]{3,2,1,0:T(8,128)(2,1)S(1)}, bf16[2,4,16,128]{3,2,1,0:T(8,128)(2,1)S(1)}, u32[]{:S(2)}, u32[]{:S(2)}) collective-permute-start(bf16[2,4,16,128]{3,2,1,0:T(8,128)(2,1)S(1)} %get-tuple-element.44), channel_id=1, source_target_pairs={{0,6},{1,7},{2,4},{3,5},{4,2},{5,3},{6,0},{7,1},{8,14},{9,15},{10,... | collective-permute-start | bytes 98312 | tf_op jit(solution)/shard_map/ppermute | solution.py:426
  24.6 0.0 collective-permute-done.6.refs_3_
  24.6 0.6 %collective-permute-start.7 = (bf16[2,4,16,128]{3,2,1,0:T(8,128)(2,1)S(1)}, bf16[2,4,16,128]{3,2,1,0:T(8,128)(2,1)S(1)}, u32[]{:S(2)}, u32[]{:S(2)}) collective-permute-start(bf16[2,4,16,128]{3,2,1,0:T(8,128)(2,1)S(1)} %get-tuple-element.43), channel_id=1, source_target_pairs={{0,4},{1,5},{2,6},{3,7},{4,0},{5,1},{6,2},{7,3},{8,12},{9,13},{10,... | collective-permute-start | bytes 98312 | tf_op jit(solution)/shard_map/ppermute | solution.py:426
  25.2 2.8 %collective-permute-done.8.refs_6_ = bf16[2,4,16,128]{3,2,1,0:T(8,128)(2,1)S(1)} collective-permute-done((bf16[2,4,16,128]{3,2,1,0:T(8,128)(2,1)S(1)}, bf16[2,4,16,128]{3,2,1,0:T(8,128)(2,1)S(1)}, u32[]{:S(2)}, u32[]{:S(2)}) %collective-permute-start.8) | collective-permute-done | bytes 32800 | tf_op jit(solution)/shard_map/ppermute | solution.py:426
  28.0 1.5 %collective-permute-done.7.refs_5_ = bf16[2,4,16,128]{3,2,1,0:T(8,128)(2,1)S(1)} collective-permute-done((bf16[2,4,16,128]{3,2,1,0:T(8,128)(2,1)S(1)}, bf16[2,4,16,128]{3,2,1,0:T(8,128)(2,1)S(1)}, u32[]{:S(2)}, u32[]{:S(2)}) %collective-permute-start.7) | collective-permute-done | bytes 32800 | tf_op jit(solution)/shard_map/ppermute | solution.py:426
  29.4 0.0 collective-permute-done.5.refs_0_
  29.5 0.1 collective-permute-start.9
  29.5 1.3 %collective-permute-done.9.even_ref = bf16[2,4,4,16,128]{4,3,2,1,0:T(8,128)(2,1)S(1)} collective-permute-done((bf16[2,4,4,16,128]{4,3,2,1,0:T(8,128)(2,1)S(1)}, bf16[2,4,4,16,128]{4,3,2,1,0:T(8,128)(2,1)S(1)}, u32[]{:S(2)}, u32[]{:S(2)}) %collective-permute-start.9) | collective-permute-done | bytes 131104 | tf_op jit(solution)/shard_map/ppermute | solution.py:420
  30.9 1.1 %gather.1 = bf16[1024,128]{1,0:T(8,128)(2,1)} custom-call(bf16[2,4,4,16,128]{4,3,2,1,0:T(8,128)(2,1)S(1)} %collective-permute-done.9.even_ref, bf16[2,2,4,16,128]{4,3,2,1,0:T(8,128)(2,1)S(1)} %collective-permute-done.5.refs_0_, bf16[2,4,16,128]{3,2,1,0:T(8,128)(2,1)S(1)} %get-tuple-element.37.refs_1_, ...), custom_call_target="tpu_custom_call" | custom-call | tf_op jit(solution)/shard_map/gather/pallas_call | solution.py:399
  (3 shorter events, 0.1 us)
Async XLA Ops:
  2.9 6.3 %collective-permute-start.1 = (bf16[2,128,128]{2,1,0:T(8,128)(2,1)S(1)}, bf16[2,128,128]{2,1,0:T(8,128)(2,1)S(1)}, u32[]{:S(2)}, u32[]{:S(2)}) collective-permute-start(bf16[2,128,128]{2,1,0:T(8,128)(2,1)S(1)} %get-tuple-element.25), channel_id=1, source_target_pairs={{8,16},{24,0},{16,8},{0,24},{9,17},{25,1},{17,9},{1,25},{10,18},{2... | collective-permute-start | bytes 196616 | tf_op jit(solution)/shard_map/ppermute | solution.py:420
  6.8 4.4 %collective-permute-start = (bf16[2,128,128]{2,1,0:T(8,128)(2,1)S(1)}, bf16[2,128,128]{2,1,0:T(8,128)(2,1)S(1)}, u32[]{:S(2)}, u32[]{:S(2)}) collective-permute-start(bf16[2,128,128]{2,1,0:T(8,128)(2,1)S(1)} %get-tuple-element.25), channel_id=1, source_target_pairs={{0,8},{16,24},{8,0},{24,16},{1,9},{17,25},{9,1},{25,17},{2,10},{18... | collective-permute-start | bytes 196616 | tf_op jit(solution)/shard_map/ppermute | solution.py:420
  11.2 1.5 %collective-permute-start.3 = (bf16[2,128,384]{2,1,0:T(8,128)(2,1)S(1)}, bf16[2,128,384]{2,1,0:T(8,128)(2,1)S(1)}, u32[]{:S(2)}, u32[]{:S(2)}) collective-permute-start(bf16[2,128,384]{2,1,0:T(8,128)(2,1)S(1)} %pad_maximum_fusion.own_ref), channel_id=1, source_target_pairs={{0,1},{2,3},{4,5},{6,7},{1,0},{3,2},{5,4},{7,6},{8,9},{10,11},{12,... | collective-permute-start | bytes 589832 | tf_op jit(solution)/shard_map/ppermute | solution.py:420
  11.3 8.4 %collective-permute-start.2 = (bf16[2,128,384]{2,1,0:T(8,128)(2,1)S(1)}, bf16[2,128,384]{2,1,0:T(8,128)(2,1)S(1)}, u32[]{:S(2)}, u32[]{:S(2)}) collective-permute-start(bf16[2,128,384]{2,1,0:T(8,128)(2,1)S(1)} %pad_maximum_fusion.own_ref), channel_id=1, source_target_pairs={{1,2},{3,4},{5,6},{2,1},{4,3},{6,5},{9,10},{11,12},{13,14},{10,9},... | collective-permute-start | bytes 589832 | tf_op jit(solution)/shard_map/ppermute | solution.py:420
  14.6 6.0 %collective-permute-start.4 = (bf16[2,4,16,128]{3,2,1,0:T(8,128)(2,1)S(1)}, bf16[2,4,16,128]{3,2,1,0:T(8,128)(2,1)S(1)}, u32[]{:S(2)}, u32[]{:S(2)}) collective-permute-start(bf16[2,4,16,128]{3,2,1,0:T(8,128)(2,1)S(1)} %get-tuple-element.35), channel_id=1, source_target_pairs={{0,4},{1,5},{2,6},{3,7},{4,0},{5,1},{6,2},{7,3},{8,12},{9,13},{10,... | collective-permute-start | bytes 98312 | tf_op jit(solution)/shard_map/ppermute | solution.py:426
  18.2 6.4 %collective-permute-start.6 = (bf16[2,4,16,128]{3,2,1,0:T(8,128)(2,1)S(1)}, bf16[2,4,16,128]{3,2,1,0:T(8,128)(2,1)S(1)}, u32[]{:S(2)}, u32[]{:S(2)}) collective-permute-start(bf16[2,4,16,128]{3,2,1,0:T(8,128)(2,1)S(1)} %get-tuple-element.40), channel_id=1, source_target_pairs={{0,6},{1,7},{2,4},{3,5},{4,2},{5,3},{6,0},{7,1},{8,14},{9,15},{10,... | collective-permute-start | bytes 98312 | tf_op jit(solution)/shard_map/ppermute | solution.py:426
  20.6 8.9 %collective-permute-start.5 = (bf16[2,2,4,16,128]{4,3,2,1,0:T(8,128)(2,1)S(1)}, bf16[2,2,4,16,128]{4,3,2,1,0:T(8,128)(2,1)S(1)}, u32[]{:S(2)}, u32[]{:S(2)}) collective-permute-start(bf16[2,2,4,16,128]{4,3,2,1,0:T(8,128)(2,1)S(1)} %get-tuple-element.36), channel_id=1, source_target_pairs={{0,2},{1,3},{2,0},{3,1},{4,6},{5,7},{6,4},{7,5},{8,10},{9,11},{10,... | collective-permute-start | bytes 196616 | tf_op jit(solution)/shard_map/ppermute | solution.py:426
  22.1 5.8 %collective-permute-start.8 = (bf16[2,4,16,128]{3,2,1,0:T(8,128)(2,1)S(1)}, bf16[2,4,16,128]{3,2,1,0:T(8,128)(2,1)S(1)}, u32[]{:S(2)}, u32[]{:S(2)}) collective-permute-start(bf16[2,4,16,128]{3,2,1,0:T(8,128)(2,1)S(1)} %get-tuple-element.44), channel_id=1, source_target_pairs={{0,6},{1,7},{2,4},{3,5},{4,2},{5,3},{6,0},{7,1},{8,14},{9,15},{10,... | collective-permute-start | bytes 98312 | tf_op jit(solution)/shard_map/ppermute | solution.py:426
  24.6 4.8 %collective-permute-start.7 = (bf16[2,4,16,128]{3,2,1,0:T(8,128)(2,1)S(1)}, bf16[2,4,16,128]{3,2,1,0:T(8,128)(2,1)S(1)}, u32[]{:S(2)}, u32[]{:S(2)}) collective-permute-start(bf16[2,4,16,128]{3,2,1,0:T(8,128)(2,1)S(1)} %get-tuple-element.43), channel_id=1, source_target_pairs={{0,4},{1,5},{2,6},{3,7},{4,0},{5,1},{6,2},{7,3},{8,12},{9,13},{10,... | collective-permute-start | bytes 98312 | tf_op jit(solution)/shard_map/ppermute | solution.py:426
  29.5 1.4 %collective-permute-start.9 = (bf16[2,4,4,16,128]{4,3,2,1,0:T(8,128)(2,1)S(1)}, bf16[2,4,4,16,128]{4,3,2,1,0:T(8,128)(2,1)S(1)}, u32[]{:S(2)}, u32[]{:S(2)}) collective-permute-start(bf16[2,4,4,16,128]{4,3,2,1,0:T(8,128)(2,1)S(1)} %pack.1), channel_id=1, source_target_pairs={{0,1},{2,3},{4,5},{6,7},{1,0},{3,2},{5,4},{7,6},{8,9},{10,11},{12,... | collective-permute-start | bytes 393224 | tf_op jit(solution)/shard_map/ppermute | solution.py:420

commit v11 on v10

--- a/solution.py
+++ b/solution.py
@@ -96,39 +96,43 @@
     tile_y = lax.axis_index("gy")
     square = (OBS_TILE, OBS_TILE)
     pairs = [
-        (pred_hbm.at[0, 0], pred_ref),
         (obs_hbm.at[tile_x], obs_ref),
         (var_hbm.at[0], var_ref),
+        (pred_hbm.at[0, 0], pred_ref),
         (mv_hbm.at[0], mv_ref),
         (jit_hbm.at[0, 0], jit_ref),
         (params_hbm, params_ref),
     ]
     copies = fetch(pairs, sems)
-    for copy in copies[:3]:
-        copy.wait()
-    pred = pred_ref[...]
-    var = var_ref[...]
-    mean = jnp.sum(pred, axis=0, keepdims=True) / members
-    deviation = (pred - mean).astype(BF16)
-    out_ref[0] = deviation
+    copies[0].wait()
     obs = obs_ref[pl.ds(tile_y, 1), :]
     groups = (iota((BLOCKS, OBS_TILE), 0) == obs).astype(BF16)
     same = dot(groups, groups, ((0,), (0,)))
-    gram = dot(deviation, deviation, ((0,), (0,))) / (members - 1)
     row, col = iota(square, 0), iota(square, 1)
-    system = jnp.where(same > 0.5, gram, 0.0) + jnp.where(row == col, var, 0.0)
     size = jnp.sum(same, axis=0, keepdims=True)
     count = jnp.max(size).astype(jnp.int32)
     size = size.astype(jnp.int32)
     rank = jnp.sum(jnp.where(row < col, same, 0.0), axis=0, keepdims=True).astype(jnp.int32)
     place = row == rank
     hot = place.astype(BF16)
+    numbered = jnp.where(place, col, 0).astype(F32).astype(BF16)
+    idx_ref[...] = dot(numbered, same.astype(BF16), ((1,), (0,))).astype(jnp.int32)
+    for copy in copies[1:3]:
+        copy.wait()
+    var = var_ref[...]
+    pred = pred_ref[...]
+    mean = jnp.sum(pred, axis=0, keepdims=True) / members
+    deviation = (pred - mean).astype(BF16)
+    out_ref[0] = deviation
+    gram = dot(deviation, deviation, ((0,), (0,))) / (members - 1)
+    system = jnp.where(same > 0.5, gram, 0.0) + jnp.where(row == col, var, 0.0)
     high, mid, low = split3(system)
     x_ref[...] = (
         dot(hot, low, ((1,), (0,))) + dot(hot, mid, ((1,), (0,))) + dot(hot, high, ((1,), (0,)))
     )
-    numbered = jnp.where(place, col, 0).astype(F32).astype(BF16)
-    idx_ref[...] = dot(numbered, same.astype(BF16), ((1,), (0,))).astype(jnp.int32)
+    for copy in copies[3:]:
+        copy.wait()
+    pred_ref[...] = mv_ref[...] + jnp.sqrt(var) * jit_ref[...] - pred
 
     def solve(rows):
         sweep(rows, count, x_ref, idx_ref, rank, size)
@@ -145,10 +149,7 @@
     def _():
         solve(OBS_TILE)
 
-    for copy in copies[3:]:
-        copy.wait()
-    innovation = mv_ref[...] + jnp.sqrt(var) * jit_ref[...] - pred
-    weighted = dot(innovation, full_ref[...], ((1,), (0,)), lax.Precision.HIGHEST)
+    weighted = dot(pred_ref[...], full_ref[...], ((1,), (0,)), lax.Precision.HIGHEST)
     out_ref[1] = weighted.astype(BF16)
 
 
@@ -294,8 +295,8 @@
 
 
 def far_kernel(turned_ref, taper_ref, odd_ref, part_ref, near_ref, *refs):
-    both_ref, rows_ref = refs[1], refs[-1]
-    piece_refs = (refs[0], both_ref.at[1], *refs[2:-1])
+    both_ref, rows_ref = refs[-2], refs[-1]
+    piece_refs = (*refs[:-2], both_ref.at[1])
     both_ref[0] = near_ref[...]
     tile_y = lax.axis_index("gy")
     for k in range(SIDE):
@@ -303,35 +304,37 @@
         put(piece_refs, rows_ref, k, (part_ref[k] + moved(b, 2, turned_ref, taper_ref, odd_ref)).astype(BF16))
 
 
-def sorted_pieces(refs):
-    both_ref, rest = refs[0], refs[1:]
-    near, far = rest[: len(rest) // 2], rest[len(rest) // 2 :]
-    return [(near[0], both_ref.at[0], *near[1:]), (far[0], both_ref.at[1], *far[1:])]
-
-
 def pack_kernel(*refs):
-    out_ref = refs[-1]
-    for side, pieces in enumerate(sorted_pieces(refs[:-1])):
-        for r, piece in enumerate(pieces):
-            out_ref[side, r] = piece[1]
-
-
-def gather_kernel(even_ref, *refs):
-    out_hbm, rows_ref, out_ref, sems = refs[-4:]
-    pieces = sorted_pieces(refs[:-4])
-    chips, share = even_ref.shape[1], even_ref.shape[3]
+    at = 0
+    for ref in refs[:-1]:
+        for piece in halves(ref):
+            refs[-1][at] = piece[1]
+            at += 1
+
+
+def halves(ref):
+    return [ref] if len(ref.shape) == 4 else [ref.at[side] for side in range(ref.shape[0])]
+
+
+def gather_kernel(chips, *refs):
+    early, late = refs[: chips + 1], refs[chips + 1 : 2 * chips + 1]
+    out_hbm, rows_ref, out_ref, sems = refs[2 * chips + 1 :]
+    last = chips - 1
+    places = [(0, 0), (1, 0)] + [(0, r) for r in range(1, last)] + [(0, last), (1, last)] + [(1, r) for r in range(1, last)]
+    mine_pieces = [piece for ref in early[1:] + late[1:] for piece in halves(ref)]
+    even_pieces = [ref.at[k] for ref in (early[0], late[0]) for k in range(ref.shape[0])]
+    share = early[0].shape[2]
     mine = lax.axis_index("gy")
     chip, core = mine >> 1, mine & 1
     line = 2 * chips * BLK_Y
-    for r in range(chips):
+    for (side, r), own, even in zip(places, mine_pieces, even_pieces):
         for flip in (0, 1):
             other = core ^ flip
             tile = 2 * source(chip, r, chips) + other
-            for side in (0, 1):
-                for k in range(SIDE):
-                    piece = even_ref[side, r, k] if flip else pieces[side][r][0, k]
-                    start = (k >> 1) * line + tile * BLK_Y + first_of(side, other) + (k & 1)
-                    rows_ref[pl.ds(start, share, stride=BLK_X * line), :] = piece.astype(F32)
+            for k in range(SIDE):
+                piece = even[k] if flip else own[0, k]
+                start = (k >> 1) * line + tile * BLK_Y + first_of(side, other) + (k & 1)
+                rows_ref[pl.ds(start, share, stride=BLK_X * line), :] = piece.astype(F32)
     pieces = sems.shape[0]
     step = rows_ref.shape[0] // pieces
     copies = []
@@ -368,7 +371,7 @@
     members = part.shape[1]
     parts = members // near[0].shape[2]
     piece = jax.ShapeDtypeStruct(near[0].shape, BF16)
-    shapes = (piece, jax.ShapeDtypeStruct((2, *piece.shape), BF16)) + (piece,) * (parts // 2 - 2)
+    shapes = (piece,) * (parts // 2 - 1) + (jax.ShapeDtypeStruct((2, *piece.shape), BF16),)
     return pl.pallas_call(
         far_kernel,
         out_shape=shapes,
@@ -378,14 +381,14 @@
         compiler_params=LIMIT,
         cost_estimate=LONG,
         name="far",
-    )(turned, taper, odd, part, near[1])
+    )(turned, taper, odd, part, near[-1])
 
 
 def pack(pieces):
-    chips = len(pieces) // 2 + 1
+    count = sum(1 if piece.ndim == 4 else piece.shape[0] for piece in pieces)
     return pl.pallas_call(
         pack_kernel,
-        out_shape=jax.ShapeDtypeStruct((2, chips, *pieces[1].shape[1:]), BF16),
+        out_shape=jax.ShapeDtypeStruct((count, *pieces[-1].shape[-3:]), BF16),
         in_specs=[VMEM] * len(pieces),
         out_specs=VMEM,
         compiler_params=LIMIT,
@@ -393,13 +396,13 @@
     )(*pieces)
 
 
-def gather(even, pieces):
-    _, chips, _, share, _ = even.shape
+def gather(chips, early_even, early, late_even, late):
+    share = early[0].shape[2]
     rows = share * BLOCKS * 2 * chips
     out = pl.pallas_call(
-        gather_kernel,
+        functools.partial(gather_kernel, chips),
         out_shape=jax.ShapeDtypeStruct((rows, CELLS), BF16),
-        in_specs=[VMEM] * (1 + len(pieces)),
+        in_specs=[VMEM] * (2 + len(early) + len(late)),
         out_specs=pl.BlockSpec(memory_space=pl.ANY),
         scratch_shapes=[
             pltpu.VMEM((rows, CELLS), F32),
@@ -408,7 +411,7 @@
         ],
         compiler_params=LIMIT,
         name="gather",
-    )(even, *pieces)
+    )(early_even, *early, late_even, *late)
     return out.reshape(share, BLK_X, 2 * chips * BLK_Y, CELLS)
 
 
@@ -450,18 +453,17 @@
     even = swap(column, "gy", 0)
     odd = swap(column, "gy", 1)
     part, *near = update_near(by_block, turned, taper, column, even, parts)
-    rounds = range(parts // 2 - 1, 1, -1)
-    near_hops = [hop(near[r], r) for r in rounds]
-    far_own, both, *far = update_far(turned, taper, odd, part, near)
-    far_hops = []
-    for k, r in enumerate(rounds):
-        far_hops.append(hop(far[r - 2], r))
-        if k + 1 < len(rounds):
-            far[r - 3], near_hops[k] = lax.optimization_barrier((far[r - 3], near_hops[k]))
-        else:
-            both, near_hops[k] = lax.optimization_barrier((both, near_hops[k]))
-    pieces = [hop(both, 1), near[0], *near_hops[::-1], far_own, *far_hops[::-1]]
-    return gather(swap(pack(pieces), "gy", 0), pieces)
+    last = parts // 2 - 1
+    near_hops = {r: hop(near[r], r) for r in range(1, last)}
+    *far, both = update_far(turned, taper, odd, part, near)
+    for r in range(1, last):
+        far[r], near_hops[r] = lax.optimization_barrier((far[r], near_hops[r]))
+    far_hops = {r: hop(far[r], r) for r in range(1, last)}
+    early = [near[0], far[0], *(near_hops[r] for r in range(1, last))]
+    late = [hop(both, last), *(far_hops[r] for r in range(1, last))]
+    late_even = swap(pack(late), "gy", 0)
+    early_even = swap(pack(early), "gy", 0)
+    return gather(parts // 2, early_even, early, late_even, late)
 
 
 def solution(mesh):

time: 32.4 us -> 31 us (0.957)
  waiting for transfers between devices: 8.93 us -> 7.28 us
    ppermute x5, waiting for transfers between devices: 4.26 us -> 2.75 us  [hop(): return lax.ppermute(piece, 'gy', pairs)]
    ppermute x5 -> x6, starting transfers between devices: 5.42 us -> 5.21 us  [swap(): return lax.ppermute(block, axis, pairs + [(b, a) for a, b in pairs])]
    ppermute x5 -> x6, waiting for transfers between devices: 4.68 us -> 4.53 us  [swap(): return lax.ppermute(block, axis, pairs + [(b, a) for a, b in pairs])]
    pallas_call x2 -> x3, Pallas kernels: 1.16 us -> 1.16 us  [the longest x1 1.15 us: gather(): pl.pallas_call(functools.partial(gather_kernel, chips), out_shape=jax.Sha...]
  transfers between devices with their start and end apart: 10 -> 11, of which waited for: 6 -> 4; matrix products, arithmetic and copies ran while one was open for 0% -> 0% of each run, Pallas kernels for 12% -> 12%
where the time goes in v11:
time: 31 us; the launch traced here: 30.6 us
  starting transfers between devices  15 us (48%)
  Pallas kernels  8.16 us (26%)
  waiting for transfers between devices  7.28 us (23%)
    ppermute x5, starting transfers between devices, hop(): return lax.ppermute(piece, 'gy', pairs)  9.76 us
    ppermute x6, starting transfers between devices, swap(): return lax.ppermute(block, axis, pairs + [(b, a) for a, b in pairs])  5.21 us
    ppermute x6, waiting for transfers between devices, swap(): return lax.ppermute(block, axis, pairs + [(b, a) for a, b in pairs])  4.53 us
    pallas_call x1, Pallas kernels, weigh(): pl.pallas_call(weigh_kernel, out_shape=(jax.ShapeDtypeStruct((2, members,...  3.22 us
    ppermute x5, waiting for transfers between devices, hop(): return lax.ppermute(piece, 'gy', pairs)  2.75 us
    pallas_call x1, Pallas kernels, update_near(): pl.pallas_call(near_kernel, out_shape=(jax.ShapeDtypeStruct((SIDE, member...  1.9 us
    pallas_call x1, Pallas kernels, gather(): pl.pallas_call(functools.partial(gather_kernel, chips), out_shape=jax.Sha...  1.15 us
    pallas_call x1, Pallas kernels, prepare(): pl.pallas_call(prepare_kernel, out_shape=(jax.ShapeDtypeStruct((BLOCKS, C...  0.97 us
  transfers between devices with their start and end apart: 11, of which 4 were waited for; matrix products, arithmetic and copies ran while one was open for 0% of the time, Pallas kernels for 12%

profile of v11, /device:TPU:0, one launch (start us, length us, event | category | flops | bytes accessed | tf_op | source)
XLA Modules:
  0.0 30.6 jit_solution(5001387251322107832)
XLA Ops:
  0.0 3.2 %weigh.1 = (bf16[2,128,128]{2,1,0:T(8,128)(2,1)S(1)}, bf16[128,2,4,128]{3,2,1,0:T(4,128)(2,1)S(1)}) custom-call(f32[1,1,128,128]{3,2,1,0:T(8,128)} %pred_hbm.1, f32[1,1,128]{2,1,0:T(1,128)} %mv_hbm.1, f32[1,1,128]{2,1,0:T(1,128)} %var_hbm.1, f32[1,1,128,128]{3,2,1,0:T(8,128)} %jit_hbm.1, s32[4,8,128]{2,1,0:T(8,128)} %obs_hbm.3, ...), custom_call_target="tpu_custom_call" | custom-call | tf_op jit(solution)/shard_map/weigh/pallas_call | solution.py:158
  3.2 2.8 %collective-permute-start = (bf16[2,128,128]{2,1,0:T(8,128)(2,1)S(1)}, bf16[2,128,128]{2,1,0:T(8,128)(2,1)S(1)}, u32[]{:S(2)}, u32[]{:S(2)}) collective-permute-start(bf16[2,128,128]{2,1,0:T(8,128)(2,1)S(1)} %get-tuple-element.26), channel_id=1, source_target_pairs={{0,8},{16,24},{8,0},{24,16},{1,9},{17,25},{9,1},{25,17},{2,10},{18... | collective-permute-start | bytes 196616 | tf_op jit(solution)/shard_map/ppermute | solution.py:423
  6.0 1.6 %collective-permute-start.1 = (bf16[2,128,128]{2,1,0:T(8,128)(2,1)S(1)}, bf16[2,128,128]{2,1,0:T(8,128)(2,1)S(1)}, u32[]{:S(2)}, u32[]{:S(2)}) collective-permute-start(bf16[2,128,128]{2,1,0:T(8,128)(2,1)S(1)} %get-tuple-element.26), channel_id=1, source_target_pairs={{8,16},{24,0},{16,8},{0,24},{9,17},{25,1},{17,9},{1,25},{10,18},{2... | collective-permute-start | bytes 196616 | tf_op jit(solution)/shard_map/ppermute | solution.py:423
  7.7 1.0 %prepare.1 = (bf16[8,128,128]{2,1,0:T(8,128)(2,1)S(1)}, f32[3,3,8,128]{3,2,1,0:T(8,128)S(1)}) custom-call(bf16[8,128,128]{2,1,0:T(8,128)(2,1)S(1)} %bitcast.4, s32[2,4]{1,0:T(2,128)} %radius_hbm.1, s32[2,4,25]{2,1,0:T(4,128)} %pattern_hbm.1, s32[4,8,128]{2,1,0:T(8,128)} %obs_hbm.3), custom_call_target="tpu_custom_call" | custom-call | flops 4000000 | bytes 1000000 | tf_op jit(solution)/shard_map/prepare/pallas_call | solution.py:231
  8.6 0.0 collective-permute-done
  8.6 2.5 %collective-permute-done.1 = bf16[2,128,128]{2,1,0:T(8,128)(2,1)S(1)} collective-permute-done((bf16[2,128,128]{2,1,0:T(8,128)(2,1)S(1)}, bf16[2,128,128]{2,1,0:T(8,128)(2,1)S(1)}, u32[]{:S(2)}, u32[]{:S(2)}) %collective-permute-start.1) | collective-permute-done | bytes 65568 | tf_op jit(solution)/shard_map/ppermute | solution.py:423
  11.2 0.1 collective-permute-start.2
  11.3 0.7 %collective-permute-start.3 = (bf16[2,128,384]{2,1,0:T(8,128)(2,1)S(1)}, bf16[2,128,384]{2,1,0:T(8,128)(2,1)S(1)}, u32[]{:S(2)}, u32[]{:S(2)}) collective-permute-start(bf16[2,128,384]{2,1,0:T(8,128)(2,1)S(1)} %pad_maximum_fusion.own_ref), channel_id=1, source_target_pairs={{1,2},{3,4},{5,6},{2,1},{4,3},{6,5},{9,10},{11,12},{13,14},{10,9},... | collective-permute-start | bytes 589832 | tf_op jit(solution)/shard_map/ppermute | solution.py:423
  12.0 0.7 %collective-permute-done.2.even_ref = bf16[2,128,384]{2,1,0:T(8,128)(2,1)S(1)} collective-permute-done((bf16[2,128,384]{2,1,0:T(8,128)(2,1)S(1)}, bf16[2,128,384]{2,1,0:T(8,128)(2,1)S(1)}, u32[]{:S(2)}, u32[]{:S(2)}) %collective-permute-start.2) | collective-permute-done | bytes 196640 | tf_op jit(solution)/shard_map/ppermute | solution.py:423
  12.7 1.9 %near.1 = (f32[4,128,128]{2,1,0:T(8,128)S(1)}, bf16[2,4,16,128]{3,2,1,0:T(8,128)(2,1)S(1)}, bf16[2,4,16,128]{3,2,1,0:T(8,128)(2,1)S(1)}, bf16[2,4,16,128]{3,2,1,0:T(8,128)(2,1)S(1)}, bf16[2,4,16,128]{3,2,1,0:T(8,128)(2,1)S(1)}) custom-call(bf16[8,128,128]{2,1,0:T(8,128)(2,1)S(1)} %bitcast.5, bf16[8,128,128]{2,1,0:T(8,128)(2,1)S(1)} %get-tuple-element.29.turned_ref, ...), custom_call_target="tpu_custom_call" | custom-call | flops 4000000000 | bytes 10000000 | tf_op jit(solution)/shard_map/near/pallas_call | solution.py:358
  14.6 3.7 %collective-permute-start.5 = (bf16[2,4,16,128]{3,2,1,0:T(8,128)(2,1)S(1)}, bf16[2,4,16,128]{3,2,1,0:T(8,128)(2,1)S(1)}, u32[]{:S(2)}, u32[]{:S(2)}) collective-permute-start(bf16[2,4,16,128]{3,2,1,0:T(8,128)(2,1)S(1)} %get-tuple-element.40), channel_id=1, source_target_pairs={{0,4},{1,5},{2,6},{3,7},{4,0},{5,1},{6,2},{7,3},{8,12},{9,13},{10,... | collective-permute-start | bytes 98312 | tf_op jit(solution)/shard_map/ppermute | solution.py:429
  18.3 1.6 %collective-permute-start.4 = (bf16[2,4,16,128]{3,2,1,0:T(8,128)(2,1)S(1)}, bf16[2,4,16,128]{3,2,1,0:T(8,128)(2,1)S(1)}, u32[]{:S(2)}, u32[]{:S(2)}) collective-permute-start(bf16[2,4,16,128]{3,2,1,0:T(8,128)(2,1)S(1)} %get-tuple-element.37), channel_id=1, source_target_pairs={{0,2},{1,3},{2,0},{3,1},{4,6},{5,7},{6,4},{7,5},{8,10},{9,11},{10,... | collective-permute-start | bytes 98312 | tf_op jit(solution)/shard_map/ppermute | solution.py:429
  19.9 0.0 collective-permute-done.3.odd_ref
  19.9 0.9 %far.1 = (bf16[2,4,16,128]{3,2,1,0:T(8,128)(2,1)S(1)}, bf16[2,4,16,128]{3,2,1,0:T(8,128)(2,1)S(1)}, bf16[2,4,16,128]{3,2,1,0:T(8,128)(2,1)S(1)}, bf16[2,2,4,16,128]{4,3,2,1,0:T(8,128)(2,1)S(1)}) custom-call(bf16[8,128,128]{2,1,0:T(8,128)(2,1)S(1)} %get-tuple-element.29.turned_ref, f32[3,3,8,128]{3,2,1,0:T(8,128)S(1)} %get-tuple-element.30.taper_ref, ...), custom_call_target="tpu_custom_call" | custom-call | flops 4000000000 | bytes 10000000 | tf_op jit(solution)/shard_map/far/pallas_call | solution.py:375
  20.8 1.9 %collective-permute-start.7 = (bf16[2,2,4,16,128]{4,3,2,1,0:T(8,128)(2,1)S(1)}, bf16[2,2,4,16,128]{4,3,2,1,0:T(8,128)(2,1)S(1)}, u32[]{:S(2)}, u32[]{:S(2)}) collective-permute-start(bf16[2,2,4,16,128]{4,3,2,1,0:T(8,128)(2,1)S(1)} %get-tuple-element.42), channel_id=1, source_target_pairs={{0,6},{1,7},{2,4},{3,5},{4,2},{5,3},{6,0},{7,1},{8,14},{9,15},{10,... | collective-permute-start | bytes 196616 | tf_op jit(solution)/shard_map/ppermute | solution.py:429
  22.8 0.0 collective-permute-done.5.refs_3_.refs_4_
  22.8 0.7 %collective-permute-start.9 = (bf16[2,4,16,128]{3,2,1,0:T(8,128)(2,1)S(1)}, bf16[2,4,16,128]{3,2,1,0:T(8,128)(2,1)S(1)}, u32[]{:S(2)}, u32[]{:S(2)}) collective-permute-start(bf16[2,4,16,128]{3,2,1,0:T(8,128)(2,1)S(1)} %get-tuple-element.44), channel_id=1, source_target_pairs={{0,4},{1,5},{2,6},{3,7},{4,0},{5,1},{6,2},{7,3},{8,12},{9,13},{10,... | collective-permute-start | bytes 98312 | tf_op jit(solution)/shard_map/ppermute | solution.py:429
  23.5 0.0 collective-permute-done.4.refs_2_.refs_3_
  23.5 1.8 %collective-permute-start.8 = (bf16[2,4,16,128]{3,2,1,0:T(8,128)(2,1)S(1)}, bf16[2,4,16,128]{3,2,1,0:T(8,128)(2,1)S(1)}, u32[]{:S(2)}, u32[]{:S(2)}) collective-permute-start(bf16[2,4,16,128]{3,2,1,0:T(8,128)(2,1)S(1)} %get-tuple-element.43), channel_id=1, source_target_pairs={{0,2},{1,3},{2,0},{3,1},{4,6},{5,7},{6,4},{7,5},{8,10},{9,11},{10,... | collective-permute-start | bytes 98312 | tf_op jit(solution)/shard_map/ppermute | solution.py:429
  25.3 0.0 collective-permute-start.6
  25.3 2.7 %collective-permute-done.9.refs_2_.refs_8_ = bf16[2,4,16,128]{3,2,1,0:T(8,128)(2,1)S(1)} collective-permute-done((bf16[2,4,16,128]{3,2,1,0:T(8,128)(2,1)S(1)}, bf16[2,4,16,128]{3,2,1,0:T(8,128)(2,1)S(1)}, u32[]{:S(2)}, u32[]{:S(2)}) %collective-permute-start.9) | collective-permute-done | bytes 32800 | tf_op jit(solution)/shard_map/ppermute | solution.py:429
  28.1 0.0 collective-permute-done.8.refs_1_.refs_7_
  28.1 0.0 collective-permute-done.7.refs_0_.refs_6_
  28.1 0.1 collective-permute-start.10
  28.2 0.0 collective-permute-done.6.refs_0_
  28.2 1.2 %collective-permute-done.10.refs_5_ = bf16[4,4,16,128]{3,2,1,0:T(8,128)(2,1)S(1)} collective-permute-done((bf16[4,4,16,128]{3,2,1,0:T(8,128)(2,1)S(1)}, bf16[4,4,16,128]{3,2,1,0:T(8,128)(2,1)S(1)}, u32[]{:S(2)}, u32[]{:S(2)}) %collective-permute-start.10) | collective-permute-done | bytes 65568 | tf_op jit(solution)/shard_map/ppermute | solution.py:423
  29.4 1.2 %gather.1 = bf16[1024,128]{1,0:T(8,128)(2,1)} custom-call(bf16[4,4,16,128]{3,2,1,0:T(8,128)(2,1)S(1)} %collective-permute-done.6.refs_0_, bf16[2,4,16,128]{3,2,1,0:T(8,128)(2,1)S(1)} %get-tuple-element.32.refs_0_.refs_1_, bf16[2,4,16,128]{3,2,1,0:T(8,128)(2,1)S(1)} %get-tuple-element.35.refs_1_.refs_2_, ...), custom_call_target="tpu_custom_call" | custom-call | tf_op jit(solution)/shard_map/gather/pallas_call | solution.py:402
  (4 shorter events, 0.1 us)
Async XLA Ops:
  3.2 5.4 %collective-permute-start = (bf16[2,128,128]{2,1,0:T(8,128)(2,1)S(1)}, bf16[2,128,128]{2,1,0:T(8,128)(2,1)S(1)}, u32[]{:S(2)}, u32[]{:S(2)}) collective-permute-start(bf16[2,128,128]{2,1,0:T(8,128)(2,1)S(1)} %get-tuple-element.26), channel_id=1, source_target_pairs={{0,8},{16,24},{8,0},{24,16},{1,9},{17,25},{9,1},{25,17},{2,10},{18... | collective-permute-start | bytes 196616 | tf_op jit(solution)/shard_map/ppermute | solution.py:423
  6.0 5.2 %collective-permute-start.1 = (bf16[2,128,128]{2,1,0:T(8,128)(2,1)S(1)}, bf16[2,128,128]{2,1,0:T(8,128)(2,1)S(1)}, u32[]{:S(2)}, u32[]{:S(2)}) collective-permute-start(bf16[2,128,128]{2,1,0:T(8,128)(2,1)S(1)} %get-tuple-element.26), channel_id=1, source_target_pairs={{8,16},{24,0},{16,8},{0,24},{9,17},{25,1},{17,9},{1,25},{10,18},{2... | collective-permute-start | bytes 196616 | tf_op jit(solution)/shard_map/ppermute | solution.py:423
  11.2 1.5 %collective-permute-start.2 = (bf16[2,128,384]{2,1,0:T(8,128)(2,1)S(1)}, bf16[2,128,384]{2,1,0:T(8,128)(2,1)S(1)}, u32[]{:S(2)}, u32[]{:S(2)}) collective-permute-start(bf16[2,128,384]{2,1,0:T(8,128)(2,1)S(1)} %pad_maximum_fusion.own_ref), channel_id=1, source_target_pairs={{0,1},{2,3},{4,5},{6,7},{1,0},{3,2},{5,4},{7,6},{8,9},{10,11},{12,... | collective-permute-start | bytes 589832 | tf_op jit(solution)/shard_map/ppermute | solution.py:423
  11.3 8.6 %collective-permute-start.3 = (bf16[2,128,384]{2,1,0:T(8,128)(2,1)S(1)}, bf16[2,128,384]{2,1,0:T(8,128)(2,1)S(1)}, u32[]{:S(2)}, u32[]{:S(2)}) collective-permute-start(bf16[2,128,384]{2,1,0:T(8,128)(2,1)S(1)} %pad_maximum_fusion.own_ref), channel_id=1, source_target_pairs={{1,2},{3,4},{5,6},{2,1},{4,3},{6,5},{9,10},{11,12},{13,14},{10,9},... | collective-permute-start | bytes 589832 | tf_op jit(solution)/shard_map/ppermute | solution.py:423
  14.6 8.1 %collective-permute-start.5 = (bf16[2,4,16,128]{3,2,1,0:T(8,128)(2,1)S(1)}, bf16[2,4,16,128]{3,2,1,0:T(8,128)(2,1)S(1)}, u32[]{:S(2)}, u32[]{:S(2)}) collective-permute-start(bf16[2,4,16,128]{3,2,1,0:T(8,128)(2,1)S(1)} %get-tuple-element.40), channel_id=1, source_target_pairs={{0,4},{1,5},{2,6},{3,7},{4,0},{5,1},{6,2},{7,3},{8,12},{9,13},{10,... | collective-permute-start | bytes 98312 | tf_op jit(solution)/shard_map/ppermute | solution.py:429
  18.3 5.1 %collective-permute-start.4 = (bf16[2,4,16,128]{3,2,1,0:T(8,128)(2,1)S(1)}, bf16[2,4,16,128]{3,2,1,0:T(8,128)(2,1)S(1)}, u32[]{:S(2)}, u32[]{:S(2)}) collective-permute-start(bf16[2,4,16,128]{3,2,1,0:T(8,128)(2,1)S(1)} %get-tuple-element.37), channel_id=1, source_target_pairs={{0,2},{1,3},{2,0},{3,1},{4,6},{5,7},{6,4},{7,5},{8,10},{9,11},{10,... | collective-permute-start | bytes 98312 | tf_op jit(solution)/shard_map/ppermute | solution.py:429
  20.8 7.2 %collective-permute-start.7 = (bf16[2,2,4,16,128]{4,3,2,1,0:T(8,128)(2,1)S(1)}, bf16[2,2,4,16,128]{4,3,2,1,0:T(8,128)(2,1)S(1)}, u32[]{:S(2)}, u32[]{:S(2)}) collective-permute-start(bf16[2,2,4,16,128]{4,3,2,1,0:T(8,128)(2,1)S(1)} %get-tuple-element.42), channel_id=1, source_target_pairs={{0,6},{1,7},{2,4},{3,5},{4,2},{5,3},{6,0},{7,1},{8,14},{9,15},{10,... | collective-permute-start | bytes 196616 | tf_op jit(solution)/shard_map/ppermute | solution.py:429
  22.8 5.3 %collective-permute-start.9 = (bf16[2,4,16,128]{3,2,1,0:T(8,128)(2,1)S(1)}, bf16[2,4,16,128]{3,2,1,0:T(8,128)(2,1)S(1)}, u32[]{:S(2)}, u32[]{:S(2)}) collective-permute-start(bf16[2,4,16,128]{3,2,1,0:T(8,128)(2,1)S(1)} %get-tuple-element.44), channel_id=1, source_target_pairs={{0,4},{1,5},{2,6},{3,7},{4,0},{5,1},{6,2},{7,3},{8,12},{9,13},{10,... | collective-permute-start | bytes 98312 | tf_op jit(solution)/shard_map/ppermute | solution.py:429
  23.5 4.6 %collective-permute-start.8 = (bf16[2,4,16,128]{3,2,1,0:T(8,128)(2,1)S(1)}, bf16[2,4,16,128]{3,2,1,0:T(8,128)(2,1)S(1)}, u32[]{:S(2)}, u32[]{:S(2)}) collective-permute-start(bf16[2,4,16,128]{3,2,1,0:T(8,128)(2,1)S(1)} %get-tuple-element.43), channel_id=1, source_target_pairs={{0,2},{1,3},{2,0},{3,1},{4,6},{5,7},{6,4},{7,5},{8,10},{9,11},{10,... | collective-permute-start | bytes 98312 | tf_op jit(solution)/shard_map/ppermute | solution.py:429
  25.3 2.8 %collective-permute-start.6 = (bf16[4,4,16,128]{3,2,1,0:T(8,128)(2,1)S(1)}, bf16[4,4,16,128]{3,2,1,0:T(8,128)(2,1)S(1)}, u32[]{:S(2)}, u32[]{:S(2)}) collective-permute-start(bf16[4,4,16,128]{3,2,1,0:T(8,128)(2,1)S(1)} %pack.2), channel_id=1, source_target_pairs={{0,1},{2,3},{4,5},{6,7},{1,0},{3,2},{5,4},{7,6},{8,9},{10,11},{12,... | collective-permute-start | bytes 196616 | tf_op jit(solution)/shard_map/ppermute | solution.py:423
  28.1 1.3 %collective-permute-start.10 = (bf16[4,4,16,128]{3,2,1,0:T(8,128)(2,1)S(1)}, bf16[4,4,16,128]{3,2,1,0:T(8,128)(2,1)S(1)}, u32[]{:S(2)}, u32[]{:S(2)}) collective-permute-start(bf16[4,4,16,128]{3,2,1,0:T(8,128)(2,1)S(1)} %pack.3), channel_id=1, source_target_pairs={{0,1},{2,3},{4,5},{6,7},{1,0},{3,2},{5,4},{7,6},{8,9},{10,11},{12,... | collective-permute-start | bytes 196616 | tf_op jit(solution)/shard_map/ppermute | solution.py:423

commit v12 on v10

--- a/solution.py
+++ b/solution.py
@@ -303,35 +303,41 @@
         put(piece_refs, rows_ref, k, (part_ref[k] + moved(b, 2, turned_ref, taper_ref, odd_ref)).astype(BF16))
 
 
-def sorted_pieces(refs):
-    both_ref, rest = refs[0], refs[1:]
-    near, far = rest[: len(rest) // 2], rest[len(rest) // 2 :]
-    return [(near[0], both_ref.at[0], *near[1:]), (far[0], both_ref.at[1], *far[1:])]
-
-
 def pack_kernel(*refs):
-    out_ref = refs[-1]
-    for side, pieces in enumerate(sorted_pieces(refs[:-1])):
-        for r, piece in enumerate(pieces):
-            out_ref[side, r] = piece[1]
-
-
-def gather_kernel(even_ref, *refs):
-    out_hbm, rows_ref, out_ref, sems = refs[-4:]
-    pieces = sorted_pieces(refs[:-4])
-    chips, share = even_ref.shape[1], even_ref.shape[3]
+    at = 0
+    for ref in refs[:-1]:
+        for piece in halves(ref):
+            refs[-1][at] = piece[1]
+            at += 1
+
+
+def halves(ref):
+    return [ref] if len(ref.shape) == 4 else [ref.at[side] for side in range(ref.shape[0])]
+
+
+def settle(chips, sides, refs, rows_ref):
+    even_ref, pieces = refs[0], [piece for ref in refs[1:] for piece in halves(ref)]
+    share = even_ref.shape[2]
     mine = lax.axis_index("gy")
     chip, core = mine >> 1, mine & 1
     line = 2 * chips * BLK_Y
-    for r in range(chips):
+    for at, ((side, r), own) in enumerate(zip(sides, pieces)):
         for flip in (0, 1):
             other = core ^ flip
             tile = 2 * source(chip, r, chips) + other
-            for side in (0, 1):
-                for k in range(SIDE):
-                    piece = even_ref[side, r, k] if flip else pieces[side][r][0, k]
-                    start = (k >> 1) * line + tile * BLK_Y + first_of(side, other) + (k & 1)
-                    rows_ref[pl.ds(start, share, stride=BLK_X * line), :] = piece.astype(F32)
+            for k in range(SIDE):
+                piece = even_ref[at, k] if flip else own[0, k]
+                start = (k >> 1) * line + tile * BLK_Y + first_of(side, other) + (k & 1)
+                rows_ref[pl.ds(start, share, stride=BLK_X * line), :] = piece.astype(F32)
+
+
+def early_kernel(chips, *refs):
+    settle(chips, [(0, 0), (1, 0)] + [(0, r) for r in range(2, chips)], refs[:-1], refs[-1])
+
+
+def late_kernel(chips, *refs):
+    late_refs, out_hbm, rows_ref, out_ref, sems = refs[1:-4], *refs[-4:]
+    settle(chips, [(0, 1), (1, 1)] + [(1, r) for r in range(2, chips)], late_refs, rows_ref)
     pieces = sems.shape[0]
     step = rows_ref.shape[0] // pieces
     copies = []
@@ -382,10 +388,10 @@
 
 
 def pack(pieces):
-    chips = len(pieces) // 2 + 1
+    count = sum(1 if piece.ndim == 4 else piece.shape[0] for piece in pieces)
     return pl.pallas_call(
         pack_kernel,
-        out_shape=jax.ShapeDtypeStruct((2, chips, *pieces[1].shape[1:]), BF16),
+        out_shape=jax.ShapeDtypeStruct((count, *pieces[-1].shape[-3:]), BF16),
         in_specs=[VMEM] * len(pieces),
         out_specs=VMEM,
         compiler_params=LIMIT,
@@ -393,22 +399,31 @@
     )(*pieces)
 
 
-def gather(even, pieces):
-    _, chips, _, share, _ = even.shape
+def gather(chips, early_even, early, late_even, late):
+    share = early[0].shape[2]
     rows = share * BLOCKS * 2 * chips
-    out = pl.pallas_call(
-        gather_kernel,
-        out_shape=jax.ShapeDtypeStruct((rows, CELLS), BF16),
-        in_specs=[VMEM] * (1 + len(pieces)),
-        out_specs=pl.BlockSpec(memory_space=pl.ANY),
+    placed = pl.pallas_call(
+        functools.partial(early_kernel, chips),
+        out_shape=jax.ShapeDtypeStruct((rows, CELLS), F32),
+        in_specs=[VMEM] * (1 + len(early)),
+        out_specs=VMEM,
+        compiler_params=LIMIT,
+        cost_estimate=LONG,
+        name="early",
+    )(early_even, *early)
+    out, _ = pl.pallas_call(
+        functools.partial(late_kernel, chips),
+        out_shape=(jax.ShapeDtypeStruct((rows, CELLS), BF16), jax.ShapeDtypeStruct((rows, CELLS), F32)),
+        in_specs=[VMEM] * (2 + len(late)),
+        out_specs=(pl.BlockSpec(memory_space=pl.ANY), VMEM),
         scratch_shapes=[
-            pltpu.VMEM((rows, CELLS), F32),
             pltpu.VMEM((rows, CELLS), BF16),
             pltpu.SemaphoreType.DMA((4,)),
         ],
+        input_output_aliases={0: 1},
         compiler_params=LIMIT,
-        name="gather",
-    )(even, *pieces)
+        name="late",
+    )(placed, late_even, *late)
     return out.reshape(share, BLK_X, 2 * chips * BLK_Y, CELLS)
 
 
@@ -450,18 +465,18 @@
     even = swap(column, "gy", 0)
     odd = swap(column, "gy", 1)
     part, *near = update_near(by_block, turned, taper, column, even, parts)
-    rounds = range(parts // 2 - 1, 1, -1)
-    near_hops = [hop(near[r], r) for r in rounds]
-    far_own, both, *far = update_far(turned, taper, odd, part, near)
-    far_hops = []
-    for k, r in enumerate(rounds):
-        far_hops.append(hop(far[r - 2], r))
-        if k + 1 < len(rounds):
-            far[r - 3], near_hops[k] = lax.optimization_barrier((far[r - 3], near_hops[k]))
-        else:
-            both, near_hops[k] = lax.optimization_barrier((both, near_hops[k]))
-    pieces = [hop(both, 1), near[0], *near_hops[::-1], far_own, *far_hops[::-1]]
-    return gather(swap(pack(pieces), "gy", 0), pieces)
+    chips = parts // 2
+    near_hops = {r: hop(near[r], r) for r in range(2, chips)}
+    own_far, both, *far = update_far(turned, taper, odd, part, near)
+    far = {r: far[r - 2] for r in range(2, chips)}
+    for r in range(2, chips):
+        far[r], near_hops[r] = lax.optimization_barrier((far[r], near_hops[r]))
+    far_hops = {r: hop(far[r], r) for r in range(2, chips)}
+    early = [near[0], own_far, *(near_hops[r] for r in range(2, chips))]
+    late = [hop(both, 1), *(far_hops[r] for r in range(2, chips))]
+    late_even = swap(pack(late), "gy", 0)
+    early_even = swap(pack(early), "gy", 0)
+    return gather(chips, early_even, early, late_even, late)
 
 
 def solution(mesh):

time: 32.4 us -> 33.7 us (1.040)
  waiting for transfers between devices: 8.93 us -> 13 us
  starting transfers between devices: 15.1 us -> 12.4 us
    ppermute x5, waiting for transfers between devices: 4.26 us -> 8.64 us  [hop(): return lax.ppermute(piece, 'gy', pairs)]
    ppermute x5, starting transfers between devices: 9.66 us -> 6.91 us  [hop(): return lax.ppermute(piece, 'gy', pairs)]
    ppermute x5 -> x6, waiting for transfers between devices: 4.68 us -> 4.37 us  [swap(): return lax.ppermute(block, axis, pairs + [(b, a) for a, b in pairs])]
    ppermute x5 -> x6, starting transfers between devices: 5.42 us -> 5.45 us  [swap(): return lax.ppermute(block, axis, pairs + [(b, a) for a, b in pairs])]
    pallas_call x2 -> x4, Pallas kernels: 1.16 us -> 1.16 us  [the longest x1 0.94 us: gather(): pl.pallas_call(functools.partial(late_kernel, chips), out_shape=(jax.Shap...]
  transfers between devices with their start and end apart: 10 -> 11, of which waited for: 6 -> 7; matrix products, arithmetic and copies ran while one was open for 0% -> 0% of each run, Pallas kernels for 12% -> 12%
where the time goes in v12:
time: 33.7 us; the launch traced here: 33.3 us
  waiting for transfers between devices  13 us (39%)
  starting transfers between devices  12.4 us (37%)
  Pallas kernels  7.76 us (23%)
    ppermute x5, waiting for transfers between devices, hop(): return lax.ppermute(piece, 'gy', pairs)  8.64 us
    ppermute x5, starting transfers between devices, hop(): return lax.ppermute(piece, 'gy', pairs)  6.91 us
    ppermute x6, starting transfers between devices, swap(): return lax.ppermute(block, axis, pairs + [(b, a) for a, b in pairs])  5.45 us
    ppermute x6, waiting for transfers between devices, swap(): return lax.ppermute(block, axis, pairs + [(b, a) for a, b in pairs])  4.37 us
    pallas_call x1, Pallas kernels, weigh(): pl.pallas_call(weigh_kernel, out_shape=(jax.ShapeDtypeStruct((2, members,...  2.82 us
    pallas_call x1, Pallas kernels, update_near(): pl.pallas_call(near_kernel, out_shape=(jax.ShapeDtypeStruct((SIDE, member...  1.9 us
    pallas_call x1, Pallas kernels, prepare(): pl.pallas_call(prepare_kernel, out_shape=(jax.ShapeDtypeStruct((BLOCKS, C...  0.97 us
    pallas_call x1, Pallas kernels, gather(): pl.pallas_call(functools.partial(late_kernel, chips), out_shape=(jax.Shap...  0.94 us
  transfers between devices with their start and end apart: 11, of which 7 were waited for; matrix products, arithmetic and copies ran while one was open for 0% of the time, Pallas kernels for 12%

profile of v12, /device:TPU:0, one launch (start us, length us, event | category | flops | bytes accessed | tf_op | source)
XLA Modules:
  0.0 33.3 jit_solution(13117437673352579646)
XLA Ops:
  0.0 2.8 %weigh.1 = (bf16[2,128,128]{2,1,0:T(8,128)(2,1)S(1)}, bf16[128,2,4,128]{3,2,1,0:T(4,128)(2,1)S(1)}) custom-call(f32[1,1,128,128]{3,2,1,0:T(8,128)} %pred_hbm.1, f32[1,1,128]{2,1,0:T(1,128)} %mv_hbm.1, f32[1,1,128]{2,1,0:T(1,128)} %var_hbm.1, f32[1,1,128,128]{3,2,1,0:T(8,128)} %jit_hbm.1, s32[4,8,128]{2,1,0:T(8,128)} %obs_hbm.3, ...), custom_call_target="tpu_custom_call" | custom-call | tf_op jit(solution)/shard_map/weigh/pallas_call | solution.py:157
  2.8 3.0 %collective-permute-start = (bf16[2,128,128]{2,1,0:T(8,128)(2,1)S(1)}, bf16[2,128,128]{2,1,0:T(8,128)(2,1)S(1)}, u32[]{:S(2)}, u32[]{:S(2)}) collective-permute-start(bf16[2,128,128]{2,1,0:T(8,128)(2,1)S(1)} %get-tuple-element.27), channel_id=1, source_target_pairs={{0,8},{16,24},{8,0},{24,16},{1,9},{17,25},{9,1},{25,17},{2,10},{18... | collective-permute-start | bytes 196616 | tf_op jit(solution)/shard_map/ppermute | solution.py:435
  5.8 1.6 %collective-permute-start.1 = (bf16[2,128,128]{2,1,0:T(8,128)(2,1)S(1)}, bf16[2,128,128]{2,1,0:T(8,128)(2,1)S(1)}, u32[]{:S(2)}, u32[]{:S(2)}) collective-permute-start(bf16[2,128,128]{2,1,0:T(8,128)(2,1)S(1)} %get-tuple-element.27), channel_id=1, source_target_pairs={{8,16},{24,0},{16,8},{0,24},{9,17},{25,1},{17,9},{1,25},{10,18},{2... | collective-permute-start | bytes 196616 | tf_op jit(solution)/shard_map/ppermute | solution.py:435
  7.5 1.0 %prepare.1 = (bf16[8,128,128]{2,1,0:T(8,128)(2,1)S(1)}, f32[3,3,8,128]{3,2,1,0:T(8,128)S(1)}) custom-call(bf16[8,128,128]{2,1,0:T(8,128)(2,1)S(1)} %bitcast.4, s32[2,4]{1,0:T(2,128)} %radius_hbm.1, s32[2,4,25]{2,1,0:T(4,128)} %pattern_hbm.1, s32[4,8,128]{2,1,0:T(8,128)} %obs_hbm.3), custom_call_target="tpu_custom_call" | custom-call | flops 4000000 | bytes 1000000 | tf_op jit(solution)/shard_map/prepare/pallas_call | solution.py:230
  8.4 0.0 collective-permute-done
  8.5 2.6 %collective-permute-done.1 = bf16[2,128,128]{2,1,0:T(8,128)(2,1)S(1)} collective-permute-done((bf16[2,128,128]{2,1,0:T(8,128)(2,1)S(1)}, bf16[2,128,128]{2,1,0:T(8,128)(2,1)S(1)}, u32[]{:S(2)}, u32[]{:S(2)}) %collective-permute-start.1) | collective-permute-done | bytes 65568 | tf_op jit(solution)/shard_map/ppermute | solution.py:435
  11.1 0.1 collective-permute-start.2
  11.2 0.7 %collective-permute-start.3 = (bf16[2,128,384]{2,1,0:T(8,128)(2,1)S(1)}, bf16[2,128,384]{2,1,0:T(8,128)(2,1)S(1)}, u32[]{:S(2)}, u32[]{:S(2)}) collective-permute-start(bf16[2,128,384]{2,1,0:T(8,128)(2,1)S(1)} %pad_maximum_fusion.own_ref), channel_id=1, source_target_pairs={{1,2},{3,4},{5,6},{2,1},{4,3},{6,5},{9,10},{11,12},{13,14},{10,9},... | collective-permute-start | bytes 589832 | tf_op jit(solution)/shard_map/ppermute | solution.py:435
  11.9 0.7 %collective-permute-done.2.even_ref = bf16[2,128,384]{2,1,0:T(8,128)(2,1)S(1)} collective-permute-done((bf16[2,128,384]{2,1,0:T(8,128)(2,1)S(1)}, bf16[2,128,384]{2,1,0:T(8,128)(2,1)S(1)}, u32[]{:S(2)}, u32[]{:S(2)}) %collective-permute-start.2) | collective-permute-done | bytes 196640 | tf_op jit(solution)/shard_map/ppermute | solution.py:435
  12.6 1.9 %near.1 = (f32[4,128,128]{2,1,0:T(8,128)S(1)}, bf16[2,4,16,128]{3,2,1,0:T(8,128)(2,1)S(1)}, bf16[2,4,16,128]{3,2,1,0:T(8,128)(2,1)S(1)}, bf16[2,4,16,128]{3,2,1,0:T(8,128)(2,1)S(1)}, bf16[2,4,16,128]{3,2,1,0:T(8,128)(2,1)S(1)}) custom-call(bf16[8,128,128]{2,1,0:T(8,128)(2,1)S(1)} %bitcast.5, bf16[8,128,128]{2,1,0:T(8,128)(2,1)S(1)} %get-tuple-element.30.turned_ref, ...), custom_call_target="tpu_custom_call" | custom-call | flops 4000000000 | bytes 10000000 | tf_op jit(solution)/shard_map/near/pallas_call | solution.py:361
  14.5 4.6 %collective-permute-start.5 = (bf16[2,4,16,128]{3,2,1,0:T(8,128)(2,1)S(1)}, bf16[2,4,16,128]{3,2,1,0:T(8,128)(2,1)S(1)}, u32[]{:S(2)}, u32[]{:S(2)}) collective-permute-start(bf16[2,4,16,128]{3,2,1,0:T(8,128)(2,1)S(1)} %get-tuple-element.41), channel_id=1, source_target_pairs={{0,6},{1,7},{2,4},{3,5},{4,2},{5,3},{6,0},{7,1},{8,14},{9,15},{10,... | collective-permute-start | bytes 98312 | tf_op jit(solution)/shard_map/ppermute | solution.py:441
  19.2 0.0 collective-permute-start.4
  19.2 0.0 collective-permute-done.3.odd_ref
  19.2 0.9 %far.1 = (bf16[2,4,16,128]{3,2,1,0:T(8,128)(2,1)S(1)}, bf16[2,2,4,16,128]{4,3,2,1,0:T(8,128)(2,1)S(1)}, bf16[2,4,16,128]{3,2,1,0:T(8,128)(2,1)S(1)}, bf16[2,4,16,128]{3,2,1,0:T(8,128)(2,1)S(1)}) custom-call(bf16[8,128,128]{2,1,0:T(8,128)(2,1)S(1)} %get-tuple-element.30.turned_ref, f32[3,3,8,128]{3,2,1,0:T(8,128)S(1)} %get-tuple-element.31.taper_ref, ...), custom_call_target="tpu_custom_call" | custom-call | flops 4000000000 | bytes 10000000 | tf_op jit(solution)/shard_map/far/pallas_call | solution.py:378
  20.1 0.7 %collective-permute-start.7 = (bf16[2,2,4,16,128]{4,3,2,1,0:T(8,128)(2,1)S(1)}, bf16[2,2,4,16,128]{4,3,2,1,0:T(8,128)(2,1)S(1)}, u32[]{:S(2)}, u32[]{:S(2)}) collective-permute-start(bf16[2,2,4,16,128]{4,3,2,1,0:T(8,128)(2,1)S(1)} %get-tuple-element.43), channel_id=1, source_target_pairs={{0,2},{1,3},{2,0},{3,1},{4,6},{5,7},{6,4},{7,5},{8,10},{9,11},{10,... | collective-permute-start | bytes 196616 | tf_op jit(solution)/shard_map/ppermute | solution.py:441
  20.8 0.5 %collective-permute-done.5.refs_3_.refs_4_ = bf16[2,4,16,128]{3,2,1,0:T(8,128)(2,1)S(1)} collective-permute-done((bf16[2,4,16,128]{3,2,1,0:T(8,128)(2,1)S(1)}, bf16[2,4,16,128]{3,2,1,0:T(8,128)(2,1)S(1)}, u32[]{:S(2)}, u32[]{:S(2)}) %collective-permute-start.5) | collective-permute-done | bytes 32800 | tf_op jit(solution)/shard_map/ppermute | solution.py:441
  21.2 2.8 %collective-permute-done.4.refs_2_.refs_3_ = bf16[2,4,16,128]{3,2,1,0:T(8,128)(2,1)S(1)} collective-permute-done((bf16[2,4,16,128]{3,2,1,0:T(8,128)(2,1)S(1)}, bf16[2,4,16,128]{3,2,1,0:T(8,128)(2,1)S(1)}, u32[]{:S(2)}, u32[]{:S(2)}) %collective-permute-start.4) | collective-permute-done | bytes 32800 | tf_op jit(solution)/shard_map/ppermute | solution.py:441
  24.0 0.0 collective-permute-start.6
  24.0 1.6 %collective-permute-start.9 = (bf16[2,4,16,128]{3,2,1,0:T(8,128)(2,1)S(1)}, bf16[2,4,16,128]{3,2,1,0:T(8,128)(2,1)S(1)}, u32[]{:S(2)}, u32[]{:S(2)}) collective-permute-start(bf16[2,4,16,128]{3,2,1,0:T(8,128)(2,1)S(1)} %get-tuple-element.45), channel_id=1, source_target_pairs={{0,6},{1,7},{2,4},{3,5},{4,2},{5,3},{6,0},{7,1},{8,14},{9,15},{10,... | collective-permute-start | bytes 98312 | tf_op jit(solution)/shard_map/ppermute | solution.py:441
  25.6 0.0 collective-permute-start.8
  25.6 4.4 %collective-permute-done.9.refs_2_.refs_4_ = bf16[2,4,16,128]{3,2,1,0:T(8,128)(2,1)S(1)} collective-permute-done((bf16[2,4,16,128]{3,2,1,0:T(8,128)(2,1)S(1)}, bf16[2,4,16,128]{3,2,1,0:T(8,128)(2,1)S(1)}, u32[]{:S(2)}, u32[]{:S(2)}) %collective-permute-start.9) | collective-permute-done | bytes 32800 | tf_op jit(solution)/shard_map/ppermute | solution.py:441
  30.0 1.0 %collective-permute-done.8.refs_1_.refs_3_ = bf16[2,4,16,128]{3,2,1,0:T(8,128)(2,1)S(1)} collective-permute-done((bf16[2,4,16,128]{3,2,1,0:T(8,128)(2,1)S(1)}, bf16[2,4,16,128]{3,2,1,0:T(8,128)(2,1)S(1)}, u32[]{:S(2)}, u32[]{:S(2)}) %collective-permute-start.8) | collective-permute-done | bytes 32800 | tf_op jit(solution)/shard_map/ppermute | solution.py:441
  31.0 0.0 collective-permute-done.7.refs_0_.refs_2_
  31.0 0.1 collective-permute-start.10
  31.1 0.0 collective-permute-done.6.refs_0_
  31.1 0.2 early.1.refs_0_
  31.3 1.0 %collective-permute-done.10.refs_1_ = bf16[4,4,16,128]{3,2,1,0:T(8,128)(2,1)S(1)} collective-permute-done((bf16[4,4,16,128]{3,2,1,0:T(8,128)(2,1)S(1)}, bf16[4,4,16,128]{3,2,1,0:T(8,128)(2,1)S(1)}, u32[]{:S(2)}, u32[]{:S(2)}) %collective-permute-start.10) | collective-permute-done | bytes 65568 | tf_op jit(solution)/shard_map/ppermute | solution.py:435
  32.3 0.9 %late.1 = (bf16[1024,128]{1,0:T(8,128)(2,1)}, f32[1024,128]{1,0:T(8,128)S(1)}) custom-call(f32[1024,128]{1,0:T(8,128)S(1)} %early.1.refs_0_, bf16[4,4,16,128]{3,2,1,0:T(8,128)(2,1)S(1)} %collective-permute-done.10.refs_1_, bf16[2,2,4,16,128]{4,3,2,1,0:T(8,128)(2,1)S(1)} %collective-permute-done.7.refs_0_.refs_2_, ...), custom_call_target="tpu_custom_call", output_to_operand_aliasing={{1}: (0, {})} | custom-call | tf_op jit(solution)/shard_map/late/pallas_call | solution.py:414
  (4 shorter events, 0.1 us)
Async XLA Ops:
  2.8 5.6 %collective-permute-start = (bf16[2,128,128]{2,1,0:T(8,128)(2,1)S(1)}, bf16[2,128,128]{2,1,0:T(8,128)(2,1)S(1)}, u32[]{:S(2)}, u32[]{:S(2)}) collective-permute-start(bf16[2,128,128]{2,1,0:T(8,128)(2,1)S(1)} %get-tuple-element.27), channel_id=1, source_target_pairs={{0,8},{16,24},{8,0},{24,16},{1,9},{17,25},{9,1},{25,17},{2,10},{18... | collective-permute-start | bytes 196616 | tf_op jit(solution)/shard_map/ppermute | solution.py:435
  5.8 5.2 %collective-permute-start.1 = (bf16[2,128,128]{2,1,0:T(8,128)(2,1)S(1)}, bf16[2,128,128]{2,1,0:T(8,128)(2,1)S(1)}, u32[]{:S(2)}, u32[]{:S(2)}) collective-permute-start(bf16[2,128,128]{2,1,0:T(8,128)(2,1)S(1)} %get-tuple-element.27), channel_id=1, source_target_pairs={{8,16},{24,0},{16,8},{0,24},{9,17},{25,1},{17,9},{1,25},{10,18},{2... | collective-permute-start | bytes 196616 | tf_op jit(solution)/shard_map/ppermute | solution.py:435
  11.1 1.5 %collective-permute-start.2 = (bf16[2,128,384]{2,1,0:T(8,128)(2,1)S(1)}, bf16[2,128,384]{2,1,0:T(8,128)(2,1)S(1)}, u32[]{:S(2)}, u32[]{:S(2)}) collective-permute-start(bf16[2,128,384]{2,1,0:T(8,128)(2,1)S(1)} %pad_maximum_fusion.own_ref), channel_id=1, source_target_pairs={{0,1},{2,3},{4,5},{6,7},{1,0},{3,2},{5,4},{7,6},{8,9},{10,11},{12,... | collective-permute-start | bytes 589832 | tf_op jit(solution)/shard_map/ppermute | solution.py:435
  11.2 8.0 %collective-permute-start.3 = (bf16[2,128,384]{2,1,0:T(8,128)(2,1)S(1)}, bf16[2,128,384]{2,1,0:T(8,128)(2,1)S(1)}, u32[]{:S(2)}, u32[]{:S(2)}) collective-permute-start(bf16[2,128,384]{2,1,0:T(8,128)(2,1)S(1)} %pad_maximum_fusion.own_ref), channel_id=1, source_target_pairs={{1,2},{3,4},{5,6},{2,1},{4,3},{6,5},{9,10},{11,12},{13,14},{10,9},... | collective-permute-start | bytes 589832 | tf_op jit(solution)/shard_map/ppermute | solution.py:435
  14.5 6.7 %collective-permute-start.5 = (bf16[2,4,16,128]{3,2,1,0:T(8,128)(2,1)S(1)}, bf16[2,4,16,128]{3,2,1,0:T(8,128)(2,1)S(1)}, u32[]{:S(2)}, u32[]{:S(2)}) collective-permute-start(bf16[2,4,16,128]{3,2,1,0:T(8,128)(2,1)S(1)} %get-tuple-element.41), channel_id=1, source_target_pairs={{0,6},{1,7},{2,4},{3,5},{4,2},{5,3},{6,0},{7,1},{8,14},{9,15},{10,... | collective-permute-start | bytes 98312 | tf_op jit(solution)/shard_map/ppermute | solution.py:441
  19.2 4.8 %collective-permute-start.4 = (bf16[2,4,16,128]{3,2,1,0:T(8,128)(2,1)S(1)}, bf16[2,4,16,128]{3,2,1,0:T(8,128)(2,1)S(1)}, u32[]{:S(2)}, u32[]{:S(2)}) collective-permute-start(bf16[2,4,16,128]{3,2,1,0:T(8,128)(2,1)S(1)} %get-tuple-element.38), channel_id=1, source_target_pairs={{0,4},{1,5},{2,6},{3,7},{4,0},{5,1},{6,2},{7,3},{8,12},{9,13},{10,... | collective-permute-start | bytes 98312 | tf_op jit(solution)/shard_map/ppermute | solution.py:441
  20.1 10.9 %collective-permute-start.7 = (bf16[2,2,4,16,128]{4,3,2,1,0:T(8,128)(2,1)S(1)}, bf16[2,2,4,16,128]{4,3,2,1,0:T(8,128)(2,1)S(1)}, u32[]{:S(2)}, u32[]{:S(2)}) collective-permute-start(bf16[2,2,4,16,128]{4,3,2,1,0:T(8,128)(2,1)S(1)} %get-tuple-element.43), channel_id=1, source_target_pairs={{0,2},{1,3},{2,0},{3,1},{4,6},{5,7},{6,4},{7,5},{8,10},{9,11},{10,... | collective-permute-start | bytes 196616 | tf_op jit(solution)/shard_map/ppermute | solution.py:441
  24.0 7.1 %collective-permute-start.6 = (bf16[4,4,16,128]{3,2,1,0:T(8,128)(2,1)S(1)}, bf16[4,4,16,128]{3,2,1,0:T(8,128)(2,1)S(1)}, u32[]{:S(2)}, u32[]{:S(2)}) collective-permute-start(bf16[4,4,16,128]{3,2,1,0:T(8,128)(2,1)S(1)} %pack.2), channel_id=1, source_target_pairs={{0,1},{2,3},{4,5},{6,7},{1,0},{3,2},{5,4},{7,6},{8,9},{10,11},{12,... | collective-permute-start | bytes 196616 | tf_op jit(solution)/shard_map/ppermute | solution.py:435
  24.0 6.0 %collective-permute-start.9 = (bf16[2,4,16,128]{3,2,1,0:T(8,128)(2,1)S(1)}, bf16[2,4,16,128]{3,2,1,0:T(8,128)(2,1)S(1)}, u32[]{:S(2)}, u32[]{:S(2)}) collective-permute-start(bf16[2,4,16,128]{3,2,1,0:T(8,128)(2,1)S(1)} %get-tuple-element.45), channel_id=1, source_target_pairs={{0,6},{1,7},{2,4},{3,5},{4,2},{5,3},{6,0},{7,1},{8,14},{9,15},{10,... | collective-permute-start | bytes 98312 | tf_op jit(solution)/shard_map/ppermute | solution.py:441
  25.6 5.4 %collective-permute-start.8 = (bf16[2,4,16,128]{3,2,1,0:T(8,128)(2,1)S(1)}, bf16[2,4,16,128]{3,2,1,0:T(8,128)(2,1)S(1)}, u32[]{:S(2)}, u32[]{:S(2)}) collective-permute-start(bf16[2,4,16,128]{3,2,1,0:T(8,128)(2,1)S(1)} %get-tuple-element.44), channel_id=1, source_target_pairs={{0,4},{1,5},{2,6},{3,7},{4,0},{5,1},{6,2},{7,3},{8,12},{9,13},{10,... | collective-permute-start | bytes 98312 | tf_op jit(solution)/shard_map/ppermute | solution.py:441
  31.0 1.3 %collective-permute-start.10 = (bf16[4,4,16,128]{3,2,1,0:T(8,128)(2,1)S(1)}, bf16[4,4,16,128]{3,2,1,0:T(8,128)(2,1)S(1)}, u32[]{:S(2)}, u32[]{:S(2)}) collective-permute-start(bf16[4,4,16,128]{3,2,1,0:T(8,128)(2,1)S(1)} %pack.3), channel_id=1, source_target_pairs={{0,1},{2,3},{4,5},{6,7},{1,0},{3,2},{5,4},{7,6},{8,9},{10,11},{12,... | collective-permute-start | bytes 196616 | tf_op jit(solution)/shard_map/ppermute | solution.py:435

commit v13 on v12

--- a/solution.py
+++ b/solution.py
@@ -294,8 +294,8 @@
 
 
 def far_kernel(turned_ref, taper_ref, odd_ref, part_ref, near_ref, *refs):
-    both_ref, rows_ref = refs[1], refs[-1]
-    piece_refs = (refs[0], both_ref.at[1], *refs[2:-1])
+    both_ref, rows_ref = refs[-2], refs[-1]
+    piece_refs = (*refs[:-2], both_ref.at[1])
     both_ref[0] = near_ref[...]
     tile_y = lax.axis_index("gy")
     for k in range(SIDE):
@@ -332,12 +332,13 @@
 
 
 def early_kernel(chips, *refs):
-    settle(chips, [(0, 0), (1, 0)] + [(0, r) for r in range(2, chips)], refs[:-1], refs[-1])
+    settle(chips, [(0, 0), (1, 0)] + [(0, r) for r in range(1, chips - 1)], refs[:-1], refs[-1])
 
 
 def late_kernel(chips, *refs):
     late_refs, out_hbm, rows_ref, out_ref, sems = refs[1:-4], *refs[-4:]
-    settle(chips, [(0, 1), (1, 1)] + [(1, r) for r in range(2, chips)], late_refs, rows_ref)
+    last = chips - 1
+    settle(chips, [(0, last), (1, last)] + [(1, r) for r in range(1, last)], late_refs, rows_ref)
     pieces = sems.shape[0]
     step = rows_ref.shape[0] // pieces
     copies = []
@@ -374,7 +375,7 @@
     members = part.shape[1]
     parts = members // near[0].shape[2]
     piece = jax.ShapeDtypeStruct(near[0].shape, BF16)
-    shapes = (piece, jax.ShapeDtypeStruct((2, *piece.shape), BF16)) + (piece,) * (parts // 2 - 2)
+    shapes = (piece,) * (parts // 2 - 1) + (jax.ShapeDtypeStruct((2, *piece.shape), BF16),)
     return pl.pallas_call(
         far_kernel,
         out_shape=shapes,
@@ -384,7 +385,7 @@
         compiler_params=LIMIT,
         cost_estimate=LONG,
         name="far",
-    )(turned, taper, odd, part, near[1])
+    )(turned, taper, odd, part, near[-1])
 
 
 def pack(pieces):
@@ -408,7 +409,6 @@
         in_specs=[VMEM] * (1 + len(early)),
         out_specs=VMEM,
         compiler_params=LIMIT,
-        cost_estimate=LONG,
         name="early",
     )(early_even, *early)
     out, _ = pl.pallas_call(
@@ -465,18 +465,17 @@
     even = swap(column, "gy", 0)
     odd = swap(column, "gy", 1)
     part, *near = update_near(by_block, turned, taper, column, even, parts)
-    chips = parts // 2
-    near_hops = {r: hop(near[r], r) for r in range(2, chips)}
-    own_far, both, *far = update_far(turned, taper, odd, part, near)
-    far = {r: far[r - 2] for r in range(2, chips)}
-    for r in range(2, chips):
+    last = parts // 2 - 1
+    near_hops = {r: hop(near[r], r) for r in range(1, last)}
+    *far, both = update_far(turned, taper, odd, part, near)
+    for r in range(1, last):
         far[r], near_hops[r] = lax.optimization_barrier((far[r], near_hops[r]))
-    far_hops = {r: hop(far[r], r) for r in range(2, chips)}
-    early = [near[0], own_far, *(near_hops[r] for r in range(2, chips))]
-    late = [hop(both, 1), *(far_hops[r] for r in range(2, chips))]
+    far_hops = {r: hop(far[r], r) for r in range(1, last)}
+    early = [near[0], far[0], *(near_hops[r] for r in range(1, last))]
+    late = [hop(both, last), *(far_hops[r] for r in range(1, last))]
     late_even = swap(pack(late), "gy", 0)
     early_even = swap(pack(early), "gy", 0)
-    return gather(chips, early_even, early, late_even, late)
+    return gather(parts // 2, early_even, early, late_even, late)
 
 
 def solution(mesh):

time: 33.7 us -> 30.6 us (0.908)
  waiting for transfers between devices: 13 us -> 6.86 us
  starting transfers between devices: 12.4 us -> 15.5 us
    ppermute x5, waiting for transfers between devices: 8.64 us -> 2.47 us  [hop(): return lax.ppermute(piece, 'gy', pairs)]
    ppermute x5, starting transfers between devices: 6.91 us -> 10.1 us  [hop(): return lax.ppermute(piece, 'gy', pairs)]
  transfers between devices with their start and end apart: 11 -> 11, of which waited for: 7 -> 4; matrix products, arithmetic and copies ran while one was open for 0% -> 0% of each run, Pallas kernels for 12% -> 13%
where the time goes in v13:
time: 30.6 us; the launch traced here: 30.3 us
  starting transfers between devices  15.5 us (51%)
  Pallas kernels  7.76 us (25%)
  waiting for transfers between devices  6.86 us (22%)
    ppermute x5, starting transfers between devices, hop(): return lax.ppermute(piece, 'gy', pairs)  10.1 us
    ppermute x6, starting transfers between devices, swap(): return lax.ppermute(block, axis, pairs + [(b, a) for a, b in pairs])  5.41 us
    ppermute x6, waiting for transfers between devices, swap(): return lax.ppermute(block, axis, pairs + [(b, a) for a, b in pairs])  4.39 us
    pallas_call x1, Pallas kernels, weigh(): pl.pallas_call(weigh_kernel, out_shape=(jax.ShapeDtypeStruct((2, members,...  2.82 us
    ppermute x5, waiting for transfers between devices, hop(): return lax.ppermute(piece, 'gy', pairs)  2.47 us
    pallas_call x1, Pallas kernels, update_near(): pl.pallas_call(near_kernel, out_shape=(jax.ShapeDtypeStruct((SIDE, member...  1.9 us
    pallas_call x1, Pallas kernels, prepare(): pl.pallas_call(prepare_kernel, out_shape=(jax.ShapeDtypeStruct((BLOCKS, C...  0.97 us
    pallas_call x1, Pallas kernels, gather(): pl.pallas_call(functools.partial(late_kernel, chips), out_shape=(jax.Shap...  0.94 us
  transfers between devices with their start and end apart: 11, of which 4 were waited for; matrix products, arithmetic and copies ran while one was open for 0% of the time, Pallas kernels for 13%

profile of v13, /device:TPU:0, one launch (start us, length us, event | category | flops | bytes accessed | tf_op | source)
XLA Modules:
  0.0 30.3 jit_solution(159361620842958553)
XLA Ops:
  0.0 2.8 %weigh.1 = (bf16[2,128,128]{2,1,0:T(8,128)(2,1)S(1)}, bf16[128,2,4,128]{3,2,1,0:T(4,128)(2,1)S(1)}) custom-call(f32[1,1,128,128]{3,2,1,0:T(8,128)} %pred_hbm.1, f32[1,1,128]{2,1,0:T(1,128)} %mv_hbm.1, f32[1,1,128]{2,1,0:T(1,128)} %var_hbm.1, f32[1,1,128,128]{3,2,1,0:T(8,128)} %jit_hbm.1, s32[4,8,128]{2,1,0:T(8,128)} %obs_hbm.3, ...), custom_call_target="tpu_custom_call" | custom-call | tf_op jit(solution)/shard_map/weigh/pallas_call | solution.py:157
  2.8 3.0 %collective-permute-start = (bf16[2,128,128]{2,1,0:T(8,128)(2,1)S(1)}, bf16[2,128,128]{2,1,0:T(8,128)(2,1)S(1)}, u32[]{:S(2)}, u32[]{:S(2)}) collective-permute-start(bf16[2,128,128]{2,1,0:T(8,128)(2,1)S(1)} %get-tuple-element.27), channel_id=1, source_target_pairs={{0,8},{16,24},{8,0},{24,16},{1,9},{17,25},{9,1},{25,17},{2,10},{18... | collective-permute-start | bytes 196616 | tf_op jit(solution)/shard_map/ppermute | solution.py:435
  5.8 1.6 %collective-permute-start.1 = (bf16[2,128,128]{2,1,0:T(8,128)(2,1)S(1)}, bf16[2,128,128]{2,1,0:T(8,128)(2,1)S(1)}, u32[]{:S(2)}, u32[]{:S(2)}) collective-permute-start(bf16[2,128,128]{2,1,0:T(8,128)(2,1)S(1)} %get-tuple-element.27), channel_id=1, source_target_pairs={{8,16},{24,0},{16,8},{0,24},{9,17},{25,1},{17,9},{1,25},{10,18},{2... | collective-permute-start | bytes 196616 | tf_op jit(solution)/shard_map/ppermute | solution.py:435
  7.5 1.0 %prepare.1 = (bf16[8,128,128]{2,1,0:T(8,128)(2,1)S(1)}, f32[3,3,8,128]{3,2,1,0:T(8,128)S(1)}) custom-call(bf16[8,128,128]{2,1,0:T(8,128)(2,1)S(1)} %bitcast.4, s32[2,4]{1,0:T(2,128)} %radius_hbm.1, s32[2,4,25]{2,1,0:T(4,128)} %pattern_hbm.1, s32[4,8,128]{2,1,0:T(8,128)} %obs_hbm.3), custom_call_target="tpu_custom_call" | custom-call | flops 4000000 | bytes 1000000 | tf_op jit(solution)/shard_map/prepare/pallas_call | solution.py:230
  8.4 0.0 collective-permute-done
  8.5 2.6 %collective-permute-done.1 = bf16[2,128,128]{2,1,0:T(8,128)(2,1)S(1)} collective-permute-done((bf16[2,128,128]{2,1,0:T(8,128)(2,1)S(1)}, bf16[2,128,128]{2,1,0:T(8,128)(2,1)S(1)}, u32[]{:S(2)}, u32[]{:S(2)}) %collective-permute-start.1) | collective-permute-done | bytes 65568 | tf_op jit(solution)/shard_map/ppermute | solution.py:435
  11.1 0.1 collective-permute-start.2
  11.2 0.7 %collective-permute-start.3 = (bf16[2,128,384]{2,1,0:T(8,128)(2,1)S(1)}, bf16[2,128,384]{2,1,0:T(8,128)(2,1)S(1)}, u32[]{:S(2)}, u32[]{:S(2)}) collective-permute-start(bf16[2,128,384]{2,1,0:T(8,128)(2,1)S(1)} %pad_maximum_fusion.own_ref), channel_id=1, source_target_pairs={{1,2},{3,4},{5,6},{2,1},{4,3},{6,5},{9,10},{11,12},{13,14},{10,9},... | collective-permute-start | bytes 589832 | tf_op jit(solution)/shard_map/ppermute | solution.py:435
  11.9 0.7 %collective-permute-done.2.even_ref = bf16[2,128,384]{2,1,0:T(8,128)(2,1)S(1)} collective-permute-done((bf16[2,128,384]{2,1,0:T(8,128)(2,1)S(1)}, bf16[2,128,384]{2,1,0:T(8,128)(2,1)S(1)}, u32[]{:S(2)}, u32[]{:S(2)}) %collective-permute-start.2) | collective-permute-done | bytes 196640 | tf_op jit(solution)/shard_map/ppermute | solution.py:435
  12.6 1.9 %near.1 = (f32[4,128,128]{2,1,0:T(8,128)S(1)}, bf16[2,4,16,128]{3,2,1,0:T(8,128)(2,1)S(1)}, bf16[2,4,16,128]{3,2,1,0:T(8,128)(2,1)S(1)}, bf16[2,4,16,128]{3,2,1,0:T(8,128)(2,1)S(1)}, bf16[2,4,16,128]{3,2,1,0:T(8,128)(2,1)S(1)}) custom-call(bf16[8,128,128]{2,1,0:T(8,128)(2,1)S(1)} %bitcast.5, bf16[8,128,128]{2,1,0:T(8,128)(2,1)S(1)} %get-tuple-element.30.turned_ref, ...), custom_call_target="tpu_custom_call" | custom-call | flops 4000000000 | bytes 10000000 | tf_op jit(solution)/shard_map/near/pallas_call | solution.py:362
  14.5 3.6 %collective-permute-start.5 = (bf16[2,4,16,128]{3,2,1,0:T(8,128)(2,1)S(1)}, bf16[2,4,16,128]{3,2,1,0:T(8,128)(2,1)S(1)}, u32[]{:S(2)}, u32[]{:S(2)}) collective-permute-start(bf16[2,4,16,128]{3,2,1,0:T(8,128)(2,1)S(1)} %get-tuple-element.41), channel_id=1, source_target_pairs={{0,4},{1,5},{2,6},{3,7},{4,0},{5,1},{6,2},{7,3},{8,12},{9,13},{10,... | collective-permute-start | bytes 98312 | tf_op jit(solution)/shard_map/ppermute | solution.py:441
  18.1 2.0 %collective-permute-start.4 = (bf16[2,4,16,128]{3,2,1,0:T(8,128)(2,1)S(1)}, bf16[2,4,16,128]{3,2,1,0:T(8,128)(2,1)S(1)}, u32[]{:S(2)}, u32[]{:S(2)}) collective-permute-start(bf16[2,4,16,128]{3,2,1,0:T(8,128)(2,1)S(1)} %get-tuple-element.38), channel_id=1, source_target_pairs={{0,2},{1,3},{2,0},{3,1},{4,6},{5,7},{6,4},{7,5},{8,10},{9,11},{10,... | collective-permute-start | bytes 98312 | tf_op jit(solution)/shard_map/ppermute | solution.py:441
  20.1 0.0 collective-permute-done.3.odd_ref
  20.1 0.9 %far.1 = (bf16[2,4,16,128]{3,2,1,0:T(8,128)(2,1)S(1)}, bf16[2,4,16,128]{3,2,1,0:T(8,128)(2,1)S(1)}, bf16[2,4,16,128]{3,2,1,0:T(8,128)(2,1)S(1)}, bf16[2,2,4,16,128]{4,3,2,1,0:T(8,128)(2,1)S(1)}) custom-call(bf16[8,128,128]{2,1,0:T(8,128)(2,1)S(1)} %get-tuple-element.30.turned_ref, f32[3,3,8,128]{3,2,1,0:T(8,128)S(1)} %get-tuple-element.31.taper_ref, ...), custom_call_target="tpu_custom_call" | custom-call | flops 4000000000 | bytes 10000000 | tf_op jit(solution)/shard_map/far/pallas_call | solution.py:379
  21.1 1.6 %collective-permute-start.7 = (bf16[2,2,4,16,128]{4,3,2,1,0:T(8,128)(2,1)S(1)}, bf16[2,2,4,16,128]{4,3,2,1,0:T(8,128)(2,1)S(1)}, u32[]{:S(2)}, u32[]{:S(2)}) collective-permute-start(bf16[2,2,4,16,128]{4,3,2,1,0:T(8,128)(2,1)S(1)} %get-tuple-element.43), channel_id=1, source_target_pairs={{0,6},{1,7},{2,4},{3,5},{4,2},{5,3},{6,0},{7,1},{8,14},{9,15},{10,... | collective-permute-start | bytes 196616 | tf_op jit(solution)/shard_map/ppermute | solution.py:441
  22.7 0.0 collective-permute-done.5.refs_3_.refs_4_
  22.7 0.4 %collective-permute-start.9 = (bf16[2,4,16,128]{3,2,1,0:T(8,128)(2,1)S(1)}, bf16[2,4,16,128]{3,2,1,0:T(8,128)(2,1)S(1)}, u32[]{:S(2)}, u32[]{:S(2)}) collective-permute-start(bf16[2,4,16,128]{3,2,1,0:T(8,128)(2,1)S(1)} %get-tuple-element.45), channel_id=1, source_target_pairs={{0,4},{1,5},{2,6},{3,7},{4,0},{5,1},{6,2},{7,3},{8,12},{9,13},{10,... | collective-permute-start | bytes 98312 | tf_op jit(solution)/shard_map/ppermute | solution.py:441
  23.1 0.0 collective-permute-done.4.refs_2_.refs_3_
  23.1 2.4 %collective-permute-start.8 = (bf16[2,4,16,128]{3,2,1,0:T(8,128)(2,1)S(1)}, bf16[2,4,16,128]{3,2,1,0:T(8,128)(2,1)S(1)}, u32[]{:S(2)}, u32[]{:S(2)}) collective-permute-start(bf16[2,4,16,128]{3,2,1,0:T(8,128)(2,1)S(1)} %get-tuple-element.44), channel_id=1, source_target_pairs={{0,2},{1,3},{2,0},{3,1},{4,6},{5,7},{6,4},{7,5},{8,10},{9,11},{10,... | collective-permute-start | bytes 98312 | tf_op jit(solution)/shard_map/ppermute | solution.py:441
  25.5 0.0 collective-permute-start.6
  25.5 2.5 %collective-permute-done.9.refs_2_.refs_4_ = bf16[2,4,16,128]{3,2,1,0:T(8,128)(2,1)S(1)} collective-permute-done((bf16[2,4,16,128]{3,2,1,0:T(8,128)(2,1)S(1)}, bf16[2,4,16,128]{3,2,1,0:T(8,128)(2,1)S(1)}, u32[]{:S(2)}, u32[]{:S(2)}) %collective-permute-start.9) | collective-permute-done | bytes 32800 | tf_op jit(solution)/shard_map/ppermute | solution.py:441
  28.0 0.0 collective-permute-done.8.refs_1_.refs_3_
  28.0 0.0 collective-permute-done.7.refs_0_.refs_2_
  28.0 0.1 collective-permute-start.10
  28.1 0.0 collective-permute-done.6.refs_0_
  28.1 0.2 early.1.refs_0_
  28.3 1.0 %collective-permute-done.10.refs_1_ = bf16[4,4,16,128]{3,2,1,0:T(8,128)(2,1)S(1)} collective-permute-done((bf16[4,4,16,128]{3,2,1,0:T(8,128)(2,1)S(1)}, bf16[4,4,16,128]{3,2,1,0:T(8,128)(2,1)S(1)}, u32[]{:S(2)}, u32[]{:S(2)}) %collective-permute-start.10) | collective-permute-done | bytes 65568 | tf_op jit(solution)/shard_map/ppermute | solution.py:435
  29.3 0.9 %late.1 = (bf16[1024,128]{1,0:T(8,128)(2,1)}, f32[1024,128]{1,0:T(8,128)S(1)}) custom-call(f32[1024,128]{1,0:T(8,128)S(1)} %early.1.refs_0_, bf16[4,4,16,128]{3,2,1,0:T(8,128)(2,1)S(1)} %collective-permute-done.10.refs_1_, bf16[2,2,4,16,128]{4,3,2,1,0:T(8,128)(2,1)S(1)} %collective-permute-done.7.refs_0_.refs_2_, ...), custom_call_target="tpu_custom_call", output_to_operand_aliasing={{1}: (0, {})} | custom-call | tf_op jit(solution)/shard_map/late/pallas_call | solution.py:414
  (4 shorter events, 0.1 us)
Async XLA Ops:
  2.8 5.6 %collective-permute-start = (bf16[2,128,128]{2,1,0:T(8,128)(2,1)S(1)}, bf16[2,128,128]{2,1,0:T(8,128)(2,1)S(1)}, u32[]{:S(2)}, u32[]{:S(2)}) collective-permute-start(bf16[2,128,128]{2,1,0:T(8,128)(2,1)S(1)} %get-tuple-element.27), channel_id=1, source_target_pairs={{0,8},{16,24},{8,0},{24,16},{1,9},{17,25},{9,1},{25,17},{2,10},{18... | collective-permute-start | bytes 196616 | tf_op jit(solution)/shard_map/ppermute | solution.py:435
  5.8 5.2 %collective-permute-start.1 = (bf16[2,128,128]{2,1,0:T(8,128)(2,1)S(1)}, bf16[2,128,128]{2,1,0:T(8,128)(2,1)S(1)}, u32[]{:S(2)}, u32[]{:S(2)}) collective-permute-start(bf16[2,128,128]{2,1,0:T(8,128)(2,1)S(1)} %get-tuple-element.27), channel_id=1, source_target_pairs={{8,16},{24,0},{16,8},{0,24},{9,17},{25,1},{17,9},{1,25},{10,18},{2... | collective-permute-start | bytes 196616 | tf_op jit(solution)/shard_map/ppermute | solution.py:435
  11.1 1.5 %collective-permute-start.2 = (bf16[2,128,384]{2,1,0:T(8,128)(2,1)S(1)}, bf16[2,128,384]{2,1,0:T(8,128)(2,1)S(1)}, u32[]{:S(2)}, u32[]{:S(2)}) collective-permute-start(bf16[2,128,384]{2,1,0:T(8,128)(2,1)S(1)} %pad_maximum_fusion.own_ref), channel_id=1, source_target_pairs={{0,1},{2,3},{4,5},{6,7},{1,0},{3,2},{5,4},{7,6},{8,9},{10,11},{12,... | collective-permute-start | bytes 589832 | tf_op jit(solution)/shard_map/ppermute | solution.py:435
  11.2 9.0 %collective-permute-start.3 = (bf16[2,128,384]{2,1,0:T(8,128)(2,1)S(1)}, bf16[2,128,384]{2,1,0:T(8,128)(2,1)S(1)}, u32[]{:S(2)}, u32[]{:S(2)}) collective-permute-start(bf16[2,128,384]{2,1,0:T(8,128)(2,1)S(1)} %pad_maximum_fusion.own_ref), channel_id=1, source_target_pairs={{1,2},{3,4},{5,6},{2,1},{4,3},{6,5},{9,10},{11,12},{13,14},{10,9},... | collective-permute-start | bytes 589832 | tf_op jit(solution)/shard_map/ppermute | solution.py:435
  14.5 8.2 %collective-permute-start.5 = (bf16[2,4,16,128]{3,2,1,0:T(8,128)(2,1)S(1)}, bf16[2,4,16,128]{3,2,1,0:T(8,128)(2,1)S(1)}, u32[]{:S(2)}, u32[]{:S(2)}) collective-permute-start(bf16[2,4,16,128]{3,2,1,0:T(8,128)(2,1)S(1)} %get-tuple-element.41), channel_id=1, source_target_pairs={{0,4},{1,5},{2,6},{3,7},{4,0},{5,1},{6,2},{7,3},{8,12},{9,13},{10,... | collective-permute-start | bytes 98312 | tf_op jit(solution)/shard_map/ppermute | solution.py:441
  18.1 5.0 %collective-permute-start.4 = (bf16[2,4,16,128]{3,2,1,0:T(8,128)(2,1)S(1)}, bf16[2,4,16,128]{3,2,1,0:T(8,128)(2,1)S(1)}, u32[]{:S(2)}, u32[]{:S(2)}) collective-permute-start(bf16[2,4,16,128]{3,2,1,0:T(8,128)(2,1)S(1)} %get-tuple-element.38), channel_id=1, source_target_pairs={{0,2},{1,3},{2,0},{3,1},{4,6},{5,7},{6,4},{7,5},{8,10},{9,11},{10,... | collective-permute-start | bytes 98312 | tf_op jit(solution)/shard_map/ppermute | solution.py:441
  21.1 6.9 %collective-permute-start.7 = (bf16[2,2,4,16,128]{4,3,2,1,0:T(8,128)(2,1)S(1)}, bf16[2,2,4,16,128]{4,3,2,1,0:T(8,128)(2,1)S(1)}, u32[]{:S(2)}, u32[]{:S(2)}) collective-permute-start(bf16[2,2,4,16,128]{4,3,2,1,0:T(8,128)(2,1)S(1)} %get-tuple-element.43), channel_id=1, source_target_pairs={{0,6},{1,7},{2,4},{3,5},{4,2},{5,3},{6,0},{7,1},{8,14},{9,15},{10,... | collective-permute-start | bytes 196616 | tf_op jit(solution)/shard_map/ppermute | solution.py:441
  22.7 5.3 %collective-permute-start.9 = (bf16[2,4,16,128]{3,2,1,0:T(8,128)(2,1)S(1)}, bf16[2,4,16,128]{3,2,1,0:T(8,128)(2,1)S(1)}, u32[]{:S(2)}, u32[]{:S(2)}) collective-permute-start(bf16[2,4,16,128]{3,2,1,0:T(8,128)(2,1)S(1)} %get-tuple-element.45), channel_id=1, source_target_pairs={{0,4},{1,5},{2,6},{3,7},{4,0},{5,1},{6,2},{7,3},{8,12},{9,13},{10,... | collective-permute-start | bytes 98312 | tf_op jit(solution)/shard_map/ppermute | solution.py:441
  23.1 4.9 %collective-permute-start.8 = (bf16[2,4,16,128]{3,2,1,0:T(8,128)(2,1)S(1)}, bf16[2,4,16,128]{3,2,1,0:T(8,128)(2,1)S(1)}, u32[]{:S(2)}, u32[]{:S(2)}) collective-permute-start(bf16[2,4,16,128]{3,2,1,0:T(8,128)(2,1)S(1)} %get-tuple-element.44), channel_id=1, source_target_pairs={{0,2},{1,3},{2,0},{3,1},{4,6},{5,7},{6,4},{7,5},{8,10},{9,11},{10,... | collective-permute-start | bytes 98312 | tf_op jit(solution)/shard_map/ppermute | solution.py:441
  25.5 2.6 %collective-permute-start.6 = (bf16[4,4,16,128]{3,2,1,0:T(8,128)(2,1)S(1)}, bf16[4,4,16,128]{3,2,1,0:T(8,128)(2,1)S(1)}, u32[]{:S(2)}, u32[]{:S(2)}) collective-permute-start(bf16[4,4,16,128]{3,2,1,0:T(8,128)(2,1)S(1)} %pack.2), channel_id=1, source_target_pairs={{0,1},{2,3},{4,5},{6,7},{1,0},{3,2},{5,4},{7,6},{8,9},{10,11},{12,... | collective-permute-start | bytes 196616 | tf_op jit(solution)/shard_map/ppermute | solution.py:435
  28.0 1.3 %collective-permute-start.10 = (bf16[4,4,16,128]{3,2,1,0:T(8,128)(2,1)S(1)}, bf16[4,4,16,128]{3,2,1,0:T(8,128)(2,1)S(1)}, u32[]{:S(2)}, u32[]{:S(2)}) collective-permute-start(bf16[4,4,16,128]{3,2,1,0:T(8,128)(2,1)S(1)} %pack.3), channel_id=1, source_target_pairs={{0,1},{2,3},{4,5},{6,7},{1,0},{3,2},{5,4},{7,6},{8,9},{10,11},{12,... | collective-permute-start | bytes 196616 | tf_op jit(solution)/shard_map/ppermute | solution.py:435

commit v14 on v13

--- a/solution.py
+++ b/solution.py
@@ -281,16 +281,20 @@
             ref[flip, k] = rows_ref[k, pl.ds(pl.multiple_of(owner * share, share), share), :]
 
 
-def near_kernel(params_ref, turned_ref, taper_ref, own_ref, even_ref, part_ref, *refs):
+def begin_kernel(params_ref, turned_ref, taper_ref, own_ref, part_ref):
+    tile_y = lax.axis_index("gy")
+    for k in range(SIDE):
+        b = block_of(k, 1, tile_y)
+        part_ref[k] = params_ref[b].astype(F32) + moved(b, 0, turned_ref, taper_ref, own_ref)
+
+
+def near_kernel(params_ref, turned_ref, taper_ref, own_ref, even_ref, *refs):
     piece_refs, rows_ref = refs[:-1], refs[-1]
     tile_y = lax.axis_index("gy")
     for k in range(SIDE):
         b = block_of(k, 0, tile_y)
         delta = moved(b, 0, turned_ref, taper_ref, own_ref) + moved(b, 1, turned_ref, taper_ref, even_ref)
         put(piece_refs, rows_ref, k, (params_ref[b].astype(F32) + delta).astype(BF16))
-    for k in range(SIDE):
-        b = block_of(k, 1, tile_y)
-        part_ref[k] = params_ref[b].astype(F32) + moved(b, 0, turned_ref, taper_ref, own_ref)
 
 
 def far_kernel(turned_ref, taper_ref, odd_ref, part_ref, near_ref, *refs):
@@ -356,14 +360,26 @@
 LIMIT = pltpu.CompilerParams(vmem_limit_bytes=24 * 2**20)
 
 
+def update_begin(by_block, turned, taper, own):
+    return pl.pallas_call(
+        begin_kernel,
+        out_shape=jax.ShapeDtypeStruct((SIDE, by_block.shape[1], CELLS), F32),
+        in_specs=[VMEM] * 4,
+        out_specs=VMEM,
+        compiler_params=LIMIT,
+        cost_estimate=LONG,
+        name="begin",
+    )(by_block, turned, taper, own)
+
+
 def update_near(by_block, turned, taper, own, even, parts):
     members = by_block.shape[1]
     pieces = [jax.ShapeDtypeStruct((2, SIDE, members // parts, CELLS), BF16)] * (parts // 2)
     return pl.pallas_call(
         near_kernel,
-        out_shape=(jax.ShapeDtypeStruct((SIDE, members, CELLS), F32), *pieces),
+        out_shape=tuple(pieces),
         in_specs=[VMEM] * 5,
-        out_specs=(VMEM,) * (1 + len(pieces)),
+        out_specs=(VMEM,) * len(pieces),
         scratch_shapes=[pltpu.VMEM((SIDE, members, CELLS), BF16)],
         compiler_params=LIMIT,
         cost_estimate=LONG,
@@ -462,9 +478,10 @@
     turned, taper = prepare(by_block, taper_radius, taper_pattern, obs_block)
     column = jnp.concatenate([own, even, odd], axis=2)
     column, turned, taper = lax.optimization_barrier((column, turned, taper))
+    odd = swap(column, "gy", 1)
     even = swap(column, "gy", 0)
-    odd = swap(column, "gy", 1)
-    part, *near = update_near(by_block, turned, taper, column, even, parts)
+    part = update_begin(by_block, turned, taper, column)
+    near = update_near(by_block, turned, taper, column, even, parts)
     last = parts // 2 - 1
     near_hops = {r: hop(near[r], r) for r in range(1, last)}
     *far, both = update_far(turned, taper, odd, part, near)

time: 30.6 us -> 31.2 us (1.020)
  waiting for transfers between devices: 6.86 us -> 7.84 us
  starting transfers between devices: 15.5 us -> 15 us
    ppermute x5, starting transfers between devices: 10.1 us -> 6.59 us  [hop(): return lax.ppermute(piece, 'gy', pairs)]
    ppermute x6, starting transfers between devices: 5.41 us -> 8.42 us  [swap(): return lax.ppermute(block, axis, pairs + [(b, a) for a, b in pairs])]
    ppermute x5, waiting for transfers between devices: 2.47 us -> 4.02 us  [hop(): return lax.ppermute(piece, 'gy', pairs)]
    ppermute x6, waiting for transfers between devices: 4.39 us -> 3.82 us  [swap(): return lax.ppermute(block, axis, pairs + [(b, a) for a, b in pairs])]
    pallas_call x1 -> x2, Pallas kernels: 1.9 us -> 2.05 us  [the longest x1 1.16 us: update_near(): pl.pallas_call(near_kernel, out_shape=tuple(pieces), in_specs=[VMEM] * 5,...]
  transfers between devices with their start and end apart: 11 -> 11, of which waited for: 4 -> 7; matrix products, arithmetic and copies ran while one was open for 0% -> 0% of each run, Pallas kernels for 13% -> 13%
where the time goes in v14:
time: 31.2 us; the launch traced here: 30.9 us
  starting transfers between devices  15 us (48%)
  Pallas kernels  7.9 us (25%)
  waiting for transfers between devices  7.84 us (25%)
    ppermute x6, starting transfers between devices, swap(): return lax.ppermute(block, axis, pairs + [(b, a) for a, b in pairs])  8.42 us
    ppermute x5, starting transfers between devices, hop(): return lax.ppermute(piece, 'gy', pairs)  6.59 us
    ppermute x5, waiting for transfers between devices, hop(): return lax.ppermute(piece, 'gy', pairs)  4.02 us
    ppermute x6, waiting for transfers between devices, swap(): return lax.ppermute(block, axis, pairs + [(b, a) for a, b in pairs])  3.82 us
    pallas_call x1, Pallas kernels, weigh(): pl.pallas_call(weigh_kernel, out_shape=(jax.ShapeDtypeStruct((2, members,...  2.82 us
    pallas_call x1, Pallas kernels, update_near(): pl.pallas_call(near_kernel, out_shape=tuple(pieces), in_specs=[VMEM] * 5,...  1.16 us
    pallas_call x1, Pallas kernels, prepare(): pl.pallas_call(prepare_kernel, out_shape=(jax.ShapeDtypeStruct((BLOCKS, C...  0.97 us
    pallas_call x1, Pallas kernels, gather(): pl.pallas_call(functools.partial(late_kernel, chips), out_shape=(jax.Shap...  0.94 us
  transfers between devices with their start and end apart: 11, of which 7 were waited for; matrix products, arithmetic and copies ran while one was open for 0% of the time, Pallas kernels for 13%

profile of v14, /device:TPU:0, one launch (start us, length us, event | category | flops | bytes accessed | tf_op | source)
XLA Modules:
  0.0 30.9 jit_solution(3295037308858689957)
XLA Ops:
  0.0 2.8 %weigh.1 = (bf16[2,128,128]{2,1,0:T(8,128)(2,1)S(1)}, bf16[128,2,4,128]{3,2,1,0:T(4,128)(2,1)S(1)}) custom-call(f32[1,1,128,128]{3,2,1,0:T(8,128)} %pred_hbm.1, f32[1,1,128]{2,1,0:T(1,128)} %mv_hbm.1, f32[1,1,128]{2,1,0:T(1,128)} %var_hbm.1, f32[1,1,128,128]{3,2,1,0:T(8,128)} %jit_hbm.1, s32[4,8,128]{2,1,0:T(8,128)} %obs_hbm.3, ...), custom_call_target="tpu_custom_call" | custom-call | tf_op jit(solution)/shard_map/weigh/pallas_call | solution.py:157
  2.8 3.9 %collective-permute-start.1 = (bf16[2,128,128]{2,1,0:T(8,128)(2,1)S(1)}, bf16[2,128,128]{2,1,0:T(8,128)(2,1)S(1)}, u32[]{:S(2)}, u32[]{:S(2)}) collective-permute-start(bf16[2,128,128]{2,1,0:T(8,128)(2,1)S(1)} %get-tuple-element.26), channel_id=1, source_target_pairs={{8,16},{24,0},{16,8},{0,24},{9,17},{25,1},{17,9},{1,25},{10,18},{2... | collective-permute-start | bytes 196616 | tf_op jit(solution)/shard_map/ppermute | solution.py:451
  6.7 0.7 %collective-permute-start = (bf16[2,128,128]{2,1,0:T(8,128)(2,1)S(1)}, bf16[2,128,128]{2,1,0:T(8,128)(2,1)S(1)}, u32[]{:S(2)}, u32[]{:S(2)}) collective-permute-start(bf16[2,128,128]{2,1,0:T(8,128)(2,1)S(1)} %get-tuple-element.26), channel_id=1, source_target_pairs={{0,8},{16,24},{8,0},{24,16},{1,9},{17,25},{9,1},{25,17},{2,10},{18... | collective-permute-start | bytes 196616 | tf_op jit(solution)/shard_map/ppermute | solution.py:451
  7.5 1.0 %prepare.1 = (bf16[8,128,128]{2,1,0:T(8,128)(2,1)S(1)}, f32[3,3,8,128]{3,2,1,0:T(8,128)S(1)}) custom-call(bf16[8,128,128]{2,1,0:T(8,128)(2,1)S(1)} %bitcast.4, s32[2,4]{1,0:T(2,128)} %radius_hbm.1, s32[2,4,25]{2,1,0:T(4,128)} %pattern_hbm.1, s32[4,8,128]{2,1,0:T(8,128)} %obs_hbm.3), custom_call_target="tpu_custom_call" | custom-call | flops 4000000 | bytes 1000000 | tf_op jit(solution)/shard_map/prepare/pallas_call | solution.py:230
  8.4 0.5 %collective-permute-done.1 = bf16[2,128,128]{2,1,0:T(8,128)(2,1)S(1)} collective-permute-done((bf16[2,128,128]{2,1,0:T(8,128)(2,1)S(1)}, bf16[2,128,128]{2,1,0:T(8,128)(2,1)S(1)}, u32[]{:S(2)}, u32[]{:S(2)}) %collective-permute-start.1) | collective-permute-done | bytes 65568 | tf_op jit(solution)/shard_map/ppermute | solution.py:451
  9.0 2.1 %collective-permute-done = bf16[2,128,128]{2,1,0:T(8,128)(2,1)S(1)} collective-permute-done((bf16[2,128,128]{2,1,0:T(8,128)(2,1)S(1)}, bf16[2,128,128]{2,1,0:T(8,128)(2,1)S(1)}, u32[]{:S(2)}, u32[]{:S(2)}) %collective-permute-start) | collective-permute-done | bytes 65568 | tf_op jit(solution)/shard_map/ppermute | solution.py:451
  11.1 0.7 %collective-permute-start.3 = (bf16[2,128,384]{2,1,0:T(8,128)(2,1)S(1)}, bf16[2,128,384]{2,1,0:T(8,128)(2,1)S(1)}, u32[]{:S(2)}, u32[]{:S(2)}) collective-permute-start(bf16[2,128,384]{2,1,0:T(8,128)(2,1)S(1)} %pad_maximum_fusion.own_ref), channel_id=1, source_target_pairs={{1,2},{3,4},{5,6},{2,1},{4,3},{6,5},{9,10},{11,12},{13,14},{10,9},... | collective-permute-start | bytes 589832 | tf_op jit(solution)/shard_map/ppermute | solution.py:451
  11.8 3.1 %collective-permute-start.2 = (bf16[2,128,384]{2,1,0:T(8,128)(2,1)S(1)}, bf16[2,128,384]{2,1,0:T(8,128)(2,1)S(1)}, u32[]{:S(2)}, u32[]{:S(2)}) collective-permute-start(bf16[2,128,384]{2,1,0:T(8,128)(2,1)S(1)} %pad_maximum_fusion.own_ref), channel_id=1, source_target_pairs={{0,1},{2,3},{4,5},{6,7},{1,0},{3,2},{5,4},{7,6},{8,9},{10,11},{12,... | collective-permute-start | bytes 589832 | tf_op jit(solution)/shard_map/ppermute | solution.py:451
  14.9 0.9 %begin.1.part_ref = f32[4,128,128]{2,1,0:T(8,128)S(1)} custom-call(bf16[8,128,128]{2,1,0:T(8,128)(2,1)S(1)} %bitcast.5, bf16[8,128,128]{2,1,0:T(8,128)(2,1)S(1)} %get-tuple-element.29.turned_ref, f32[3,3,8,128]{3,2,1,0:T(8,128)S(1)} %get-tuple-element.30.taper_ref, bf16[2,128,384]{2,1,0:T(8,128)(2,1)S(1)} %pad_maximum_fusion.own_ref), custom_call_target="tpu_custom_call" | custom-call | flops 4000000000 | bytes 10000000 | tf_op jit(solution)/shard_map/begin/pallas_call | solution.py:364
  15.8 0.2 collective-permute-done.2.even_ref
  15.9 1.2 %near.1 = (bf16[2,4,16,128]{3,2,1,0:T(8,128)(2,1)S(1)}, bf16[2,4,16,128]{3,2,1,0:T(8,128)(2,1)S(1)}, bf16[2,4,16,128]{3,2,1,0:T(8,128)(2,1)S(1)}, bf16[2,4,16,128]{3,2,1,0:T(8,128)(2,1)S(1)}) custom-call(bf16[8,128,128]{2,1,0:T(8,128)(2,1)S(1)} %bitcast.6, bf16[8,128,128]{2,1,0:T(8,128)(2,1)S(1)} %get-tuple-element.29.turned_ref, ...), custom_call_target="tpu_custom_call" | custom-call | flops 4000000000 | bytes 10000000 | tf_op jit(solution)/shard_map/near/pallas_call | solution.py:378
  17.1 1.6 %collective-permute-start.4 = (bf16[2,4,16,128]{3,2,1,0:T(8,128)(2,1)S(1)}, bf16[2,4,16,128]{3,2,1,0:T(8,128)(2,1)S(1)}, u32[]{:S(2)}, u32[]{:S(2)}) collective-permute-start(bf16[2,4,16,128]{3,2,1,0:T(8,128)(2,1)S(1)} %get-tuple-element.36), channel_id=1, source_target_pairs={{0,2},{1,3},{2,0},{3,1},{4,6},{5,7},{6,4},{7,5},{8,10},{9,11},{10,... | collective-permute-start | bytes 98312 | tf_op jit(solution)/shard_map/ppermute | solution.py:457
  18.7 1.3 %collective-permute-start.5 = (bf16[2,4,16,128]{3,2,1,0:T(8,128)(2,1)S(1)}, bf16[2,4,16,128]{3,2,1,0:T(8,128)(2,1)S(1)}, u32[]{:S(2)}, u32[]{:S(2)}) collective-permute-start(bf16[2,4,16,128]{3,2,1,0:T(8,128)(2,1)S(1)} %get-tuple-element.39), channel_id=1, source_target_pairs={{0,4},{1,5},{2,6},{3,7},{4,0},{5,1},{6,2},{7,3},{8,12},{9,13},{10,... | collective-permute-start | bytes 98312 | tf_op jit(solution)/shard_map/ppermute | solution.py:457
  19.9 0.0 collective-permute-done.3.odd_ref
  19.9 0.9 %far.1 = (bf16[2,4,16,128]{3,2,1,0:T(8,128)(2,1)S(1)}, bf16[2,4,16,128]{3,2,1,0:T(8,128)(2,1)S(1)}, bf16[2,4,16,128]{3,2,1,0:T(8,128)(2,1)S(1)}, bf16[2,2,4,16,128]{4,3,2,1,0:T(8,128)(2,1)S(1)}) custom-call(bf16[8,128,128]{2,1,0:T(8,128)(2,1)S(1)} %get-tuple-element.29.turned_ref, f32[3,3,8,128]{3,2,1,0:T(8,128)S(1)} %get-tuple-element.30.taper_ref, ...), custom_call_target="tpu_custom_call" | custom-call | flops 4000000000 | bytes 10000000 | tf_op jit(solution)/shard_map/far/pallas_call | solution.py:395
  20.8 1.8 %collective-permute-start.7 = (bf16[2,2,4,16,128]{4,3,2,1,0:T(8,128)(2,1)S(1)}, bf16[2,2,4,16,128]{4,3,2,1,0:T(8,128)(2,1)S(1)}, u32[]{:S(2)}, u32[]{:S(2)}) collective-permute-start(bf16[2,2,4,16,128]{4,3,2,1,0:T(8,128)(2,1)S(1)} %get-tuple-element.41), channel_id=1, source_target_pairs={{0,6},{1,7},{2,4},{3,5},{4,2},{5,3},{6,0},{7,1},{8,14},{9,15},{10,... | collective-permute-start | bytes 196616 | tf_op jit(solution)/shard_map/ppermute | solution.py:457
  22.7 0.0 collective-permute-done.4.refs_2_.refs_3_
  22.7 0.5 %collective-permute-start.8 = (bf16[2,4,16,128]{3,2,1,0:T(8,128)(2,1)S(1)}, bf16[2,4,16,128]{3,2,1,0:T(8,128)(2,1)S(1)}, u32[]{:S(2)}, u32[]{:S(2)}) collective-permute-start(bf16[2,4,16,128]{3,2,1,0:T(8,128)(2,1)S(1)} %get-tuple-element.42), channel_id=1, source_target_pairs={{0,2},{1,3},{2,0},{3,1},{4,6},{5,7},{6,4},{7,5},{8,10},{9,11},{10,... | collective-permute-start | bytes 98312 | tf_op jit(solution)/shard_map/ppermute | solution.py:457
  23.1 0.7 %collective-permute-done.5.refs_3_.refs_4_ = bf16[2,4,16,128]{3,2,1,0:T(8,128)(2,1)S(1)} collective-permute-done((bf16[2,4,16,128]{3,2,1,0:T(8,128)(2,1)S(1)}, bf16[2,4,16,128]{3,2,1,0:T(8,128)(2,1)S(1)}, u32[]{:S(2)}, u32[]{:S(2)}) %collective-permute-start.5) | collective-permute-done | bytes 32800 | tf_op jit(solution)/shard_map/ppermute | solution.py:457
  23.8 1.5 %collective-permute-start.9 = (bf16[2,4,16,128]{3,2,1,0:T(8,128)(2,1)S(1)}, bf16[2,4,16,128]{3,2,1,0:T(8,128)(2,1)S(1)}, u32[]{:S(2)}, u32[]{:S(2)}) collective-permute-start(bf16[2,4,16,128]{3,2,1,0:T(8,128)(2,1)S(1)} %get-tuple-element.43), channel_id=1, source_target_pairs={{0,4},{1,5},{2,6},{3,7},{4,0},{5,1},{6,2},{7,3},{8,12},{9,13},{10,... | collective-permute-start | bytes 98312 | tf_op jit(solution)/shard_map/ppermute | solution.py:457
  25.3 0.0 collective-permute-start.6
  25.3 2.0 %collective-permute-done.8.refs_1_.refs_3_ = bf16[2,4,16,128]{3,2,1,0:T(8,128)(2,1)S(1)} collective-permute-done((bf16[2,4,16,128]{3,2,1,0:T(8,128)(2,1)S(1)}, bf16[2,4,16,128]{3,2,1,0:T(8,128)(2,1)S(1)}, u32[]{:S(2)}, u32[]{:S(2)}) %collective-permute-start.8) | collective-permute-done | bytes 32800 | tf_op jit(solution)/shard_map/ppermute | solution.py:457
  27.3 1.4 %collective-permute-done.9.refs_2_.refs_4_ = bf16[2,4,16,128]{3,2,1,0:T(8,128)(2,1)S(1)} collective-permute-done((bf16[2,4,16,128]{3,2,1,0:T(8,128)(2,1)S(1)}, bf16[2,4,16,128]{3,2,1,0:T(8,128)(2,1)S(1)}, u32[]{:S(2)}, u32[]{:S(2)}) %collective-permute-start.9) | collective-permute-done | bytes 32800 | tf_op jit(solution)/shard_map/ppermute | solution.py:457
  28.6 0.0 collective-permute-done.7.refs_0_.refs_2_
  28.7 0.1 collective-permute-start.10
  28.7 0.0 collective-permute-done.6.refs_0_
  28.7 0.2 early.1.refs_0_
  29.0 1.0 %collective-permute-done.10.refs_1_ = bf16[4,4,16,128]{3,2,1,0:T(8,128)(2,1)S(1)} collective-permute-done((bf16[4,4,16,128]{3,2,1,0:T(8,128)(2,1)S(1)}, bf16[4,4,16,128]{3,2,1,0:T(8,128)(2,1)S(1)}, u32[]{:S(2)}, u32[]{:S(2)}) %collective-permute-start.10) | collective-permute-done | bytes 65568 | tf_op jit(solution)/shard_map/ppermute | solution.py:451
  30.0 0.9 %late.1 = (bf16[1024,128]{1,0:T(8,128)(2,1)}, f32[1024,128]{1,0:T(8,128)S(1)}) custom-call(f32[1024,128]{1,0:T(8,128)S(1)} %early.1.refs_0_, bf16[4,4,16,128]{3,2,1,0:T(8,128)(2,1)S(1)} %collective-permute-done.10.refs_1_, bf16[2,2,4,16,128]{4,3,2,1,0:T(8,128)(2,1)S(1)} %collective-permute-done.7.refs_0_.refs_2_, ...), custom_call_target="tpu_custom_call", output_to_operand_aliasing={{1}: (0, {})} | custom-call | tf_op jit(solution)/shard_map/late/pallas_call | solution.py:430
  (4 shorter events, 0.1 us)
Async XLA Ops:
  2.8 6.2 %collective-permute-start.1 = (bf16[2,128,128]{2,1,0:T(8,128)(2,1)S(1)}, bf16[2,128,128]{2,1,0:T(8,128)(2,1)S(1)}, u32[]{:S(2)}, u32[]{:S(2)}) collective-permute-start(bf16[2,128,128]{2,1,0:T(8,128)(2,1)S(1)} %get-tuple-element.26), channel_id=1, source_target_pairs={{8,16},{24,0},{16,8},{0,24},{9,17},{25,1},{17,9},{1,25},{10,18},{2... | collective-permute-start | bytes 196616 | tf_op jit(solution)/shard_map/ppermute | solution.py:451
  6.7 4.4 %collective-permute-start = (bf16[2,128,128]{2,1,0:T(8,128)(2,1)S(1)}, bf16[2,128,128]{2,1,0:T(8,128)(2,1)S(1)}, u32[]{:S(2)}, u32[]{:S(2)}) collective-permute-start(bf16[2,128,128]{2,1,0:T(8,128)(2,1)S(1)} %get-tuple-element.26), channel_id=1, source_target_pairs={{0,8},{16,24},{8,0},{24,16},{1,9},{17,25},{9,1},{25,17},{2,10},{18... | collective-permute-start | bytes 196616 | tf_op jit(solution)/shard_map/ppermute | solution.py:451
  11.1 8.8 %collective-permute-start.3 = (bf16[2,128,384]{2,1,0:T(8,128)(2,1)S(1)}, bf16[2,128,384]{2,1,0:T(8,128)(2,1)S(1)}, u32[]{:S(2)}, u32[]{:S(2)}) collective-permute-start(bf16[2,128,384]{2,1,0:T(8,128)(2,1)S(1)} %pad_maximum_fusion.own_ref), channel_id=1, source_target_pairs={{1,2},{3,4},{5,6},{2,1},{4,3},{6,5},{9,10},{11,12},{13,14},{10,9},... | collective-permute-start | bytes 589832 | tf_op jit(solution)/shard_map/ppermute | solution.py:451
  11.8 4.2 %collective-permute-start.2 = (bf16[2,128,384]{2,1,0:T(8,128)(2,1)S(1)}, bf16[2,128,384]{2,1,0:T(8,128)(2,1)S(1)}, u32[]{:S(2)}, u32[]{:S(2)}) collective-permute-start(bf16[2,128,384]{2,1,0:T(8,128)(2,1)S(1)} %pad_maximum_fusion.own_ref), channel_id=1, source_target_pairs={{0,1},{2,3},{4,5},{6,7},{1,0},{3,2},{5,4},{7,6},{8,9},{10,11},{12,... | collective-permute-start | bytes 589832 | tf_op jit(solution)/shard_map/ppermute | solution.py:451
  17.1 5.6 %collective-permute-start.4 = (bf16[2,4,16,128]{3,2,1,0:T(8,128)(2,1)S(1)}, bf16[2,4,16,128]{3,2,1,0:T(8,128)(2,1)S(1)}, u32[]{:S(2)}, u32[]{:S(2)}) collective-permute-start(bf16[2,4,16,128]{3,2,1,0:T(8,128)(2,1)S(1)} %get-tuple-element.36), channel_id=1, source_target_pairs={{0,2},{1,3},{2,0},{3,1},{4,6},{5,7},{6,4},{7,5},{8,10},{9,11},{10,... | collective-permute-start | bytes 98312 | tf_op jit(solution)/shard_map/ppermute | solution.py:457
  18.7 5.2 %collective-permute-start.5 = (bf16[2,4,16,128]{3,2,1,0:T(8,128)(2,1)S(1)}, bf16[2,4,16,128]{3,2,1,0:T(8,128)(2,1)S(1)}, u32[]{:S(2)}, u32[]{:S(2)}) collective-permute-start(bf16[2,4,16,128]{3,2,1,0:T(8,128)(2,1)S(1)} %get-tuple-element.39), channel_id=1, source_target_pairs={{0,4},{1,5},{2,6},{3,7},{4,0},{5,1},{6,2},{7,3},{8,12},{9,13},{10,... | collective-permute-start | bytes 98312 | tf_op jit(solution)/shard_map/ppermute | solution.py:457
  20.8 7.8 %collective-permute-start.7 = (bf16[2,2,4,16,128]{4,3,2,1,0:T(8,128)(2,1)S(1)}, bf16[2,2,4,16,128]{4,3,2,1,0:T(8,128)(2,1)S(1)}, u32[]{:S(2)}, u32[]{:S(2)}) collective-permute-start(bf16[2,2,4,16,128]{4,3,2,1,0:T(8,128)(2,1)S(1)} %get-tuple-element.41), channel_id=1, source_target_pairs={{0,6},{1,7},{2,4},{3,5},{4,2},{5,3},{6,0},{7,1},{8,14},{9,15},{10,... | collective-permute-start | bytes 196616 | tf_op jit(solution)/shard_map/ppermute | solution.py:457
  22.7 4.6 %collective-permute-start.8 = (bf16[2,4,16,128]{3,2,1,0:T(8,128)(2,1)S(1)}, bf16[2,4,16,128]{3,2,1,0:T(8,128)(2,1)S(1)}, u32[]{:S(2)}, u32[]{:S(2)}) collective-permute-start(bf16[2,4,16,128]{3,2,1,0:T(8,128)(2,1)S(1)} %get-tuple-element.42), channel_id=1, source_target_pairs={{0,2},{1,3},{2,0},{3,1},{4,6},{5,7},{6,4},{7,5},{8,10},{9,11},{10,... | collective-permute-start | bytes 98312 | tf_op jit(solution)/shard_map/ppermute | solution.py:457
  23.8 4.8 %collective-permute-start.9 = (bf16[2,4,16,128]{3,2,1,0:T(8,128)(2,1)S(1)}, bf16[2,4,16,128]{3,2,1,0:T(8,128)(2,1)S(1)}, u32[]{:S(2)}, u32[]{:S(2)}) collective-permute-start(bf16[2,4,16,128]{3,2,1,0:T(8,128)(2,1)S(1)} %get-tuple-element.43), channel_id=1, source_target_pairs={{0,4},{1,5},{2,6},{3,7},{4,0},{5,1},{6,2},{7,3},{8,12},{9,13},{10,... | collective-permute-start | bytes 98312 | tf_op jit(solution)/shard_map/ppermute | solution.py:457
  25.3 3.4 %collective-permute-start.6 = (bf16[4,4,16,128]{3,2,1,0:T(8,128)(2,1)S(1)}, bf16[4,4,16,128]{3,2,1,0:T(8,128)(2,1)S(1)}, u32[]{:S(2)}, u32[]{:S(2)}) collective-permute-start(bf16[4,4,16,128]{3,2,1,0:T(8,128)(2,1)S(1)} %pack.2), channel_id=1, source_target_pairs={{0,1},{2,3},{4,5},{6,7},{1,0},{3,2},{5,4},{7,6},{8,9},{10,11},{12,... | collective-permute-start | bytes 196616 | tf_op jit(solution)/shard_map/ppermute | solution.py:451
  28.7 1.3 %collective-permute-start.10 = (bf16[4,4,16,128]{3,2,1,0:T(8,128)(2,1)S(1)}, bf16[4,4,16,128]{3,2,1,0:T(8,128)(2,1)S(1)}, u32[]{:S(2)}, u32[]{:S(2)}) collective-permute-start(bf16[4,4,16,128]{3,2,1,0:T(8,128)(2,1)S(1)} %pack.3), channel_id=1, source_target_pairs={{0,1},{2,3},{4,5},{6,7},{1,0},{3,2},{5,4},{7,6},{8,9},{10,11},{12,... | collective-permute-start | bytes 196616 | tf_op jit(solution)/shard_map/ppermute | solution.py:451

commit v15 on v13

--- a/solution.py
+++ b/solution.py
@@ -247,12 +247,15 @@
     )(by_block, *in_hbm(taper_radius, taper_pattern, obs_block))
 
 
-def moved(b, which, turned_ref, taper_ref, tiles_ref):
-    cross = dot(turned_ref[b], tiles_ref[0], ((1,), (0,)))
-    count = tiles_ref.shape[2] // OBS_TILE
-    taper = jnp.concatenate([taper_ref[which, k, pl.ds(b, 1), :] for k in range(count)], axis=1)
-    gain = (cross * taper).astype(BF16)
-    return dot(tiles_ref[1], gain, ((1,), (1,)))
+def moved(b, which, turned_ref, taper_ref, column_ref):
+    members = turned_ref.shape[2]
+    turned = turned_ref[pl.ds(b, 2)].reshape(2 * CELLS, members)
+    cross = dot(turned, column_ref[0], ((1,), (0,)))
+    gains = []
+    for k in range(2):
+        taper = jnp.concatenate([taper_ref[which, ix, pl.ds(b + k, 1), :] for ix in range(3)], axis=1)
+        gains.append((cross[k * CELLS : (k + 1) * CELLS] * taper).astype(BF16))
+    return dot(column_ref[1], jnp.concatenate(gains, axis=0), ((1,), (1,)))
 
 
 def first_of(side, tile_y):
@@ -284,13 +287,17 @@
 def near_kernel(params_ref, turned_ref, taper_ref, own_ref, even_ref, part_ref, *refs):
     piece_refs, rows_ref = refs[:-1], refs[-1]
     tile_y = lax.axis_index("gy")
-    for k in range(SIDE):
+    for k in range(0, SIDE, 2):
         b = block_of(k, 0, tile_y)
         delta = moved(b, 0, turned_ref, taper_ref, own_ref) + moved(b, 1, turned_ref, taper_ref, even_ref)
-        put(piece_refs, rows_ref, k, (params_ref[b].astype(F32) + delta).astype(BF16))
-    for k in range(SIDE):
+        for j in range(2):
+            half = delta[:, j * CELLS : (j + 1) * CELLS]
+            put(piece_refs, rows_ref, k + j, (params_ref[b + j].astype(F32) + half).astype(BF16))
+    for k in range(0, SIDE, 2):
         b = block_of(k, 1, tile_y)
-        part_ref[k] = params_ref[b].astype(F32) + moved(b, 0, turned_ref, taper_ref, own_ref)
+        delta = moved(b, 0, turned_ref, taper_ref, own_ref)
+        for j in range(2):
+            part_ref[k + j] = params_ref[b + j].astype(F32) + delta[:, j * CELLS : (j + 1) * CELLS]
 
 
 def far_kernel(turned_ref, taper_ref, odd_ref, part_ref, near_ref, *refs):
@@ -298,9 +305,11 @@
     piece_refs = (*refs[:-2], both_ref.at[1])
     both_ref[0] = near_ref[...]
     tile_y = lax.axis_index("gy")
-    for k in range(SIDE):
-        b = block_of(k, 1, tile_y)
-        put(piece_refs, rows_ref, k, (part_ref[k] + moved(b, 2, turned_ref, taper_ref, odd_ref)).astype(BF16))
+    for k in range(0, SIDE, 2):
+        delta = moved(block_of(k, 1, tile_y), 2, turned_ref, taper_ref, odd_ref)
+        for j in range(2):
+            half = delta[:, j * CELLS : (j + 1) * CELLS]
+            put(piece_refs, rows_ref, k + j, (part_ref[k + j] + half).astype(BF16))
 
 
 def pack_kernel(*refs):
@@ -468,8 +477,8 @@
     last = parts // 2 - 1
     near_hops = {r: hop(near[r], r) for r in range(1, last)}
     *far, both = update_far(turned, taper, odd, part, near)
-    for r in range(1, last):
-        far[r], near_hops[r] = lax.optimization_barrier((far[r], near_hops[r]))
+    if last > 1:
+        far[1], near_hops = lax.optimization_barrier((far[1], near_hops))
     far_hops = {r: hop(far[r], r) for r in range(1, last)}
     early = [near[0], far[0], *(near_hops[r] for r in range(1, last))]
     late = [hop(both, last), *(far_hops[r] for r in range(1, last))]

time: 30.6 us -> 30 us (0.980)
  Pallas kernels: 7.76 us -> 6.55 us
  waiting for transfers between devices: 6.86 us -> 8.04 us
  starting transfers between devices: 15.5 us -> 14.9 us
    ppermute x5, waiting for transfers between devices: 2.47 us -> 3.4 us  [hop(): return lax.ppermute(piece, 'gy', pairs)]
    pallas_call x1, Pallas kernels: 1.9 us -> 1.04 us  [update_near(): pl.pallas_call(near_kernel, out_shape=(jax.ShapeDtypeStruct((SIDE, member...]
    ppermute x5, starting transfers between devices: 10.1 us -> 9.62 us  [hop(): return lax.ppermute(piece, 'gy', pairs)]
  transfers between devices with their start and end apart: 11 -> 11, of which waited for: 4 -> 5; matrix products, arithmetic and copies ran while one was open for 0% -> 0% of each run, Pallas kernels for 13% -> 10%
where the time goes in v15:
time: 30 us; the launch traced here: 29.7 us
  starting transfers between devices  14.9 us (50%)
  waiting for transfers between devices  8.04 us (27%)
  Pallas kernels  6.55 us (22%)
    ppermute x5, starting transfers between devices, hop(): return lax.ppermute(piece, 'gy', pairs)  9.62 us
    ppermute x6, starting transfers between devices, swap(): return lax.ppermute(block, axis, pairs + [(b, a) for a, b in pairs])  5.31 us
    ppermute x6, waiting for transfers between devices, swap(): return lax.ppermute(block, axis, pairs + [(b, a) for a, b in pairs])  4.63 us
    ppermute x5, waiting for transfers between devices, hop(): return lax.ppermute(piece, 'gy', pairs)  3.4 us
    pallas_call x1, Pallas kernels, weigh(): pl.pallas_call(weigh_kernel, out_shape=(jax.ShapeDtypeStruct((2, members,...  2.72 us
    pallas_call x1, Pallas kernels, update_near(): pl.pallas_call(near_kernel, out_shape=(jax.ShapeDtypeStruct((SIDE, member...  1.04 us
    pallas_call x1, Pallas kernels, prepare(): pl.pallas_call(prepare_kernel, out_shape=(jax.ShapeDtypeStruct((BLOCKS, C...  0.97 us
    pallas_call x1, Pallas kernels, gather(): pl.pallas_call(functools.partial(late_kernel, chips), out_shape=(jax.Shap...  0.94 us
  transfers between devices with their start and end apart: 11, of which 5 were waited for; matrix products, arithmetic and copies ran while one was open for 0% of the time, Pallas kernels for 10%

profile of v15, /device:TPU:0, one launch (start us, length us, event | category | flops | bytes accessed | tf_op | source)
XLA Modules:
  0.0 29.7 jit_solution(6667469212009447887)
XLA Ops:
  0.0 2.7 %weigh.1 = (bf16[2,128,128]{2,1,0:T(8,128)(2,1)S(1)}, bf16[128,2,4,128]{3,2,1,0:T(4,128)(2,1)S(1)}) custom-call(f32[1,1,128,128]{3,2,1,0:T(8,128)} %pred_hbm.1, f32[1,1,128]{2,1,0:T(1,128)} %mv_hbm.1, f32[1,1,128]{2,1,0:T(1,128)} %var_hbm.1, f32[1,1,128,128]{3,2,1,0:T(8,128)} %jit_hbm.1, s32[4,8,128]{2,1,0:T(8,128)} %obs_hbm.3, ...), custom_call_target="tpu_custom_call" | custom-call | tf_op jit(solution)/shard_map/weigh/pallas_call | solution.py:157
  2.7 3.2 %collective-permute-start = (bf16[2,128,128]{2,1,0:T(8,128)(2,1)S(1)}, bf16[2,128,128]{2,1,0:T(8,128)(2,1)S(1)}, u32[]{:S(2)}, u32[]{:S(2)}) collective-permute-start(bf16[2,128,128]{2,1,0:T(8,128)(2,1)S(1)} %get-tuple-element.26), channel_id=1, source_target_pairs={{0,8},{16,24},{8,0},{24,16},{1,9},{17,25},{9,1},{25,17},{2,10},{18... | collective-permute-start | bytes 196616 | tf_op jit(solution)/shard_map/ppermute | solution.py:444
  5.9 1.3 %collective-permute-start.1 = (bf16[2,128,128]{2,1,0:T(8,128)(2,1)S(1)}, bf16[2,128,128]{2,1,0:T(8,128)(2,1)S(1)}, u32[]{:S(2)}, u32[]{:S(2)}) collective-permute-start(bf16[2,128,128]{2,1,0:T(8,128)(2,1)S(1)} %get-tuple-element.26), channel_id=1, source_target_pairs={{8,16},{24,0},{16,8},{0,24},{9,17},{25,1},{17,9},{1,25},{10,18},{2... | collective-permute-start | bytes 196616 | tf_op jit(solution)/shard_map/ppermute | solution.py:444
  7.3 1.0 %prepare.1 = (bf16[8,128,128]{2,1,0:T(8,128)(2,1)S(1)}, f32[3,3,8,128]{3,2,1,0:T(8,128)S(1)}) custom-call(bf16[8,128,128]{2,1,0:T(8,128)(2,1)S(1)} %bitcast.4, s32[2,4]{1,0:T(2,128)} %radius_hbm.1, s32[2,4,25]{2,1,0:T(4,128)} %pattern_hbm.1, s32[4,8,128]{2,1,0:T(8,128)} %obs_hbm.3), custom_call_target="tpu_custom_call" | custom-call | flops 4000000 | bytes 1000000 | tf_op jit(solution)/shard_map/prepare/pallas_call | solution.py:230
  8.2 0.1 collective-permute-done
  8.3 2.8 %collective-permute-done.1 = bf16[2,128,128]{2,1,0:T(8,128)(2,1)S(1)} collective-permute-done((bf16[2,128,128]{2,1,0:T(8,128)(2,1)S(1)}, bf16[2,128,128]{2,1,0:T(8,128)(2,1)S(1)}, u32[]{:S(2)}, u32[]{:S(2)}) %collective-permute-start.1) | collective-permute-done | bytes 65568 | tf_op jit(solution)/shard_map/ppermute | solution.py:444
  11.1 0.1 collective-permute-start.2
  11.2 0.7 %collective-permute-start.3 = (bf16[2,128,384]{2,1,0:T(8,128)(2,1)S(1)}, bf16[2,128,384]{2,1,0:T(8,128)(2,1)S(1)}, u32[]{:S(2)}, u32[]{:S(2)}) collective-permute-start(bf16[2,128,384]{2,1,0:T(8,128)(2,1)S(1)} %pad_maximum_fusion.own_ref), channel_id=1, source_target_pairs={{1,2},{3,4},{5,6},{2,1},{4,3},{6,5},{9,10},{11,12},{13,14},{10,9},... | collective-permute-start | bytes 589832 | tf_op jit(solution)/shard_map/ppermute | solution.py:444
  11.9 0.7 %collective-permute-done.2.even_ref = bf16[2,128,384]{2,1,0:T(8,128)(2,1)S(1)} collective-permute-done((bf16[2,128,384]{2,1,0:T(8,128)(2,1)S(1)}, bf16[2,128,384]{2,1,0:T(8,128)(2,1)S(1)}, u32[]{:S(2)}, u32[]{:S(2)}) %collective-permute-start.2) | collective-permute-done | bytes 196640 | tf_op jit(solution)/shard_map/ppermute | solution.py:444
  12.6 1.0 %near.1 = (f32[4,128,128]{2,1,0:T(8,128)S(1)}, bf16[2,4,16,128]{3,2,1,0:T(8,128)(2,1)S(1)}, bf16[2,4,16,128]{3,2,1,0:T(8,128)(2,1)S(1)}, bf16[2,4,16,128]{3,2,1,0:T(8,128)(2,1)S(1)}, bf16[2,4,16,128]{3,2,1,0:T(8,128)(2,1)S(1)}) custom-call(bf16[8,128,128]{2,1,0:T(8,128)(2,1)S(1)} %bitcast.5, bf16[8,128,128]{2,1,0:T(8,128)(2,1)S(1)} %get-tuple-element.29.turned_ref, ...), custom_call_target="tpu_custom_call" | custom-call | flops 4000000000 | bytes 10000000 | tf_op jit(solution)/shard_map/near/pallas_call | solution.py:371
  13.7 2.7 %collective-permute-start.4 = (bf16[2,4,16,128]{3,2,1,0:T(8,128)(2,1)S(1)}, bf16[2,4,16,128]{3,2,1,0:T(8,128)(2,1)S(1)}, u32[]{:S(2)}, u32[]{:S(2)}) collective-permute-start(bf16[2,4,16,128]{3,2,1,0:T(8,128)(2,1)S(1)} %get-tuple-element.37), channel_id=1, source_target_pairs={{0,2},{1,3},{2,0},{3,1},{4,6},{5,7},{6,4},{7,5},{8,10},{9,11},{10,... | collective-permute-start | bytes 98312 | tf_op jit(solution)/shard_map/ppermute | solution.py:450
  16.4 2.5 %collective-permute-start.5 = (bf16[2,4,16,128]{3,2,1,0:T(8,128)(2,1)S(1)}, bf16[2,4,16,128]{3,2,1,0:T(8,128)(2,1)S(1)}, u32[]{:S(2)}, u32[]{:S(2)}) collective-permute-start(bf16[2,4,16,128]{3,2,1,0:T(8,128)(2,1)S(1)} %get-tuple-element.38), channel_id=1, source_target_pairs={{0,4},{1,5},{2,6},{3,7},{4,0},{5,1},{6,2},{7,3},{8,12},{9,13},{10,... | collective-permute-start | bytes 98312 | tf_op jit(solution)/shard_map/ppermute | solution.py:450
  18.9 0.0 collective-permute-done.3.odd_ref
  18.9 0.7 %far.1 = (bf16[2,4,16,128]{3,2,1,0:T(8,128)(2,1)S(1)}, bf16[2,4,16,128]{3,2,1,0:T(8,128)(2,1)S(1)}, bf16[2,4,16,128]{3,2,1,0:T(8,128)(2,1)S(1)}, bf16[2,2,4,16,128]{4,3,2,1,0:T(8,128)(2,1)S(1)}) custom-call(bf16[8,128,128]{2,1,0:T(8,128)(2,1)S(1)} %get-tuple-element.29.turned_ref, f32[3,3,8,128]{3,2,1,0:T(8,128)S(1)} %get-tuple-element.30.taper_ref, ...), custom_call_target="tpu_custom_call" | custom-call | flops 4000000000 | bytes 10000000 | tf_op jit(solution)/shard_map/far/pallas_call | solution.py:388
  19.5 2.9 %collective-permute-start.7 = (bf16[2,2,4,16,128]{4,3,2,1,0:T(8,128)(2,1)S(1)}, bf16[2,2,4,16,128]{4,3,2,1,0:T(8,128)(2,1)S(1)}, u32[]{:S(2)}, u32[]{:S(2)}) collective-permute-start(bf16[2,2,4,16,128]{4,3,2,1,0:T(8,128)(2,1)S(1)} %get-tuple-element.41), channel_id=1, source_target_pairs={{0,6},{1,7},{2,4},{3,5},{4,2},{5,3},{6,0},{7,1},{8,14},{9,15},{10,... | collective-permute-start | bytes 196616 | tf_op jit(solution)/shard_map/ppermute | solution.py:450
  22.4 0.0 collective-permute-start.9
  22.4 0.0 collective-permute-done.4.refs_2_.refs_3_
  22.4 0.0 collective-permute-done.5.refs_3_.refs_4_
  22.4 1.5 %collective-permute-start.8 = (bf16[2,4,16,128]{3,2,1,0:T(8,128)(2,1)S(1)}, bf16[2,4,16,128]{3,2,1,0:T(8,128)(2,1)S(1)}, u32[]{:S(2)}, u32[]{:S(2)}) collective-permute-start(bf16[2,4,16,128]{3,2,1,0:T(8,128)(2,1)S(1)} %get-tuple-element.42), channel_id=1, source_target_pairs={{0,2},{1,3},{2,0},{3,1},{4,6},{5,7},{6,4},{7,5},{8,10},{9,11},{10,... | collective-permute-start | bytes 98312 | tf_op jit(solution)/shard_map/ppermute | solution.py:450
  24.0 0.0 collective-permute-start.6
  24.0 3.4 %collective-permute-done.9.refs_2_.refs_4_ = bf16[2,4,16,128]{3,2,1,0:T(8,128)(2,1)S(1)} collective-permute-done((bf16[2,4,16,128]{3,2,1,0:T(8,128)(2,1)S(1)}, bf16[2,4,16,128]{3,2,1,0:T(8,128)(2,1)S(1)}, u32[]{:S(2)}, u32[]{:S(2)}) %collective-permute-start.9) | collective-permute-done | bytes 32800 | tf_op jit(solution)/shard_map/ppermute | solution.py:450
  27.4 0.0 collective-permute-done.8.refs_1_.refs_3_
  27.4 0.0 collective-permute-done.7.refs_0_.refs_2_
  27.4 0.1 collective-permute-start.10
  27.5 0.0 collective-permute-done.6.refs_0_
  27.5 0.2 early.1.refs_0_
  27.7 1.0 %collective-permute-done.10.refs_1_ = bf16[4,4,16,128]{3,2,1,0:T(8,128)(2,1)S(1)} collective-permute-done((bf16[4,4,16,128]{3,2,1,0:T(8,128)(2,1)S(1)}, bf16[4,4,16,128]{3,2,1,0:T(8,128)(2,1)S(1)}, u32[]{:S(2)}, u32[]{:S(2)}) %collective-permute-start.10) | collective-permute-done | bytes 65568 | tf_op jit(solution)/shard_map/ppermute | solution.py:444
  28.7 0.9 %late.1 = (bf16[1024,128]{1,0:T(8,128)(2,1)}, f32[1024,128]{1,0:T(8,128)S(1)}) custom-call(f32[1024,128]{1,0:T(8,128)S(1)} %early.1.refs_0_, bf16[4,4,16,128]{3,2,1,0:T(8,128)(2,1)S(1)} %collective-permute-done.10.refs_1_, bf16[2,2,4,16,128]{4,3,2,1,0:T(8,128)(2,1)S(1)} %collective-permute-done.7.refs_0_.refs_2_, ...), custom_call_target="tpu_custom_call", output_to_operand_aliasing={{1}: (0, {})} | custom-call | tf_op jit(solution)/shard_map/late/pallas_call | solution.py:423
  (4 shorter events, 0.1 us)
Async XLA Ops:
  2.7 5.6 %collective-permute-start = (bf16[2,128,128]{2,1,0:T(8,128)(2,1)S(1)}, bf16[2,128,128]{2,1,0:T(8,128)(2,1)S(1)}, u32[]{:S(2)}, u32[]{:S(2)}) collective-permute-start(bf16[2,128,128]{2,1,0:T(8,128)(2,1)S(1)} %get-tuple-element.26), channel_id=1, source_target_pairs={{0,8},{16,24},{8,0},{24,16},{1,9},{17,25},{9,1},{25,17},{2,10},{18... | collective-permute-start | bytes 196616 | tf_op jit(solution)/shard_map/ppermute | solution.py:444
  5.9 5.2 %collective-permute-start.1 = (bf16[2,128,128]{2,1,0:T(8,128)(2,1)S(1)}, bf16[2,128,128]{2,1,0:T(8,128)(2,1)S(1)}, u32[]{:S(2)}, u32[]{:S(2)}) collective-permute-start(bf16[2,128,128]{2,1,0:T(8,128)(2,1)S(1)} %get-tuple-element.26), channel_id=1, source_target_pairs={{8,16},{24,0},{16,8},{0,24},{9,17},{25,1},{17,9},{1,25},{10,18},{2... | collective-permute-start | bytes 196616 | tf_op jit(solution)/shard_map/ppermute | solution.py:444
  11.1 1.5 %collective-permute-start.2 = (bf16[2,128,384]{2,1,0:T(8,128)(2,1)S(1)}, bf16[2,128,384]{2,1,0:T(8,128)(2,1)S(1)}, u32[]{:S(2)}, u32[]{:S(2)}) collective-permute-start(bf16[2,128,384]{2,1,0:T(8,128)(2,1)S(1)} %pad_maximum_fusion.own_ref), channel_id=1, source_target_pairs={{0,1},{2,3},{4,5},{6,7},{1,0},{3,2},{5,4},{7,6},{8,9},{10,11},{12,... | collective-permute-start | bytes 589832 | tf_op jit(solution)/shard_map/ppermute | solution.py:444
  11.2 7.7 %collective-permute-start.3 = (bf16[2,128,384]{2,1,0:T(8,128)(2,1)S(1)}, bf16[2,128,384]{2,1,0:T(8,128)(2,1)S(1)}, u32[]{:S(2)}, u32[]{:S(2)}) collective-permute-start(bf16[2,128,384]{2,1,0:T(8,128)(2,1)S(1)} %pad_maximum_fusion.own_ref), channel_id=1, source_target_pairs={{1,2},{3,4},{5,6},{2,1},{4,3},{6,5},{9,10},{11,12},{13,14},{10,9},... | collective-permute-start | bytes 589832 | tf_op jit(solution)/shard_map/ppermute | solution.py:444
  13.7 8.7 %collective-permute-start.4 = (bf16[2,4,16,128]{3,2,1,0:T(8,128)(2,1)S(1)}, bf16[2,4,16,128]{3,2,1,0:T(8,128)(2,1)S(1)}, u32[]{:S(2)}, u32[]{:S(2)}) collective-permute-start(bf16[2,4,16,128]{3,2,1,0:T(8,128)(2,1)S(1)} %get-tuple-element.37), channel_id=1, source_target_pairs={{0,2},{1,3},{2,0},{3,1},{4,6},{5,7},{6,4},{7,5},{8,10},{9,11},{10,... | collective-permute-start | bytes 98312 | tf_op jit(solution)/shard_map/ppermute | solution.py:450
  16.4 6.1 %collective-permute-start.5 = (bf16[2,4,16,128]{3,2,1,0:T(8,128)(2,1)S(1)}, bf16[2,4,16,128]{3,2,1,0:T(8,128)(2,1)S(1)}, u32[]{:S(2)}, u32[]{:S(2)}) collective-permute-start(bf16[2,4,16,128]{3,2,1,0:T(8,128)(2,1)S(1)} %get-tuple-element.38), channel_id=1, source_target_pairs={{0,4},{1,5},{2,6},{3,7},{4,0},{5,1},{6,2},{7,3},{8,12},{9,13},{10,... | collective-permute-start | bytes 98312 | tf_op jit(solution)/shard_map/ppermute | solution.py:450
  19.5 7.9 %collective-permute-start.7 = (bf16[2,2,4,16,128]{4,3,2,1,0:T(8,128)(2,1)S(1)}, bf16[2,2,4,16,128]{4,3,2,1,0:T(8,128)(2,1)S(1)}, u32[]{:S(2)}, u32[]{:S(2)}) collective-permute-start(bf16[2,2,4,16,128]{4,3,2,1,0:T(8,128)(2,1)S(1)} %get-tuple-element.41), channel_id=1, source_target_pairs={{0,6},{1,7},{2,4},{3,5},{4,2},{5,3},{6,0},{7,1},{8,14},{9,15},{10,... | collective-permute-start | bytes 196616 | tf_op jit(solution)/shard_map/ppermute | solution.py:450
  22.4 5.0 %collective-permute-start.9 = (bf16[2,4,16,128]{3,2,1,0:T(8,128)(2,1)S(1)}, bf16[2,4,16,128]{3,2,1,0:T(8,128)(2,1)S(1)}, u32[]{:S(2)}, u32[]{:S(2)}) collective-permute-start(bf16[2,4,16,128]{3,2,1,0:T(8,128)(2,1)S(1)} %get-tuple-element.43), channel_id=1, source_target_pairs={{0,4},{1,5},{2,6},{3,7},{4,0},{5,1},{6,2},{7,3},{8,12},{9,13},{10,... | collective-permute-start | bytes 98312 | tf_op jit(solution)/shard_map/ppermute | solution.py:450
  22.4 5.0 %collective-permute-start.8 = (bf16[2,4,16,128]{3,2,1,0:T(8,128)(2,1)S(1)}, bf16[2,4,16,128]{3,2,1,0:T(8,128)(2,1)S(1)}, u32[]{:S(2)}, u32[]{:S(2)}) collective-permute-start(bf16[2,4,16,128]{3,2,1,0:T(8,128)(2,1)S(1)} %get-tuple-element.42), channel_id=1, source_target_pairs={{0,2},{1,3},{2,0},{3,1},{4,6},{5,7},{6,4},{7,5},{8,10},{9,11},{10,... | collective-permute-start | bytes 98312 | tf_op jit(solution)/shard_map/ppermute | solution.py:450
  24.0 3.5 %collective-permute-start.6 = (bf16[4,4,16,128]{3,2,1,0:T(8,128)(2,1)S(1)}, bf16[4,4,16,128]{3,2,1,0:T(8,128)(2,1)S(1)}, u32[]{:S(2)}, u32[]{:S(2)}) collective-permute-start(bf16[4,4,16,128]{3,2,1,0:T(8,128)(2,1)S(1)} %pack.2), channel_id=1, source_target_pairs={{0,1},{2,3},{4,5},{6,7},{1,0},{3,2},{5,4},{7,6},{8,9},{10,11},{12,... | collective-permute-start | bytes 196616 | tf_op jit(solution)/shard_map/ppermute | solution.py:444
  27.4 1.3 %collective-permute-start.10 = (bf16[4,4,16,128]{3,2,1,0:T(8,128)(2,1)S(1)}, bf16[4,4,16,128]{3,2,1,0:T(8,128)(2,1)S(1)}, u32[]{:S(2)}, u32[]{:S(2)}) collective-permute-start(bf16[4,4,16,128]{3,2,1,0:T(8,128)(2,1)S(1)} %pack.3), channel_id=1, source_target_pairs={{0,1},{2,3},{4,5},{6,7},{1,0},{3,2},{5,4},{7,6},{8,9},{10,11},{12,... | collective-permute-start | bytes 196616 | tf_op jit(solution)/shard_map/ppermute | solution.py:444

commit v16 on v15

--- a/solution.py
+++ b/solution.py
@@ -32,8 +32,8 @@
     return high, mid, low
 
 
-def dot(a, b, dims, precision=None):
-    return lax.dot_general(a, b, ((dims[0], dims[1]), ((), ())), precision=precision, preferred_element_type=F32)
+def dot(a, b, dims):
+    return lax.dot_general(a, b, (dims, ((), ())), preferred_element_type=F32)
 
 
 def sweep(rows, count, x_ref, idx_ref, rank, size):
@@ -123,18 +123,14 @@
     rank = jnp.sum(jnp.where(row < col, same, 0.0), axis=0, keepdims=True).astype(jnp.int32)
     place = row == rank
     hot = place.astype(BF16)
-    high, mid, low = split3(system)
-    x_ref[...] = (
-        dot(hot, low, ((1,), (0,))) + dot(hot, mid, ((1,), (0,))) + dot(hot, high, ((1,), (0,)))
-    )
+    x_ref[...] = dot(jnp.concatenate([hot] * 3, axis=1), jnp.concatenate(split3(system), axis=0), ((1,), (0,)))
     numbered = jnp.where(place, col, 0).astype(F32).astype(BF16)
     idx_ref[...] = dot(numbered, same.astype(BF16), ((1,), (0,))).astype(jnp.int32)
 
     def solve(rows):
         sweep(rows, count, x_ref, idx_ref, rank, size)
-        high, mid, low = split3(x_ref[0:rows, :])
-        taken = hot[0:rows]
-        full = dot(taken, low, ((0,), (0,))) + dot(taken, mid, ((0,), (0,))) + dot(taken, high, ((0,), (0,)))
+        taken = jnp.concatenate([hot[0:rows]] * 3, axis=0)
+        full = dot(taken, jnp.concatenate(split3(x_ref[0:rows, :]), axis=0), ((0,), (0,)))
         full_ref[...] = jnp.where(same > 0.5, -full, 0.0)
 
     @pl.when(count <= SMALL)
@@ -148,7 +144,11 @@
     for copy in copies[3:]:
         copy.wait()
     innovation = mv_ref[...] + jnp.sqrt(var) * jit_ref[...] - pred
-    weighted = dot(innovation, full_ref[...], ((1,), (0,)), lax.Precision.HIGHEST)
+    high, mid, low = split3(innovation)
+    full_high, full_mid, full_low = split3(full_ref[...])
+    left = jnp.concatenate([low, mid, high, mid, high, high], axis=1)
+    right = jnp.concatenate([full_high, full_mid, full_low, full_high, full_mid, full_high], axis=0)
+    weighted = dot(left, right, ((1,), (0,)))
     out_ref[1] = weighted.astype(BF16)
 
 

time: 30 us -> 30 us (level)
  starting transfers between devices: 14.9 us -> 14.5 us
  waiting for transfers between devices: 8.04 us -> 8.36 us
where the time goes in v16:
time: 30 us; the launch traced here: 29.8 us
  starting transfers between devices  14.5 us (48%)
  waiting for transfers between devices  8.36 us (28%)
  Pallas kernels  6.74 us (22%)
    ppermute x5, starting transfers between devices, hop(): return lax.ppermute(piece, 'gy', pairs)  9.43 us
    ppermute x6, starting transfers between devices, swap(): return lax.ppermute(block, axis, pairs + [(b, a) for a, b in pairs])  5.11 us
    ppermute x6, waiting for transfers between devices, swap(): return lax.ppermute(block, axis, pairs + [(b, a) for a, b in pairs])  4.73 us
    ppermute x5, waiting for transfers between devices, hop(): return lax.ppermute(piece, 'gy', pairs)  3.62 us
    pallas_call x1, Pallas kernels, weigh(): pl.pallas_call(weigh_kernel, out_shape=(jax.ShapeDtypeStruct((2, members,...  2.91 us
    pallas_call x1, Pallas kernels, update_near(): pl.pallas_call(near_kernel, out_shape=(jax.ShapeDtypeStruct((SIDE, member...  1.04 us
    pallas_call x1, Pallas kernels, prepare(): pl.pallas_call(prepare_kernel, out_shape=(jax.ShapeDtypeStruct((BLOCKS, C...  0.97 us
    pallas_call x1, Pallas kernels, gather(): pl.pallas_call(functools.partial(late_kernel, chips), out_shape=(jax.Shap...  0.94 us
  transfers between devices with their start and end apart: 11, of which 5 were waited for; matrix products, arithmetic and copies ran while one was open for 0% of the time, Pallas kernels for 10%

profile of v16, /device:TPU:0, one launch (start us, length us, event | category | flops | bytes accessed | tf_op | source)
XLA Modules:
  0.0 29.8 jit_solution(12737028422073964025)
XLA Ops:
  0.0 2.9 %weigh.1 = (bf16[2,128,128]{2,1,0:T(8,128)(2,1)S(1)}, bf16[128,2,4,128]{3,2,1,0:T(4,128)(2,1)S(1)}) custom-call(f32[1,1,128,128]{3,2,1,0:T(8,128)} %pred_hbm.1, f32[1,1,128]{2,1,0:T(1,128)} %mv_hbm.1, f32[1,1,128]{2,1,0:T(1,128)} %var_hbm.1, f32[1,1,128,128]{3,2,1,0:T(8,128)} %jit_hbm.1, s32[4,8,128]{2,1,0:T(8,128)} %obs_hbm.3, ...), custom_call_target="tpu_custom_call" | custom-call | tf_op jit(solution)/shard_map/weigh/pallas_call | solution.py:157
  2.9 3.1 %collective-permute-start = (bf16[2,128,128]{2,1,0:T(8,128)(2,1)S(1)}, bf16[2,128,128]{2,1,0:T(8,128)(2,1)S(1)}, u32[]{:S(2)}, u32[]{:S(2)}) collective-permute-start(bf16[2,128,128]{2,1,0:T(8,128)(2,1)S(1)} %get-tuple-element.26), channel_id=1, source_target_pairs={{0,8},{16,24},{8,0},{24,16},{1,9},{17,25},{9,1},{25,17},{2,10},{18... | collective-permute-start | bytes 196616 | tf_op jit(solution)/shard_map/ppermute | solution.py:444
  6.0 1.2 %collective-permute-start.1 = (bf16[2,128,128]{2,1,0:T(8,128)(2,1)S(1)}, bf16[2,128,128]{2,1,0:T(8,128)(2,1)S(1)}, u32[]{:S(2)}, u32[]{:S(2)}) collective-permute-start(bf16[2,128,128]{2,1,0:T(8,128)(2,1)S(1)} %get-tuple-element.26), channel_id=1, source_target_pairs={{8,16},{24,0},{16,8},{0,24},{9,17},{25,1},{17,9},{1,25},{10,18},{2... | collective-permute-start | bytes 196616 | tf_op jit(solution)/shard_map/ppermute | solution.py:444
  7.3 1.0 %prepare.1 = (bf16[8,128,128]{2,1,0:T(8,128)(2,1)S(1)}, f32[3,3,8,128]{3,2,1,0:T(8,128)S(1)}) custom-call(bf16[8,128,128]{2,1,0:T(8,128)(2,1)S(1)} %bitcast.4, s32[2,4]{1,0:T(2,128)} %radius_hbm.1, s32[2,4,25]{2,1,0:T(4,128)} %pattern_hbm.1, s32[4,8,128]{2,1,0:T(8,128)} %obs_hbm.3), custom_call_target="tpu_custom_call" | custom-call | flops 4000000 | bytes 1000000 | tf_op jit(solution)/shard_map/prepare/pallas_call | solution.py:230
  8.2 0.2 collective-permute-done
  8.4 2.8 %collective-permute-done.1 = bf16[2,128,128]{2,1,0:T(8,128)(2,1)S(1)} collective-permute-done((bf16[2,128,128]{2,1,0:T(8,128)(2,1)S(1)}, bf16[2,128,128]{2,1,0:T(8,128)(2,1)S(1)}, u32[]{:S(2)}, u32[]{:S(2)}) %collective-permute-start.1) | collective-permute-done | bytes 65568 | tf_op jit(solution)/shard_map/ppermute | solution.py:444
  11.2 0.1 collective-permute-start.2
  11.3 0.7 %collective-permute-start.3 = (bf16[2,128,384]{2,1,0:T(8,128)(2,1)S(1)}, bf16[2,128,384]{2,1,0:T(8,128)(2,1)S(1)}, u32[]{:S(2)}, u32[]{:S(2)}) collective-permute-start(bf16[2,128,384]{2,1,0:T(8,128)(2,1)S(1)} %pad_maximum_fusion.own_ref), channel_id=1, source_target_pairs={{1,2},{3,4},{5,6},{2,1},{4,3},{6,5},{9,10},{11,12},{13,14},{10,9},... | collective-permute-start | bytes 589832 | tf_op jit(solution)/shard_map/ppermute | solution.py:444
  12.0 0.7 %collective-permute-done.2.even_ref = bf16[2,128,384]{2,1,0:T(8,128)(2,1)S(1)} collective-permute-done((bf16[2,128,384]{2,1,0:T(8,128)(2,1)S(1)}, bf16[2,128,384]{2,1,0:T(8,128)(2,1)S(1)}, u32[]{:S(2)}, u32[]{:S(2)}) %collective-permute-start.2) | collective-permute-done | bytes 196640 | tf_op jit(solution)/shard_map/ppermute | solution.py:444
  12.7 1.0 %near.1 = (f32[4,128,128]{2,1,0:T(8,128)S(1)}, bf16[2,4,16,128]{3,2,1,0:T(8,128)(2,1)S(1)}, bf16[2,4,16,128]{3,2,1,0:T(8,128)(2,1)S(1)}, bf16[2,4,16,128]{3,2,1,0:T(8,128)(2,1)S(1)}, bf16[2,4,16,128]{3,2,1,0:T(8,128)(2,1)S(1)}) custom-call(bf16[8,128,128]{2,1,0:T(8,128)(2,1)S(1)} %bitcast.5, bf16[8,128,128]{2,1,0:T(8,128)(2,1)S(1)} %get-tuple-element.29.turned_ref, ...), custom_call_target="tpu_custom_call" | custom-call | flops 4000000000 | bytes 10000000 | tf_op jit(solution)/shard_map/near/pallas_call | solution.py:371
  13.8 2.7 %collective-permute-start.4 = (bf16[2,4,16,128]{3,2,1,0:T(8,128)(2,1)S(1)}, bf16[2,4,16,128]{3,2,1,0:T(8,128)(2,1)S(1)}, u32[]{:S(2)}, u32[]{:S(2)}) collective-permute-start(bf16[2,4,16,128]{3,2,1,0:T(8,128)(2,1)S(1)} %get-tuple-element.37), channel_id=1, source_target_pairs={{0,2},{1,3},{2,0},{3,1},{4,6},{5,7},{6,4},{7,5},{8,10},{9,11},{10,... | collective-permute-start | bytes 98312 | tf_op jit(solution)/shard_map/ppermute | solution.py:450
  16.5 2.3 %collective-permute-start.5 = (bf16[2,4,16,128]{3,2,1,0:T(8,128)(2,1)S(1)}, bf16[2,4,16,128]{3,2,1,0:T(8,128)(2,1)S(1)}, u32[]{:S(2)}, u32[]{:S(2)}) collective-permute-start(bf16[2,4,16,128]{3,2,1,0:T(8,128)(2,1)S(1)} %get-tuple-element.38), channel_id=1, source_target_pairs={{0,4},{1,5},{2,6},{3,7},{4,0},{5,1},{6,2},{7,3},{8,12},{9,13},{10,... | collective-permute-start | bytes 98312 | tf_op jit(solution)/shard_map/ppermute | solution.py:450
  18.7 0.0 collective-permute-done.3.odd_ref
  18.8 0.7 %far.1 = (bf16[2,4,16,128]{3,2,1,0:T(8,128)(2,1)S(1)}, bf16[2,4,16,128]{3,2,1,0:T(8,128)(2,1)S(1)}, bf16[2,4,16,128]{3,2,1,0:T(8,128)(2,1)S(1)}, bf16[2,2,4,16,128]{4,3,2,1,0:T(8,128)(2,1)S(1)}) custom-call(bf16[8,128,128]{2,1,0:T(8,128)(2,1)S(1)} %get-tuple-element.29.turned_ref, f32[3,3,8,128]{3,2,1,0:T(8,128)S(1)} %get-tuple-element.30.taper_ref, ...), custom_call_target="tpu_custom_call" | custom-call | flops 4000000000 | bytes 10000000 | tf_op jit(solution)/shard_map/far/pallas_call | solution.py:388
  19.4 3.0 %collective-permute-start.7 = (bf16[2,2,4,16,128]{4,3,2,1,0:T(8,128)(2,1)S(1)}, bf16[2,2,4,16,128]{4,3,2,1,0:T(8,128)(2,1)S(1)}, u32[]{:S(2)}, u32[]{:S(2)}) collective-permute-start(bf16[2,2,4,16,128]{4,3,2,1,0:T(8,128)(2,1)S(1)} %get-tuple-element.41), channel_id=1, source_target_pairs={{0,6},{1,7},{2,4},{3,5},{4,2},{5,3},{6,0},{7,1},{8,14},{9,15},{10,... | collective-permute-start | bytes 196616 | tf_op jit(solution)/shard_map/ppermute | solution.py:450
  22.4 0.0 collective-permute-start.9
  22.4 0.0 collective-permute-done.4.refs_2_.refs_3_
  22.4 0.0 collective-permute-done.5.refs_3_.refs_4_
  22.4 1.5 %collective-permute-start.8 = (bf16[2,4,16,128]{3,2,1,0:T(8,128)(2,1)S(1)}, bf16[2,4,16,128]{3,2,1,0:T(8,128)(2,1)S(1)}, u32[]{:S(2)}, u32[]{:S(2)}) collective-permute-start(bf16[2,4,16,128]{3,2,1,0:T(8,128)(2,1)S(1)} %get-tuple-element.42), channel_id=1, source_target_pairs={{0,2},{1,3},{2,0},{3,1},{4,6},{5,7},{6,4},{7,5},{8,10},{9,11},{10,... | collective-permute-start | bytes 98312 | tf_op jit(solution)/shard_map/ppermute | solution.py:450
  23.9 0.0 collective-permute-start.6
  23.9 3.6 %collective-permute-done.9.refs_2_.refs_4_ = bf16[2,4,16,128]{3,2,1,0:T(8,128)(2,1)S(1)} collective-permute-done((bf16[2,4,16,128]{3,2,1,0:T(8,128)(2,1)S(1)}, bf16[2,4,16,128]{3,2,1,0:T(8,128)(2,1)S(1)}, u32[]{:S(2)}, u32[]{:S(2)}) %collective-permute-start.9) | collective-permute-done | bytes 32800 | tf_op jit(solution)/shard_map/ppermute | solution.py:450
  27.5 0.0 collective-permute-done.8.refs_1_.refs_3_
  27.5 0.0 collective-permute-done.7.refs_0_.refs_2_
  27.5 0.1 collective-permute-start.10
  27.6 0.0 collective-permute-done.6.refs_0_
  27.6 0.2 early.1.refs_0_
  27.8 1.0 %collective-permute-done.10.refs_1_ = bf16[4,4,16,128]{3,2,1,0:T(8,128)(2,1)S(1)} collective-permute-done((bf16[4,4,16,128]{3,2,1,0:T(8,128)(2,1)S(1)}, bf16[4,4,16,128]{3,2,1,0:T(8,128)(2,1)S(1)}, u32[]{:S(2)}, u32[]{:S(2)}) %collective-permute-start.10) | collective-permute-done | bytes 65568 | tf_op jit(solution)/shard_map/ppermute | solution.py:444
  28.9 0.9 %late.1 = (bf16[1024,128]{1,0:T(8,128)(2,1)}, f32[1024,128]{1,0:T(8,128)S(1)}) custom-call(f32[1024,128]{1,0:T(8,128)S(1)} %early.1.refs_0_, bf16[4,4,16,128]{3,2,1,0:T(8,128)(2,1)S(1)} %collective-permute-done.10.refs_1_, bf16[2,2,4,16,128]{4,3,2,1,0:T(8,128)(2,1)S(1)} %collective-permute-done.7.refs_0_.refs_2_, ...), custom_call_target="tpu_custom_call", output_to_operand_aliasing={{1}: (0, {})} | custom-call | tf_op jit(solution)/shard_map/late/pallas_call | solution.py:423
  (4 shorter events, 0.1 us)
Async XLA Ops:
  2.9 5.5 %collective-permute-start = (bf16[2,128,128]{2,1,0:T(8,128)(2,1)S(1)}, bf16[2,128,128]{2,1,0:T(8,128)(2,1)S(1)}, u32[]{:S(2)}, u32[]{:S(2)}) collective-permute-start(bf16[2,128,128]{2,1,0:T(8,128)(2,1)S(1)} %get-tuple-element.26), channel_id=1, source_target_pairs={{0,8},{16,24},{8,0},{24,16},{1,9},{17,25},{9,1},{25,17},{2,10},{18... | collective-permute-start | bytes 196616 | tf_op jit(solution)/shard_map/ppermute | solution.py:444
  6.0 5.2 %collective-permute-start.1 = (bf16[2,128,128]{2,1,0:T(8,128)(2,1)S(1)}, bf16[2,128,128]{2,1,0:T(8,128)(2,1)S(1)}, u32[]{:S(2)}, u32[]{:S(2)}) collective-permute-start(bf16[2,128,128]{2,1,0:T(8,128)(2,1)S(1)} %get-tuple-element.26), channel_id=1, source_target_pairs={{8,16},{24,0},{16,8},{0,24},{9,17},{25,1},{17,9},{1,25},{10,18},{2... | collective-permute-start | bytes 196616 | tf_op jit(solution)/shard_map/ppermute | solution.py:444
  11.2 1.5 %collective-permute-start.2 = (bf16[2,128,384]{2,1,0:T(8,128)(2,1)S(1)}, bf16[2,128,384]{2,1,0:T(8,128)(2,1)S(1)}, u32[]{:S(2)}, u32[]{:S(2)}) collective-permute-start(bf16[2,128,384]{2,1,0:T(8,128)(2,1)S(1)} %pad_maximum_fusion.own_ref), channel_id=1, source_target_pairs={{0,1},{2,3},{4,5},{6,7},{1,0},{3,2},{5,4},{7,6},{8,9},{10,11},{12,... | collective-permute-start | bytes 589832 | tf_op jit(solution)/shard_map/ppermute | solution.py:444
  11.3 7.4 %collective-permute-start.3 = (bf16[2,128,384]{2,1,0:T(8,128)(2,1)S(1)}, bf16[2,128,384]{2,1,0:T(8,128)(2,1)S(1)}, u32[]{:S(2)}, u32[]{:S(2)}) collective-permute-start(bf16[2,128,384]{2,1,0:T(8,128)(2,1)S(1)} %pad_maximum_fusion.own_ref), channel_id=1, source_target_pairs={{1,2},{3,4},{5,6},{2,1},{4,3},{6,5},{9,10},{11,12},{13,14},{10,9},... | collective-permute-start | bytes 589832 | tf_op jit(solution)/shard_map/ppermute | solution.py:444
  13.8 8.6 %collective-permute-start.4 = (bf16[2,4,16,128]{3,2,1,0:T(8,128)(2,1)S(1)}, bf16[2,4,16,128]{3,2,1,0:T(8,128)(2,1)S(1)}, u32[]{:S(2)}, u32[]{:S(2)}) collective-permute-start(bf16[2,4,16,128]{3,2,1,0:T(8,128)(2,1)S(1)} %get-tuple-element.37), channel_id=1, source_target_pairs={{0,2},{1,3},{2,0},{3,1},{4,6},{5,7},{6,4},{7,5},{8,10},{9,11},{10,... | collective-permute-start | bytes 98312 | tf_op jit(solution)/shard_map/ppermute | solution.py:450
  16.5 6.0 %collective-permute-start.5 = (bf16[2,4,16,128]{3,2,1,0:T(8,128)(2,1)S(1)}, bf16[2,4,16,128]{3,2,1,0:T(8,128)(2,1)S(1)}, u32[]{:S(2)}, u32[]{:S(2)}) collective-permute-start(bf16[2,4,16,128]{3,2,1,0:T(8,128)(2,1)S(1)} %get-tuple-element.38), channel_id=1, source_target_pairs={{0,4},{1,5},{2,6},{3,7},{4,0},{5,1},{6,2},{7,3},{8,12},{9,13},{10,... | collective-permute-start | bytes 98312 | tf_op jit(solution)/shard_map/ppermute | solution.py:450
  19.4 8.1 %collective-permute-start.7 = (bf16[2,2,4,16,128]{4,3,2,1,0:T(8,128)(2,1)S(1)}, bf16[2,2,4,16,128]{4,3,2,1,0:T(8,128)(2,1)S(1)}, u32[]{:S(2)}, u32[]{:S(2)}) collective-permute-start(bf16[2,2,4,16,128]{4,3,2,1,0:T(8,128)(2,1)S(1)} %get-tuple-element.41), channel_id=1, source_target_pairs={{0,6},{1,7},{2,4},{3,5},{4,2},{5,3},{6,0},{7,1},{8,14},{9,15},{10,... | collective-permute-start | bytes 196616 | tf_op jit(solution)/shard_map/ppermute | solution.py:450
  22.4 5.1 %collective-permute-start.9 = (bf16[2,4,16,128]{3,2,1,0:T(8,128)(2,1)S(1)}, bf16[2,4,16,128]{3,2,1,0:T(8,128)(2,1)S(1)}, u32[]{:S(2)}, u32[]{:S(2)}) collective-permute-start(bf16[2,4,16,128]{3,2,1,0:T(8,128)(2,1)S(1)} %get-tuple-element.43), channel_id=1, source_target_pairs={{0,4},{1,5},{2,6},{3,7},{4,0},{5,1},{6,2},{7,3},{8,12},{9,13},{10,... | collective-permute-start | bytes 98312 | tf_op jit(solution)/shard_map/ppermute | solution.py:450
  22.4 5.1 %collective-permute-start.8 = (bf16[2,4,16,128]{3,2,1,0:T(8,128)(2,1)S(1)}, bf16[2,4,16,128]{3,2,1,0:T(8,128)(2,1)S(1)}, u32[]{:S(2)}, u32[]{:S(2)}) collective-permute-start(bf16[2,4,16,128]{3,2,1,0:T(8,128)(2,1)S(1)} %get-tuple-element.42), channel_id=1, source_target_pairs={{0,2},{1,3},{2,0},{3,1},{4,6},{5,7},{6,4},{7,5},{8,10},{9,11},{10,... | collective-permute-start | bytes 98312 | tf_op jit(solution)/shard_map/ppermute | solution.py:450
  23.9 3.7 %collective-permute-start.6 = (bf16[4,4,16,128]{3,2,1,0:T(8,128)(2,1)S(1)}, bf16[4,4,16,128]{3,2,1,0:T(8,128)(2,1)S(1)}, u32[]{:S(2)}, u32[]{:S(2)}) collective-permute-start(bf16[4,4,16,128]{3,2,1,0:T(8,128)(2,1)S(1)} %pack.2), channel_id=1, source_target_pairs={{0,1},{2,3},{4,5},{6,7},{1,0},{3,2},{5,4},{7,6},{8,9},{10,11},{12,... | collective-permute-start | bytes 196616 | tf_op jit(solution)/shard_map/ppermute | solution.py:444
  27.5 1.3 %collective-permute-start.10 = (bf16[4,4,16,128]{3,2,1,0:T(8,128)(2,1)S(1)}, bf16[4,4,16,128]{3,2,1,0:T(8,128)(2,1)S(1)}, u32[]{:S(2)}, u32[]{:S(2)}) collective-permute-start(bf16[4,4,16,128]{3,2,1,0:T(8,128)(2,1)S(1)} %pack.3), channel_id=1, source_target_pairs={{0,1},{2,3},{4,5},{6,7},{1,0},{3,2},{5,4},{7,6},{8,9},{10,11},{12,... | collective-permute-start | bytes 196616 | tf_op jit(solution)/shard_map/ppermute | solution.py:444

commit v17 on v16

--- a/solution.py
+++ b/solution.py
@@ -478,7 +478,7 @@
     near_hops = {r: hop(near[r], r) for r in range(1, last)}
     *far, both = update_far(turned, taper, odd, part, near)
     if last > 1:
-        far[1], near_hops = lax.optimization_barrier((far[1], near_hops))
+        far[last - 1], near_hops = lax.optimization_barrier((far[last - 1], near_hops))
     far_hops = {r: hop(far[r], r) for r in range(1, last)}
     early = [near[0], far[0], *(near_hops[r] for r in range(1, last))]
     late = [hop(both, last), *(far_hops[r] for r in range(1, last))]

time: 30 us -> 29.8 us (level)
  waiting for transfers between devices: 8.36 us -> 7.54 us
  starting transfers between devices: 14.5 us -> 15.2 us
    ppermute x5, waiting for transfers between devices: 3.62 us -> 3.12 us  [hop(): return lax.ppermute(piece, 'gy', pairs)]
    ppermute x5, starting transfers between devices: 9.43 us -> 9.93 us  [hop(): return lax.ppermute(piece, 'gy', pairs)]
    ppermute x6, waiting for transfers between devices: 4.73 us -> 4.42 us  [swap(): return lax.ppermute(block, axis, pairs + [(b, a) for a, b in pairs])]
where the time goes in v17:
time: 29.8 us; the launch traced here: 29.5 us
  starting transfers between devices  15.2 us (51%)
  waiting for transfers between devices  7.54 us (25%)
  Pallas kernels  6.53 us (22%)
    ppermute x5, starting transfers between devices, hop(): return lax.ppermute(piece, 'gy', pairs)  9.93 us
    ppermute x6, starting transfers between devices, swap(): return lax.ppermute(block, axis, pairs + [(b, a) for a, b in pairs])  5.31 us
    ppermute x6, waiting for transfers between devices, swap(): return lax.ppermute(block, axis, pairs + [(b, a) for a, b in pairs])  4.42 us
    ppermute x5, waiting for transfers between devices, hop(): return lax.ppermute(piece, 'gy', pairs)  3.12 us
    pallas_call x1, Pallas kernels, weigh(): pl.pallas_call(weigh_kernel, out_shape=(jax.ShapeDtypeStruct((2, members,...  2.71 us
    pallas_call x1, Pallas kernels, update_near(): pl.pallas_call(near_kernel, out_shape=(jax.ShapeDtypeStruct((SIDE, member...  1.03 us
    pallas_call x1, Pallas kernels, prepare(): pl.pallas_call(prepare_kernel, out_shape=(jax.ShapeDtypeStruct((BLOCKS, C...  0.97 us
    pallas_call x1, Pallas kernels, gather(): pl.pallas_call(functools.partial(late_kernel, chips), out_shape=(jax.Shap...  0.94 us
  transfers between devices with their start and end apart: 11, of which 5 were waited for; matrix products, arithmetic and copies ran while one was open for 0% of the time, Pallas kernels for 10%

profile of v17, /device:TPU:0, one launch (start us, length us, event | category | flops | bytes accessed | tf_op | source)
XLA Modules:
  0.0 29.5 jit_solution(16767030050417387608)
XLA Ops:
  0.0 2.7 %weigh.1 = (bf16[2,128,128]{2,1,0:T(8,128)(2,1)S(1)}, bf16[128,2,4,128]{3,2,1,0:T(4,128)(2,1)S(1)}) custom-call(f32[1,1,128,128]{3,2,1,0:T(8,128)} %pred_hbm.1, f32[1,1,128]{2,1,0:T(1,128)} %mv_hbm.1, f32[1,1,128]{2,1,0:T(1,128)} %var_hbm.1, f32[1,1,128,128]{3,2,1,0:T(8,128)} %jit_hbm.1, s32[4,8,128]{2,1,0:T(8,128)} %obs_hbm.3, ...), custom_call_target="tpu_custom_call" | custom-call | tf_op jit(solution)/shard_map/weigh/pallas_call | solution.py:157
  2.7 3.0 %collective-permute-start = (bf16[2,128,128]{2,1,0:T(8,128)(2,1)S(1)}, bf16[2,128,128]{2,1,0:T(8,128)(2,1)S(1)}, u32[]{:S(2)}, u32[]{:S(2)}) collective-permute-start(bf16[2,128,128]{2,1,0:T(8,128)(2,1)S(1)} %get-tuple-element.26), channel_id=1, source_target_pairs={{0,8},{16,24},{8,0},{24,16},{1,9},{17,25},{9,1},{25,17},{2,10},{18... | collective-permute-start | bytes 196616 | tf_op jit(solution)/shard_map/ppermute | solution.py:444
  5.7 1.5 %collective-permute-start.1 = (bf16[2,128,128]{2,1,0:T(8,128)(2,1)S(1)}, bf16[2,128,128]{2,1,0:T(8,128)(2,1)S(1)}, u32[]{:S(2)}, u32[]{:S(2)}) collective-permute-start(bf16[2,128,128]{2,1,0:T(8,128)(2,1)S(1)} %get-tuple-element.26), channel_id=1, source_target_pairs={{8,16},{24,0},{16,8},{0,24},{9,17},{25,1},{17,9},{1,25},{10,18},{2... | collective-permute-start | bytes 196616 | tf_op jit(solution)/shard_map/ppermute | solution.py:444
  7.3 1.0 %prepare.1 = (bf16[8,128,128]{2,1,0:T(8,128)(2,1)S(1)}, f32[3,3,8,128]{3,2,1,0:T(8,128)S(1)}) custom-call(bf16[8,128,128]{2,1,0:T(8,128)(2,1)S(1)} %bitcast.4, s32[2,4]{1,0:T(2,128)} %radius_hbm.1, s32[2,4,25]{2,1,0:T(4,128)} %pattern_hbm.1, s32[4,8,128]{2,1,0:T(8,128)} %obs_hbm.3), custom_call_target="tpu_custom_call" | custom-call | flops 4000000 | bytes 1000000 | tf_op jit(solution)/shard_map/prepare/pallas_call | solution.py:230
  8.2 0.0 collective-permute-done
  8.2 2.6 %collective-permute-done.1 = bf16[2,128,128]{2,1,0:T(8,128)(2,1)S(1)} collective-permute-done((bf16[2,128,128]{2,1,0:T(8,128)(2,1)S(1)}, bf16[2,128,128]{2,1,0:T(8,128)(2,1)S(1)}, u32[]{:S(2)}, u32[]{:S(2)}) %collective-permute-start.1) | collective-permute-done | bytes 65568 | tf_op jit(solution)/shard_map/ppermute | solution.py:444
  10.9 0.1 collective-permute-start.2
  11.0 0.7 %collective-permute-start.3 = (bf16[2,128,384]{2,1,0:T(8,128)(2,1)S(1)}, bf16[2,128,384]{2,1,0:T(8,128)(2,1)S(1)}, u32[]{:S(2)}, u32[]{:S(2)}) collective-permute-start(bf16[2,128,384]{2,1,0:T(8,128)(2,1)S(1)} %pad_maximum_fusion.own_ref), channel_id=1, source_target_pairs={{1,2},{3,4},{5,6},{2,1},{4,3},{6,5},{9,10},{11,12},{13,14},{10,9},... | collective-permute-start | bytes 589832 | tf_op jit(solution)/shard_map/ppermute | solution.py:444
  11.7 0.7 %collective-permute-done.2.even_ref = bf16[2,128,384]{2,1,0:T(8,128)(2,1)S(1)} collective-permute-done((bf16[2,128,384]{2,1,0:T(8,128)(2,1)S(1)}, bf16[2,128,384]{2,1,0:T(8,128)(2,1)S(1)}, u32[]{:S(2)}, u32[]{:S(2)}) %collective-permute-start.2) | collective-permute-done | bytes 196640 | tf_op jit(solution)/shard_map/ppermute | solution.py:444
  12.4 1.0 %near.1 = (f32[4,128,128]{2,1,0:T(8,128)S(1)}, bf16[2,4,16,128]{3,2,1,0:T(8,128)(2,1)S(1)}, bf16[2,4,16,128]{3,2,1,0:T(8,128)(2,1)S(1)}, bf16[2,4,16,128]{3,2,1,0:T(8,128)(2,1)S(1)}, bf16[2,4,16,128]{3,2,1,0:T(8,128)(2,1)S(1)}) custom-call(bf16[8,128,128]{2,1,0:T(8,128)(2,1)S(1)} %bitcast.5, bf16[8,128,128]{2,1,0:T(8,128)(2,1)S(1)} %get-tuple-element.29.turned_ref, ...), custom_call_target="tpu_custom_call" | custom-call | flops 4000000000 | bytes 10000000 | tf_op jit(solution)/shard_map/near/pallas_call | solution.py:371
  13.5 2.7 %collective-permute-start.4 = (bf16[2,4,16,128]{3,2,1,0:T(8,128)(2,1)S(1)}, bf16[2,4,16,128]{3,2,1,0:T(8,128)(2,1)S(1)}, u32[]{:S(2)}, u32[]{:S(2)}) collective-permute-start(bf16[2,4,16,128]{3,2,1,0:T(8,128)(2,1)S(1)} %get-tuple-element.37), channel_id=1, source_target_pairs={{0,2},{1,3},{2,0},{3,1},{4,6},{5,7},{6,4},{7,5},{8,10},{9,11},{10,... | collective-permute-start | bytes 98312 | tf_op jit(solution)/shard_map/ppermute | solution.py:450
  16.2 2.8 %collective-permute-start.5 = (bf16[2,4,16,128]{3,2,1,0:T(8,128)(2,1)S(1)}, bf16[2,4,16,128]{3,2,1,0:T(8,128)(2,1)S(1)}, u32[]{:S(2)}, u32[]{:S(2)}) collective-permute-start(bf16[2,4,16,128]{3,2,1,0:T(8,128)(2,1)S(1)} %get-tuple-element.38), channel_id=1, source_target_pairs={{0,4},{1,5},{2,6},{3,7},{4,0},{5,1},{6,2},{7,3},{8,12},{9,13},{10,... | collective-permute-start | bytes 98312 | tf_op jit(solution)/shard_map/ppermute | solution.py:450
  19.0 0.0 collective-permute-done.3.odd_ref
  19.0 0.7 %far.1 = (bf16[2,4,16,128]{3,2,1,0:T(8,128)(2,1)S(1)}, bf16[2,4,16,128]{3,2,1,0:T(8,128)(2,1)S(1)}, bf16[2,4,16,128]{3,2,1,0:T(8,128)(2,1)S(1)}, bf16[2,2,4,16,128]{4,3,2,1,0:T(8,128)(2,1)S(1)}) custom-call(bf16[8,128,128]{2,1,0:T(8,128)(2,1)S(1)} %get-tuple-element.29.turned_ref, f32[3,3,8,128]{3,2,1,0:T(8,128)S(1)} %get-tuple-element.30.taper_ref, ...), custom_call_target="tpu_custom_call" | custom-call | flops 4000000000 | bytes 10000000 | tf_op jit(solution)/shard_map/far/pallas_call | solution.py:388
  19.6 2.7 %collective-permute-start.7 = (bf16[2,2,4,16,128]{4,3,2,1,0:T(8,128)(2,1)S(1)}, bf16[2,2,4,16,128]{4,3,2,1,0:T(8,128)(2,1)S(1)}, u32[]{:S(2)}, u32[]{:S(2)}) collective-permute-start(bf16[2,2,4,16,128]{4,3,2,1,0:T(8,128)(2,1)S(1)} %get-tuple-element.41), channel_id=1, source_target_pairs={{0,6},{1,7},{2,4},{3,5},{4,2},{5,3},{6,0},{7,1},{8,14},{9,15},{10,... | collective-permute-start | bytes 196616 | tf_op jit(solution)/shard_map/ppermute | solution.py:450
  22.3 0.0 collective-permute-start.8
  22.3 0.0 collective-permute-done.4.refs_2_.refs_3_
  22.3 0.0 collective-permute-done.5.refs_3_.refs_4_
  22.3 1.8 %collective-permute-start.9 = (bf16[2,4,16,128]{3,2,1,0:T(8,128)(2,1)S(1)}, bf16[2,4,16,128]{3,2,1,0:T(8,128)(2,1)S(1)}, u32[]{:S(2)}, u32[]{:S(2)}) collective-permute-start(bf16[2,4,16,128]{3,2,1,0:T(8,128)(2,1)S(1)} %get-tuple-element.43), channel_id=1, source_target_pairs={{0,4},{1,5},{2,6},{3,7},{4,0},{5,1},{6,2},{7,3},{8,12},{9,13},{10,... | collective-permute-start | bytes 98312 | tf_op jit(solution)/shard_map/ppermute | solution.py:450
  24.1 0.0 collective-permute-start.6
  24.1 2.1 %collective-permute-done.8.refs_1_.refs_3_ = bf16[2,4,16,128]{3,2,1,0:T(8,128)(2,1)S(1)} collective-permute-done((bf16[2,4,16,128]{3,2,1,0:T(8,128)(2,1)S(1)}, bf16[2,4,16,128]{3,2,1,0:T(8,128)(2,1)S(1)}, u32[]{:S(2)}, u32[]{:S(2)}) %collective-permute-start.8) | collective-permute-done | bytes 32800 | tf_op jit(solution)/shard_map/ppermute | solution.py:450
  26.2 1.0 %collective-permute-done.9.refs_2_.refs_4_ = bf16[2,4,16,128]{3,2,1,0:T(8,128)(2,1)S(1)} collective-permute-done((bf16[2,4,16,128]{3,2,1,0:T(8,128)(2,1)S(1)}, bf16[2,4,16,128]{3,2,1,0:T(8,128)(2,1)S(1)}, u32[]{:S(2)}, u32[]{:S(2)}) %collective-permute-start.9) | collective-permute-done | bytes 32800 | tf_op jit(solution)/shard_map/ppermute | solution.py:450
  27.2 0.0 collective-permute-done.7.refs_0_.refs_2_
  27.2 0.1 collective-permute-start.10
  27.3 0.0 collective-permute-done.6.refs_0_
  27.3 0.2 early.1.refs_0_
  27.5 1.0 %collective-permute-done.10.refs_1_ = bf16[4,4,16,128]{3,2,1,0:T(8,128)(2,1)S(1)} collective-permute-done((bf16[4,4,16,128]{3,2,1,0:T(8,128)(2,1)S(1)}, bf16[4,4,16,128]{3,2,1,0:T(8,128)(2,1)S(1)}, u32[]{:S(2)}, u32[]{:S(2)}) %collective-permute-start.10) | collective-permute-done | bytes 65568 | tf_op jit(solution)/shard_map/ppermute | solution.py:444
  28.5 0.9 %late.1 = (bf16[1024,128]{1,0:T(8,128)(2,1)}, f32[1024,128]{1,0:T(8,128)S(1)}) custom-call(f32[1024,128]{1,0:T(8,128)S(1)} %early.1.refs_0_, bf16[4,4,16,128]{3,2,1,0:T(8,128)(2,1)S(1)} %collective-permute-done.10.refs_1_, bf16[2,2,4,16,128]{4,3,2,1,0:T(8,128)(2,1)S(1)} %collective-permute-done.7.refs_0_.refs_2_, ...), custom_call_target="tpu_custom_call", output_to_operand_aliasing={{1}: (0, {})} | custom-call | tf_op jit(solution)/shard_map/late/pallas_call | solution.py:423
  (4 shorter events, 0.1 us)
Async XLA Ops:
  2.7 5.5 %collective-permute-start = (bf16[2,128,128]{2,1,0:T(8,128)(2,1)S(1)}, bf16[2,128,128]{2,1,0:T(8,128)(2,1)S(1)}, u32[]{:S(2)}, u32[]{:S(2)}) collective-permute-start(bf16[2,128,128]{2,1,0:T(8,128)(2,1)S(1)} %get-tuple-element.26), channel_id=1, source_target_pairs={{0,8},{16,24},{8,0},{24,16},{1,9},{17,25},{9,1},{25,17},{2,10},{18... | collective-permute-start | bytes 196616 | tf_op jit(solution)/shard_map/ppermute | solution.py:444
  5.7 5.2 %collective-permute-start.1 = (bf16[2,128,128]{2,1,0:T(8,128)(2,1)S(1)}, bf16[2,128,128]{2,1,0:T(8,128)(2,1)S(1)}, u32[]{:S(2)}, u32[]{:S(2)}) collective-permute-start(bf16[2,128,128]{2,1,0:T(8,128)(2,1)S(1)} %get-tuple-element.26), channel_id=1, source_target_pairs={{8,16},{24,0},{16,8},{0,24},{9,17},{25,1},{17,9},{1,25},{10,18},{2... | collective-permute-start | bytes 196616 | tf_op jit(solution)/shard_map/ppermute | solution.py:444
  10.9 1.5 %collective-permute-start.2 = (bf16[2,128,384]{2,1,0:T(8,128)(2,1)S(1)}, bf16[2,128,384]{2,1,0:T(8,128)(2,1)S(1)}, u32[]{:S(2)}, u32[]{:S(2)}) collective-permute-start(bf16[2,128,384]{2,1,0:T(8,128)(2,1)S(1)} %pad_maximum_fusion.own_ref), channel_id=1, source_target_pairs={{0,1},{2,3},{4,5},{6,7},{1,0},{3,2},{5,4},{7,6},{8,9},{10,11},{12,... | collective-permute-start | bytes 589832 | tf_op jit(solution)/shard_map/ppermute | solution.py:444
  11.0 8.0 %collective-permute-start.3 = (bf16[2,128,384]{2,1,0:T(8,128)(2,1)S(1)}, bf16[2,128,384]{2,1,0:T(8,128)(2,1)S(1)}, u32[]{:S(2)}, u32[]{:S(2)}) collective-permute-start(bf16[2,128,384]{2,1,0:T(8,128)(2,1)S(1)} %pad_maximum_fusion.own_ref), channel_id=1, source_target_pairs={{1,2},{3,4},{5,6},{2,1},{4,3},{6,5},{9,10},{11,12},{13,14},{10,9},... | collective-permute-start | bytes 589832 | tf_op jit(solution)/shard_map/ppermute | solution.py:444
  13.5 8.8 %collective-permute-start.4 = (bf16[2,4,16,128]{3,2,1,0:T(8,128)(2,1)S(1)}, bf16[2,4,16,128]{3,2,1,0:T(8,128)(2,1)S(1)}, u32[]{:S(2)}, u32[]{:S(2)}) collective-permute-start(bf16[2,4,16,128]{3,2,1,0:T(8,128)(2,1)S(1)} %get-tuple-element.37), channel_id=1, source_target_pairs={{0,2},{1,3},{2,0},{3,1},{4,6},{5,7},{6,4},{7,5},{8,10},{9,11},{10,... | collective-permute-start | bytes 98312 | tf_op jit(solution)/shard_map/ppermute | solution.py:450
  16.2 6.2 %collective-permute-start.5 = (bf16[2,4,16,128]{3,2,1,0:T(8,128)(2,1)S(1)}, bf16[2,4,16,128]{3,2,1,0:T(8,128)(2,1)S(1)}, u32[]{:S(2)}, u32[]{:S(2)}) collective-permute-start(bf16[2,4,16,128]{3,2,1,0:T(8,128)(2,1)S(1)} %get-tuple-element.38), channel_id=1, source_target_pairs={{0,4},{1,5},{2,6},{3,7},{4,0},{5,1},{6,2},{7,3},{8,12},{9,13},{10,... | collective-permute-start | bytes 98312 | tf_op jit(solution)/shard_map/ppermute | solution.py:450
  19.6 7.6 %collective-permute-start.7 = (bf16[2,2,4,16,128]{4,3,2,1,0:T(8,128)(2,1)S(1)}, bf16[2,2,4,16,128]{4,3,2,1,0:T(8,128)(2,1)S(1)}, u32[]{:S(2)}, u32[]{:S(2)}) collective-permute-start(bf16[2,2,4,16,128]{4,3,2,1,0:T(8,128)(2,1)S(1)} %get-tuple-element.41), channel_id=1, source_target_pairs={{0,6},{1,7},{2,4},{3,5},{4,2},{5,3},{6,0},{7,1},{8,14},{9,15},{10,... | collective-permute-start | bytes 196616 | tf_op jit(solution)/shard_map/ppermute | solution.py:450
  22.3 3.9 %collective-permute-start.8 = (bf16[2,4,16,128]{3,2,1,0:T(8,128)(2,1)S(1)}, bf16[2,4,16,128]{3,2,1,0:T(8,128)(2,1)S(1)}, u32[]{:S(2)}, u32[]{:S(2)}) collective-permute-start(bf16[2,4,16,128]{3,2,1,0:T(8,128)(2,1)S(1)} %get-tuple-element.42), channel_id=1, source_target_pairs={{0,2},{1,3},{2,0},{3,1},{4,6},{5,7},{6,4},{7,5},{8,10},{9,11},{10,... | collective-permute-start | bytes 98312 | tf_op jit(solution)/shard_map/ppermute | solution.py:450
  22.3 4.9 %collective-permute-start.9 = (bf16[2,4,16,128]{3,2,1,0:T(8,128)(2,1)S(1)}, bf16[2,4,16,128]{3,2,1,0:T(8,128)(2,1)S(1)}, u32[]{:S(2)}, u32[]{:S(2)}) collective-permute-start(bf16[2,4,16,128]{3,2,1,0:T(8,128)(2,1)S(1)} %get-tuple-element.43), channel_id=1, source_target_pairs={{0,4},{1,5},{2,6},{3,7},{4,0},{5,1},{6,2},{7,3},{8,12},{9,13},{10,... | collective-permute-start | bytes 98312 | tf_op jit(solution)/shard_map/ppermute | solution.py:450
  24.1 3.2 %collective-permute-start.6 = (bf16[4,4,16,128]{3,2,1,0:T(8,128)(2,1)S(1)}, bf16[4,4,16,128]{3,2,1,0:T(8,128)(2,1)S(1)}, u32[]{:S(2)}, u32[]{:S(2)}) collective-permute-start(bf16[4,4,16,128]{3,2,1,0:T(8,128)(2,1)S(1)} %pack.2), channel_id=1, source_target_pairs={{0,1},{2,3},{4,5},{6,7},{1,0},{3,2},{5,4},{7,6},{8,9},{10,11},{12,... | collective-permute-start | bytes 196616 | tf_op jit(solution)/shard_map/ppermute | solution.py:444
  27.2 1.3 %collective-permute-start.10 = (bf16[4,4,16,128]{3,2,1,0:T(8,128)(2,1)S(1)}, bf16[4,4,16,128]{3,2,1,0:T(8,128)(2,1)S(1)}, u32[]{:S(2)}, u32[]{:S(2)}) collective-permute-start(bf16[4,4,16,128]{3,2,1,0:T(8,128)(2,1)S(1)} %pack.3), channel_id=1, source_target_pairs={{0,1},{2,3},{4,5},{6,7},{1,0},{3,2},{5,4},{7,6},{8,9},{10,11},{12,... | collective-permute-start | bytes 196616 | tf_op jit(solution)/shard_map/ppermute | solution.py:444

commit v18 on v16

--- a/solution.py
+++ b/solution.py
@@ -444,6 +444,18 @@
     return lax.ppermute(block, axis, pairs + [(b, a) for a, b in pairs])
 
 
+def swap_across():
+    rows, count = lax.axis_size("gx"), lax.axis_size("gy")
+    pairs = []
+    for x in range(rows):
+        for y in range(count):
+            at, to = (x, y + 1 if y % 2 else y - 1), x * count + y
+            if not 0 <= at[1] < count:
+                at = (x ^ 1, y)
+            pairs.append((to, at[0] * count + at[1]))
+    return pairs
+
+
 def hop(piece, r):
     count = lax.axis_size("gy")
     pairs = [(i, 2 * target(i // 2, r, count // 2) + i % 2) for i in range(count)]
@@ -472,7 +484,7 @@
     column = jnp.concatenate([own, even, odd], axis=2)
     column, turned, taper = lax.optimization_barrier((column, turned, taper))
     even = swap(column, "gy", 0)
-    odd = swap(column, "gy", 1)
+    odd = lax.ppermute(column, ("gx", "gy"), swap_across())
     part, *near = update_near(by_block, turned, taper, column, even, parts)
     last = parts // 2 - 1
     near_hops = {r: hop(near[r], r) for r in range(1, last)}

time: 30 us -> 28.3 us (0.943)
  waiting for transfers between devices: 8.36 us -> 7.35 us
  starting transfers between devices: 14.5 us -> 14.1 us
    ppermute x5, waiting for transfers between devices: 3.62 us -> 2.72 us  [hop(): return lax.ppermute(piece, 'gy', pairs)]
    ppermute x0 -> x1, starting transfers between devices: none -> 0.79 us  [per_device(): odd = lax.ppermute(column, ('gx', 'gy'), swap_across())]
    ppermute x5, starting transfers between devices: 9.43 us -> 8.79 us  [hop(): return lax.ppermute(piece, 'gy', pairs)]
    ppermute x6 -> x5, starting transfers between devices: 5.11 us -> 4.54 us  [swap(): return lax.ppermute(block, axis, pairs + [(b, a) for a, b in pairs])]
    ppermute x6 -> x5, waiting for transfers between devices: 4.73 us -> 4.63 us  [swap(): return lax.ppermute(block, axis, pairs + [(b, a) for a, b in pairs])]
where the time goes in v18:
time: 28.3 us
  starting transfers between devices  14.1 us (50%)
  waiting for transfers between devices  7.35 us (26%)
  Pallas kernels  6.64 us (23%)
    ppermute x5, starting transfers between devices, hop(): return lax.ppermute(piece, 'gy', pairs)  8.79 us
    ppermute x5, waiting for transfers between devices, swap(): return lax.ppermute(block, axis, pairs + [(b, a) for a, b in pairs])  4.63 us
    ppermute x5, starting transfers between devices, swap(): return lax.ppermute(block, axis, pairs + [(b, a) for a, b in pairs])  4.54 us
    pallas_call x1, Pallas kernels, weigh(): pl.pallas_call(weigh_kernel, out_shape=(jax.ShapeDtypeStruct((2, members,...  2.81 us
    ppermute x5, waiting for transfers between devices, hop(): return lax.ppermute(piece, 'gy', pairs)  2.72 us
    pallas_call x1, Pallas kernels, update_near(): pl.pallas_call(near_kernel, out_shape=(jax.ShapeDtypeStruct((SIDE, member...  1.04 us
    pallas_call x1, Pallas kernels, prepare(): pl.pallas_call(prepare_kernel, out_shape=(jax.ShapeDtypeStruct((BLOCKS, C...  0.97 us
    pallas_call x1, Pallas kernels, gather(): pl.pallas_call(functools.partial(late_kernel, chips), out_shape=(jax.Shap...  0.94 us
  transfers between devices with their start and end apart: 11, of which 5 were waited for; matrix products, arithmetic and copies ran while one was open for 0% of the time, Pallas kernels for 10%

profile of v18, /device:TPU:0, one launch (start us, length us, event | category | flops | bytes accessed | tf_op | source)
XLA Modules:
  0.0 28.3 jit_solution(15966898877884369367)
XLA Ops:
  0.0 2.8 %weigh.1 = (bf16[2,128,128]{2,1,0:T(8,128)(2,1)S(1)}, bf16[128,2,4,128]{3,2,1,0:T(4,128)(2,1)S(1)}) custom-call(f32[1,1,128,128]{3,2,1,0:T(8,128)} %pred_hbm.1, f32[1,1,128]{2,1,0:T(1,128)} %mv_hbm.1, f32[1,1,128]{2,1,0:T(1,128)} %var_hbm.1, f32[1,1,128,128]{3,2,1,0:T(8,128)} %jit_hbm.1, s32[4,8,128]{2,1,0:T(8,128)} %obs_hbm.3, ...), custom_call_target="tpu_custom_call" | custom-call | tf_op jit(solution)/shard_map/weigh/pallas_call | solution.py:157
  2.8 3.2 %collective-permute-start = (bf16[2,128,128]{2,1,0:T(8,128)(2,1)S(1)}, bf16[2,128,128]{2,1,0:T(8,128)(2,1)S(1)}, u32[]{:S(2)}, u32[]{:S(2)}) collective-permute-start(bf16[2,128,128]{2,1,0:T(8,128)(2,1)S(1)} %get-tuple-element.26), channel_id=1, source_target_pairs={{0,8},{16,24},{8,0},{24,16},{1,9},{17,25},{9,1},{25,17},{2,10},{18... | collective-permute-start | bytes 196616 | tf_op jit(solution)/shard_map/ppermute | solution.py:444
  6.0 1.2 %collective-permute-start.1 = (bf16[2,128,128]{2,1,0:T(8,128)(2,1)S(1)}, bf16[2,128,128]{2,1,0:T(8,128)(2,1)S(1)}, u32[]{:S(2)}, u32[]{:S(2)}) collective-permute-start(bf16[2,128,128]{2,1,0:T(8,128)(2,1)S(1)} %get-tuple-element.26), channel_id=1, source_target_pairs={{8,16},{24,0},{16,8},{0,24},{9,17},{25,1},{17,9},{1,25},{10,18},{2... | collective-permute-start | bytes 196616 | tf_op jit(solution)/shard_map/ppermute | solution.py:444
  7.3 1.0 %prepare.1 = (bf16[8,128,128]{2,1,0:T(8,128)(2,1)S(1)}, f32[3,3,8,128]{3,2,1,0:T(8,128)S(1)}) custom-call(bf16[8,128,128]{2,1,0:T(8,128)(2,1)S(1)} %bitcast.4, s32[2,4]{1,0:T(2,128)} %radius_hbm.1, s32[2,4,25]{2,1,0:T(4,128)} %pattern_hbm.1, s32[4,8,128]{2,1,0:T(8,128)} %obs_hbm.3), custom_call_target="tpu_custom_call" | custom-call | flops 4000000 | bytes 1000000 | tf_op jit(solution)/shard_map/prepare/pallas_call | solution.py:230
  8.2 0.1 collective-permute-done
  8.3 2.9 %collective-permute-done.1 = bf16[2,128,128]{2,1,0:T(8,128)(2,1)S(1)} collective-permute-done((bf16[2,128,128]{2,1,0:T(8,128)(2,1)S(1)}, bf16[2,128,128]{2,1,0:T(8,128)(2,1)S(1)}, u32[]{:S(2)}, u32[]{:S(2)}) %collective-permute-start.1) | collective-permute-done | bytes 65568 | tf_op jit(solution)/shard_map/ppermute | solution.py:444
  11.2 0.1 collective-permute-start.2
  11.3 0.8 %collective-permute-start.3 = (bf16[2,128,384]{2,1,0:T(8,128)(2,1)S(1)}, bf16[2,128,384]{2,1,0:T(8,128)(2,1)S(1)}, u32[]{:S(2)}, u32[]{:S(2)}) collective-permute-start(bf16[2,128,384]{2,1,0:T(8,128)(2,1)S(1)} %pad_maximum_fusion.own_ref), channel_id=1, source_target_pairs={{0,8},{1,2},{2,1},{3,4},{4,3},{5,6},{6,5},{7,15},{8,0},{9,10},{10,... | collective-permute-start | bytes 589832 | tf_op jit(solution)/shard_map/ppermute | solution.py:487
  12.1 0.6 %collective-permute-done.2.even_ref = bf16[2,128,384]{2,1,0:T(8,128)(2,1)S(1)} collective-permute-done((bf16[2,128,384]{2,1,0:T(8,128)(2,1)S(1)}, bf16[2,128,384]{2,1,0:T(8,128)(2,1)S(1)}, u32[]{:S(2)}, u32[]{:S(2)}) %collective-permute-start.2) | collective-permute-done | bytes 196640 | tf_op jit(solution)/shard_map/ppermute | solution.py:444
  12.7 1.0 %near.1 = (f32[4,128,128]{2,1,0:T(8,128)S(1)}, bf16[2,4,16,128]{3,2,1,0:T(8,128)(2,1)S(1)}, bf16[2,4,16,128]{3,2,1,0:T(8,128)(2,1)S(1)}, bf16[2,4,16,128]{3,2,1,0:T(8,128)(2,1)S(1)}, bf16[2,4,16,128]{3,2,1,0:T(8,128)(2,1)S(1)}) custom-call(bf16[8,128,128]{2,1,0:T(8,128)(2,1)S(1)} %bitcast.5, bf16[8,128,128]{2,1,0:T(8,128)(2,1)S(1)} %get-tuple-element.29.turned_ref, ...), custom_call_target="tpu_custom_call" | custom-call | flops 4000000000 | bytes 10000000 | tf_op jit(solution)/shard_map/near/pallas_call | solution.py:371
  13.8 1.4 %collective-permute-start.4 = (bf16[2,4,16,128]{3,2,1,0:T(8,128)(2,1)S(1)}, bf16[2,4,16,128]{3,2,1,0:T(8,128)(2,1)S(1)}, u32[]{:S(2)}, u32[]{:S(2)}) collective-permute-start(bf16[2,4,16,128]{3,2,1,0:T(8,128)(2,1)S(1)} %get-tuple-element.37), channel_id=1, source_target_pairs={{0,2},{1,3},{2,0},{3,1},{4,6},{5,7},{6,4},{7,5},{8,10},{9,11},{10,... | collective-permute-start | bytes 98312 | tf_op jit(solution)/shard_map/ppermute | solution.py:462
  15.2 2.9 %collective-permute-start.5 = (bf16[2,4,16,128]{3,2,1,0:T(8,128)(2,1)S(1)}, bf16[2,4,16,128]{3,2,1,0:T(8,128)(2,1)S(1)}, u32[]{:S(2)}, u32[]{:S(2)}) collective-permute-start(bf16[2,4,16,128]{3,2,1,0:T(8,128)(2,1)S(1)} %get-tuple-element.38), channel_id=1, source_target_pairs={{0,4},{1,5},{2,6},{3,7},{4,0},{5,1},{6,2},{7,3},{8,12},{9,13},{10,... | collective-permute-start | bytes 98312 | tf_op jit(solution)/shard_map/ppermute | solution.py:462
  18.1 0.0 collective-permute-done.3.odd_ref
  18.1 0.7 %far.1 = (bf16[2,4,16,128]{3,2,1,0:T(8,128)(2,1)S(1)}, bf16[2,4,16,128]{3,2,1,0:T(8,128)(2,1)S(1)}, bf16[2,4,16,128]{3,2,1,0:T(8,128)(2,1)S(1)}, bf16[2,2,4,16,128]{4,3,2,1,0:T(8,128)(2,1)S(1)}) custom-call(bf16[8,128,128]{2,1,0:T(8,128)(2,1)S(1)} %get-tuple-element.29.turned_ref, f32[3,3,8,128]{3,2,1,0:T(8,128)S(1)} %get-tuple-element.30.taper_ref, ...), custom_call_target="tpu_custom_call" | custom-call | flops 4000000000 | bytes 10000000 | tf_op jit(solution)/shard_map/far/pallas_call | solution.py:388
  18.8 2.1 %collective-permute-start.7 = (bf16[2,2,4,16,128]{4,3,2,1,0:T(8,128)(2,1)S(1)}, bf16[2,2,4,16,128]{4,3,2,1,0:T(8,128)(2,1)S(1)}, u32[]{:S(2)}, u32[]{:S(2)}) collective-permute-start(bf16[2,2,4,16,128]{4,3,2,1,0:T(8,128)(2,1)S(1)} %get-tuple-element.41), channel_id=1, source_target_pairs={{0,6},{1,7},{2,4},{3,5},{4,2},{5,3},{6,0},{7,1},{8,14},{9,15},{10,... | collective-permute-start | bytes 196616 | tf_op jit(solution)/shard_map/ppermute | solution.py:462
  20.9 0.0 collective-permute-start.9
  20.9 0.0 collective-permute-done.4.refs_2_.refs_3_
  20.9 0.0 collective-permute-done.5.refs_3_.refs_4_
  20.9 2.3 %collective-permute-start.8 = (bf16[2,4,16,128]{3,2,1,0:T(8,128)(2,1)S(1)}, bf16[2,4,16,128]{3,2,1,0:T(8,128)(2,1)S(1)}, u32[]{:S(2)}, u32[]{:S(2)}) collective-permute-start(bf16[2,4,16,128]{3,2,1,0:T(8,128)(2,1)S(1)} %get-tuple-element.42), channel_id=1, source_target_pairs={{0,2},{1,3},{2,0},{3,1},{4,6},{5,7},{6,4},{7,5},{8,10},{9,11},{10,... | collective-permute-start | bytes 98312 | tf_op jit(solution)/shard_map/ppermute | solution.py:462
  23.3 0.0 collective-permute-start.6
  23.3 2.7 %collective-permute-done.9.refs_2_.refs_4_ = bf16[2,4,16,128]{3,2,1,0:T(8,128)(2,1)S(1)} collective-permute-done((bf16[2,4,16,128]{3,2,1,0:T(8,128)(2,1)S(1)}, bf16[2,4,16,128]{3,2,1,0:T(8,128)(2,1)S(1)}, u32[]{:S(2)}, u32[]{:S(2)}) %collective-permute-start.9) | collective-permute-done | bytes 32800 | tf_op jit(solution)/shard_map/ppermute | solution.py:462
  26.0 0.0 collective-permute-done.8.refs_1_.refs_3_
  26.0 0.0 collective-permute-done.7.refs_0_.refs_2_
  26.0 0.1 collective-permute-start.10
  26.1 0.0 collective-permute-done.6.refs_0_
  26.1 0.2 early.1.refs_0_
  26.3 1.0 %collective-permute-done.10.refs_1_ = bf16[4,4,16,128]{3,2,1,0:T(8,128)(2,1)S(1)} collective-permute-done((bf16[4,4,16,128]{3,2,1,0:T(8,128)(2,1)S(1)}, bf16[4,4,16,128]{3,2,1,0:T(8,128)(2,1)S(1)}, u32[]{:S(2)}, u32[]{:S(2)}) %collective-permute-start.10) | collective-permute-done | bytes 65568 | tf_op jit(solution)/shard_map/ppermute | solution.py:444
  27.3 0.9 %late.1 = (bf16[1024,128]{1,0:T(8,128)(2,1)}, f32[1024,128]{1,0:T(8,128)S(1)}) custom-call(f32[1024,128]{1,0:T(8,128)S(1)} %early.1.refs_0_, bf16[4,4,16,128]{3,2,1,0:T(8,128)(2,1)S(1)} %collective-permute-done.10.refs_1_, bf16[2,2,4,16,128]{4,3,2,1,0:T(8,128)(2,1)S(1)} %collective-permute-done.7.refs_0_.refs_2_, ...), custom_call_target="tpu_custom_call", output_to_operand_aliasing={{1}: (0, {})} | custom-call | tf_op jit(solution)/shard_map/late/pallas_call | solution.py:423
  (4 shorter events, 0.1 us)
Async XLA Ops:
  2.8 5.5 %collective-permute-start = (bf16[2,128,128]{2,1,0:T(8,128)(2,1)S(1)}, bf16[2,128,128]{2,1,0:T(8,128)(2,1)S(1)}, u32[]{:S(2)}, u32[]{:S(2)}) collective-permute-start(bf16[2,128,128]{2,1,0:T(8,128)(2,1)S(1)} %get-tuple-element.26), channel_id=1, source_target_pairs={{0,8},{16,24},{8,0},{24,16},{1,9},{17,25},{9,1},{25,17},{2,10},{18... | collective-permute-start | bytes 196616 | tf_op jit(solution)/shard_map/ppermute | solution.py:444
  6.0 5.2 %collective-permute-start.1 = (bf16[2,128,128]{2,1,0:T(8,128)(2,1)S(1)}, bf16[2,128,128]{2,1,0:T(8,128)(2,1)S(1)}, u32[]{:S(2)}, u32[]{:S(2)}) collective-permute-start(bf16[2,128,128]{2,1,0:T(8,128)(2,1)S(1)} %get-tuple-element.26), channel_id=1, source_target_pairs={{8,16},{24,0},{16,8},{0,24},{9,17},{25,1},{17,9},{1,25},{10,18},{2... | collective-permute-start | bytes 196616 | tf_op jit(solution)/shard_map/ppermute | solution.py:444
  11.2 1.5 %collective-permute-start.2 = (bf16[2,128,384]{2,1,0:T(8,128)(2,1)S(1)}, bf16[2,128,384]{2,1,0:T(8,128)(2,1)S(1)}, u32[]{:S(2)}, u32[]{:S(2)}) collective-permute-start(bf16[2,128,384]{2,1,0:T(8,128)(2,1)S(1)} %pad_maximum_fusion.own_ref), channel_id=1, source_target_pairs={{0,1},{2,3},{4,5},{6,7},{1,0},{3,2},{5,4},{7,6},{8,9},{10,11},{12,... | collective-permute-start | bytes 589832 | tf_op jit(solution)/shard_map/ppermute | solution.py:444
  11.3 6.8 %collective-permute-start.3 = (bf16[2,128,384]{2,1,0:T(8,128)(2,1)S(1)}, bf16[2,128,384]{2,1,0:T(8,128)(2,1)S(1)}, u32[]{:S(2)}, u32[]{:S(2)}) collective-permute-start(bf16[2,128,384]{2,1,0:T(8,128)(2,1)S(1)} %pad_maximum_fusion.own_ref), channel_id=1, source_target_pairs={{0,8},{1,2},{2,1},{3,4},{4,3},{5,6},{6,5},{7,15},{8,0},{9,10},{10,... | collective-permute-start | bytes 589832 | tf_op jit(solution)/shard_map/ppermute | solution.py:487
  13.8 7.1 %collective-permute-start.4 = (bf16[2,4,16,128]{3,2,1,0:T(8,128)(2,1)S(1)}, bf16[2,4,16,128]{3,2,1,0:T(8,128)(2,1)S(1)}, u32[]{:S(2)}, u32[]{:S(2)}) collective-permute-start(bf16[2,4,16,128]{3,2,1,0:T(8,128)(2,1)S(1)} %get-tuple-element.37), channel_id=1, source_target_pairs={{0,2},{1,3},{2,0},{3,1},{4,6},{5,7},{6,4},{7,5},{8,10},{9,11},{10,... | collective-permute-start | bytes 98312 | tf_op jit(solution)/shard_map/ppermute | solution.py:462
  15.2 5.7 %collective-permute-start.5 = (bf16[2,4,16,128]{3,2,1,0:T(8,128)(2,1)S(1)}, bf16[2,4,16,128]{3,2,1,0:T(8,128)(2,1)S(1)}, u32[]{:S(2)}, u32[]{:S(2)}) collective-permute-start(bf16[2,4,16,128]{3,2,1,0:T(8,128)(2,1)S(1)} %get-tuple-element.38), channel_id=1, source_target_pairs={{0,4},{1,5},{2,6},{3,7},{4,0},{5,1},{6,2},{7,3},{8,12},{9,13},{10,... | collective-permute-start | bytes 98312 | tf_op jit(solution)/shard_map/ppermute | solution.py:462
  18.8 7.2 %collective-permute-start.7 = (bf16[2,2,4,16,128]{4,3,2,1,0:T(8,128)(2,1)S(1)}, bf16[2,2,4,16,128]{4,3,2,1,0:T(8,128)(2,1)S(1)}, u32[]{:S(2)}, u32[]{:S(2)}) collective-permute-start(bf16[2,2,4,16,128]{4,3,2,1,0:T(8,128)(2,1)S(1)} %get-tuple-element.41), channel_id=1, source_target_pairs={{0,6},{1,7},{2,4},{3,5},{4,2},{5,3},{6,0},{7,1},{8,14},{9,15},{10,... | collective-permute-start | bytes 196616 | tf_op jit(solution)/shard_map/ppermute | solution.py:462
  20.9 5.1 %collective-permute-start.9 = (bf16[2,4,16,128]{3,2,1,0:T(8,128)(2,1)S(1)}, bf16[2,4,16,128]{3,2,1,0:T(8,128)(2,1)S(1)}, u32[]{:S(2)}, u32[]{:S(2)}) collective-permute-start(bf16[2,4,16,128]{3,2,1,0:T(8,128)(2,1)S(1)} %get-tuple-element.43), channel_id=1, source_target_pairs={{0,4},{1,5},{2,6},{3,7},{4,0},{5,1},{6,2},{7,3},{8,12},{9,13},{10,... | collective-permute-start | bytes 98312 | tf_op jit(solution)/shard_map/ppermute | solution.py:462
  20.9 5.1 %collective-permute-start.8 = (bf16[2,4,16,128]{3,2,1,0:T(8,128)(2,1)S(1)}, bf16[2,4,16,128]{3,2,1,0:T(8,128)(2,1)S(1)}, u32[]{:S(2)}, u32[]{:S(2)}) collective-permute-start(bf16[2,4,16,128]{3,2,1,0:T(8,128)(2,1)S(1)} %get-tuple-element.42), channel_id=1, source_target_pairs={{0,2},{1,3},{2,0},{3,1},{4,6},{5,7},{6,4},{7,5},{8,10},{9,11},{10,... | collective-permute-start | bytes 98312 | tf_op jit(solution)/shard_map/ppermute | solution.py:462
  23.3 2.8 %collective-permute-start.6 = (bf16[4,4,16,128]{3,2,1,0:T(8,128)(2,1)S(1)}, bf16[4,4,16,128]{3,2,1,0:T(8,128)(2,1)S(1)}, u32[]{:S(2)}, u32[]{:S(2)}) collective-permute-start(bf16[4,4,16,128]{3,2,1,0:T(8,128)(2,1)S(1)} %pack.2), channel_id=1, source_target_pairs={{0,1},{2,3},{4,5},{6,7},{1,0},{3,2},{5,4},{7,6},{8,9},{10,11},{12,... | collective-permute-start | bytes 196616 | tf_op jit(solution)/shard_map/ppermute | solution.py:444
  26.0 1.3 %collective-permute-start.10 = (bf16[4,4,16,128]{3,2,1,0:T(8,128)(2,1)S(1)}, bf16[4,4,16,128]{3,2,1,0:T(8,128)(2,1)S(1)}, u32[]{:S(2)}, u32[]{:S(2)}) collective-permute-start(bf16[4,4,16,128]{3,2,1,0:T(8,128)(2,1)S(1)} %pack.3), channel_id=1, source_target_pairs={{0,1},{2,3},{4,5},{6,7},{1,0},{3,2},{5,4},{7,6},{8,9},{10,11},{12,... | collective-permute-start | bytes 196616 | tf_op jit(solution)/shard_map/ppermute | solution.py:444

commit v19 on v16

--- a/solution.py
+++ b/solution.py
@@ -247,15 +247,20 @@
     )(by_block, *in_hbm(taper_radius, taper_pattern, obs_block))
 
 
-def moved(b, which, turned_ref, taper_ref, column_ref):
+def moved(b, which, turned_ref, taper_ref, tiles_refs):
     members = turned_ref.shape[2]
     turned = turned_ref[pl.ds(b, 2)].reshape(2 * CELLS, members)
-    cross = dot(turned, column_ref[0], ((1,), (0,)))
-    gains = []
-    for k in range(2):
-        taper = jnp.concatenate([taper_ref[which, ix, pl.ds(b + k, 1), :] for ix in range(3)], axis=1)
-        gains.append((cross[k * CELLS : (k + 1) * CELLS] * taper).astype(BF16))
-    return dot(column_ref[1], jnp.concatenate(gains, axis=0), ((1,), (1,)))
+    total, first = 0.0, 0
+    for tiles_ref in tiles_refs:
+        count = tiles_ref.shape[2] // OBS_TILE
+        cross = dot(turned, tiles_ref[0], ((1,), (0,)))
+        gains = []
+        for k in range(2):
+            tapers = [taper_ref[which, ix, pl.ds(b + k, 1), :] for ix in range(first, first + count)]
+            gains.append((cross[k * CELLS : (k + 1) * CELLS] * jnp.concatenate(tapers, axis=1)).astype(BF16))
+        total = total + dot(tiles_ref[1], jnp.concatenate(gains, axis=0), ((1,), (1,)))
+        first += count
+    return total
 
 
 def first_of(side, tile_y):
@@ -289,24 +294,25 @@
     tile_y = lax.axis_index("gy")
     for k in range(0, SIDE, 2):
         b = block_of(k, 0, tile_y)
-        delta = moved(b, 0, turned_ref, taper_ref, own_ref) + moved(b, 1, turned_ref, taper_ref, even_ref)
+        delta = moved(b, 0, turned_ref, taper_ref, [own_ref]) + moved(b, 1, turned_ref, taper_ref, [even_ref])
         for j in range(2):
             half = delta[:, j * CELLS : (j + 1) * CELLS]
             put(piece_refs, rows_ref, k + j, (params_ref[b + j].astype(F32) + half).astype(BF16))
     for k in range(0, SIDE, 2):
         b = block_of(k, 1, tile_y)
-        delta = moved(b, 0, turned_ref, taper_ref, own_ref)
+        delta = moved(b, 0, turned_ref, taper_ref, [own_ref])
         for j in range(2):
             part_ref[k + j] = params_ref[b + j].astype(F32) + delta[:, j * CELLS : (j + 1) * CELLS]
 
 
-def far_kernel(turned_ref, taper_ref, odd_ref, part_ref, near_ref, *refs):
-    both_ref, rows_ref = refs[-2], refs[-1]
-    piece_refs = (*refs[:-2], both_ref.at[1])
-    both_ref[0] = near_ref[...]
+def far_kernel(turned_ref, taper_ref, odd_ref, beside_ref, part_ref, first_ref, last_ref, *refs):
+    rows_ref, refs = refs[-1], refs[:-1]
+    piece_refs = [halves(ref)[-1] for ref in refs]
+    refs[1][0] = first_ref[...]
+    refs[-1][0] = last_ref[...]
     tile_y = lax.axis_index("gy")
     for k in range(0, SIDE, 2):
-        delta = moved(block_of(k, 1, tile_y), 2, turned_ref, taper_ref, odd_ref)
+        delta = moved(block_of(k, 1, tile_y), 2, turned_ref, taper_ref, [odd_ref, beside_ref])
         for j in range(2):
             half = delta[:, j * CELLS : (j + 1) * CELLS]
             put(piece_refs, rows_ref, k + j, (part_ref[k + j] + half).astype(BF16))
@@ -341,13 +347,13 @@
 
 
 def early_kernel(chips, *refs):
-    settle(chips, [(0, 0), (1, 0)] + [(0, r) for r in range(1, chips - 1)], refs[:-1], refs[-1])
+    settle(chips, [(0, 0), (1, 0)] + [(0, r) for r in range(2, chips - 1)], refs[:-1], refs[-1])
 
 
 def late_kernel(chips, *refs):
     late_refs, out_hbm, rows_ref, out_ref, sems = refs[1:-4], *refs[-4:]
-    last = chips - 1
-    settle(chips, [(0, last), (1, last)] + [(1, r) for r in range(1, last)], late_refs, rows_ref)
+    sides = [(side, r) for r in range(1, chips) for side in ((0, 1) if r in (1, chips - 1) else (1,))]
+    settle(chips, sides, late_refs, rows_ref)
     pieces = sems.shape[0]
     step = rows_ref.shape[0] // pieces
     copies = []
@@ -380,21 +386,22 @@
     )(by_block, turned, taper, own, even)
 
 
-def update_far(turned, taper, odd, part, near):
+def update_far(turned, taper, odd, beside, part, near):
     members = part.shape[1]
-    parts = members // near[0].shape[2]
+    chips = len(near)
     piece = jax.ShapeDtypeStruct(near[0].shape, BF16)
-    shapes = (piece,) * (parts // 2 - 1) + (jax.ShapeDtypeStruct((2, *piece.shape), BF16),)
+    both = jax.ShapeDtypeStruct((2, *piece.shape), BF16)
+    shapes = [both if r in (1, chips - 1) else piece for r in range(chips)]
     return pl.pallas_call(
         far_kernel,
-        out_shape=shapes,
-        in_specs=[VMEM] * 5,
-        out_specs=(VMEM,) * len(shapes),
+        out_shape=tuple(shapes),
+        in_specs=[VMEM] * 7,
+        out_specs=(VMEM,) * chips,
         scratch_shapes=[pltpu.VMEM((SIDE, members, CELLS), BF16)],
         compiler_params=LIMIT,
         cost_estimate=LONG,
         name="far",
-    )(turned, taper, odd, part, near[-1])
+    )(turned, taper, odd, beside, part, near[1], near[-1])
 
 
 def pack(pieces):
@@ -436,12 +443,23 @@
     return out.reshape(share, BLK_X, 2 * chips * BLK_Y, CELLS)
 
 
-def swap(block, axis, first, close=False):
-    count = lax.axis_size(axis)
-    pairs = [(i, i + 1) for i in range(first, count - 1, 2)]
-    if close:
-        pairs.append((count - 1, 0))
-    return lax.ppermute(block, axis, pairs + [(b, a) for a, b in pairs])
+def swap(block, axis):
+    return lax.ppermute(block, axis, [(i, i ^ 1) for i in range(lax.axis_size(axis))])
+
+
+def swap_odd(block, axis):
+    rows, count = lax.axis_size("gx"), lax.axis_size("gy")
+    pairs = []
+    for x in range(rows):
+        for y in range(count):
+            if axis == "gy":
+                to = (x, y + 1 if y % 2 else y - 1)
+                to = to if 0 <= to[1] < count else (x ^ 1, y)
+            else:
+                to = (x + 1 if x % 2 else x - 1, y)
+                to = to if 0 <= to[0] < rows else (x, y ^ 1)
+            pairs.append((x * count + y, to[0] * count + to[1]))
+    return lax.ppermute(block, ("gx", "gy"), pairs)
 
 
 def hop(piece, r):
@@ -466,25 +484,27 @@
         predicted, measured_value, measurement_variance, observation_jitter, obs_block, params
     )
     by_block = params.reshape(members, BLOCKS, CELLS).transpose(1, 0, 2)
-    even = swap(own, "gx", 0)
-    odd = swap(own, "gx", 1, close=True)
+    sent, by_block = lax.optimization_barrier((own, by_block))
+    across = swap_odd(sent, "gy")
+    even = swap(own, "gx")
+    odd = swap_odd(own, "gx")
     turned, taper = prepare(by_block, taper_radius, taper_pattern, obs_block)
-    column = jnp.concatenate([own, even, odd], axis=2)
-    column, turned, taper = lax.optimization_barrier((column, turned, taper))
-    even = swap(column, "gy", 0)
-    odd = swap(column, "gy", 1)
+    beside, column = jnp.concatenate([even, odd], axis=2), jnp.concatenate([own, even, odd], axis=2)
+    beside, column, across, turned, taper = lax.optimization_barrier((beside, column, across, turned, taper))
+    even = swap(column, "gy")
+    beside = swap_odd(beside, "gy")
     part, *near = update_near(by_block, turned, taper, column, even, parts)
-    last = parts // 2 - 1
-    near_hops = {r: hop(near[r], r) for r in range(1, last)}
-    *far, both = update_far(turned, taper, odd, part, near)
-    if last > 1:
+    chips = parts // 2
+    near_hops = [hop(near[r], r) for r in range(2, chips - 1)]
+    far = list(update_far(turned, taper, across, beside, part, near))
+    if near_hops:
         far[1], near_hops = lax.optimization_barrier((far[1], near_hops))
-    far_hops = {r: hop(far[r], r) for r in range(1, last)}
-    early = [near[0], far[0], *(near_hops[r] for r in range(1, last))]
-    late = [hop(both, last), *(far_hops[r] for r in range(1, last))]
-    late_even = swap(pack(late), "gy", 0)
-    early_even = swap(pack(early), "gy", 0)
-    return gather(parts // 2, early_even, early, late_even, late)
+    early = [near[0], far[0], *near_hops]
+    late = [hop(far[r], r) for r in range(1, chips)]
+    early_even = swap(pack(early), "gy")
+    late, early_even = lax.optimization_barrier((late, early_even))
+    late_even = swap(pack(late), "gy")
+    return gather(chips, early_even, early, late_even, late)
 
 
 def solution(mesh):

time: 30 us -> 27.9 us (0.930)
  starting transfers between devices: 14.5 us -> 13.2 us
  waiting for transfers between devices: 8.36 us -> 7.68 us
    ppermute x5 -> x4, waiting for transfers between devices: 3.62 us -> 2.23 us  [hop(): return lax.ppermute(piece, 'gy', pairs)]
    ppermute x5 -> x4, starting transfers between devices: 9.43 us -> 8.05 us  [hop(): return lax.ppermute(piece, 'gy', pairs)]
    ppermute x6 -> x7, waiting for transfers between devices: 4.73 us -> 5.45 us  [the longest x4 4.15 us: swap(): lax.ppermute(block, axis, [(i, i ^ 1) for i in range(lax.axis_size(axis))])]
    ppermute x6 -> x7, starting transfers between devices: 5.11 us -> 5.17 us  [the longest x4 3.89 us: swap(): lax.ppermute(block, axis, [(i, i ^ 1) for i in range(lax.axis_size(axis))])]
  transfers between devices with their start and end apart: 11 -> 11, of which waited for: 5 -> 7; matrix products, arithmetic and copies ran while one was open for 0% -> 0% of each run, Pallas kernels for 10% -> 10%
where the time goes in v19:
time: 27.9 us; the launch traced here: 27.7 us
  starting transfers between devices  13.2 us (47%)
  waiting for transfers between devices  7.68 us (28%)
  Pallas kernels  6.65 us (24%)
    ppermute x4, starting transfers between devices, hop(): return lax.ppermute(piece, 'gy', pairs)  8.05 us
    ppermute x4, waiting for transfers between devices, swap(): lax.ppermute(block, axis, [(i, i ^ 1) for i in range(lax.axis_size(axis))])  4.15 us
    ppermute x4, starting transfers between devices, swap(): lax.ppermute(block, axis, [(i, i ^ 1) for i in range(lax.axis_size(axis))])  3.89 us
    pallas_call x1, Pallas kernels, weigh(): pl.pallas_call(weigh_kernel, out_shape=(jax.ShapeDtypeStruct((2, members,...  2.81 us
    ppermute x4, waiting for transfers between devices, hop(): return lax.ppermute(piece, 'gy', pairs)  2.23 us
    ppermute x3, waiting for transfers between devices, swap_odd(): return lax.ppermute(block, ('gx', 'gy'), pairs)  1.3 us
    ppermute x3, starting transfers between devices, swap_odd(): return lax.ppermute(block, ('gx', 'gy'), pairs)  1.29 us
    pallas_call x1, Pallas kernels, update_near(): pl.pallas_call(near_kernel, out_shape=(jax.ShapeDtypeStruct((SIDE, member...  1.04 us
  transfers between devices with their start and end apart: 11, of which 7 were waited for; matrix products, arithmetic and copies ran while one was open for 0% of the time, Pallas kernels for 10%

profile of v19, /device:TPU:0, one launch (start us, length us, event | category | flops | bytes accessed | tf_op | source)
XLA Modules:
  0.0 27.7 jit_solution(2299751011975748055)
XLA Ops:
  0.0 2.8 %weigh.1 = (bf16[2,128,128]{2,1,0:T(8,128)(2,1)S(1)}, bf16[128,2,4,128]{3,2,1,0:T(4,128)(2,1)S(1)}) custom-call(f32[1,1,128,128]{3,2,1,0:T(8,128)} %pred_hbm.1, f32[1,1,128]{2,1,0:T(1,128)} %mv_hbm.1, f32[1,1,128]{2,1,0:T(1,128)} %var_hbm.1, f32[1,1,128,128]{3,2,1,0:T(8,128)} %jit_hbm.1, s32[4,8,128]{2,1,0:T(8,128)} %obs_hbm.3, ...), custom_call_target="tpu_custom_call" | custom-call | tf_op jit(solution)/shard_map/weigh/pallas_call | solution.py:157
  2.8 0.6 %collective-permute-start.1 = (bf16[2,128,128]{2,1,0:T(8,128)(2,1)S(1)}, bf16[2,128,128]{2,1,0:T(8,128)(2,1)S(1)}, u32[]{:S(2)}, u32[]{:S(2)}) collective-permute-start(bf16[2,128,128]{2,1,0:T(8,128)(2,1)S(1)} %get-tuple-element.34), channel_id=1, source_target_pairs={{0,1},{1,0},{2,3},{3,2},{4,5},{5,4},{6,7},{7,6},{8,16},{9,17},{10,... | collective-permute-start | bytes 196616 | tf_op jit(solution)/shard_map/ppermute | solution.py:462
  3.4 3.8 %collective-permute-start = (bf16[2,128,128]{2,1,0:T(8,128)(2,1)S(1)}, bf16[2,128,128]{2,1,0:T(8,128)(2,1)S(1)}, u32[]{:S(2)}, u32[]{:S(2)}) collective-permute-start(bf16[2,128,128]{2,1,0:T(8,128)(2,1)S(1)} %get-tuple-element.34), channel_id=1, source_target_pairs={{0,8},{8,0},{16,24},{24,16},{1,9},{9,1},{17,25},{25,17},{2,10},{10... | collective-permute-start | bytes 196616 | tf_op jit(solution)/shard_map/ppermute | solution.py:447
  7.3 0.1 collective-permute-start.2
  7.3 1.0 %prepare.1 = (bf16[8,128,128]{2,1,0:T(8,128)(2,1)S(1)}, f32[3,3,8,128]{3,2,1,0:T(8,128)S(1)}) custom-call(bf16[8,128,128]{2,1,0:T(8,128)(2,1)S(1)} %bitcast.4, s32[2,4]{1,0:T(2,128)} %radius_hbm.1, s32[2,4,25]{2,1,0:T(4,128)} %pattern_hbm.1, s32[4,8,128]{2,1,0:T(8,128)} %obs_hbm.3), custom_call_target="tpu_custom_call" | custom-call | flops 4000000 | bytes 1000000 | tf_op jit(solution)/shard_map/prepare/pallas_call | solution.py:230
  8.3 0.0 collective-permute-done.1
  8.3 2.2 %collective-permute-done = bf16[2,128,128]{2,1,0:T(8,128)(2,1)S(1)} collective-permute-done((bf16[2,128,128]{2,1,0:T(8,128)(2,1)S(1)}, bf16[2,128,128]{2,1,0:T(8,128)(2,1)S(1)}, u32[]{:S(2)}, u32[]{:S(2)}) %collective-permute-start) | collective-permute-done | bytes 65568 | tf_op jit(solution)/shard_map/ppermute | solution.py:447
  10.6 1.0 %collective-permute-done.2.odd_ref = bf16[2,128,128]{2,1,0:T(8,128)(2,1)S(1)} collective-permute-done((bf16[2,128,128]{2,1,0:T(8,128)(2,1)S(1)}, bf16[2,128,128]{2,1,0:T(8,128)(2,1)S(1)}, u32[]{:S(2)}, u32[]{:S(2)}) %collective-permute-start.2) | collective-permute-done | bytes 65568 | tf_op jit(solution)/shard_map/ppermute | solution.py:462
  11.6 0.0 collective-permute-start.4
  11.6 0.6 %collective-permute-start.3 = (bf16[2,128,256]{2,1,0:T(8,128)(2,1)S(1)}, bf16[2,128,256]{2,1,0:T(8,128)(2,1)S(1)}, u32[]{:S(2)}, u32[]{:S(2)}) collective-permute-start(bf16[2,128,256]{2,1,0:T(8,128)(2,1)S(1)} %pad_maximum_fusion.1), channel_id=1, source_target_pairs={{0,8},{1,2},{2,1},{3,4},{4,3},{5,6},{6,5},{7,15},{8,0},{9,10},{10,... | collective-permute-start | bytes 393224 | tf_op jit(solution)/shard_map/ppermute | solution.py:462
  12.2 0.8 %collective-permute-done.4.even_ref = bf16[2,128,384]{2,1,0:T(8,128)(2,1)S(1)} collective-permute-done((bf16[2,128,384]{2,1,0:T(8,128)(2,1)S(1)}, bf16[2,128,384]{2,1,0:T(8,128)(2,1)S(1)}, u32[]{:S(2)}, u32[]{:S(2)}) %collective-permute-start.4) | collective-permute-done | bytes 196640 | tf_op jit(solution)/shard_map/ppermute | solution.py:447
  13.0 1.0 %near.1 = (f32[4,128,128]{2,1,0:T(8,128)S(1)}, bf16[2,4,16,128]{3,2,1,0:T(8,128)(2,1)S(1)}, bf16[2,4,16,128]{3,2,1,0:T(8,128)(2,1)S(1)}, bf16[2,4,16,128]{3,2,1,0:T(8,128)(2,1)S(1)}, bf16[2,4,16,128]{3,2,1,0:T(8,128)(2,1)S(1)}) custom-call(bf16[8,128,128]{2,1,0:T(8,128)(2,1)S(1)} %bitcast.5, bf16[8,128,128]{2,1,0:T(8,128)(2,1)S(1)} %get-tuple-element.38.turned_ref, ...), custom_call_target="tpu_custom_call" | custom-call | flops 4000000000 | bytes 10000000 | tf_op jit(solution)/shard_map/near/pallas_call | solution.py:377
  14.1 2.2 %collective-permute-start.5 = (bf16[2,4,16,128]{3,2,1,0:T(8,128)(2,1)S(1)}, bf16[2,4,16,128]{3,2,1,0:T(8,128)(2,1)S(1)}, u32[]{:S(2)}, u32[]{:S(2)}) collective-permute-start(bf16[2,4,16,128]{3,2,1,0:T(8,128)(2,1)S(1)} %get-tuple-element.47), channel_id=1, source_target_pairs={{0,4},{1,5},{2,6},{3,7},{4,0},{5,1},{6,2},{7,3},{8,12},{9,13},{10,... | collective-permute-start | bytes 98312 | tf_op jit(solution)/shard_map/ppermute | solution.py:468
  16.3 0.3 %collective-permute-done.3.beside_ref = bf16[2,128,256]{2,1,0:T(8,128)(2,1)S(1)} collective-permute-done((bf16[2,128,256]{2,1,0:T(8,128)(2,1)S(1)}, bf16[2,128,256]{2,1,0:T(8,128)(2,1)S(1)}, u32[]{:S(2)}, u32[]{:S(2)}) %collective-permute-start.3) | collective-permute-done | bytes 131104 | tf_op jit(solution)/shard_map/ppermute | solution.py:462
  16.6 0.7 %far.1 = (bf16[2,4,16,128]{3,2,1,0:T(8,128)(2,1)S(1)}, bf16[2,2,4,16,128]{4,3,2,1,0:T(8,128)(2,1)S(1)}, bf16[2,4,16,128]{3,2,1,0:T(8,128)(2,1)S(1)}, bf16[2,2,4,16,128]{4,3,2,1,0:T(8,128)(2,1)S(1)}) custom-call(bf16[8,128,128]{2,1,0:T(8,128)(2,1)S(1)} %get-tuple-element.38.turned_ref, f32[3,3,8,128]{3,2,1,0:T(8,128)S(1)} %get-tuple-element.39.taper_ref, ...), custom_call_target="tpu_custom_call" | custom-call | flops 4000000000 | bytes 10000000 | tf_op jit(solution)/shard_map/far/pallas_call | solution.py:395
  17.2 2.9 %collective-permute-start.8 = (bf16[2,2,4,16,128]{4,3,2,1,0:T(8,128)(2,1)S(1)}, bf16[2,2,4,16,128]{4,3,2,1,0:T(8,128)(2,1)S(1)}, u32[]{:S(2)}, u32[]{:S(2)}) collective-permute-start(bf16[2,2,4,16,128]{4,3,2,1,0:T(8,128)(2,1)S(1)} %get-tuple-element.50), channel_id=1, source_target_pairs={{0,6},{1,7},{2,4},{3,5},{4,2},{5,3},{6,0},{7,1},{8,14},{9,15},{10,... | collective-permute-start | bytes 196616 | tf_op jit(solution)/shard_map/ppermute | solution.py:468
  20.2 0.0 collective-permute-done.5.refs_2_.refs_3_
  20.2 0.0 collective-permute-start.6
  20.2 0.1 collective-permute-start.9
  20.3 2.9 %collective-permute-start.7 = (bf16[2,4,16,128]{3,2,1,0:T(8,128)(2,1)S(1)}, bf16[2,4,16,128]{3,2,1,0:T(8,128)(2,1)S(1)}, u32[]{:S(2)}, u32[]{:S(2)}) collective-permute-start(bf16[2,4,16,128]{3,2,1,0:T(8,128)(2,1)S(1)} %get-tuple-element.49), channel_id=1, source_target_pairs={{0,4},{1,5},{2,6},{3,7},{4,0},{5,1},{6,2},{7,3},{8,12},{9,13},{10,... | collective-permute-start | bytes 98312 | tf_op jit(solution)/shard_map/ppermute | solution.py:468
  23.2 2.1 %collective-permute-done.7.refs_1_.refs_3_ = bf16[2,4,16,128]{3,2,1,0:T(8,128)(2,1)S(1)} collective-permute-done((bf16[2,4,16,128]{3,2,1,0:T(8,128)(2,1)S(1)}, bf16[2,4,16,128]{3,2,1,0:T(8,128)(2,1)S(1)}, u32[]{:S(2)}, u32[]{:S(2)}) %collective-permute-start.7) | collective-permute-done | bytes 32800 | tf_op jit(solution)/shard_map/ppermute | solution.py:468
  25.3 0.0 collective-permute-done.8.refs_2_.refs_4_
  25.3 0.0 collective-permute-done.9.refs_0_
  25.3 0.1 collective-permute-done.6.refs_0_.refs_2_
  25.4 0.0 collective-permute-start.10
  25.5 0.2 early.1.refs_0_
  25.6 1.1 %collective-permute-done.10.refs_1_ = bf16[5,4,16,128]{3,2,1,0:T(8,128)(2,1)S(1)} collective-permute-done((bf16[5,4,16,128]{3,2,1,0:T(8,128)(2,1)S(1)}, bf16[5,4,16,128]{3,2,1,0:T(8,128)(2,1)S(1)}, u32[]{:S(2)}, u32[]{:S(2)}) %collective-permute-start.10) | collective-permute-done | bytes 81952 | tf_op jit(solution)/shard_map/ppermute | solution.py:447
  26.7 1.0 %late.1 = (bf16[1024,128]{1,0:T(8,128)(2,1)}, f32[1024,128]{1,0:T(8,128)S(1)}) custom-call(f32[1024,128]{1,0:T(8,128)S(1)} %early.1.refs_0_, bf16[5,4,16,128]{3,2,1,0:T(8,128)(2,1)S(1)} %collective-permute-done.10.refs_1_, bf16[2,2,4,16,128]{4,3,2,1,0:T(8,128)(2,1)S(1)} %collective-permute-done.6.refs_0_.refs_2_, ...), custom_call_target="tpu_custom_call", output_to_operand_aliasing={{1}: (0, {})} | custom-call | tf_op jit(solution)/shard_map/late/pallas_call | solution.py:430
  (5 shorter events, 0.1 us)
Async XLA Ops:
  2.8 5.5 %collective-permute-start.1 = (bf16[2,128,128]{2,1,0:T(8,128)(2,1)S(1)}, bf16[2,128,128]{2,1,0:T(8,128)(2,1)S(1)}, u32[]{:S(2)}, u32[]{:S(2)}) collective-permute-start(bf16[2,128,128]{2,1,0:T(8,128)(2,1)S(1)} %get-tuple-element.34), channel_id=1, source_target_pairs={{0,1},{1,0},{2,3},{3,2},{4,5},{5,4},{6,7},{7,6},{8,16},{9,17},{10,... | collective-permute-start | bytes 196616 | tf_op jit(solution)/shard_map/ppermute | solution.py:462
  3.4 7.1 %collective-permute-start = (bf16[2,128,128]{2,1,0:T(8,128)(2,1)S(1)}, bf16[2,128,128]{2,1,0:T(8,128)(2,1)S(1)}, u32[]{:S(2)}, u32[]{:S(2)}) collective-permute-start(bf16[2,128,128]{2,1,0:T(8,128)(2,1)S(1)} %get-tuple-element.34), channel_id=1, source_target_pairs={{0,8},{8,0},{16,24},{24,16},{1,9},{9,1},{17,25},{25,17},{2,10},{10... | collective-permute-start | bytes 196616 | tf_op jit(solution)/shard_map/ppermute | solution.py:447
  7.3 4.3 %collective-permute-start.2 = (bf16[2,128,128]{2,1,0:T(8,128)(2,1)S(1)}, bf16[2,128,128]{2,1,0:T(8,128)(2,1)S(1)}, u32[]{:S(2)}, u32[]{:S(2)}) collective-permute-start(bf16[2,128,128]{2,1,0:T(8,128)(2,1)S(1)} %get-tuple-element.34), channel_id=1, source_target_pairs={{0,8},{1,2},{2,1},{3,4},{4,3},{5,6},{6,5},{7,15},{8,0},{9,10},{10,... | collective-permute-start | bytes 196616 | tf_op jit(solution)/shard_map/ppermute | solution.py:462
  11.6 1.4 %collective-permute-start.4 = (bf16[2,128,384]{2,1,0:T(8,128)(2,1)S(1)}, bf16[2,128,384]{2,1,0:T(8,128)(2,1)S(1)}, u32[]{:S(2)}, u32[]{:S(2)}) collective-permute-start(bf16[2,128,384]{2,1,0:T(8,128)(2,1)S(1)} %pad_maximum_fusion.own_ref), channel_id=1, source_target_pairs={{0,1},{1,0},{2,3},{3,2},{4,5},{5,4},{6,7},{7,6},{8,9},{9,8},{10,11... | collective-permute-start | bytes 589832 | tf_op jit(solution)/shard_map/ppermute | solution.py:447
  11.6 5.0 %collective-permute-start.3 = (bf16[2,128,256]{2,1,0:T(8,128)(2,1)S(1)}, bf16[2,128,256]{2,1,0:T(8,128)(2,1)S(1)}, u32[]{:S(2)}, u32[]{:S(2)}) collective-permute-start(bf16[2,128,256]{2,1,0:T(8,128)(2,1)S(1)} %pad_maximum_fusion.1), channel_id=1, source_target_pairs={{0,8},{1,2},{2,1},{3,4},{4,3},{5,6},{6,5},{7,15},{8,0},{9,10},{10,... | collective-permute-start | bytes 393224 | tf_op jit(solution)/shard_map/ppermute | solution.py:462
  14.1 6.1 %collective-permute-start.5 = (bf16[2,4,16,128]{3,2,1,0:T(8,128)(2,1)S(1)}, bf16[2,4,16,128]{3,2,1,0:T(8,128)(2,1)S(1)}, u32[]{:S(2)}, u32[]{:S(2)}) collective-permute-start(bf16[2,4,16,128]{3,2,1,0:T(8,128)(2,1)S(1)} %get-tuple-element.47), channel_id=1, source_target_pairs={{0,4},{1,5},{2,6},{3,7},{4,0},{5,1},{6,2},{7,3},{8,12},{9,13},{10,... | collective-permute-start | bytes 98312 | tf_op jit(solution)/shard_map/ppermute | solution.py:468
  17.2 8.1 %collective-permute-start.8 = (bf16[2,2,4,16,128]{4,3,2,1,0:T(8,128)(2,1)S(1)}, bf16[2,2,4,16,128]{4,3,2,1,0:T(8,128)(2,1)S(1)}, u32[]{:S(2)}, u32[]{:S(2)}) collective-permute-start(bf16[2,2,4,16,128]{4,3,2,1,0:T(8,128)(2,1)S(1)} %get-tuple-element.50), channel_id=1, source_target_pairs={{0,6},{1,7},{2,4},{3,5},{4,2},{5,3},{6,0},{7,1},{8,14},{9,15},{10,... | collective-permute-start | bytes 196616 | tf_op jit(solution)/shard_map/ppermute | solution.py:468
  20.2 5.2 %collective-permute-start.6 = (bf16[2,2,4,16,128]{4,3,2,1,0:T(8,128)(2,1)S(1)}, bf16[2,2,4,16,128]{4,3,2,1,0:T(8,128)(2,1)S(1)}, u32[]{:S(2)}, u32[]{:S(2)}) collective-permute-start(bf16[2,2,4,16,128]{4,3,2,1,0:T(8,128)(2,1)S(1)} %get-tuple-element.48), channel_id=1, source_target_pairs={{0,2},{1,3},{2,0},{3,1},{4,6},{5,7},{6,4},{7,5},{8,10},{9,11},{10,... | collective-permute-start | bytes 196616 | tf_op jit(solution)/shard_map/ppermute | solution.py:468
  20.2 5.1 %collective-permute-start.9 = (bf16[3,4,16,128]{3,2,1,0:T(8,128)(2,1)S(1)}, bf16[3,4,16,128]{3,2,1,0:T(8,128)(2,1)S(1)}, u32[]{:S(2)}, u32[]{:S(2)}) collective-permute-start(bf16[3,4,16,128]{3,2,1,0:T(8,128)(2,1)S(1)} %pack.2), channel_id=1, source_target_pairs={{0,1},{1,0},{2,3},{3,2},{4,5},{5,4},{6,7},{7,6},{8,9},{9,8},{10,11... | collective-permute-start | bytes 147464 | tf_op jit(solution)/shard_map/ppermute | solution.py:447
  20.3 5.0 %collective-permute-start.7 = (bf16[2,4,16,128]{3,2,1,0:T(8,128)(2,1)S(1)}, bf16[2,4,16,128]{3,2,1,0:T(8,128)(2,1)S(1)}, u32[]{:S(2)}, u32[]{:S(2)}) collective-permute-start(bf16[2,4,16,128]{3,2,1,0:T(8,128)(2,1)S(1)} %get-tuple-element.49), channel_id=1, source_target_pairs={{0,4},{1,5},{2,6},{3,7},{4,0},{5,1},{6,2},{7,3},{8,12},{9,13},{10,... | collective-permute-start | bytes 98312 | tf_op jit(solution)/shard_map/ppermute | solution.py:468
  25.4 1.3 %collective-permute-start.10 = (bf16[5,4,16,128]{3,2,1,0:T(8,128)(2,1)S(1)}, bf16[5,4,16,128]{3,2,1,0:T(8,128)(2,1)S(1)}, u32[]{:S(2)}, u32[]{:S(2)}) collective-permute-start(bf16[5,4,16,128]{3,2,1,0:T(8,128)(2,1)S(1)} %pack.3), channel_id=1, source_target_pairs={{0,1},{1,0},{2,3},{3,2},{4,5},{5,4},{6,7},{7,6},{8,9},{9,8},{10,11... | collective-permute-start | bytes 245768 | tf_op jit(solution)/shard_map/ppermute | solution.py:447

commit v20 on v19

--- a/solution.py
+++ b/solution.py
@@ -305,11 +305,10 @@
             part_ref[k + j] = params_ref[b + j].astype(F32) + delta[:, j * CELLS : (j + 1) * CELLS]
 
 
-def far_kernel(turned_ref, taper_ref, odd_ref, beside_ref, part_ref, first_ref, last_ref, *refs):
+def far_kernel(turned_ref, taper_ref, odd_ref, beside_ref, part_ref, near_ref, *refs):
     rows_ref, refs = refs[-1], refs[:-1]
     piece_refs = [halves(ref)[-1] for ref in refs]
-    refs[1][0] = first_ref[...]
-    refs[-1][0] = last_ref[...]
+    refs[-1][0] = near_ref[...]
     tile_y = lax.axis_index("gy")
     for k in range(0, SIDE, 2):
         delta = moved(block_of(k, 1, tile_y), 2, turned_ref, taper_ref, [odd_ref, beside_ref])
@@ -347,12 +346,12 @@
 
 
 def early_kernel(chips, *refs):
-    settle(chips, [(0, 0), (1, 0)] + [(0, r) for r in range(2, chips - 1)], refs[:-1], refs[-1])
+    settle(chips, [(0, 0), (1, 0)] + [(0, r) for r in range(1, chips - 1)], refs[:-1], refs[-1])
 
 
 def late_kernel(chips, *refs):
     late_refs, out_hbm, rows_ref, out_ref, sems = refs[1:-4], *refs[-4:]
-    sides = [(side, r) for r in range(1, chips) for side in ((0, 1) if r in (1, chips - 1) else (1,))]
+    sides = [(side, r) for r in range(1, chips) for side in ((0, 1) if r == chips - 1 else (1,))]
     settle(chips, sides, late_refs, rows_ref)
     pieces = sems.shape[0]
     step = rows_ref.shape[0] // pieces
@@ -391,17 +390,17 @@
     chips = len(near)
     piece = jax.ShapeDtypeStruct(near[0].shape, BF16)
     both = jax.ShapeDtypeStruct((2, *piece.shape), BF16)
-    shapes = [both if r in (1, chips - 1) else piece for r in range(chips)]
+    shapes = [piece] * (chips - 1) + [both]
     return pl.pallas_call(
         far_kernel,
         out_shape=tuple(shapes),
-        in_specs=[VMEM] * 7,
+        in_specs=[VMEM] * 6,
         out_specs=(VMEM,) * chips,
         scratch_shapes=[pltpu.VMEM((SIDE, members, CELLS), BF16)],
         compiler_params=LIMIT,
         cost_estimate=LONG,
         name="far",
-    )(turned, taper, odd, beside, part, near[1], near[-1])
+    )(turned, taper, odd, beside, part, near[-1])
 
 
 def pack(pieces):
@@ -495,15 +494,14 @@
     beside = swap_odd(beside, "gy")
     part, *near = update_near(by_block, turned, taper, column, even, parts)
     chips = parts // 2
-    near_hops = [hop(near[r], r) for r in range(2, chips - 1)]
+    near_hops = [hop(near[r], r) for r in range(1, chips - 1)]
     far = list(update_far(turned, taper, across, beside, part, near))
     if near_hops:
         far[1], near_hops = lax.optimization_barrier((far[1], near_hops))
     early = [near[0], far[0], *near_hops]
     late = [hop(far[r], r) for r in range(1, chips)]
+    late_even = swap(pack(late), "gy")
     early_even = swap(pack(early), "gy")
-    late, early_even = lax.optimization_barrier((late, early_even))
-    late_even = swap(pack(late), "gy")
     return gather(chips, early_even, early, late_even, late)
 
 

time: 27.9 us -> 28.1 us (level)
  starting transfers between devices: 13.2 us -> 13.7 us
    ppermute x4 -> x5, starting transfers between devices: 8.05 us -> 8.36 us  [hop(): return lax.ppermute(piece, 'gy', pairs)]
    ppermute x4 -> x5, waiting for transfers between devices: 2.23 us -> 2.41 us  [hop(): return lax.ppermute(piece, 'gy', pairs)]
  transfers between devices with their start and end apart: 11 -> 12, of which waited for: 7 -> 5; matrix products, arithmetic and copies ran while one was open for 0% -> 0% of each run, Pallas kernels for 10% -> 10%
where the time goes in v20:
time: 28.1 us; the launch traced here: 27.9 us
  starting transfers between devices  13.7 us (49%)
  waiting for transfers between devices  7.49 us (27%)
  Pallas kernels  6.55 us (23%)
    ppermute x5, starting transfers between devices, hop(): return lax.ppermute(piece, 'gy', pairs)  8.36 us
    ppermute x4, starting transfers between devices, swap(): lax.ppermute(block, axis, [(i, i ^ 1) for i in range(lax.axis_size(axis))])  4.05 us
    ppermute x4, waiting for transfers between devices, swap(): lax.ppermute(block, axis, [(i, i ^ 1) for i in range(lax.axis_size(axis))])  3.96 us
    pallas_call x1, Pallas kernels, weigh(): pl.pallas_call(weigh_kernel, out_shape=(jax.ShapeDtypeStruct((2, members,...  2.71 us
    ppermute x5, waiting for transfers between devices, hop(): return lax.ppermute(piece, 'gy', pairs)  2.41 us
    ppermute x3, starting transfers between devices, swap_odd(): return lax.ppermute(block, ('gx', 'gy'), pairs)  1.29 us
    ppermute x3, waiting for transfers between devices, swap_odd(): return lax.ppermute(block, ('gx', 'gy'), pairs)  1.11 us
    pallas_call x1, Pallas kernels, update_near(): pl.pallas_call(near_kernel, out_shape=(jax.ShapeDtypeStruct((SIDE, member...  1.04 us
  transfers between devices with their start and end apart: 12, of which 5 were waited for; matrix products, arithmetic and copies ran while one was open for 0% of the time, Pallas kernels for 10%

profile of v20, /device:TPU:0, one launch (start us, length us, event | category | flops | bytes accessed | tf_op | source)
XLA Modules:
  0.0 27.9 jit_solution(13941394936018984465)
XLA Ops:
  0.0 2.7 %weigh.1 = (bf16[2,128,128]{2,1,0:T(8,128)(2,1)S(1)}, bf16[128,2,4,128]{3,2,1,0:T(4,128)(2,1)S(1)}) custom-call(f32[1,1,128,128]{3,2,1,0:T(8,128)} %pred_hbm.1, f32[1,1,128]{2,1,0:T(1,128)} %mv_hbm.1, f32[1,1,128]{2,1,0:T(1,128)} %var_hbm.1, f32[1,1,128,128]{3,2,1,0:T(8,128)} %jit_hbm.1, s32[4,8,128]{2,1,0:T(8,128)} %obs_hbm.3, ...), custom_call_target="tpu_custom_call" | custom-call | tf_op jit(solution)/shard_map/weigh/pallas_call | solution.py:157
  2.7 0.6 %collective-permute-start.1 = (bf16[2,128,128]{2,1,0:T(8,128)(2,1)S(1)}, bf16[2,128,128]{2,1,0:T(8,128)(2,1)S(1)}, u32[]{:S(2)}, u32[]{:S(2)}) collective-permute-start(bf16[2,128,128]{2,1,0:T(8,128)(2,1)S(1)} %get-tuple-element.32), channel_id=1, source_target_pairs={{0,1},{1,0},{2,3},{3,2},{4,5},{5,4},{6,7},{7,6},{8,16},{9,17},{10,... | collective-permute-start | bytes 196616 | tf_op jit(solution)/shard_map/ppermute | solution.py:461
  3.3 4.0 %collective-permute-start = (bf16[2,128,128]{2,1,0:T(8,128)(2,1)S(1)}, bf16[2,128,128]{2,1,0:T(8,128)(2,1)S(1)}, u32[]{:S(2)}, u32[]{:S(2)}) collective-permute-start(bf16[2,128,128]{2,1,0:T(8,128)(2,1)S(1)} %get-tuple-element.32), channel_id=1, source_target_pairs={{0,8},{8,0},{16,24},{24,16},{1,9},{9,1},{17,25},{25,17},{2,10},{10... | collective-permute-start | bytes 196616 | tf_op jit(solution)/shard_map/ppermute | solution.py:446
  7.4 0.1 collective-permute-start.2
  7.4 1.0 %prepare.1 = (bf16[8,128,128]{2,1,0:T(8,128)(2,1)S(1)}, f32[3,3,8,128]{3,2,1,0:T(8,128)S(1)}) custom-call(bf16[8,128,128]{2,1,0:T(8,128)(2,1)S(1)} %bitcast.4, s32[2,4]{1,0:T(2,128)} %radius_hbm.1, s32[2,4,25]{2,1,0:T(4,128)} %pattern_hbm.1, s32[4,8,128]{2,1,0:T(8,128)} %obs_hbm.3), custom_call_target="tpu_custom_call" | custom-call | flops 4000000 | bytes 1000000 | tf_op jit(solution)/shard_map/prepare/pallas_call | solution.py:230
  8.4 0.0 collective-permute-done.1
  8.4 2.1 %collective-permute-done = bf16[2,128,128]{2,1,0:T(8,128)(2,1)S(1)} collective-permute-done((bf16[2,128,128]{2,1,0:T(8,128)(2,1)S(1)}, bf16[2,128,128]{2,1,0:T(8,128)(2,1)S(1)}, u32[]{:S(2)}, u32[]{:S(2)}) %collective-permute-start) | collective-permute-done | bytes 65568 | tf_op jit(solution)/shard_map/ppermute | solution.py:446
  10.6 1.1 %collective-permute-done.2.odd_ref = bf16[2,128,128]{2,1,0:T(8,128)(2,1)S(1)} collective-permute-done((bf16[2,128,128]{2,1,0:T(8,128)(2,1)S(1)}, bf16[2,128,128]{2,1,0:T(8,128)(2,1)S(1)}, u32[]{:S(2)}, u32[]{:S(2)}) %collective-permute-start.2) | collective-permute-done | bytes 65568 | tf_op jit(solution)/shard_map/ppermute | solution.py:461
  11.7 0.0 collective-permute-start.3
  11.7 0.6 %collective-permute-start.4 = (bf16[2,128,256]{2,1,0:T(8,128)(2,1)S(1)}, bf16[2,128,256]{2,1,0:T(8,128)(2,1)S(1)}, u32[]{:S(2)}, u32[]{:S(2)}) collective-permute-start(bf16[2,128,256]{2,1,0:T(8,128)(2,1)S(1)} %pad_maximum_fusion.1), channel_id=1, source_target_pairs={{0,8},{1,2},{2,1},{3,4},{4,3},{5,6},{6,5},{7,15},{8,0},{9,10},{10,... | collective-permute-start | bytes 393224 | tf_op jit(solution)/shard_map/ppermute | solution.py:461
  12.3 0.8 %collective-permute-done.3.even_ref = bf16[2,128,384]{2,1,0:T(8,128)(2,1)S(1)} collective-permute-done((bf16[2,128,384]{2,1,0:T(8,128)(2,1)S(1)}, bf16[2,128,384]{2,1,0:T(8,128)(2,1)S(1)}, u32[]{:S(2)}, u32[]{:S(2)}) %collective-permute-start.3) | collective-permute-done | bytes 196640 | tf_op jit(solution)/shard_map/ppermute | solution.py:446
  13.1 1.0 %near.1 = (f32[4,128,128]{2,1,0:T(8,128)S(1)}, bf16[2,4,16,128]{3,2,1,0:T(8,128)(2,1)S(1)}, bf16[2,4,16,128]{3,2,1,0:T(8,128)(2,1)S(1)}, bf16[2,4,16,128]{3,2,1,0:T(8,128)(2,1)S(1)}, bf16[2,4,16,128]{3,2,1,0:T(8,128)(2,1)S(1)}) custom-call(bf16[8,128,128]{2,1,0:T(8,128)(2,1)S(1)} %bitcast.5, bf16[8,128,128]{2,1,0:T(8,128)(2,1)S(1)} %get-tuple-element.35.turned_ref, ...), custom_call_target="tpu_custom_call" | custom-call | flops 4000000000 | bytes 10000000 | tf_op jit(solution)/shard_map/near/pallas_call | solution.py:376
  14.2 1.1 %collective-permute-start.5 = (bf16[2,4,16,128]{3,2,1,0:T(8,128)(2,1)S(1)}, bf16[2,4,16,128]{3,2,1,0:T(8,128)(2,1)S(1)}, u32[]{:S(2)}, u32[]{:S(2)}) collective-permute-start(bf16[2,4,16,128]{3,2,1,0:T(8,128)(2,1)S(1)} %get-tuple-element.45), channel_id=1, source_target_pairs={{0,2},{1,3},{2,0},{3,1},{4,6},{5,7},{6,4},{7,5},{8,10},{9,11},{10,... | collective-permute-start | bytes 98312 | tf_op jit(solution)/shard_map/ppermute | solution.py:467
  15.3 2.8 %collective-permute-start.6 = (bf16[2,4,16,128]{3,2,1,0:T(8,128)(2,1)S(1)}, bf16[2,4,16,128]{3,2,1,0:T(8,128)(2,1)S(1)}, u32[]{:S(2)}, u32[]{:S(2)}) collective-permute-start(bf16[2,4,16,128]{3,2,1,0:T(8,128)(2,1)S(1)} %get-tuple-element.46), channel_id=1, source_target_pairs={{0,4},{1,5},{2,6},{3,7},{4,0},{5,1},{6,2},{7,3},{8,12},{9,13},{10,... | collective-permute-start | bytes 98312 | tf_op jit(solution)/shard_map/ppermute | solution.py:467
  18.1 0.0 collective-permute-done.4.beside_ref
  18.1 0.7 %far.1 = (bf16[2,4,16,128]{3,2,1,0:T(8,128)(2,1)S(1)}, bf16[2,4,16,128]{3,2,1,0:T(8,128)(2,1)S(1)}, bf16[2,4,16,128]{3,2,1,0:T(8,128)(2,1)S(1)}, bf16[2,2,4,16,128]{4,3,2,1,0:T(8,128)(2,1)S(1)}) custom-call(bf16[8,128,128]{2,1,0:T(8,128)(2,1)S(1)} %get-tuple-element.35.turned_ref, f32[3,3,8,128]{3,2,1,0:T(8,128)S(1)} %get-tuple-element.36.taper_ref, ...), custom_call_target="tpu_custom_call" | custom-call | flops 4000000000 | bytes 10000000 | tf_op jit(solution)/shard_map/far/pallas_call | solution.py:394
  18.8 1.4 %collective-permute-start.10 = (bf16[2,2,4,16,128]{4,3,2,1,0:T(8,128)(2,1)S(1)}, bf16[2,2,4,16,128]{4,3,2,1,0:T(8,128)(2,1)S(1)}, u32[]{:S(2)}, u32[]{:S(2)}) collective-permute-start(bf16[2,2,4,16,128]{4,3,2,1,0:T(8,128)(2,1)S(1)} %get-tuple-element.51), channel_id=1, source_target_pairs={{0,6},{1,7},{2,4},{3,5},{4,2},{5,3},{6,0},{7,1},{8,14},{9,15},{10,... | collective-permute-start | bytes 196616 | tf_op jit(solution)/shard_map/ppermute | solution.py:467
  20.2 0.4 %collective-permute-start.9 = (bf16[2,4,16,128]{3,2,1,0:T(8,128)(2,1)S(1)}, bf16[2,4,16,128]{3,2,1,0:T(8,128)(2,1)S(1)}, u32[]{:S(2)}, u32[]{:S(2)}) collective-permute-start(bf16[2,4,16,128]{3,2,1,0:T(8,128)(2,1)S(1)} %get-tuple-element.50), channel_id=1, source_target_pairs={{0,4},{1,5},{2,6},{3,7},{4,0},{5,1},{6,2},{7,3},{8,12},{9,13},{10,... | collective-permute-start | bytes 98312 | tf_op jit(solution)/shard_map/ppermute | solution.py:467
  20.6 0.0 collective-permute-done.5.refs_2_.refs_3_
  20.6 0.0 collective-permute-done.6.refs_3_.refs_4_
  20.6 2.6 %collective-permute-start.8 = (bf16[2,4,16,128]{3,2,1,0:T(8,128)(2,1)S(1)}, bf16[2,4,16,128]{3,2,1,0:T(8,128)(2,1)S(1)}, u32[]{:S(2)}, u32[]{:S(2)}) collective-permute-start(bf16[2,4,16,128]{3,2,1,0:T(8,128)(2,1)S(1)} %get-tuple-element.49), channel_id=1, source_target_pairs={{0,2},{1,3},{2,0},{3,1},{4,6},{5,7},{6,4},{7,5},{8,10},{9,11},{10,... | collective-permute-start | bytes 98312 | tf_op jit(solution)/shard_map/ppermute | solution.py:467
  23.2 0.0 collective-permute-start.7
  23.2 2.4 %collective-permute-done.9.refs_1_.refs_3_ = bf16[2,4,16,128]{3,2,1,0:T(8,128)(2,1)S(1)} collective-permute-done((bf16[2,4,16,128]{3,2,1,0:T(8,128)(2,1)S(1)}, bf16[2,4,16,128]{3,2,1,0:T(8,128)(2,1)S(1)}, u32[]{:S(2)}, u32[]{:S(2)}) %collective-permute-start.9) | collective-permute-done | bytes 32800 | tf_op jit(solution)/shard_map/ppermute | solution.py:467
  25.6 0.0 collective-permute-done.8.refs_0_.refs_2_
  25.6 0.0 collective-permute-done.10.refs_2_.refs_4_
  25.7 0.1 collective-permute-start.11
  25.7 0.0 collective-permute-done.7.refs_0_
  25.7 0.2 early.1.refs_0_
  26.0 1.0 %collective-permute-done.11.refs_1_ = bf16[4,4,16,128]{3,2,1,0:T(8,128)(2,1)S(1)} collective-permute-done((bf16[4,4,16,128]{3,2,1,0:T(8,128)(2,1)S(1)}, bf16[4,4,16,128]{3,2,1,0:T(8,128)(2,1)S(1)}, u32[]{:S(2)}, u32[]{:S(2)}) %collective-permute-start.11) | collective-permute-done | bytes 65568 | tf_op jit(solution)/shard_map/ppermute | solution.py:446
  27.0 0.9 %late.1 = (bf16[1024,128]{1,0:T(8,128)(2,1)}, f32[1024,128]{1,0:T(8,128)S(1)}) custom-call(f32[1024,128]{1,0:T(8,128)S(1)} %early.1.refs_0_, bf16[4,4,16,128]{3,2,1,0:T(8,128)(2,1)S(1)} %collective-permute-done.11.refs_1_, bf16[2,4,16,128]{3,2,1,0:T(8,128)(2,1)S(1)} %collective-permute-done.8.refs_0_.refs_2_, ...), custom_call_target="tpu_custom_call", output_to_operand_aliasing={{1}: (0, {})} | custom-call | tf_op jit(solution)/shard_map/late/pallas_call | solution.py:429
  (5 shorter events, 0.1 us)
Async XLA Ops:
  2.7 5.7 %collective-permute-start.1 = (bf16[2,128,128]{2,1,0:T(8,128)(2,1)S(1)}, bf16[2,128,128]{2,1,0:T(8,128)(2,1)S(1)}, u32[]{:S(2)}, u32[]{:S(2)}) collective-permute-start(bf16[2,128,128]{2,1,0:T(8,128)(2,1)S(1)} %get-tuple-element.32), channel_id=1, source_target_pairs={{0,1},{1,0},{2,3},{3,2},{4,5},{5,4},{6,7},{7,6},{8,16},{9,17},{10,... | collective-permute-start | bytes 196616 | tf_op jit(solution)/shard_map/ppermute | solution.py:461
  3.3 7.2 %collective-permute-start = (bf16[2,128,128]{2,1,0:T(8,128)(2,1)S(1)}, bf16[2,128,128]{2,1,0:T(8,128)(2,1)S(1)}, u32[]{:S(2)}, u32[]{:S(2)}) collective-permute-start(bf16[2,128,128]{2,1,0:T(8,128)(2,1)S(1)} %get-tuple-element.32), channel_id=1, source_target_pairs={{0,8},{8,0},{16,24},{24,16},{1,9},{9,1},{17,25},{25,17},{2,10},{10... | collective-permute-start | bytes 196616 | tf_op jit(solution)/shard_map/ppermute | solution.py:446
  7.4 4.3 %collective-permute-start.2 = (bf16[2,128,128]{2,1,0:T(8,128)(2,1)S(1)}, bf16[2,128,128]{2,1,0:T(8,128)(2,1)S(1)}, u32[]{:S(2)}, u32[]{:S(2)}) collective-permute-start(bf16[2,128,128]{2,1,0:T(8,128)(2,1)S(1)} %get-tuple-element.32), channel_id=1, source_target_pairs={{0,8},{1,2},{2,1},{3,4},{4,3},{5,6},{6,5},{7,15},{8,0},{9,10},{10,... | collective-permute-start | bytes 196616 | tf_op jit(solution)/shard_map/ppermute | solution.py:461
  11.7 1.4 %collective-permute-start.3 = (bf16[2,128,384]{2,1,0:T(8,128)(2,1)S(1)}, bf16[2,128,384]{2,1,0:T(8,128)(2,1)S(1)}, u32[]{:S(2)}, u32[]{:S(2)}) collective-permute-start(bf16[2,128,384]{2,1,0:T(8,128)(2,1)S(1)} %pad_maximum_fusion.own_ref), channel_id=1, source_target_pairs={{0,1},{1,0},{2,3},{3,2},{4,5},{5,4},{6,7},{7,6},{8,9},{9,8},{10,11... | collective-permute-start | bytes 589832 | tf_op jit(solution)/shard_map/ppermute | solution.py:446
  11.7 6.4 %collective-permute-start.4 = (bf16[2,128,256]{2,1,0:T(8,128)(2,1)S(1)}, bf16[2,128,256]{2,1,0:T(8,128)(2,1)S(1)}, u32[]{:S(2)}, u32[]{:S(2)}) collective-permute-start(bf16[2,128,256]{2,1,0:T(8,128)(2,1)S(1)} %pad_maximum_fusion.1), channel_id=1, source_target_pairs={{0,8},{1,2},{2,1},{3,4},{4,3},{5,6},{6,5},{7,15},{8,0},{9,10},{10,... | collective-permute-start | bytes 393224 | tf_op jit(solution)/shard_map/ppermute | solution.py:461
  14.2 6.4 %collective-permute-start.5 = (bf16[2,4,16,128]{3,2,1,0:T(8,128)(2,1)S(1)}, bf16[2,4,16,128]{3,2,1,0:T(8,128)(2,1)S(1)}, u32[]{:S(2)}, u32[]{:S(2)}) collective-permute-start(bf16[2,4,16,128]{3,2,1,0:T(8,128)(2,1)S(1)} %get-tuple-element.45), channel_id=1, source_target_pairs={{0,2},{1,3},{2,0},{3,1},{4,6},{5,7},{6,4},{7,5},{8,10},{9,11},{10,... | collective-permute-start | bytes 98312 | tf_op jit(solution)/shard_map/ppermute | solution.py:467
  15.3 5.3 %collective-permute-start.6 = (bf16[2,4,16,128]{3,2,1,0:T(8,128)(2,1)S(1)}, bf16[2,4,16,128]{3,2,1,0:T(8,128)(2,1)S(1)}, u32[]{:S(2)}, u32[]{:S(2)}) collective-permute-start(bf16[2,4,16,128]{3,2,1,0:T(8,128)(2,1)S(1)} %get-tuple-element.46), channel_id=1, source_target_pairs={{0,4},{1,5},{2,6},{3,7},{4,0},{5,1},{6,2},{7,3},{8,12},{9,13},{10,... | collective-permute-start | bytes 98312 | tf_op jit(solution)/shard_map/ppermute | solution.py:467
  18.8 6.9 %collective-permute-start.10 = (bf16[2,2,4,16,128]{4,3,2,1,0:T(8,128)(2,1)S(1)}, bf16[2,2,4,16,128]{4,3,2,1,0:T(8,128)(2,1)S(1)}, u32[]{:S(2)}, u32[]{:S(2)}) collective-permute-start(bf16[2,2,4,16,128]{4,3,2,1,0:T(8,128)(2,1)S(1)} %get-tuple-element.51), channel_id=1, source_target_pairs={{0,6},{1,7},{2,4},{3,5},{4,2},{5,3},{6,0},{7,1},{8,14},{9,15},{10,... | collective-permute-start | bytes 196616 | tf_op jit(solution)/shard_map/ppermute | solution.py:467
  20.2 5.5 %collective-permute-start.9 = (bf16[2,4,16,128]{3,2,1,0:T(8,128)(2,1)S(1)}, bf16[2,4,16,128]{3,2,1,0:T(8,128)(2,1)S(1)}, u32[]{:S(2)}, u32[]{:S(2)}) collective-permute-start(bf16[2,4,16,128]{3,2,1,0:T(8,128)(2,1)S(1)} %get-tuple-element.50), channel_id=1, source_target_pairs={{0,4},{1,5},{2,6},{3,7},{4,0},{5,1},{6,2},{7,3},{8,12},{9,13},{10,... | collective-permute-start | bytes 98312 | tf_op jit(solution)/shard_map/ppermute | solution.py:467
  20.6 5.0 %collective-permute-start.8 = (bf16[2,4,16,128]{3,2,1,0:T(8,128)(2,1)S(1)}, bf16[2,4,16,128]{3,2,1,0:T(8,128)(2,1)S(1)}, u32[]{:S(2)}, u32[]{:S(2)}) collective-permute-start(bf16[2,4,16,128]{3,2,1,0:T(8,128)(2,1)S(1)} %get-tuple-element.49), channel_id=1, source_target_pairs={{0,2},{1,3},{2,0},{3,1},{4,6},{5,7},{6,4},{7,5},{8,10},{9,11},{10,... | collective-permute-start | bytes 98312 | tf_op jit(solution)/shard_map/ppermute | solution.py:467
  23.2 2.5 %collective-permute-start.7 = (bf16[4,4,16,128]{3,2,1,0:T(8,128)(2,1)S(1)}, bf16[4,4,16,128]{3,2,1,0:T(8,128)(2,1)S(1)}, u32[]{:S(2)}, u32[]{:S(2)}) collective-permute-start(bf16[4,4,16,128]{3,2,1,0:T(8,128)(2,1)S(1)} %pack.2), channel_id=1, source_target_pairs={{0,1},{1,0},{2,3},{3,2},{4,5},{5,4},{6,7},{7,6},{8,9},{9,8},{10,11... | collective-permute-start | bytes 196616 | tf_op jit(solution)/shard_map/ppermute | solution.py:446
  25.7 1.3 %collective-permute-start.11 = (bf16[4,4,16,128]{3,2,1,0:T(8,128)(2,1)S(1)}, bf16[4,4,16,128]{3,2,1,0:T(8,128)(2,1)S(1)}, u32[]{:S(2)}, u32[]{:S(2)}) collective-permute-start(bf16[4,4,16,128]{3,2,1,0:T(8,128)(2,1)S(1)} %pack.3), channel_id=1, source_target_pairs={{0,1},{1,0},{2,3},{3,2},{4,5},{5,4},{6,7},{7,6},{8,9},{9,8},{10,11... | collective-permute-start | bytes 196616 | tf_op jit(solution)/shard_map/ppermute | solution.py:446

commit v21 on v19

--- a/solution.py
+++ b/solution.py
@@ -279,6 +279,10 @@
     return chip ^ r if chips & (chips - 1) == 0 else (chip + chips - r) % chips
 
 
+def early_rounds(chips):
+    return max(1, chips // 2)
+
+
 def put(piece_refs, rows_ref, k, updated):
     chips, share = len(piece_refs), piece_refs[0].shape[2]
     mine = lax.axis_index("gy")
@@ -305,11 +309,11 @@
             part_ref[k + j] = params_ref[b + j].astype(F32) + delta[:, j * CELLS : (j + 1) * CELLS]
 
 
-def far_kernel(turned_ref, taper_ref, odd_ref, beside_ref, part_ref, first_ref, last_ref, *refs):
-    rows_ref, refs = refs[-1], refs[:-1]
+def far_kernel(late, turned_ref, taper_ref, odd_ref, beside_ref, part_ref, *refs):
+    near_refs, refs, rows_ref = refs[:late], refs[late:-1], refs[-1]
     piece_refs = [halves(ref)[-1] for ref in refs]
-    refs[1][0] = first_ref[...]
-    refs[-1][0] = last_ref[...]
+    for near_ref, both_ref in zip(near_refs, refs[-late:]):
+        both_ref[0] = near_ref[...]
     tile_y = lax.axis_index("gy")
     for k in range(0, SIDE, 2):
         delta = moved(block_of(k, 1, tile_y), 2, turned_ref, taper_ref, [odd_ref, beside_ref])
@@ -347,12 +351,12 @@
 
 
 def early_kernel(chips, *refs):
-    settle(chips, [(0, 0), (1, 0)] + [(0, r) for r in range(2, chips - 1)], refs[:-1], refs[-1])
+    settle(chips, [(0, 0), (1, 0)] + [(0, r) for r in range(1, early_rounds(chips))], refs[:-1], refs[-1])
 
 
 def late_kernel(chips, *refs):
     late_refs, out_hbm, rows_ref, out_ref, sems = refs[1:-4], *refs[-4:]
-    sides = [(side, r) for r in range(1, chips) for side in ((0, 1) if r in (1, chips - 1) else (1,))]
+    sides = [(side, r) for r in range(chips - 1, 0, -1) for side in ((0, 1) if r >= early_rounds(chips) else (1,))]
     settle(chips, sides, late_refs, rows_ref)
     pieces = sems.shape[0]
     step = rows_ref.shape[0] // pieces
@@ -391,17 +395,18 @@
     chips = len(near)
     piece = jax.ShapeDtypeStruct(near[0].shape, BF16)
     both = jax.ShapeDtypeStruct((2, *piece.shape), BF16)
-    shapes = [both if r in (1, chips - 1) else piece for r in range(chips)]
+    late = chips - early_rounds(chips)
+    shapes = [piece] * early_rounds(chips) + [both] * late
     return pl.pallas_call(
-        far_kernel,
+        functools.partial(far_kernel, late),
         out_shape=tuple(shapes),
-        in_specs=[VMEM] * 7,
+        in_specs=[VMEM] * (5 + late),
         out_specs=(VMEM,) * chips,
         scratch_shapes=[pltpu.VMEM((SIDE, members, CELLS), BF16)],
         compiler_params=LIMIT,
         cost_estimate=LONG,
         name="far",
-    )(turned, taper, odd, beside, part, near[1], near[-1])
+    )(turned, taper, odd, beside, part, *near[-late:])
 
 
 def pack(pieces):
@@ -495,12 +500,12 @@
     beside = swap_odd(beside, "gy")
     part, *near = update_near(by_block, turned, taper, column, even, parts)
     chips = parts // 2
-    near_hops = [hop(near[r], r) for r in range(2, chips - 1)]
+    near_hops = [hop(near[r], r) for r in range(1, early_rounds(chips))]
     far = list(update_far(turned, taper, across, beside, part, near))
     if near_hops:
         far[1], near_hops = lax.optimization_barrier((far[1], near_hops))
     early = [near[0], far[0], *near_hops]
-    late = [hop(far[r], r) for r in range(1, chips)]
+    late = [hop(far[r], r) for r in range(chips - 1, 0, -1)]
     early_even = swap(pack(early), "gy")
     late, early_even = lax.optimization_barrier((late, early_even))
     late_even = swap(pack(late), "gy")

time: 27.9 us -> 28.6 us (1.025)
  waiting for transfers between devices: 7.68 us -> 10.6 us
  starting transfers between devices: 13.2 us -> 11.1 us
    ppermute x4, starting transfers between devices: 8.05 us -> 5.68 us  [hop(): return lax.ppermute(piece, 'gy', pairs)]
    ppermute x4, waiting for transfers between devices: 2.23 us -> 4.18 us  [hop(): return lax.ppermute(piece, 'gy', pairs)]
    ppermute x3, waiting for transfers between devices: 1.3 us -> 2.32 us  [swap_odd(): return lax.ppermute(block, ('gx', 'gy'), pairs)]
    ppermute x3, starting transfers between devices: 1.29 us -> 1.8 us  [swap_odd(): return lax.ppermute(block, ('gx', 'gy'), pairs)]
where the time goes in v21:
time: 28.6 us; the launch traced here: 28.4 us
  starting transfers between devices  11.1 us (39%)
  waiting for transfers between devices  10.6 us (37%)
  Pallas kernels  6.44 us (23%)
    ppermute x4, starting transfers between devices, hop(): return lax.ppermute(piece, 'gy', pairs)  5.68 us
    ppermute x4, waiting for transfers between devices, hop(): return lax.ppermute(piece, 'gy', pairs)  4.18 us
    ppermute x4, waiting for transfers between devices, swap(): lax.ppermute(block, axis, [(i, i ^ 1) for i in range(lax.axis_size(axis))])  4.15 us
    ppermute x4, starting transfers between devices, swap(): lax.ppermute(block, axis, [(i, i ^ 1) for i in range(lax.axis_size(axis))])  3.62 us
    pallas_call x1, Pallas kernels, weigh(): pl.pallas_call(weigh_kernel, out_shape=(jax.ShapeDtypeStruct((2, members,...  2.61 us
    ppermute x3, waiting for transfers between devices, swap_odd(): return lax.ppermute(block, ('gx', 'gy'), pairs)  2.32 us
    ppermute x3, starting transfers between devices, swap_odd(): return lax.ppermute(block, ('gx', 'gy'), pairs)  1.8 us
    pallas_call x1, Pallas kernels, update_near(): pl.pallas_call(near_kernel, out_shape=(jax.ShapeDtypeStruct((SIDE, member...  1.04 us
  transfers between devices with their start and end apart: 11, of which 7 were waited for; matrix products, arithmetic and copies ran while one was open for 0% of the time, Pallas kernels for 10%

profile of v21, /device:TPU:0, one launch (start us, length us, event | category | flops | bytes accessed | tf_op | source)
XLA Modules:
  0.0 28.4 jit_solution(5422415521301637091)
XLA Ops:
  0.0 2.6 %weigh.1 = (bf16[2,128,128]{2,1,0:T(8,128)(2,1)S(1)}, bf16[128,2,4,128]{3,2,1,0:T(4,128)(2,1)S(1)}) custom-call(f32[1,1,128,128]{3,2,1,0:T(8,128)} %pred_hbm.1, f32[1,1,128]{2,1,0:T(1,128)} %mv_hbm.1, f32[1,1,128]{2,1,0:T(1,128)} %var_hbm.1, f32[1,1,128,128]{3,2,1,0:T(8,128)} %jit_hbm.1, s32[4,8,128]{2,1,0:T(8,128)} %obs_hbm.3, ...), custom_call_target="tpu_custom_call" | custom-call | tf_op jit(solution)/shard_map/weigh/pallas_call | solution.py:157
  2.6 1.1 %collective-permute-start.1 = (bf16[2,128,128]{2,1,0:T(8,128)(2,1)S(1)}, bf16[2,128,128]{2,1,0:T(8,128)(2,1)S(1)}, u32[]{:S(2)}, u32[]{:S(2)}) collective-permute-start(bf16[2,128,128]{2,1,0:T(8,128)(2,1)S(1)} %get-tuple-element.34), channel_id=1, source_target_pairs={{0,1},{1,0},{2,3},{3,2},{4,5},{5,4},{6,7},{7,6},{8,16},{9,17},{10,... | collective-permute-start | bytes 196616 | tf_op jit(solution)/shard_map/ppermute | solution.py:467
  3.8 3.5 %collective-permute-start = (bf16[2,128,128]{2,1,0:T(8,128)(2,1)S(1)}, bf16[2,128,128]{2,1,0:T(8,128)(2,1)S(1)}, u32[]{:S(2)}, u32[]{:S(2)}) collective-permute-start(bf16[2,128,128]{2,1,0:T(8,128)(2,1)S(1)} %get-tuple-element.34), channel_id=1, source_target_pairs={{0,8},{8,0},{16,24},{24,16},{1,9},{9,1},{17,25},{25,17},{2,10},{10... | collective-permute-start | bytes 196616 | tf_op jit(solution)/shard_map/ppermute | solution.py:452
  7.3 0.1 collective-permute-start.2
  7.3 1.0 %prepare.1 = (bf16[8,128,128]{2,1,0:T(8,128)(2,1)S(1)}, f32[3,3,8,128]{3,2,1,0:T(8,128)S(1)}) custom-call(bf16[8,128,128]{2,1,0:T(8,128)(2,1)S(1)} %bitcast.4, s32[2,4]{1,0:T(2,128)} %radius_hbm.1, s32[2,4,25]{2,1,0:T(4,128)} %pattern_hbm.1, s32[4,8,128]{2,1,0:T(8,128)} %obs_hbm.3), custom_call_target="tpu_custom_call" | custom-call | flops 4000000 | bytes 1000000 | tf_op jit(solution)/shard_map/prepare/pallas_call | solution.py:230
  8.3 0.0 collective-permute-done.1
  8.3 2.2 %collective-permute-done = bf16[2,128,128]{2,1,0:T(8,128)(2,1)S(1)} collective-permute-done((bf16[2,128,128]{2,1,0:T(8,128)(2,1)S(1)}, bf16[2,128,128]{2,1,0:T(8,128)(2,1)S(1)}, u32[]{:S(2)}, u32[]{:S(2)}) %collective-permute-start) | collective-permute-done | bytes 65568 | tf_op jit(solution)/shard_map/ppermute | solution.py:452
  10.6 1.0 %collective-permute-done.2.odd_ref = bf16[2,128,128]{2,1,0:T(8,128)(2,1)S(1)} collective-permute-done((bf16[2,128,128]{2,1,0:T(8,128)(2,1)S(1)}, bf16[2,128,128]{2,1,0:T(8,128)(2,1)S(1)}, u32[]{:S(2)}, u32[]{:S(2)}) %collective-permute-start.2) | collective-permute-done | bytes 65568 | tf_op jit(solution)/shard_map/ppermute | solution.py:467
  11.6 0.0 collective-permute-start.4
  11.6 0.6 %collective-permute-start.3 = (bf16[2,128,256]{2,1,0:T(8,128)(2,1)S(1)}, bf16[2,128,256]{2,1,0:T(8,128)(2,1)S(1)}, u32[]{:S(2)}, u32[]{:S(2)}) collective-permute-start(bf16[2,128,256]{2,1,0:T(8,128)(2,1)S(1)} %pad_maximum_fusion.1), channel_id=1, source_target_pairs={{0,8},{1,2},{2,1},{3,4},{4,3},{5,6},{6,5},{7,15},{8,0},{9,10},{10,... | collective-permute-start | bytes 393224 | tf_op jit(solution)/shard_map/ppermute | solution.py:467
  12.2 0.8 %collective-permute-done.4.even_ref = bf16[2,128,384]{2,1,0:T(8,128)(2,1)S(1)} collective-permute-done((bf16[2,128,384]{2,1,0:T(8,128)(2,1)S(1)}, bf16[2,128,384]{2,1,0:T(8,128)(2,1)S(1)}, u32[]{:S(2)}, u32[]{:S(2)}) %collective-permute-start.4) | collective-permute-done | bytes 196640 | tf_op jit(solution)/shard_map/ppermute | solution.py:452
  13.0 1.0 %near.1 = (f32[4,128,128]{2,1,0:T(8,128)S(1)}, bf16[2,4,16,128]{3,2,1,0:T(8,128)(2,1)S(1)}, bf16[2,4,16,128]{3,2,1,0:T(8,128)(2,1)S(1)}, bf16[2,4,16,128]{3,2,1,0:T(8,128)(2,1)S(1)}, bf16[2,4,16,128]{3,2,1,0:T(8,128)(2,1)S(1)}) custom-call(bf16[8,128,128]{2,1,0:T(8,128)(2,1)S(1)} %bitcast.5, bf16[8,128,128]{2,1,0:T(8,128)(2,1)S(1)} %get-tuple-element.38.turned_ref, ...), custom_call_target="tpu_custom_call" | custom-call | flops 4000000000 | bytes 10000000 | tf_op jit(solution)/shard_map/near/pallas_call | solution.py:381
  14.1 1.2 %collective-permute-start.7 = (bf16[2,4,16,128]{3,2,1,0:T(8,128)(2,1)S(1)}, bf16[2,4,16,128]{3,2,1,0:T(8,128)(2,1)S(1)}, u32[]{:S(2)}, u32[]{:S(2)}) collective-permute-start(bf16[2,4,16,128]{3,2,1,0:T(8,128)(2,1)S(1)} %get-tuple-element.49), channel_id=1, source_target_pairs={{0,2},{1,3},{2,0},{3,1},{4,6},{5,7},{6,4},{7,5},{8,10},{9,11},{10,... | collective-permute-start | bytes 98312 | tf_op jit(solution)/shard_map/ppermute | solution.py:473
  15.2 1.3 %collective-permute-done.3.beside_ref = bf16[2,128,256]{2,1,0:T(8,128)(2,1)S(1)} collective-permute-done((bf16[2,128,256]{2,1,0:T(8,128)(2,1)S(1)}, bf16[2,128,256]{2,1,0:T(8,128)(2,1)S(1)}, u32[]{:S(2)}, u32[]{:S(2)}) %collective-permute-start.3) | collective-permute-done | bytes 131104 | tf_op jit(solution)/shard_map/ppermute | solution.py:467
  16.6 0.7 %far.1 = (bf16[2,4,16,128]{3,2,1,0:T(8,128)(2,1)S(1)}, bf16[2,4,16,128]{3,2,1,0:T(8,128)(2,1)S(1)}, bf16[2,2,4,16,128]{4,3,2,1,0:T(8,128)(2,1)S(1)}, bf16[2,2,4,16,128]{4,3,2,1,0:T(8,128)(2,1)S(1)}) custom-call(bf16[8,128,128]{2,1,0:T(8,128)(2,1)S(1)} %get-tuple-element.38.turned_ref, f32[3,3,8,128]{3,2,1,0:T(8,128)S(1)} %get-tuple-element.39.taper_ref, ...), custom_call_target="tpu_custom_call" | custom-call | flops 4000000000 | bytes 10000000 | tf_op jit(solution)/shard_map/far/pallas_call | solution.py:400
  17.2 2.8 %collective-permute-start.5 = (bf16[2,2,4,16,128]{4,3,2,1,0:T(8,128)(2,1)S(1)}, bf16[2,2,4,16,128]{4,3,2,1,0:T(8,128)(2,1)S(1)}, u32[]{:S(2)}, u32[]{:S(2)}) collective-permute-start(bf16[2,2,4,16,128]{4,3,2,1,0:T(8,128)(2,1)S(1)} %get-tuple-element.46), channel_id=1, source_target_pairs={{0,6},{1,7},{2,4},{3,5},{4,2},{5,3},{6,0},{7,1},{8,14},{9,15},{10,... | collective-permute-start | bytes 196616 | tf_op jit(solution)/shard_map/ppermute | solution.py:473
  20.1 0.0 collective-permute-start.6
  20.1 0.0 collective-permute-done.7.refs_2_.refs_3_
  20.1 0.1 collective-permute-start.9
  20.2 1.7 %collective-permute-start.8 = (bf16[2,4,16,128]{3,2,1,0:T(8,128)(2,1)S(1)}, bf16[2,4,16,128]{3,2,1,0:T(8,128)(2,1)S(1)}, u32[]{:S(2)}, u32[]{:S(2)}) collective-permute-start(bf16[2,4,16,128]{3,2,1,0:T(8,128)(2,1)S(1)} %get-tuple-element.50), channel_id=1, source_target_pairs={{0,2},{1,3},{2,0},{3,1},{4,6},{5,7},{6,4},{7,5},{8,10},{9,11},{10,... | collective-permute-start | bytes 98312 | tf_op jit(solution)/shard_map/ppermute | solution.py:473
  21.8 2.6 %collective-permute-done.8.refs_2_.refs_4_ = bf16[2,4,16,128]{3,2,1,0:T(8,128)(2,1)S(1)} collective-permute-done((bf16[2,4,16,128]{3,2,1,0:T(8,128)(2,1)S(1)}, bf16[2,4,16,128]{3,2,1,0:T(8,128)(2,1)S(1)}, u32[]{:S(2)}, u32[]{:S(2)}) %collective-permute-start.8) | collective-permute-done | bytes 32800 | tf_op jit(solution)/shard_map/ppermute | solution.py:473
  24.5 0.0 collective-permute-done.5.refs_0_.refs_2_
  24.5 1.6 %collective-permute-done.6.refs_1_.refs_3_ = bf16[2,2,4,16,128]{4,3,2,1,0:T(8,128)(2,1)S(1)} collective-permute-done((bf16[2,2,4,16,128]{4,3,2,1,0:T(8,128)(2,1)S(1)}, bf16[2,2,4,16,128]{4,3,2,1,0:T(8,128)(2,1)S(1)}, u32[]{:S(2)}, u32[]{:S(2)}) %collective-permute-start.6) | collective-permute-done | bytes 65568 | tf_op jit(solution)/shard_map/ppermute | solution.py:473
  26.0 0.0 collective-permute-done.9.refs_0_
  26.0 0.1 collective-permute-start.10
  26.1 0.2 early.1.refs_0_
  26.3 1.1 %collective-permute-done.10.refs_1_ = bf16[5,4,16,128]{3,2,1,0:T(8,128)(2,1)S(1)} collective-permute-done((bf16[5,4,16,128]{3,2,1,0:T(8,128)(2,1)S(1)}, bf16[5,4,16,128]{3,2,1,0:T(8,128)(2,1)S(1)}, u32[]{:S(2)}, u32[]{:S(2)}) %collective-permute-start.10) | collective-permute-done | bytes 81952 | tf_op jit(solution)/shard_map/ppermute | solution.py:452
  27.4 1.0 %late.1 = (bf16[1024,128]{1,0:T(8,128)(2,1)}, f32[1024,128]{1,0:T(8,128)S(1)}) custom-call(f32[1024,128]{1,0:T(8,128)S(1)} %early.1.refs_0_, bf16[5,4,16,128]{3,2,1,0:T(8,128)(2,1)S(1)} %collective-permute-done.10.refs_1_, bf16[2,2,4,16,128]{4,3,2,1,0:T(8,128)(2,1)S(1)} %collective-permute-done.5.refs_0_.refs_2_, ...), custom_call_target="tpu_custom_call", output_to_operand_aliasing={{1}: (0, {})} | custom-call | tf_op jit(solution)/shard_map/late/pallas_call | solution.py:435
  (5 shorter events, 0.1 us)
Async XLA Ops:
  2.6 5.7 %collective-permute-start.1 = (bf16[2,128,128]{2,1,0:T(8,128)(2,1)S(1)}, bf16[2,128,128]{2,1,0:T(8,128)(2,1)S(1)}, u32[]{:S(2)}, u32[]{:S(2)}) collective-permute-start(bf16[2,128,128]{2,1,0:T(8,128)(2,1)S(1)} %get-tuple-element.34), channel_id=1, source_target_pairs={{0,1},{1,0},{2,3},{3,2},{4,5},{5,4},{6,7},{7,6},{8,16},{9,17},{10,... | collective-permute-start | bytes 196616 | tf_op jit(solution)/shard_map/ppermute | solution.py:467
  3.8 6.8 %collective-permute-start = (bf16[2,128,128]{2,1,0:T(8,128)(2,1)S(1)}, bf16[2,128,128]{2,1,0:T(8,128)(2,1)S(1)}, u32[]{:S(2)}, u32[]{:S(2)}) collective-permute-start(bf16[2,128,128]{2,1,0:T(8,128)(2,1)S(1)} %get-tuple-element.34), channel_id=1, source_target_pairs={{0,8},{8,0},{16,24},{24,16},{1,9},{9,1},{17,25},{25,17},{2,10},{10... | collective-permute-start | bytes 196616 | tf_op jit(solution)/shard_map/ppermute | solution.py:452
  7.3 4.3 %collective-permute-start.2 = (bf16[2,128,128]{2,1,0:T(8,128)(2,1)S(1)}, bf16[2,128,128]{2,1,0:T(8,128)(2,1)S(1)}, u32[]{:S(2)}, u32[]{:S(2)}) collective-permute-start(bf16[2,128,128]{2,1,0:T(8,128)(2,1)S(1)} %get-tuple-element.34), channel_id=1, source_target_pairs={{0,8},{1,2},{2,1},{3,4},{4,3},{5,6},{6,5},{7,15},{8,0},{9,10},{10,... | collective-permute-start | bytes 196616 | tf_op jit(solution)/shard_map/ppermute | solution.py:467
  11.6 1.4 %collective-permute-start.4 = (bf16[2,128,384]{2,1,0:T(8,128)(2,1)S(1)}, bf16[2,128,384]{2,1,0:T(8,128)(2,1)S(1)}, u32[]{:S(2)}, u32[]{:S(2)}) collective-permute-start(bf16[2,128,384]{2,1,0:T(8,128)(2,1)S(1)} %pad_maximum_fusion.own_ref), channel_id=1, source_target_pairs={{0,1},{1,0},{2,3},{3,2},{4,5},{5,4},{6,7},{7,6},{8,9},{9,8},{10,11... | collective-permute-start | bytes 589832 | tf_op jit(solution)/shard_map/ppermute | solution.py:452
  11.6 5.0 %collective-permute-start.3 = (bf16[2,128,256]{2,1,0:T(8,128)(2,1)S(1)}, bf16[2,128,256]{2,1,0:T(8,128)(2,1)S(1)}, u32[]{:S(2)}, u32[]{:S(2)}) collective-permute-start(bf16[2,128,256]{2,1,0:T(8,128)(2,1)S(1)} %pad_maximum_fusion.1), channel_id=1, source_target_pairs={{0,8},{1,2},{2,1},{3,4},{4,3},{5,6},{6,5},{7,15},{8,0},{9,10},{10,... | collective-permute-start | bytes 393224 | tf_op jit(solution)/shard_map/ppermute | solution.py:467
  14.1 6.0 %collective-permute-start.7 = (bf16[2,4,16,128]{3,2,1,0:T(8,128)(2,1)S(1)}, bf16[2,4,16,128]{3,2,1,0:T(8,128)(2,1)S(1)}, u32[]{:S(2)}, u32[]{:S(2)}) collective-permute-start(bf16[2,4,16,128]{3,2,1,0:T(8,128)(2,1)S(1)} %get-tuple-element.49), channel_id=1, source_target_pairs={{0,2},{1,3},{2,0},{3,1},{4,6},{5,7},{6,4},{7,5},{8,10},{9,11},{10,... | collective-permute-start | bytes 98312 | tf_op jit(solution)/shard_map/ppermute | solution.py:473
  17.2 7.2 %collective-permute-start.5 = (bf16[2,2,4,16,128]{4,3,2,1,0:T(8,128)(2,1)S(1)}, bf16[2,2,4,16,128]{4,3,2,1,0:T(8,128)(2,1)S(1)}, u32[]{:S(2)}, u32[]{:S(2)}) collective-permute-start(bf16[2,2,4,16,128]{4,3,2,1,0:T(8,128)(2,1)S(1)} %get-tuple-element.46), channel_id=1, source_target_pairs={{0,6},{1,7},{2,4},{3,5},{4,2},{5,3},{6,0},{7,1},{8,14},{9,15},{10,... | collective-permute-start | bytes 196616 | tf_op jit(solution)/shard_map/ppermute | solution.py:473
  20.1 5.9 %collective-permute-start.6 = (bf16[2,2,4,16,128]{4,3,2,1,0:T(8,128)(2,1)S(1)}, bf16[2,2,4,16,128]{4,3,2,1,0:T(8,128)(2,1)S(1)}, u32[]{:S(2)}, u32[]{:S(2)}) collective-permute-start(bf16[2,2,4,16,128]{4,3,2,1,0:T(8,128)(2,1)S(1)} %get-tuple-element.47), channel_id=1, source_target_pairs={{0,4},{1,5},{2,6},{3,7},{4,0},{5,1},{6,2},{7,3},{8,12},{9,13},{10,... | collective-permute-start | bytes 196616 | tf_op jit(solution)/shard_map/ppermute | solution.py:473
  20.1 5.9 %collective-permute-start.9 = (bf16[3,4,16,128]{3,2,1,0:T(8,128)(2,1)S(1)}, bf16[3,4,16,128]{3,2,1,0:T(8,128)(2,1)S(1)}, u32[]{:S(2)}, u32[]{:S(2)}) collective-permute-start(bf16[3,4,16,128]{3,2,1,0:T(8,128)(2,1)S(1)} %pack.2), channel_id=1, source_target_pairs={{0,1},{1,0},{2,3},{3,2},{4,5},{5,4},{6,7},{7,6},{8,9},{9,8},{10,11... | collective-permute-start | bytes 147464 | tf_op jit(solution)/shard_map/ppermute | solution.py:452
  20.2 4.3 %collective-permute-start.8 = (bf16[2,4,16,128]{3,2,1,0:T(8,128)(2,1)S(1)}, bf16[2,4,16,128]{3,2,1,0:T(8,128)(2,1)S(1)}, u32[]{:S(2)}, u32[]{:S(2)}) collective-permute-start(bf16[2,4,16,128]{3,2,1,0:T(8,128)(2,1)S(1)} %get-tuple-element.50), channel_id=1, source_target_pairs={{0,2},{1,3},{2,0},{3,1},{4,6},{5,7},{6,4},{7,5},{8,10},{9,11},{10,... | collective-permute-start | bytes 98312 | tf_op jit(solution)/shard_map/ppermute | solution.py:473
  26.0 1.3 %collective-permute-start.10 = (bf16[5,4,16,128]{3,2,1,0:T(8,128)(2,1)S(1)}, bf16[5,4,16,128]{3,2,1,0:T(8,128)(2,1)S(1)}, u32[]{:S(2)}, u32[]{:S(2)}) collective-permute-start(bf16[5,4,16,128]{3,2,1,0:T(8,128)(2,1)S(1)} %pack.3), channel_id=1, source_target_pairs={{0,1},{1,0},{2,3},{3,2},{4,5},{5,4},{6,7},{7,6},{8,9},{9,8},{10,11... | collective-permute-start | bytes 245768 | tf_op jit(solution)/shard_map/ppermute | solution.py:452

commit v22 on v19

--- a/solution.py
+++ b/solution.py
@@ -352,7 +352,7 @@
 
 def late_kernel(chips, *refs):
     late_refs, out_hbm, rows_ref, out_ref, sems = refs[1:-4], *refs[-4:]
-    sides = [(side, r) for r in range(1, chips) for side in ((0, 1) if r in (1, chips - 1) else (1,))]
+    sides = [(side, r) for r in range(chips - 1, 0, -1) for side in ((0, 1) if r in (1, chips - 1) else (1,))]
     settle(chips, sides, late_refs, rows_ref)
     pieces = sems.shape[0]
     step = rows_ref.shape[0] // pieces
@@ -497,10 +497,10 @@
     chips = parts // 2
     near_hops = [hop(near[r], r) for r in range(2, chips - 1)]
     far = list(update_far(turned, taper, across, beside, part, near))
-    if near_hops:
-        far[1], near_hops = lax.optimization_barrier((far[1], near_hops))
+    for r in range(2, chips - 1):
+        far[r], near_hops[r - 2] = lax.optimization_barrier((far[r], near_hops[r - 2]))
     early = [near[0], far[0], *near_hops]
-    late = [hop(far[r], r) for r in range(1, chips)]
+    late = [hop(far[r], r) for r in range(chips - 1, 0, -1)]
     early_even = swap(pack(early), "gy")
     late, early_even = lax.optimization_barrier((late, early_even))
     late_even = swap(pack(late), "gy")

time: 27.9 us -> 28 us (level)
  waiting for transfers between devices: 7.68 us -> 8.94 us
  starting transfers between devices: 13.2 us -> 12 us
    ppermute x4, waiting for transfers between devices: 2.23 us -> 3.59 us  [hop(): return lax.ppermute(piece, 'gy', pairs)]
    ppermute x4, starting transfers between devices: 8.05 us -> 6.8 us  [hop(): return lax.ppermute(piece, 'gy', pairs)]
where the time goes in v22:
time: 28 us; the launch traced here: 27.7 us
  starting transfers between devices  12 us (43%)
  waiting for transfers between devices  8.94 us (32%)
  Pallas kernels  6.55 us (23%)
    ppermute x4, starting transfers between devices, hop(): return lax.ppermute(piece, 'gy', pairs)  6.8 us
    ppermute x4, waiting for transfers between devices, swap(): lax.ppermute(block, axis, [(i, i ^ 1) for i in range(lax.axis_size(axis))])  4.05 us
    ppermute x4, starting transfers between devices, swap(): lax.ppermute(block, axis, [(i, i ^ 1) for i in range(lax.axis_size(axis))])  3.92 us
    ppermute x4, waiting for transfers between devices, hop(): return lax.ppermute(piece, 'gy', pairs)  3.59 us
    pallas_call x1, Pallas kernels, weigh(): pl.pallas_call(weigh_kernel, out_shape=(jax.ShapeDtypeStruct((2, members,...  2.71 us
    ppermute x3, waiting for transfers between devices, swap_odd(): return lax.ppermute(block, ('gx', 'gy'), pairs)  1.3 us
    ppermute x3, starting transfers between devices, swap_odd(): return lax.ppermute(block, ('gx', 'gy'), pairs)  1.29 us
    pallas_call x1, Pallas kernels, update_near(): pl.pallas_call(near_kernel, out_shape=(jax.ShapeDtypeStruct((SIDE, member...  1.04 us
  transfers between devices with their start and end apart: 11, of which 7 were waited for; matrix products, arithmetic and copies ran while one was open for 0% of the time, Pallas kernels for 10%

profile of v22, /device:TPU:0, one launch (start us, length us, event | category | flops | bytes accessed | tf_op | source)
XLA Modules:
  0.0 27.7 jit_solution(10033346746471599056)
XLA Ops:
  0.0 2.7 %weigh.1 = (bf16[2,128,128]{2,1,0:T(8,128)(2,1)S(1)}, bf16[128,2,4,128]{3,2,1,0:T(4,128)(2,1)S(1)}) custom-call(f32[1,1,128,128]{3,2,1,0:T(8,128)} %pred_hbm.1, f32[1,1,128]{2,1,0:T(1,128)} %mv_hbm.1, f32[1,1,128]{2,1,0:T(1,128)} %var_hbm.1, f32[1,1,128,128]{3,2,1,0:T(8,128)} %jit_hbm.1, s32[4,8,128]{2,1,0:T(8,128)} %obs_hbm.3, ...), custom_call_target="tpu_custom_call" | custom-call | tf_op jit(solution)/shard_map/weigh/pallas_call | solution.py:157
  2.7 0.6 %collective-permute-start.1 = (bf16[2,128,128]{2,1,0:T(8,128)(2,1)S(1)}, bf16[2,128,128]{2,1,0:T(8,128)(2,1)S(1)}, u32[]{:S(2)}, u32[]{:S(2)}) collective-permute-start(bf16[2,128,128]{2,1,0:T(8,128)(2,1)S(1)} %get-tuple-element.34), channel_id=1, source_target_pairs={{0,1},{1,0},{2,3},{3,2},{4,5},{5,4},{6,7},{7,6},{8,16},{9,17},{10,... | collective-permute-start | bytes 196616 | tf_op jit(solution)/shard_map/ppermute | solution.py:462
  3.3 3.8 %collective-permute-start = (bf16[2,128,128]{2,1,0:T(8,128)(2,1)S(1)}, bf16[2,128,128]{2,1,0:T(8,128)(2,1)S(1)}, u32[]{:S(2)}, u32[]{:S(2)}) collective-permute-start(bf16[2,128,128]{2,1,0:T(8,128)(2,1)S(1)} %get-tuple-element.34), channel_id=1, source_target_pairs={{0,8},{8,0},{16,24},{24,16},{1,9},{9,1},{17,25},{25,17},{2,10},{10... | collective-permute-start | bytes 196616 | tf_op jit(solution)/shard_map/ppermute | solution.py:447
  7.2 0.1 collective-permute-start.2
  7.2 1.0 %prepare.1 = (bf16[8,128,128]{2,1,0:T(8,128)(2,1)S(1)}, f32[3,3,8,128]{3,2,1,0:T(8,128)S(1)}) custom-call(bf16[8,128,128]{2,1,0:T(8,128)(2,1)S(1)} %bitcast.4, s32[2,4]{1,0:T(2,128)} %radius_hbm.1, s32[2,4,25]{2,1,0:T(4,128)} %pattern_hbm.1, s32[4,8,128]{2,1,0:T(8,128)} %obs_hbm.3), custom_call_target="tpu_custom_call" | custom-call | flops 4000000 | bytes 1000000 | tf_op jit(solution)/shard_map/prepare/pallas_call | solution.py:230
  8.2 0.0 collective-permute-done.1
  8.2 2.1 %collective-permute-done = bf16[2,128,128]{2,1,0:T(8,128)(2,1)S(1)} collective-permute-done((bf16[2,128,128]{2,1,0:T(8,128)(2,1)S(1)}, bf16[2,128,128]{2,1,0:T(8,128)(2,1)S(1)}, u32[]{:S(2)}, u32[]{:S(2)}) %collective-permute-start) | collective-permute-done | bytes 65568 | tf_op jit(solution)/shard_map/ppermute | solution.py:447
  10.4 1.1 %collective-permute-done.2.odd_ref = bf16[2,128,128]{2,1,0:T(8,128)(2,1)S(1)} collective-permute-done((bf16[2,128,128]{2,1,0:T(8,128)(2,1)S(1)}, bf16[2,128,128]{2,1,0:T(8,128)(2,1)S(1)}, u32[]{:S(2)}, u32[]{:S(2)}) %collective-permute-start.2) | collective-permute-done | bytes 65568 | tf_op jit(solution)/shard_map/ppermute | solution.py:462
  11.5 0.0 collective-permute-start.4
  11.5 0.6 %collective-permute-start.3 = (bf16[2,128,256]{2,1,0:T(8,128)(2,1)S(1)}, bf16[2,128,256]{2,1,0:T(8,128)(2,1)S(1)}, u32[]{:S(2)}, u32[]{:S(2)}) collective-permute-start(bf16[2,128,256]{2,1,0:T(8,128)(2,1)S(1)} %pad_maximum_fusion.1), channel_id=1, source_target_pairs={{0,8},{1,2},{2,1},{3,4},{4,3},{5,6},{6,5},{7,15},{8,0},{9,10},{10,... | collective-permute-start | bytes 393224 | tf_op jit(solution)/shard_map/ppermute | solution.py:462
  12.1 0.8 %collective-permute-done.4.even_ref = bf16[2,128,384]{2,1,0:T(8,128)(2,1)S(1)} collective-permute-done((bf16[2,128,384]{2,1,0:T(8,128)(2,1)S(1)}, bf16[2,128,384]{2,1,0:T(8,128)(2,1)S(1)}, u32[]{:S(2)}, u32[]{:S(2)}) %collective-permute-start.4) | collective-permute-done | bytes 196640 | tf_op jit(solution)/shard_map/ppermute | solution.py:447
  12.9 1.0 %near.1 = (f32[4,128,128]{2,1,0:T(8,128)S(1)}, bf16[2,4,16,128]{3,2,1,0:T(8,128)(2,1)S(1)}, bf16[2,4,16,128]{3,2,1,0:T(8,128)(2,1)S(1)}, bf16[2,4,16,128]{3,2,1,0:T(8,128)(2,1)S(1)}, bf16[2,4,16,128]{3,2,1,0:T(8,128)(2,1)S(1)}) custom-call(bf16[8,128,128]{2,1,0:T(8,128)(2,1)S(1)} %bitcast.5, bf16[8,128,128]{2,1,0:T(8,128)(2,1)S(1)} %get-tuple-element.38.turned_ref, ...), custom_call_target="tpu_custom_call" | custom-call | flops 4000000000 | bytes 10000000 | tf_op jit(solution)/shard_map/near/pallas_call | solution.py:377
  14.0 2.3 %collective-permute-start.6 = (bf16[2,4,16,128]{3,2,1,0:T(8,128)(2,1)S(1)}, bf16[2,4,16,128]{3,2,1,0:T(8,128)(2,1)S(1)}, u32[]{:S(2)}, u32[]{:S(2)}) collective-permute-start(bf16[2,4,16,128]{3,2,1,0:T(8,128)(2,1)S(1)} %get-tuple-element.48), channel_id=1, source_target_pairs={{0,4},{1,5},{2,6},{3,7},{4,0},{5,1},{6,2},{7,3},{8,12},{9,13},{10,... | collective-permute-start | bytes 98312 | tf_op jit(solution)/shard_map/ppermute | solution.py:468
  16.3 0.2 collective-permute-done.3.beside_ref
  16.5 0.7 %far.1 = (bf16[2,4,16,128]{3,2,1,0:T(8,128)(2,1)S(1)}, bf16[2,2,4,16,128]{4,3,2,1,0:T(8,128)(2,1)S(1)}, bf16[2,4,16,128]{3,2,1,0:T(8,128)(2,1)S(1)}, bf16[2,2,4,16,128]{4,3,2,1,0:T(8,128)(2,1)S(1)}) custom-call(bf16[8,128,128]{2,1,0:T(8,128)(2,1)S(1)} %get-tuple-element.38.turned_ref, f32[3,3,8,128]{3,2,1,0:T(8,128)S(1)} %get-tuple-element.39.taper_ref, ...), custom_call_target="tpu_custom_call" | custom-call | flops 4000000000 | bytes 10000000 | tf_op jit(solution)/shard_map/far/pallas_call | solution.py:395
  17.1 2.9 %collective-permute-start.5 = (bf16[2,2,4,16,128]{4,3,2,1,0:T(8,128)(2,1)S(1)}, bf16[2,2,4,16,128]{4,3,2,1,0:T(8,128)(2,1)S(1)}, u32[]{:S(2)}, u32[]{:S(2)}) collective-permute-start(bf16[2,2,4,16,128]{4,3,2,1,0:T(8,128)(2,1)S(1)} %get-tuple-element.46), channel_id=1, source_target_pairs={{0,6},{1,7},{2,4},{3,5},{4,2},{5,3},{6,0},{7,1},{8,14},{9,15},{10,... | collective-permute-start | bytes 196616 | tf_op jit(solution)/shard_map/ppermute | solution.py:468
  20.1 0.0 collective-permute-start.8
  20.1 0.0 collective-permute-done.6.refs_2_.refs_3_
  20.1 0.1 collective-permute-start.9
  20.2 1.6 %collective-permute-start.7 = (bf16[2,4,16,128]{3,2,1,0:T(8,128)(2,1)S(1)}, bf16[2,4,16,128]{3,2,1,0:T(8,128)(2,1)S(1)}, u32[]{:S(2)}, u32[]{:S(2)}) collective-permute-start(bf16[2,4,16,128]{3,2,1,0:T(8,128)(2,1)S(1)} %get-tuple-element.49), channel_id=1, source_target_pairs={{0,4},{1,5},{2,6},{3,7},{4,0},{5,1},{6,2},{7,3},{8,12},{9,13},{10,... | collective-permute-start | bytes 98312 | tf_op jit(solution)/shard_map/ppermute | solution.py:468
  21.7 3.4 %collective-permute-done.7.refs_1_.refs_3_ = bf16[2,4,16,128]{3,2,1,0:T(8,128)(2,1)S(1)} collective-permute-done((bf16[2,4,16,128]{3,2,1,0:T(8,128)(2,1)S(1)}, bf16[2,4,16,128]{3,2,1,0:T(8,128)(2,1)S(1)}, u32[]{:S(2)}, u32[]{:S(2)}) %collective-permute-start.7) | collective-permute-done | bytes 32800 | tf_op jit(solution)/shard_map/ppermute | solution.py:468
  25.1 0.0 collective-permute-done.5.refs_0_.refs_2_
  25.1 0.2 collective-permute-done.8.refs_2_.refs_4_
  25.3 0.0 collective-permute-done.9.refs_0_
  25.3 0.1 collective-permute-start.10
  25.4 0.2 early.1.refs_0_
  25.6 1.1 %collective-permute-done.10.refs_1_ = bf16[5,4,16,128]{3,2,1,0:T(8,128)(2,1)S(1)} collective-permute-done((bf16[5,4,16,128]{3,2,1,0:T(8,128)(2,1)S(1)}, bf16[5,4,16,128]{3,2,1,0:T(8,128)(2,1)S(1)}, u32[]{:S(2)}, u32[]{:S(2)}) %collective-permute-start.10) | collective-permute-done | bytes 81952 | tf_op jit(solution)/shard_map/ppermute | solution.py:447
  26.7 1.0 %late.1 = (bf16[1024,128]{1,0:T(8,128)(2,1)}, f32[1024,128]{1,0:T(8,128)S(1)}) custom-call(f32[1024,128]{1,0:T(8,128)S(1)} %early.1.refs_0_, bf16[5,4,16,128]{3,2,1,0:T(8,128)(2,1)S(1)} %collective-permute-done.10.refs_1_, bf16[2,2,4,16,128]{4,3,2,1,0:T(8,128)(2,1)S(1)} %collective-permute-done.5.refs_0_.refs_2_, ...), custom_call_target="tpu_custom_call", output_to_operand_aliasing={{1}: (0, {})} | custom-call | tf_op jit(solution)/shard_map/late/pallas_call | solution.py:430
  (5 shorter events, 0.1 us)
Async XLA Ops:
  2.7 5.5 %collective-permute-start.1 = (bf16[2,128,128]{2,1,0:T(8,128)(2,1)S(1)}, bf16[2,128,128]{2,1,0:T(8,128)(2,1)S(1)}, u32[]{:S(2)}, u32[]{:S(2)}) collective-permute-start(bf16[2,128,128]{2,1,0:T(8,128)(2,1)S(1)} %get-tuple-element.34), channel_id=1, source_target_pairs={{0,1},{1,0},{2,3},{3,2},{4,5},{5,4},{6,7},{7,6},{8,16},{9,17},{10,... | collective-permute-start | bytes 196616 | tf_op jit(solution)/shard_map/ppermute | solution.py:462
  3.3 7.0 %collective-permute-start = (bf16[2,128,128]{2,1,0:T(8,128)(2,1)S(1)}, bf16[2,128,128]{2,1,0:T(8,128)(2,1)S(1)}, u32[]{:S(2)}, u32[]{:S(2)}) collective-permute-start(bf16[2,128,128]{2,1,0:T(8,128)(2,1)S(1)} %get-tuple-element.34), channel_id=1, source_target_pairs={{0,8},{8,0},{16,24},{24,16},{1,9},{9,1},{17,25},{25,17},{2,10},{10... | collective-permute-start | bytes 196616 | tf_op jit(solution)/shard_map/ppermute | solution.py:447
  7.2 4.3 %collective-permute-start.2 = (bf16[2,128,128]{2,1,0:T(8,128)(2,1)S(1)}, bf16[2,128,128]{2,1,0:T(8,128)(2,1)S(1)}, u32[]{:S(2)}, u32[]{:S(2)}) collective-permute-start(bf16[2,128,128]{2,1,0:T(8,128)(2,1)S(1)} %get-tuple-element.34), channel_id=1, source_target_pairs={{0,8},{1,2},{2,1},{3,4},{4,3},{5,6},{6,5},{7,15},{8,0},{9,10},{10,... | collective-permute-start | bytes 196616 | tf_op jit(solution)/shard_map/ppermute | solution.py:462
  11.5 1.4 %collective-permute-start.4 = (bf16[2,128,384]{2,1,0:T(8,128)(2,1)S(1)}, bf16[2,128,384]{2,1,0:T(8,128)(2,1)S(1)}, u32[]{:S(2)}, u32[]{:S(2)}) collective-permute-start(bf16[2,128,384]{2,1,0:T(8,128)(2,1)S(1)} %pad_maximum_fusion.own_ref), channel_id=1, source_target_pairs={{0,1},{1,0},{2,3},{3,2},{4,5},{5,4},{6,7},{7,6},{8,9},{9,8},{10,11... | collective-permute-start | bytes 589832 | tf_op jit(solution)/shard_map/ppermute | solution.py:447
  11.5 5.0 %collective-permute-start.3 = (bf16[2,128,256]{2,1,0:T(8,128)(2,1)S(1)}, bf16[2,128,256]{2,1,0:T(8,128)(2,1)S(1)}, u32[]{:S(2)}, u32[]{:S(2)}) collective-permute-start(bf16[2,128,256]{2,1,0:T(8,128)(2,1)S(1)} %pad_maximum_fusion.1), channel_id=1, source_target_pairs={{0,8},{1,2},{2,1},{3,4},{4,3},{5,6},{6,5},{7,15},{8,0},{9,10},{10,... | collective-permute-start | bytes 393224 | tf_op jit(solution)/shard_map/ppermute | solution.py:462
  14.0 6.1 %collective-permute-start.6 = (bf16[2,4,16,128]{3,2,1,0:T(8,128)(2,1)S(1)}, bf16[2,4,16,128]{3,2,1,0:T(8,128)(2,1)S(1)}, u32[]{:S(2)}, u32[]{:S(2)}) collective-permute-start(bf16[2,4,16,128]{3,2,1,0:T(8,128)(2,1)S(1)} %get-tuple-element.48), channel_id=1, source_target_pairs={{0,4},{1,5},{2,6},{3,7},{4,0},{5,1},{6,2},{7,3},{8,12},{9,13},{10,... | collective-permute-start | bytes 98312 | tf_op jit(solution)/shard_map/ppermute | solution.py:468
  17.1 8.0 %collective-permute-start.5 = (bf16[2,2,4,16,128]{4,3,2,1,0:T(8,128)(2,1)S(1)}, bf16[2,2,4,16,128]{4,3,2,1,0:T(8,128)(2,1)S(1)}, u32[]{:S(2)}, u32[]{:S(2)}) collective-permute-start(bf16[2,2,4,16,128]{4,3,2,1,0:T(8,128)(2,1)S(1)} %get-tuple-element.46), channel_id=1, source_target_pairs={{0,6},{1,7},{2,4},{3,5},{4,2},{5,3},{6,0},{7,1},{8,14},{9,15},{10,... | collective-permute-start | bytes 196616 | tf_op jit(solution)/shard_map/ppermute | solution.py:468
  20.1 5.2 %collective-permute-start.8 = (bf16[2,2,4,16,128]{4,3,2,1,0:T(8,128)(2,1)S(1)}, bf16[2,2,4,16,128]{4,3,2,1,0:T(8,128)(2,1)S(1)}, u32[]{:S(2)}, u32[]{:S(2)}) collective-permute-start(bf16[2,2,4,16,128]{4,3,2,1,0:T(8,128)(2,1)S(1)} %get-tuple-element.50), channel_id=1, source_target_pairs={{0,2},{1,3},{2,0},{3,1},{4,6},{5,7},{6,4},{7,5},{8,10},{9,11},{10,... | collective-permute-start | bytes 196616 | tf_op jit(solution)/shard_map/ppermute | solution.py:468
  20.1 5.2 %collective-permute-start.9 = (bf16[3,4,16,128]{3,2,1,0:T(8,128)(2,1)S(1)}, bf16[3,4,16,128]{3,2,1,0:T(8,128)(2,1)S(1)}, u32[]{:S(2)}, u32[]{:S(2)}) collective-permute-start(bf16[3,4,16,128]{3,2,1,0:T(8,128)(2,1)S(1)} %pack.2), channel_id=1, source_target_pairs={{0,1},{1,0},{2,3},{3,2},{4,5},{5,4},{6,7},{7,6},{8,9},{9,8},{10,11... | collective-permute-start | bytes 147464 | tf_op jit(solution)/shard_map/ppermute | solution.py:447
  20.2 4.9 %collective-permute-start.7 = (bf16[2,4,16,128]{3,2,1,0:T(8,128)(2,1)S(1)}, bf16[2,4,16,128]{3,2,1,0:T(8,128)(2,1)S(1)}, u32[]{:S(2)}, u32[]{:S(2)}) collective-permute-start(bf16[2,4,16,128]{3,2,1,0:T(8,128)(2,1)S(1)} %get-tuple-element.49), channel_id=1, source_target_pairs={{0,4},{1,5},{2,6},{3,7},{4,0},{5,1},{6,2},{7,3},{8,12},{9,13},{10,... | collective-permute-start | bytes 98312 | tf_op jit(solution)/shard_map/ppermute | solution.py:468
  25.3 1.3 %collective-permute-start.10 = (bf16[5,4,16,128]{3,2,1,0:T(8,128)(2,1)S(1)}, bf16[5,4,16,128]{3,2,1,0:T(8,128)(2,1)S(1)}, u32[]{:S(2)}, u32[]{:S(2)}) collective-permute-start(bf16[5,4,16,128]{3,2,1,0:T(8,128)(2,1)S(1)} %pack.3), channel_id=1, source_target_pairs={{0,1},{1,0},{2,3},{3,2},{4,5},{5,4},{6,7},{7,6},{8,9},{9,8},{10,11... | collective-permute-start | bytes 245768 | tf_op jit(solution)/shard_map/ppermute | solution.py:447

commit v23 on v22

--- a/solution.py
+++ b/solution.py
@@ -89,7 +89,7 @@
 
 def weigh_kernel(
     pred_hbm, mv_hbm, var_hbm, jit_hbm, obs_hbm, params_hbm, out_ref, params_ref,
-    pred_ref, mv_ref, var_ref, jit_ref, obs_ref, x_ref, idx_ref, full_ref, sems,
+    pred_ref, mv_ref, var_ref, jit_ref, obs_ref, x_ref, idx_ref, full_ref, left_ref, sems,
 ):
     members = pred_ref.shape[0]
     tile_x = lax.axis_index("gx")
@@ -104,7 +104,7 @@
         (params_hbm, params_ref),
     ]
     copies = fetch(pairs, sems)
-    for copy in copies[:3]:
+    for copy in copies[:5]:
         copy.wait()
     pred = pred_ref[...]
     var = var_ref[...]
@@ -127,6 +127,10 @@
     numbered = jnp.where(place, col, 0).astype(F32).astype(BF16)
     idx_ref[...] = dot(numbered, same.astype(BF16), ((1,), (0,))).astype(jnp.int32)
 
+    innovation = mv_ref[...] + jnp.sqrt(var) * jit_ref[...] - pred
+    high, mid, low = split3(innovation)
+    left_ref[...] = jnp.concatenate([low, mid, high, mid, high, high], axis=1)
+
     def solve(rows):
         sweep(rows, count, x_ref, idx_ref, rank, size)
         taken = jnp.concatenate([hot[0:rows]] * 3, axis=0)
@@ -141,15 +145,11 @@
     def _():
         solve(OBS_TILE)
 
-    for copy in copies[3:]:
-        copy.wait()
-    innovation = mv_ref[...] + jnp.sqrt(var) * jit_ref[...] - pred
-    high, mid, low = split3(innovation)
     full_high, full_mid, full_low = split3(full_ref[...])
-    left = jnp.concatenate([low, mid, high, mid, high, high], axis=1)
     right = jnp.concatenate([full_high, full_mid, full_low, full_high, full_mid, full_high], axis=0)
-    weighted = dot(left, right, ((1,), (0,)))
+    weighted = dot(left_ref[...], right, ((1,), (0,)))
     out_ref[1] = weighted.astype(BF16)
+    copies[5].wait()
 
 
 def weigh(predicted, measured_value, measurement_variance, observation_jitter, obs_block, params):
@@ -168,6 +168,7 @@
             pltpu.VMEM((OBS_TILE, OBS_TILE), F32),
             pltpu.VMEM((OBS_TILE, OBS_TILE), jnp.int32),
             pltpu.VMEM((OBS_TILE, OBS_TILE), F32),
+            pltpu.VMEM((members, 6 * OBS_TILE), BF16),
             pltpu.SemaphoreType.DMA((6,)),
         ],
         compiler_params=pltpu.CompilerParams(vmem_limit_bytes=16 * 2**20),

time: 28 us -> 28.2 us (level)
  waiting for transfers between devices: 8.94 us -> 9.24 us
    ppermute x3, waiting for transfers between devices: 1.3 us -> 1.7 us  [swap_odd(): return lax.ppermute(block, ('gx', 'gy'), pairs)]
    ppermute x3, starting transfers between devices: 1.29 us -> 1.61 us  [swap_odd(): return lax.ppermute(block, ('gx', 'gy'), pairs)]
    ppermute x4, starting transfers between devices: 6.8 us -> 6.49 us  [hop(): return lax.ppermute(piece, 'gy', pairs)]
where the time goes in v23:
time: 28.2 us; the launch traced here: 28.1 us
  starting transfers between devices  11.9 us (42%)
  waiting for transfers between devices  9.24 us (33%)
  Pallas kernels  6.74 us (24%)
    ppermute x4, starting transfers between devices, hop(): return lax.ppermute(piece, 'gy', pairs)  6.49 us
    ppermute x4, waiting for transfers between devices, swap(): lax.ppermute(block, axis, [(i, i ^ 1) for i in range(lax.axis_size(axis))])  3.95 us
    ppermute x4, starting transfers between devices, swap(): lax.ppermute(block, axis, [(i, i ^ 1) for i in range(lax.axis_size(axis))])  3.8 us
    ppermute x4, waiting for transfers between devices, hop(): return lax.ppermute(piece, 'gy', pairs)  3.58 us
    pallas_call x1, Pallas kernels, weigh(): pl.pallas_call(weigh_kernel, out_shape=(jax.ShapeDtypeStruct((2, members,...  2.89 us
    ppermute x3, waiting for transfers between devices, swap_odd(): return lax.ppermute(block, ('gx', 'gy'), pairs)  1.7 us
    ppermute x3, starting transfers between devices, swap_odd(): return lax.ppermute(block, ('gx', 'gy'), pairs)  1.61 us
    pallas_call x1, Pallas kernels, update_near(): pl.pallas_call(near_kernel, out_shape=(jax.ShapeDtypeStruct((SIDE, member...  1.04 us
  transfers between devices with their start and end apart: 11, of which 7 were waited for; matrix products, arithmetic and copies ran while one was open for 0% of the time, Pallas kernels for 10%

profile of v23, /device:TPU:0, one launch (start us, length us, event | category | flops | bytes accessed | tf_op | source)
XLA Modules:
  0.0 28.1 jit_solution(2177907007333976330)
XLA Ops:
  0.0 2.9 %weigh.1 = (bf16[2,128,128]{2,1,0:T(8,128)(2,1)S(1)}, bf16[128,2,4,128]{3,2,1,0:T(4,128)(2,1)S(1)}) custom-call(f32[1,1,128,128]{3,2,1,0:T(8,128)} %pred_hbm.1, f32[1,1,128]{2,1,0:T(1,128)} %mv_hbm.1, f32[1,1,128]{2,1,0:T(1,128)} %var_hbm.1, f32[1,1,128,128]{3,2,1,0:T(8,128)} %jit_hbm.1, s32[4,8,128]{2,1,0:T(8,128)} %obs_hbm.3, ...), custom_call_target="tpu_custom_call" | custom-call | tf_op jit(solution)/shard_map/weigh/pallas_call | solution.py:157
  2.9 0.9 %collective-permute-start.1 = (bf16[2,128,128]{2,1,0:T(8,128)(2,1)S(1)}, bf16[2,128,128]{2,1,0:T(8,128)(2,1)S(1)}, u32[]{:S(2)}, u32[]{:S(2)}) collective-permute-start(bf16[2,128,128]{2,1,0:T(8,128)(2,1)S(1)} %get-tuple-element.34), channel_id=1, source_target_pairs={{0,1},{1,0},{2,3},{3,2},{4,5},{5,4},{6,7},{7,6},{8,16},{9,17},{10,... | collective-permute-start | bytes 196616 | tf_op jit(solution)/shard_map/ppermute | solution.py:463
  3.8 3.7 %collective-permute-start = (bf16[2,128,128]{2,1,0:T(8,128)(2,1)S(1)}, bf16[2,128,128]{2,1,0:T(8,128)(2,1)S(1)}, u32[]{:S(2)}, u32[]{:S(2)}) collective-permute-start(bf16[2,128,128]{2,1,0:T(8,128)(2,1)S(1)} %get-tuple-element.34), channel_id=1, source_target_pairs={{0,8},{8,0},{16,24},{24,16},{1,9},{9,1},{17,25},{25,17},{2,10},{10... | collective-permute-start | bytes 196616 | tf_op jit(solution)/shard_map/ppermute | solution.py:448
  7.5 0.1 collective-permute-start.2
  7.6 1.0 %prepare.1 = (bf16[8,128,128]{2,1,0:T(8,128)(2,1)S(1)}, f32[3,3,8,128]{3,2,1,0:T(8,128)S(1)}) custom-call(bf16[8,128,128]{2,1,0:T(8,128)(2,1)S(1)} %bitcast.4, s32[2,4]{1,0:T(2,128)} %radius_hbm.1, s32[2,4,25]{2,1,0:T(4,128)} %pattern_hbm.1, s32[4,8,128]{2,1,0:T(8,128)} %obs_hbm.3), custom_call_target="tpu_custom_call" | custom-call | flops 4000000 | bytes 1000000 | tf_op jit(solution)/shard_map/prepare/pallas_call | solution.py:231
  8.6 0.0 collective-permute-done.1
  8.6 2.0 %collective-permute-done = bf16[2,128,128]{2,1,0:T(8,128)(2,1)S(1)} collective-permute-done((bf16[2,128,128]{2,1,0:T(8,128)(2,1)S(1)}, bf16[2,128,128]{2,1,0:T(8,128)(2,1)S(1)}, u32[]{:S(2)}, u32[]{:S(2)}) %collective-permute-start) | collective-permute-done | bytes 65568 | tf_op jit(solution)/shard_map/ppermute | solution.py:448
  10.7 1.2 %collective-permute-done.2.odd_ref = bf16[2,128,128]{2,1,0:T(8,128)(2,1)S(1)} collective-permute-done((bf16[2,128,128]{2,1,0:T(8,128)(2,1)S(1)}, bf16[2,128,128]{2,1,0:T(8,128)(2,1)S(1)}, u32[]{:S(2)}, u32[]{:S(2)}) %collective-permute-start.2) | collective-permute-done | bytes 65568 | tf_op jit(solution)/shard_map/ppermute | solution.py:463
  11.9 0.0 collective-permute-start.4
  11.9 0.6 %collective-permute-start.3 = (bf16[2,128,256]{2,1,0:T(8,128)(2,1)S(1)}, bf16[2,128,256]{2,1,0:T(8,128)(2,1)S(1)}, u32[]{:S(2)}, u32[]{:S(2)}) collective-permute-start(bf16[2,128,256]{2,1,0:T(8,128)(2,1)S(1)} %pad_maximum_fusion.1), channel_id=1, source_target_pairs={{0,8},{1,2},{2,1},{3,4},{4,3},{5,6},{6,5},{7,15},{8,0},{9,10},{10,... | collective-permute-start | bytes 393224 | tf_op jit(solution)/shard_map/ppermute | solution.py:463
  12.5 0.8 %collective-permute-done.4.even_ref = bf16[2,128,384]{2,1,0:T(8,128)(2,1)S(1)} collective-permute-done((bf16[2,128,384]{2,1,0:T(8,128)(2,1)S(1)}, bf16[2,128,384]{2,1,0:T(8,128)(2,1)S(1)}, u32[]{:S(2)}, u32[]{:S(2)}) %collective-permute-start.4) | collective-permute-done | bytes 196640 | tf_op jit(solution)/shard_map/ppermute | solution.py:448
  13.3 1.0 %near.1 = (f32[4,128,128]{2,1,0:T(8,128)S(1)}, bf16[2,4,16,128]{3,2,1,0:T(8,128)(2,1)S(1)}, bf16[2,4,16,128]{3,2,1,0:T(8,128)(2,1)S(1)}, bf16[2,4,16,128]{3,2,1,0:T(8,128)(2,1)S(1)}, bf16[2,4,16,128]{3,2,1,0:T(8,128)(2,1)S(1)}) custom-call(bf16[8,128,128]{2,1,0:T(8,128)(2,1)S(1)} %bitcast.5, bf16[8,128,128]{2,1,0:T(8,128)(2,1)S(1)} %get-tuple-element.38.turned_ref, ...), custom_call_target="tpu_custom_call" | custom-call | flops 4000000000 | bytes 10000000 | tf_op jit(solution)/shard_map/near/pallas_call | solution.py:378
  14.4 2.0 %collective-permute-start.6 = (bf16[2,4,16,128]{3,2,1,0:T(8,128)(2,1)S(1)}, bf16[2,4,16,128]{3,2,1,0:T(8,128)(2,1)S(1)}, u32[]{:S(2)}, u32[]{:S(2)}) collective-permute-start(bf16[2,4,16,128]{3,2,1,0:T(8,128)(2,1)S(1)} %get-tuple-element.48), channel_id=1, source_target_pairs={{0,4},{1,5},{2,6},{3,7},{4,0},{5,1},{6,2},{7,3},{8,12},{9,13},{10,... | collective-permute-start | bytes 98312 | tf_op jit(solution)/shard_map/ppermute | solution.py:469
  16.3 0.5 %collective-permute-done.3.beside_ref = bf16[2,128,256]{2,1,0:T(8,128)(2,1)S(1)} collective-permute-done((bf16[2,128,256]{2,1,0:T(8,128)(2,1)S(1)}, bf16[2,128,256]{2,1,0:T(8,128)(2,1)S(1)}, u32[]{:S(2)}, u32[]{:S(2)}) %collective-permute-start.3) | collective-permute-done | bytes 131104 | tf_op jit(solution)/shard_map/ppermute | solution.py:463
  16.8 0.7 %far.1 = (bf16[2,4,16,128]{3,2,1,0:T(8,128)(2,1)S(1)}, bf16[2,2,4,16,128]{4,3,2,1,0:T(8,128)(2,1)S(1)}, bf16[2,4,16,128]{3,2,1,0:T(8,128)(2,1)S(1)}, bf16[2,2,4,16,128]{4,3,2,1,0:T(8,128)(2,1)S(1)}) custom-call(bf16[8,128,128]{2,1,0:T(8,128)(2,1)S(1)} %get-tuple-element.38.turned_ref, f32[3,3,8,128]{3,2,1,0:T(8,128)S(1)} %get-tuple-element.39.taper_ref, ...), custom_call_target="tpu_custom_call" | custom-call | flops 4000000000 | bytes 10000000 | tf_op jit(solution)/shard_map/far/pallas_call | solution.py:396
  17.5 2.8 %collective-permute-start.5 = (bf16[2,2,4,16,128]{4,3,2,1,0:T(8,128)(2,1)S(1)}, bf16[2,2,4,16,128]{4,3,2,1,0:T(8,128)(2,1)S(1)}, u32[]{:S(2)}, u32[]{:S(2)}) collective-permute-start(bf16[2,2,4,16,128]{4,3,2,1,0:T(8,128)(2,1)S(1)} %get-tuple-element.46), channel_id=1, source_target_pairs={{0,6},{1,7},{2,4},{3,5},{4,2},{5,3},{6,0},{7,1},{8,14},{9,15},{10,... | collective-permute-start | bytes 196616 | tf_op jit(solution)/shard_map/ppermute | solution.py:469
  20.4 0.0 collective-permute-start.8
  20.4 0.0 collective-permute-done.6.refs_2_.refs_3_
  20.4 0.1 collective-permute-start.9
  20.5 1.7 %collective-permute-start.7 = (bf16[2,4,16,128]{3,2,1,0:T(8,128)(2,1)S(1)}, bf16[2,4,16,128]{3,2,1,0:T(8,128)(2,1)S(1)}, u32[]{:S(2)}, u32[]{:S(2)}) collective-permute-start(bf16[2,4,16,128]{3,2,1,0:T(8,128)(2,1)S(1)} %get-tuple-element.49), channel_id=1, source_target_pairs={{0,4},{1,5},{2,6},{3,7},{4,0},{5,1},{6,2},{7,3},{8,12},{9,13},{10,... | collective-permute-start | bytes 98312 | tf_op jit(solution)/shard_map/ppermute | solution.py:469
  22.1 3.3 %collective-permute-done.7.refs_1_.refs_3_ = bf16[2,4,16,128]{3,2,1,0:T(8,128)(2,1)S(1)} collective-permute-done((bf16[2,4,16,128]{3,2,1,0:T(8,128)(2,1)S(1)}, bf16[2,4,16,128]{3,2,1,0:T(8,128)(2,1)S(1)}, u32[]{:S(2)}, u32[]{:S(2)}) %collective-permute-start.7) | collective-permute-done | bytes 32800 | tf_op jit(solution)/shard_map/ppermute | solution.py:469
  25.4 0.0 collective-permute-done.5.refs_0_.refs_2_
  25.4 0.3 %collective-permute-done.8.refs_2_.refs_4_ = bf16[2,2,4,16,128]{4,3,2,1,0:T(8,128)(2,1)S(1)} collective-permute-done((bf16[2,2,4,16,128]{4,3,2,1,0:T(8,128)(2,1)S(1)}, bf16[2,2,4,16,128]{4,3,2,1,0:T(8,128)(2,1)S(1)}, u32[]{:S(2)}, u32[]{:S(2)}) %collective-permute-start.8) | collective-permute-done | bytes 65568 | tf_op jit(solution)/shard_map/ppermute | solution.py:469
  25.7 0.0 collective-permute-done.9.refs_0_
  25.7 0.1 collective-permute-start.10
  25.8 0.2 early.1.refs_0_
  26.0 1.1 %collective-permute-done.10.refs_1_ = bf16[5,4,16,128]{3,2,1,0:T(8,128)(2,1)S(1)} collective-permute-done((bf16[5,4,16,128]{3,2,1,0:T(8,128)(2,1)S(1)}, bf16[5,4,16,128]{3,2,1,0:T(8,128)(2,1)S(1)}, u32[]{:S(2)}, u32[]{:S(2)}) %collective-permute-start.10) | collective-permute-done | bytes 81952 | tf_op jit(solution)/shard_map/ppermute | solution.py:448
  27.1 1.0 %late.1 = (bf16[1024,128]{1,0:T(8,128)(2,1)}, f32[1024,128]{1,0:T(8,128)S(1)}) custom-call(f32[1024,128]{1,0:T(8,128)S(1)} %early.1.refs_0_, bf16[5,4,16,128]{3,2,1,0:T(8,128)(2,1)S(1)} %collective-permute-done.10.refs_1_, bf16[2,2,4,16,128]{4,3,2,1,0:T(8,128)(2,1)S(1)} %collective-permute-done.5.refs_0_.refs_2_, ...), custom_call_target="tpu_custom_call", output_to_operand_aliasing={{1}: (0, {})} | custom-call | tf_op jit(solution)/shard_map/late/pallas_call | solution.py:431
  (5 shorter events, 0.1 us)
Async XLA Ops:
  2.9 5.7 %collective-permute-start.1 = (bf16[2,128,128]{2,1,0:T(8,128)(2,1)S(1)}, bf16[2,128,128]{2,1,0:T(8,128)(2,1)S(1)}, u32[]{:S(2)}, u32[]{:S(2)}) collective-permute-start(bf16[2,128,128]{2,1,0:T(8,128)(2,1)S(1)} %get-tuple-element.34), channel_id=1, source_target_pairs={{0,1},{1,0},{2,3},{3,2},{4,5},{5,4},{6,7},{7,6},{8,16},{9,17},{10,... | collective-permute-start | bytes 196616 | tf_op jit(solution)/shard_map/ppermute | solution.py:463
  3.8 6.8 %collective-permute-start = (bf16[2,128,128]{2,1,0:T(8,128)(2,1)S(1)}, bf16[2,128,128]{2,1,0:T(8,128)(2,1)S(1)}, u32[]{:S(2)}, u32[]{:S(2)}) collective-permute-start(bf16[2,128,128]{2,1,0:T(8,128)(2,1)S(1)} %get-tuple-element.34), channel_id=1, source_target_pairs={{0,8},{8,0},{16,24},{24,16},{1,9},{9,1},{17,25},{25,17},{2,10},{10... | collective-permute-start | bytes 196616 | tf_op jit(solution)/shard_map/ppermute | solution.py:448
  7.5 4.3 %collective-permute-start.2 = (bf16[2,128,128]{2,1,0:T(8,128)(2,1)S(1)}, bf16[2,128,128]{2,1,0:T(8,128)(2,1)S(1)}, u32[]{:S(2)}, u32[]{:S(2)}) collective-permute-start(bf16[2,128,128]{2,1,0:T(8,128)(2,1)S(1)} %get-tuple-element.34), channel_id=1, source_target_pairs={{0,8},{1,2},{2,1},{3,4},{4,3},{5,6},{6,5},{7,15},{8,0},{9,10},{10,... | collective-permute-start | bytes 196616 | tf_op jit(solution)/shard_map/ppermute | solution.py:463
  11.9 1.4 %collective-permute-start.4 = (bf16[2,128,384]{2,1,0:T(8,128)(2,1)S(1)}, bf16[2,128,384]{2,1,0:T(8,128)(2,1)S(1)}, u32[]{:S(2)}, u32[]{:S(2)}) collective-permute-start(bf16[2,128,384]{2,1,0:T(8,128)(2,1)S(1)} %pad_maximum_fusion.own_ref), channel_id=1, source_target_pairs={{0,1},{1,0},{2,3},{3,2},{4,5},{5,4},{6,7},{7,6},{8,9},{9,8},{10,11... | collective-permute-start | bytes 589832 | tf_op jit(solution)/shard_map/ppermute | solution.py:448
  11.9 5.0 %collective-permute-start.3 = (bf16[2,128,256]{2,1,0:T(8,128)(2,1)S(1)}, bf16[2,128,256]{2,1,0:T(8,128)(2,1)S(1)}, u32[]{:S(2)}, u32[]{:S(2)}) collective-permute-start(bf16[2,128,256]{2,1,0:T(8,128)(2,1)S(1)} %pad_maximum_fusion.1), channel_id=1, source_target_pairs={{0,8},{1,2},{2,1},{3,4},{4,3},{5,6},{6,5},{7,15},{8,0},{9,10},{10,... | collective-permute-start | bytes 393224 | tf_op jit(solution)/shard_map/ppermute | solution.py:463
  14.4 6.0 %collective-permute-start.6 = (bf16[2,4,16,128]{3,2,1,0:T(8,128)(2,1)S(1)}, bf16[2,4,16,128]{3,2,1,0:T(8,128)(2,1)S(1)}, u32[]{:S(2)}, u32[]{:S(2)}) collective-permute-start(bf16[2,4,16,128]{3,2,1,0:T(8,128)(2,1)S(1)} %get-tuple-element.48), channel_id=1, source_target_pairs={{0,4},{1,5},{2,6},{3,7},{4,0},{5,1},{6,2},{7,3},{8,12},{9,13},{10,... | collective-permute-start | bytes 98312 | tf_op jit(solution)/shard_map/ppermute | solution.py:469
  17.5 7.9 %collective-permute-start.5 = (bf16[2,2,4,16,128]{4,3,2,1,0:T(8,128)(2,1)S(1)}, bf16[2,2,4,16,128]{4,3,2,1,0:T(8,128)(2,1)S(1)}, u32[]{:S(2)}, u32[]{:S(2)}) collective-permute-start(bf16[2,2,4,16,128]{4,3,2,1,0:T(8,128)(2,1)S(1)} %get-tuple-element.46), channel_id=1, source_target_pairs={{0,6},{1,7},{2,4},{3,5},{4,2},{5,3},{6,0},{7,1},{8,14},{9,15},{10,... | collective-permute-start | bytes 196616 | tf_op jit(solution)/shard_map/ppermute | solution.py:469
  20.4 5.3 %collective-permute-start.8 = (bf16[2,2,4,16,128]{4,3,2,1,0:T(8,128)(2,1)S(1)}, bf16[2,2,4,16,128]{4,3,2,1,0:T(8,128)(2,1)S(1)}, u32[]{:S(2)}, u32[]{:S(2)}) collective-permute-start(bf16[2,2,4,16,128]{4,3,2,1,0:T(8,128)(2,1)S(1)} %get-tuple-element.50), channel_id=1, source_target_pairs={{0,2},{1,3},{2,0},{3,1},{4,6},{5,7},{6,4},{7,5},{8,10},{9,11},{10,... | collective-permute-start | bytes 196616 | tf_op jit(solution)/shard_map/ppermute | solution.py:469
  20.4 5.3 %collective-permute-start.9 = (bf16[3,4,16,128]{3,2,1,0:T(8,128)(2,1)S(1)}, bf16[3,4,16,128]{3,2,1,0:T(8,128)(2,1)S(1)}, u32[]{:S(2)}, u32[]{:S(2)}) collective-permute-start(bf16[3,4,16,128]{3,2,1,0:T(8,128)(2,1)S(1)} %pack.2), channel_id=1, source_target_pairs={{0,1},{1,0},{2,3},{3,2},{4,5},{5,4},{6,7},{7,6},{8,9},{9,8},{10,11... | collective-permute-start | bytes 147464 | tf_op jit(solution)/shard_map/ppermute | solution.py:448
  20.5 4.9 %collective-permute-start.7 = (bf16[2,4,16,128]{3,2,1,0:T(8,128)(2,1)S(1)}, bf16[2,4,16,128]{3,2,1,0:T(8,128)(2,1)S(1)}, u32[]{:S(2)}, u32[]{:S(2)}) collective-permute-start(bf16[2,4,16,128]{3,2,1,0:T(8,128)(2,1)S(1)} %get-tuple-element.49), channel_id=1, source_target_pairs={{0,4},{1,5},{2,6},{3,7},{4,0},{5,1},{6,2},{7,3},{8,12},{9,13},{10,... | collective-permute-start | bytes 98312 | tf_op jit(solution)/shard_map/ppermute | solution.py:469
  25.7 1.3 %collective-permute-start.10 = (bf16[5,4,16,128]{3,2,1,0:T(8,128)(2,1)S(1)}, bf16[5,4,16,128]{3,2,1,0:T(8,128)(2,1)S(1)}, u32[]{:S(2)}, u32[]{:S(2)}) collective-permute-start(bf16[5,4,16,128]{3,2,1,0:T(8,128)(2,1)S(1)} %pack.3), channel_id=1, source_target_pairs={{0,1},{1,0},{2,3},{3,2},{4,5},{5,4},{6,7},{7,6},{8,9},{9,8},{10,11... | collective-permute-start | bytes 245768 | tf_op jit(solution)/shard_map/ppermute | solution.py:448

commit v24 on v22

--- a/solution.py
+++ b/solution.py
@@ -207,7 +207,7 @@
 
     for t in range(9):
         iy, ix = t // 3, t % 3
-        dx, dy = offset(ix, tile_x), offset(iy, tile_y)
+        dx, dy = offset((0, 2, 1)[ix], tile_x), offset(iy, tile_y)
         at_x, at_y = tile_x + dx, tile_y + dy
         valid = (at_x >= 0) & (at_x < count_x) & (at_y >= 0) & (at_y < count_y)
         at_x = jnp.clip(at_x, 0, count_x - 1)
@@ -486,10 +486,10 @@
     by_block = params.reshape(members, BLOCKS, CELLS).transpose(1, 0, 2)
     sent, by_block = lax.optimization_barrier((own, by_block))
     across = swap_odd(sent, "gy")
+    odd = swap_odd(own, "gx")
     even = swap(own, "gx")
-    odd = swap_odd(own, "gx")
     turned, taper = prepare(by_block, taper_radius, taper_pattern, obs_block)
-    beside, column = jnp.concatenate([even, odd], axis=2), jnp.concatenate([own, even, odd], axis=2)
+    beside, column = jnp.concatenate([odd, even], axis=2), jnp.concatenate([own, odd, even], axis=2)
     beside, column, across, turned, taper = lax.optimization_barrier((beside, column, across, turned, taper))
     even = swap(column, "gy")
     beside = swap_odd(beside, "gy")

time: 28 us -> 28.1 us (level)
    ppermute x3, starting transfers between devices: 1.29 us -> 4.47 us  [swap_odd(): return lax.ppermute(block, ('gx', 'gy'), pairs)]
    ppermute x4, waiting for transfers between devices: 4.05 us -> 1.05 us  [swap(): lax.ppermute(block, axis, [(i, i ^ 1) for i in range(lax.axis_size(axis))])]
    ppermute x4, starting transfers between devices: 6.8 us -> 4.44 us  [hop(): return lax.ppermute(piece, 'gy', pairs)]
    ppermute x3, waiting for transfers between devices: 1.3 us -> 3.6 us  [swap_odd(): return lax.ppermute(block, ('gx', 'gy'), pairs)]
    ppermute x4, starting transfers between devices: 3.92 us -> 3.05 us  [swap(): lax.ppermute(block, axis, [(i, i ^ 1) for i in range(lax.axis_size(axis))])]
    ppermute x4, waiting for transfers between devices: 3.59 us -> 4.3 us  [hop(): return lax.ppermute(piece, 'gy', pairs)]
  transfers between devices with their start and end apart: 11 -> 11, of which waited for: 7 -> 6; matrix products, arithmetic and copies ran while one was open for 0% -> 0% of each run, Pallas kernels for 10% -> 10%
where the time goes in v24:
time: 28.1 us; the launch traced here: 27.8 us
  starting transfers between devices  12 us (43%)
  waiting for transfers between devices  8.95 us (32%)
  Pallas kernels  6.74 us (24%)
    ppermute x3, starting transfers between devices, swap_odd(): return lax.ppermute(block, ('gx', 'gy'), pairs)  4.47 us
    ppermute x4, starting transfers between devices, hop(): return lax.ppermute(piece, 'gy', pairs)  4.44 us
    ppermute x4, waiting for transfers between devices, hop(): return lax.ppermute(piece, 'gy', pairs)  4.3 us
    ppermute x3, waiting for transfers between devices, swap_odd(): return lax.ppermute(block, ('gx', 'gy'), pairs)  3.6 us
    ppermute x4, starting transfers between devices, swap(): lax.ppermute(block, axis, [(i, i ^ 1) for i in range(lax.axis_size(axis))])  3.05 us
    pallas_call x1, Pallas kernels, weigh(): pl.pallas_call(weigh_kernel, out_shape=(jax.ShapeDtypeStruct((2, members,...  2.91 us
    ppermute x4, waiting for transfers between devices, swap(): lax.ppermute(block, axis, [(i, i ^ 1) for i in range(lax.axis_size(axis))])  1.05 us
    pallas_call x1, Pallas kernels, update_near(): pl.pallas_call(near_kernel, out_shape=(jax.ShapeDtypeStruct((SIDE, member...  1.04 us
  transfers between devices with their start and end apart: 11, of which 6 were waited for; matrix products, arithmetic and copies ran while one was open for 0% of the time, Pallas kernels for 10%

profile of v24, /device:TPU:0, one launch (start us, length us, event | category | flops | bytes accessed | tf_op | source)
XLA Modules:
  0.0 27.8 jit_solution(1013517229741502720)
XLA Ops:
  0.0 2.9 %weigh.1 = (bf16[2,128,128]{2,1,0:T(8,128)(2,1)S(1)}, bf16[128,2,4,128]{3,2,1,0:T(4,128)(2,1)S(1)}) custom-call(f32[1,1,128,128]{3,2,1,0:T(8,128)} %pred_hbm.1, f32[1,1,128]{2,1,0:T(1,128)} %mv_hbm.1, f32[1,1,128]{2,1,0:T(1,128)} %var_hbm.1, f32[1,1,128,128]{3,2,1,0:T(8,128)} %jit_hbm.1, s32[4,8,128]{2,1,0:T(8,128)} %obs_hbm.3, ...), custom_call_target="tpu_custom_call" | custom-call | tf_op jit(solution)/shard_map/weigh/pallas_call | solution.py:157
  2.9 2.9 %collective-permute-start.1 = (bf16[2,128,128]{2,1,0:T(8,128)(2,1)S(1)}, bf16[2,128,128]{2,1,0:T(8,128)(2,1)S(1)}, u32[]{:S(2)}, u32[]{:S(2)}) collective-permute-start(bf16[2,128,128]{2,1,0:T(8,128)(2,1)S(1)} %get-tuple-element.34), channel_id=1, source_target_pairs={{0,8},{8,0},{16,24},{24,16},{1,9},{9,1},{17,25},{25,17},{2,10},{10... | collective-permute-start | bytes 196616 | tf_op jit(solution)/shard_map/ppermute | solution.py:447
  5.8 0.0 collective-permute-start
  5.9 3.0 %collective-permute-start.2 = (bf16[2,128,128]{2,1,0:T(8,128)(2,1)S(1)}, bf16[2,128,128]{2,1,0:T(8,128)(2,1)S(1)}, u32[]{:S(2)}, u32[]{:S(2)}) collective-permute-start(bf16[2,128,128]{2,1,0:T(8,128)(2,1)S(1)} %get-tuple-element.34), channel_id=1, source_target_pairs={{0,8},{1,2},{2,1},{3,4},{4,3},{5,6},{6,5},{7,15},{8,0},{9,10},{10,... | collective-permute-start | bytes 196616 | tf_op jit(solution)/shard_map/ppermute | solution.py:462
  8.9 1.0 %prepare.1 = (bf16[8,128,128]{2,1,0:T(8,128)(2,1)S(1)}, f32[3,3,8,128]{3,2,1,0:T(8,128)S(1)}) custom-call(bf16[8,128,128]{2,1,0:T(8,128)(2,1)S(1)} %bitcast.4, s32[2,4]{1,0:T(2,128)} %radius_hbm.1, s32[2,4,25]{2,1,0:T(4,128)} %pattern_hbm.1, s32[4,8,128]{2,1,0:T(8,128)} %obs_hbm.3), custom_call_target="tpu_custom_call" | custom-call | flops 4000000 | bytes 1000000 | tf_op jit(solution)/shard_map/prepare/pallas_call | solution.py:230
  9.9 0.0 collective-permute-done.1
  9.9 0.0 collective-permute-done
  10.0 1.8 %collective-permute-done.2.odd_ref = bf16[2,128,128]{2,1,0:T(8,128)(2,1)S(1)} collective-permute-done((bf16[2,128,128]{2,1,0:T(8,128)(2,1)S(1)}, bf16[2,128,128]{2,1,0:T(8,128)(2,1)S(1)}, u32[]{:S(2)}, u32[]{:S(2)}) %collective-permute-start.2) | collective-permute-done | bytes 65568 | tf_op jit(solution)/shard_map/ppermute | solution.py:462
  11.7 0.0 collective-permute-start.4
  11.7 1.4 %collective-permute-start.3 = (bf16[2,128,256]{2,1,0:T(8,128)(2,1)S(1)}, bf16[2,128,256]{2,1,0:T(8,128)(2,1)S(1)}, u32[]{:S(2)}, u32[]{:S(2)}) collective-permute-start(bf16[2,128,256]{2,1,0:T(8,128)(2,1)S(1)} %pad_maximum_fusion.1), channel_id=1, source_target_pairs={{0,8},{1,2},{2,1},{3,4},{4,3},{5,6},{6,5},{7,15},{8,0},{9,10},{10,... | collective-permute-start | bytes 393224 | tf_op jit(solution)/shard_map/ppermute | solution.py:462
  13.2 0.0 collective-permute-done.4.even_ref
  13.2 1.0 %near.1 = (f32[4,128,128]{2,1,0:T(8,128)S(1)}, bf16[2,4,16,128]{3,2,1,0:T(8,128)(2,1)S(1)}, bf16[2,4,16,128]{3,2,1,0:T(8,128)(2,1)S(1)}, bf16[2,4,16,128]{3,2,1,0:T(8,128)(2,1)S(1)}, bf16[2,4,16,128]{3,2,1,0:T(8,128)(2,1)S(1)}) custom-call(bf16[8,128,128]{2,1,0:T(8,128)(2,1)S(1)} %bitcast.5, bf16[8,128,128]{2,1,0:T(8,128)(2,1)S(1)} %get-tuple-element.38.turned_ref, ...), custom_call_target="tpu_custom_call" | custom-call | flops 4000000000 | bytes 10000000 | tf_op jit(solution)/shard_map/near/pallas_call | solution.py:377
  14.2 0.7 %collective-permute-start.6 = (bf16[2,4,16,128]{3,2,1,0:T(8,128)(2,1)S(1)}, bf16[2,4,16,128]{3,2,1,0:T(8,128)(2,1)S(1)}, u32[]{:S(2)}, u32[]{:S(2)}) collective-permute-start(bf16[2,4,16,128]{3,2,1,0:T(8,128)(2,1)S(1)} %get-tuple-element.48), channel_id=1, source_target_pairs={{0,4},{1,5},{2,6},{3,7},{4,0},{5,1},{6,2},{7,3},{8,12},{9,13},{10,... | collective-permute-start | bytes 98312 | tf_op jit(solution)/shard_map/ppermute | solution.py:468
  14.9 1.8 %collective-permute-done.3.beside_ref = bf16[2,128,256]{2,1,0:T(8,128)(2,1)S(1)} collective-permute-done((bf16[2,128,256]{2,1,0:T(8,128)(2,1)S(1)}, bf16[2,128,256]{2,1,0:T(8,128)(2,1)S(1)}, u32[]{:S(2)}, u32[]{:S(2)}) %collective-permute-start.3) | collective-permute-done | bytes 131104 | tf_op jit(solution)/shard_map/ppermute | solution.py:462
  16.7 0.7 %far.1 = (bf16[2,4,16,128]{3,2,1,0:T(8,128)(2,1)S(1)}, bf16[2,2,4,16,128]{4,3,2,1,0:T(8,128)(2,1)S(1)}, bf16[2,4,16,128]{3,2,1,0:T(8,128)(2,1)S(1)}, bf16[2,2,4,16,128]{4,3,2,1,0:T(8,128)(2,1)S(1)}) custom-call(bf16[8,128,128]{2,1,0:T(8,128)(2,1)S(1)} %get-tuple-element.38.turned_ref, f32[3,3,8,128]{3,2,1,0:T(8,128)S(1)} %get-tuple-element.39.taper_ref, ...), custom_call_target="tpu_custom_call" | custom-call | flops 4000000000 | bytes 10000000 | tf_op jit(solution)/shard_map/far/pallas_call | solution.py:395
  17.4 1.5 %collective-permute-start.5 = (bf16[2,2,4,16,128]{4,3,2,1,0:T(8,128)(2,1)S(1)}, bf16[2,2,4,16,128]{4,3,2,1,0:T(8,128)(2,1)S(1)}, u32[]{:S(2)}, u32[]{:S(2)}) collective-permute-start(bf16[2,2,4,16,128]{4,3,2,1,0:T(8,128)(2,1)S(1)} %get-tuple-element.46), channel_id=1, source_target_pairs={{0,6},{1,7},{2,4},{3,5},{4,2},{5,3},{6,0},{7,1},{8,14},{9,15},{10,... | collective-permute-start | bytes 196616 | tf_op jit(solution)/shard_map/ppermute | solution.py:468
  18.9 0.0 collective-permute-start.8
  18.9 0.8 %collective-permute-done.6.refs_2_.refs_3_ = bf16[2,4,16,128]{3,2,1,0:T(8,128)(2,1)S(1)} collective-permute-done((bf16[2,4,16,128]{3,2,1,0:T(8,128)(2,1)S(1)}, bf16[2,4,16,128]{3,2,1,0:T(8,128)(2,1)S(1)}, u32[]{:S(2)}, u32[]{:S(2)}) %collective-permute-start.6) | collective-permute-done | bytes 32800 | tf_op jit(solution)/shard_map/ppermute | solution.py:468
  19.7 0.0 collective-permute-start.9
  19.7 2.3 %collective-permute-start.7 = (bf16[2,4,16,128]{3,2,1,0:T(8,128)(2,1)S(1)}, bf16[2,4,16,128]{3,2,1,0:T(8,128)(2,1)S(1)}, u32[]{:S(2)}, u32[]{:S(2)}) collective-permute-start(bf16[2,4,16,128]{3,2,1,0:T(8,128)(2,1)S(1)} %get-tuple-element.49), channel_id=1, source_target_pairs={{0,4},{1,5},{2,6},{3,7},{4,0},{5,1},{6,2},{7,3},{8,12},{9,13},{10,... | collective-permute-start | bytes 98312 | tf_op jit(solution)/shard_map/ppermute | solution.py:468
  22.0 2.8 %collective-permute-done.7.refs_1_.refs_3_ = bf16[2,4,16,128]{3,2,1,0:T(8,128)(2,1)S(1)} collective-permute-done((bf16[2,4,16,128]{3,2,1,0:T(8,128)(2,1)S(1)}, bf16[2,4,16,128]{3,2,1,0:T(8,128)(2,1)S(1)}, u32[]{:S(2)}, u32[]{:S(2)}) %collective-permute-start.7) | collective-permute-done | bytes 32800 | tf_op jit(solution)/shard_map/ppermute | solution.py:468
  24.8 0.0 collective-permute-done.5.refs_0_.refs_2_
  24.8 0.6 %collective-permute-done.8.refs_2_.refs_4_ = bf16[2,2,4,16,128]{4,3,2,1,0:T(8,128)(2,1)S(1)} collective-permute-done((bf16[2,2,4,16,128]{4,3,2,1,0:T(8,128)(2,1)S(1)}, bf16[2,2,4,16,128]{4,3,2,1,0:T(8,128)(2,1)S(1)}, u32[]{:S(2)}, u32[]{:S(2)}) %collective-permute-start.8) | collective-permute-done | bytes 65568 | tf_op jit(solution)/shard_map/ppermute | solution.py:468
  25.5 0.0 collective-permute-done.9.refs_0_
  25.5 0.1 collective-permute-start.10
  25.6 0.1 early.1.refs_0_
  25.8 1.0 %collective-permute-done.10.refs_1_ = bf16[5,4,16,128]{3,2,1,0:T(8,128)(2,1)S(1)} collective-permute-done((bf16[5,4,16,128]{3,2,1,0:T(8,128)(2,1)S(1)}, bf16[5,4,16,128]{3,2,1,0:T(8,128)(2,1)S(1)}, u32[]{:S(2)}, u32[]{:S(2)}) %collective-permute-start.10) | collective-permute-done | bytes 81952 | tf_op jit(solution)/shard_map/ppermute | solution.py:447
  26.8 1.0 %late.1 = (bf16[1024,128]{1,0:T(8,128)(2,1)}, f32[1024,128]{1,0:T(8,128)S(1)}) custom-call(f32[1024,128]{1,0:T(8,128)S(1)} %early.1.refs_0_, bf16[5,4,16,128]{3,2,1,0:T(8,128)(2,1)S(1)} %collective-permute-done.10.refs_1_, bf16[2,2,4,16,128]{4,3,2,1,0:T(8,128)(2,1)S(1)} %collective-permute-done.5.refs_0_.refs_2_, ...), custom_call_target="tpu_custom_call", output_to_operand_aliasing={{1}: (0, {})} | custom-call | tf_op jit(solution)/shard_map/late/pallas_call | solution.py:430
  (5 shorter events, 0.1 us)
Async XLA Ops:
  2.9 7.0 %collective-permute-start.1 = (bf16[2,128,128]{2,1,0:T(8,128)(2,1)S(1)}, bf16[2,128,128]{2,1,0:T(8,128)(2,1)S(1)}, u32[]{:S(2)}, u32[]{:S(2)}) collective-permute-start(bf16[2,128,128]{2,1,0:T(8,128)(2,1)S(1)} %get-tuple-element.34), channel_id=1, source_target_pairs={{0,8},{8,0},{16,24},{24,16},{1,9},{9,1},{17,25},{25,17},{2,10},{10... | collective-permute-start | bytes 196616 | tf_op jit(solution)/shard_map/ppermute | solution.py:447
  5.8 4.1 %collective-permute-start = (bf16[2,128,128]{2,1,0:T(8,128)(2,1)S(1)}, bf16[2,128,128]{2,1,0:T(8,128)(2,1)S(1)}, u32[]{:S(2)}, u32[]{:S(2)}) collective-permute-start(bf16[2,128,128]{2,1,0:T(8,128)(2,1)S(1)} %get-tuple-element.34), channel_id=1, source_target_pairs={{0,1},{1,0},{2,3},{3,2},{4,5},{5,4},{6,7},{7,6},{8,16},{9,17},{10,... | collective-permute-start | bytes 196616 | tf_op jit(solution)/shard_map/ppermute | solution.py:462
  5.9 5.9 %collective-permute-start.2 = (bf16[2,128,128]{2,1,0:T(8,128)(2,1)S(1)}, bf16[2,128,128]{2,1,0:T(8,128)(2,1)S(1)}, u32[]{:S(2)}, u32[]{:S(2)}) collective-permute-start(bf16[2,128,128]{2,1,0:T(8,128)(2,1)S(1)} %get-tuple-element.34), channel_id=1, source_target_pairs={{0,8},{1,2},{2,1},{3,4},{4,3},{5,6},{6,5},{7,15},{8,0},{9,10},{10,... | collective-permute-start | bytes 196616 | tf_op jit(solution)/shard_map/ppermute | solution.py:462
  11.7 1.4 %collective-permute-start.4 = (bf16[2,128,384]{2,1,0:T(8,128)(2,1)S(1)}, bf16[2,128,384]{2,1,0:T(8,128)(2,1)S(1)}, u32[]{:S(2)}, u32[]{:S(2)}) collective-permute-start(bf16[2,128,384]{2,1,0:T(8,128)(2,1)S(1)} %pad_maximum_fusion.own_ref), channel_id=1, source_target_pairs={{0,1},{1,0},{2,3},{3,2},{4,5},{5,4},{6,7},{7,6},{8,9},{9,8},{10,11... | collective-permute-start | bytes 589832 | tf_op jit(solution)/shard_map/ppermute | solution.py:447
  11.7 5.0 %collective-permute-start.3 = (bf16[2,128,256]{2,1,0:T(8,128)(2,1)S(1)}, bf16[2,128,256]{2,1,0:T(8,128)(2,1)S(1)}, u32[]{:S(2)}, u32[]{:S(2)}) collective-permute-start(bf16[2,128,256]{2,1,0:T(8,128)(2,1)S(1)} %pad_maximum_fusion.1), channel_id=1, source_target_pairs={{0,8},{1,2},{2,1},{3,4},{4,3},{5,6},{6,5},{7,15},{8,0},{9,10},{10,... | collective-permute-start | bytes 393224 | tf_op jit(solution)/shard_map/ppermute | solution.py:462
  14.2 5.5 %collective-permute-start.6 = (bf16[2,4,16,128]{3,2,1,0:T(8,128)(2,1)S(1)}, bf16[2,4,16,128]{3,2,1,0:T(8,128)(2,1)S(1)}, u32[]{:S(2)}, u32[]{:S(2)}) collective-permute-start(bf16[2,4,16,128]{3,2,1,0:T(8,128)(2,1)S(1)} %get-tuple-element.48), channel_id=1, source_target_pairs={{0,4},{1,5},{2,6},{3,7},{4,0},{5,1},{6,2},{7,3},{8,12},{9,13},{10,... | collective-permute-start | bytes 98312 | tf_op jit(solution)/shard_map/ppermute | solution.py:468
  17.4 7.4 %collective-permute-start.5 = (bf16[2,2,4,16,128]{4,3,2,1,0:T(8,128)(2,1)S(1)}, bf16[2,2,4,16,128]{4,3,2,1,0:T(8,128)(2,1)S(1)}, u32[]{:S(2)}, u32[]{:S(2)}) collective-permute-start(bf16[2,2,4,16,128]{4,3,2,1,0:T(8,128)(2,1)S(1)} %get-tuple-element.46), channel_id=1, source_target_pairs={{0,6},{1,7},{2,4},{3,5},{4,2},{5,3},{6,0},{7,1},{8,14},{9,15},{10,... | collective-permute-start | bytes 196616 | tf_op jit(solution)/shard_map/ppermute | solution.py:468
  18.9 6.6 %collective-permute-start.8 = (bf16[2,2,4,16,128]{4,3,2,1,0:T(8,128)(2,1)S(1)}, bf16[2,2,4,16,128]{4,3,2,1,0:T(8,128)(2,1)S(1)}, u32[]{:S(2)}, u32[]{:S(2)}) collective-permute-start(bf16[2,2,4,16,128]{4,3,2,1,0:T(8,128)(2,1)S(1)} %get-tuple-element.50), channel_id=1, source_target_pairs={{0,2},{1,3},{2,0},{3,1},{4,6},{5,7},{6,4},{7,5},{8,10},{9,11},{10,... | collective-permute-start | bytes 196616 | tf_op jit(solution)/shard_map/ppermute | solution.py:468
  19.7 5.8 %collective-permute-start.9 = (bf16[3,4,16,128]{3,2,1,0:T(8,128)(2,1)S(1)}, bf16[3,4,16,128]{3,2,1,0:T(8,128)(2,1)S(1)}, u32[]{:S(2)}, u32[]{:S(2)}) collective-permute-start(bf16[3,4,16,128]{3,2,1,0:T(8,128)(2,1)S(1)} %pack.2), channel_id=1, source_target_pairs={{0,1},{1,0},{2,3},{3,2},{4,5},{5,4},{6,7},{7,6},{8,9},{9,8},{10,11... | collective-permute-start | bytes 147464 | tf_op jit(solution)/shard_map/ppermute | solution.py:447
  19.7 5.1 %collective-permute-start.7 = (bf16[2,4,16,128]{3,2,1,0:T(8,128)(2,1)S(1)}, bf16[2,4,16,128]{3,2,1,0:T(8,128)(2,1)S(1)}, u32[]{:S(2)}, u32[]{:S(2)}) collective-permute-start(bf16[2,4,16,128]{3,2,1,0:T(8,128)(2,1)S(1)} %get-tuple-element.49), channel_id=1, source_target_pairs={{0,4},{1,5},{2,6},{3,7},{4,0},{5,1},{6,2},{7,3},{8,12},{9,13},{10,... | collective-permute-start | bytes 98312 | tf_op jit(solution)/shard_map/ppermute | solution.py:468
  25.5 1.3 %collective-permute-start.10 = (bf16[5,4,16,128]{3,2,1,0:T(8,128)(2,1)S(1)}, bf16[5,4,16,128]{3,2,1,0:T(8,128)(2,1)S(1)}, u32[]{:S(2)}, u32[]{:S(2)}) collective-permute-start(bf16[5,4,16,128]{3,2,1,0:T(8,128)(2,1)S(1)} %pack.3), channel_id=1, source_target_pairs={{0,1},{1,0},{2,3},{3,2},{4,5},{5,4},{6,7},{7,6},{8,9},{9,8},{10,11... | collective-permute-start | bytes 245768 | tf_op jit(solution)/shard_map/ppermute | solution.py:447

commit v25 on v22

--- a/solution.py
+++ b/solution.py
@@ -434,7 +434,7 @@
         out_specs=(pl.BlockSpec(memory_space=pl.ANY), VMEM),
         scratch_shapes=[
             pltpu.VMEM((rows, CELLS), BF16),
-            pltpu.SemaphoreType.DMA((4,)),
+            pltpu.SemaphoreType.DMA((8,)),
         ],
         input_output_aliases={0: 1},
         compiler_params=LIMIT,

time: 28 us -> 28.1 us (level)
  no operation moved by 1% of the time
where the time goes in v25:
time: 28.1 us; the launch traced here: 27.8 us
  starting transfers between devices  11.9 us (42%)
  waiting for transfers between devices  9.04 us (32%)
  Pallas kernels  6.68 us (24%)
    ppermute x4, starting transfers between devices, hop(): return lax.ppermute(piece, 'gy', pairs)  6.69 us
    ppermute x4, waiting for transfers between devices, swap(): lax.ppermute(block, axis, [(i, i ^ 1) for i in range(lax.axis_size(axis))])  4.05 us
    ppermute x4, starting transfers between devices, swap(): lax.ppermute(block, axis, [(i, i ^ 1) for i in range(lax.axis_size(axis))])  4.02 us
    ppermute x4, waiting for transfers between devices, hop(): return lax.ppermute(piece, 'gy', pairs)  3.59 us
    pallas_call x1, Pallas kernels, weigh(): pl.pallas_call(weigh_kernel, out_shape=(jax.ShapeDtypeStruct((2, members,...  2.81 us
    ppermute x3, waiting for transfers between devices, swap_odd(): return lax.ppermute(block, ('gx', 'gy'), pairs)  1.4 us
    ppermute x3, starting transfers between devices, swap_odd(): return lax.ppermute(block, ('gx', 'gy'), pairs)  1.19 us
    pallas_call x1, Pallas kernels, update_near(): pl.pallas_call(near_kernel, out_shape=(jax.ShapeDtypeStruct((SIDE, member...  1.04 us
  transfers between devices with their start and end apart: 11, of which 7 were waited for; matrix products, arithmetic and copies ran while one was open for 0% of the time, Pallas kernels for 10%

profile of v25, /device:TPU:0, one launch (start us, length us, event | category | flops | bytes accessed | tf_op | source)
XLA Modules:
  0.0 27.8 jit_solution(14870225444679419386)
XLA Ops:
  0.0 2.8 %weigh.1 = (bf16[2,128,128]{2,1,0:T(8,128)(2,1)S(1)}, bf16[128,2,4,128]{3,2,1,0:T(4,128)(2,1)S(1)}) custom-call(f32[1,1,128,128]{3,2,1,0:T(8,128)} %pred_hbm.1, f32[1,1,128]{2,1,0:T(1,128)} %mv_hbm.1, f32[1,1,128]{2,1,0:T(1,128)} %var_hbm.1, f32[1,1,128,128]{3,2,1,0:T(8,128)} %jit_hbm.1, s32[4,8,128]{2,1,0:T(8,128)} %obs_hbm.3, ...), custom_call_target="tpu_custom_call" | custom-call | tf_op jit(solution)/shard_map/weigh/pallas_call | solution.py:157
  2.8 0.5 %collective-permute-start.1 = (bf16[2,128,128]{2,1,0:T(8,128)(2,1)S(1)}, bf16[2,128,128]{2,1,0:T(8,128)(2,1)S(1)}, u32[]{:S(2)}, u32[]{:S(2)}) collective-permute-start(bf16[2,128,128]{2,1,0:T(8,128)(2,1)S(1)} %get-tuple-element.34), channel_id=1, source_target_pairs={{0,1},{1,0},{2,3},{3,2},{4,5},{5,4},{6,7},{7,6},{8,16},{9,17},{10,... | collective-permute-start | bytes 196616 | tf_op jit(solution)/shard_map/ppermute | solution.py:462
  3.3 3.9 %collective-permute-start = (bf16[2,128,128]{2,1,0:T(8,128)(2,1)S(1)}, bf16[2,128,128]{2,1,0:T(8,128)(2,1)S(1)}, u32[]{:S(2)}, u32[]{:S(2)}) collective-permute-start(bf16[2,128,128]{2,1,0:T(8,128)(2,1)S(1)} %get-tuple-element.34), channel_id=1, source_target_pairs={{0,8},{8,0},{16,24},{24,16},{1,9},{9,1},{17,25},{25,17},{2,10},{10... | collective-permute-start | bytes 196616 | tf_op jit(solution)/shard_map/ppermute | solution.py:447
  7.3 0.1 collective-permute-start.2
  7.3 1.0 %prepare.1 = (bf16[8,128,128]{2,1,0:T(8,128)(2,1)S(1)}, f32[3,3,8,128]{3,2,1,0:T(8,128)S(1)}) custom-call(bf16[8,128,128]{2,1,0:T(8,128)(2,1)S(1)} %bitcast.4, s32[2,4]{1,0:T(2,128)} %radius_hbm.1, s32[2,4,25]{2,1,0:T(4,128)} %pattern_hbm.1, s32[4,8,128]{2,1,0:T(8,128)} %obs_hbm.3), custom_call_target="tpu_custom_call" | custom-call | flops 4000000 | bytes 1000000 | tf_op jit(solution)/shard_map/prepare/pallas_call | solution.py:230
  8.3 0.0 collective-permute-done.1
  8.3 2.1 %collective-permute-done = bf16[2,128,128]{2,1,0:T(8,128)(2,1)S(1)} collective-permute-done((bf16[2,128,128]{2,1,0:T(8,128)(2,1)S(1)}, bf16[2,128,128]{2,1,0:T(8,128)(2,1)S(1)}, u32[]{:S(2)}, u32[]{:S(2)}) %collective-permute-start) | collective-permute-done | bytes 65568 | tf_op jit(solution)/shard_map/ppermute | solution.py:447
  10.5 1.1 %collective-permute-done.2.odd_ref = bf16[2,128,128]{2,1,0:T(8,128)(2,1)S(1)} collective-permute-done((bf16[2,128,128]{2,1,0:T(8,128)(2,1)S(1)}, bf16[2,128,128]{2,1,0:T(8,128)(2,1)S(1)}, u32[]{:S(2)}, u32[]{:S(2)}) %collective-permute-start.2) | collective-permute-done | bytes 65568 | tf_op jit(solution)/shard_map/ppermute | solution.py:462
  11.6 0.0 collective-permute-start.4
  11.6 0.6 %collective-permute-start.3 = (bf16[2,128,256]{2,1,0:T(8,128)(2,1)S(1)}, bf16[2,128,256]{2,1,0:T(8,128)(2,1)S(1)}, u32[]{:S(2)}, u32[]{:S(2)}) collective-permute-start(bf16[2,128,256]{2,1,0:T(8,128)(2,1)S(1)} %pad_maximum_fusion.1), channel_id=1, source_target_pairs={{0,8},{1,2},{2,1},{3,4},{4,3},{5,6},{6,5},{7,15},{8,0},{9,10},{10,... | collective-permute-start | bytes 393224 | tf_op jit(solution)/shard_map/ppermute | solution.py:462
  12.2 0.8 %collective-permute-done.4.even_ref = bf16[2,128,384]{2,1,0:T(8,128)(2,1)S(1)} collective-permute-done((bf16[2,128,384]{2,1,0:T(8,128)(2,1)S(1)}, bf16[2,128,384]{2,1,0:T(8,128)(2,1)S(1)}, u32[]{:S(2)}, u32[]{:S(2)}) %collective-permute-start.4) | collective-permute-done | bytes 196640 | tf_op jit(solution)/shard_map/ppermute | solution.py:447
  13.0 1.0 %near.1 = (f32[4,128,128]{2,1,0:T(8,128)S(1)}, bf16[2,4,16,128]{3,2,1,0:T(8,128)(2,1)S(1)}, bf16[2,4,16,128]{3,2,1,0:T(8,128)(2,1)S(1)}, bf16[2,4,16,128]{3,2,1,0:T(8,128)(2,1)S(1)}, bf16[2,4,16,128]{3,2,1,0:T(8,128)(2,1)S(1)}) custom-call(bf16[8,128,128]{2,1,0:T(8,128)(2,1)S(1)} %bitcast.5, bf16[8,128,128]{2,1,0:T(8,128)(2,1)S(1)} %get-tuple-element.38.turned_ref, ...), custom_call_target="tpu_custom_call" | custom-call | flops 4000000000 | bytes 10000000 | tf_op jit(solution)/shard_map/near/pallas_call | solution.py:377
  14.1 2.2 %collective-permute-start.6 = (bf16[2,4,16,128]{3,2,1,0:T(8,128)(2,1)S(1)}, bf16[2,4,16,128]{3,2,1,0:T(8,128)(2,1)S(1)}, u32[]{:S(2)}, u32[]{:S(2)}) collective-permute-start(bf16[2,4,16,128]{3,2,1,0:T(8,128)(2,1)S(1)} %get-tuple-element.48), channel_id=1, source_target_pairs={{0,4},{1,5},{2,6},{3,7},{4,0},{5,1},{6,2},{7,3},{8,12},{9,13},{10,... | collective-permute-start | bytes 98312 | tf_op jit(solution)/shard_map/ppermute | solution.py:468
  16.3 0.3 %collective-permute-done.3.beside_ref = bf16[2,128,256]{2,1,0:T(8,128)(2,1)S(1)} collective-permute-done((bf16[2,128,256]{2,1,0:T(8,128)(2,1)S(1)}, bf16[2,128,256]{2,1,0:T(8,128)(2,1)S(1)}, u32[]{:S(2)}, u32[]{:S(2)}) %collective-permute-start.3) | collective-permute-done | bytes 131104 | tf_op jit(solution)/shard_map/ppermute | solution.py:462
  16.6 0.7 %far.1 = (bf16[2,4,16,128]{3,2,1,0:T(8,128)(2,1)S(1)}, bf16[2,2,4,16,128]{4,3,2,1,0:T(8,128)(2,1)S(1)}, bf16[2,4,16,128]{3,2,1,0:T(8,128)(2,1)S(1)}, bf16[2,2,4,16,128]{4,3,2,1,0:T(8,128)(2,1)S(1)}) custom-call(bf16[8,128,128]{2,1,0:T(8,128)(2,1)S(1)} %get-tuple-element.38.turned_ref, f32[3,3,8,128]{3,2,1,0:T(8,128)S(1)} %get-tuple-element.39.taper_ref, ...), custom_call_target="tpu_custom_call" | custom-call | flops 4000000000 | bytes 10000000 | tf_op jit(solution)/shard_map/far/pallas_call | solution.py:395
  17.2 2.9 %collective-permute-start.5 = (bf16[2,2,4,16,128]{4,3,2,1,0:T(8,128)(2,1)S(1)}, bf16[2,2,4,16,128]{4,3,2,1,0:T(8,128)(2,1)S(1)}, u32[]{:S(2)}, u32[]{:S(2)}) collective-permute-start(bf16[2,2,4,16,128]{4,3,2,1,0:T(8,128)(2,1)S(1)} %get-tuple-element.46), channel_id=1, source_target_pairs={{0,6},{1,7},{2,4},{3,5},{4,2},{5,3},{6,0},{7,1},{8,14},{9,15},{10,... | collective-permute-start | bytes 196616 | tf_op jit(solution)/shard_map/ppermute | solution.py:468
  20.2 0.0 collective-permute-start.8
  20.2 0.0 collective-permute-done.6.refs_2_.refs_3_
  20.2 0.1 collective-permute-start.9
  20.3 1.6 %collective-permute-start.7 = (bf16[2,4,16,128]{3,2,1,0:T(8,128)(2,1)S(1)}, bf16[2,4,16,128]{3,2,1,0:T(8,128)(2,1)S(1)}, u32[]{:S(2)}, u32[]{:S(2)}) collective-permute-start(bf16[2,4,16,128]{3,2,1,0:T(8,128)(2,1)S(1)} %get-tuple-element.49), channel_id=1, source_target_pairs={{0,4},{1,5},{2,6},{3,7},{4,0},{5,1},{6,2},{7,3},{8,12},{9,13},{10,... | collective-permute-start | bytes 98312 | tf_op jit(solution)/shard_map/ppermute | solution.py:468
  21.8 3.4 %collective-permute-done.7.refs_1_.refs_3_ = bf16[2,4,16,128]{3,2,1,0:T(8,128)(2,1)S(1)} collective-permute-done((bf16[2,4,16,128]{3,2,1,0:T(8,128)(2,1)S(1)}, bf16[2,4,16,128]{3,2,1,0:T(8,128)(2,1)S(1)}, u32[]{:S(2)}, u32[]{:S(2)}) %collective-permute-start.7) | collective-permute-done | bytes 32800 | tf_op jit(solution)/shard_map/ppermute | solution.py:468
  25.2 0.0 collective-permute-done.5.refs_0_.refs_2_
  25.2 0.2 collective-permute-done.8.refs_2_.refs_4_
  25.4 0.0 collective-permute-done.9.refs_0_
  25.4 0.1 collective-permute-start.10
  25.5 0.2 early.1.refs_0_
  25.7 1.1 %collective-permute-done.10.refs_1_ = bf16[5,4,16,128]{3,2,1,0:T(8,128)(2,1)S(1)} collective-permute-done((bf16[5,4,16,128]{3,2,1,0:T(8,128)(2,1)S(1)}, bf16[5,4,16,128]{3,2,1,0:T(8,128)(2,1)S(1)}, u32[]{:S(2)}, u32[]{:S(2)}) %collective-permute-start.10) | collective-permute-done | bytes 81952 | tf_op jit(solution)/shard_map/ppermute | solution.py:447
  26.8 1.0 %late.1 = (bf16[1024,128]{1,0:T(8,128)(2,1)}, f32[1024,128]{1,0:T(8,128)S(1)}) custom-call(f32[1024,128]{1,0:T(8,128)S(1)} %early.1.refs_0_, bf16[5,4,16,128]{3,2,1,0:T(8,128)(2,1)S(1)} %collective-permute-done.10.refs_1_, bf16[2,2,4,16,128]{4,3,2,1,0:T(8,128)(2,1)S(1)} %collective-permute-done.5.refs_0_.refs_2_, ...), custom_call_target="tpu_custom_call", output_to_operand_aliasing={{1}: (0, {})} | custom-call | tf_op jit(solution)/shard_map/late/pallas_call | solution.py:430
  (5 shorter events, 0.1 us)
Async XLA Ops:
  2.8 5.5 %collective-permute-start.1 = (bf16[2,128,128]{2,1,0:T(8,128)(2,1)S(1)}, bf16[2,128,128]{2,1,0:T(8,128)(2,1)S(1)}, u32[]{:S(2)}, u32[]{:S(2)}) collective-permute-start(bf16[2,128,128]{2,1,0:T(8,128)(2,1)S(1)} %get-tuple-element.34), channel_id=1, source_target_pairs={{0,1},{1,0},{2,3},{3,2},{4,5},{5,4},{6,7},{7,6},{8,16},{9,17},{10,... | collective-permute-start | bytes 196616 | tf_op jit(solution)/shard_map/ppermute | solution.py:462
  3.3 7.1 %collective-permute-start = (bf16[2,128,128]{2,1,0:T(8,128)(2,1)S(1)}, bf16[2,128,128]{2,1,0:T(8,128)(2,1)S(1)}, u32[]{:S(2)}, u32[]{:S(2)}) collective-permute-start(bf16[2,128,128]{2,1,0:T(8,128)(2,1)S(1)} %get-tuple-element.34), channel_id=1, source_target_pairs={{0,8},{8,0},{16,24},{24,16},{1,9},{9,1},{17,25},{25,17},{2,10},{10... | collective-permute-start | bytes 196616 | tf_op jit(solution)/shard_map/ppermute | solution.py:447
  7.3 4.3 %collective-permute-start.2 = (bf16[2,128,128]{2,1,0:T(8,128)(2,1)S(1)}, bf16[2,128,128]{2,1,0:T(8,128)(2,1)S(1)}, u32[]{:S(2)}, u32[]{:S(2)}) collective-permute-start(bf16[2,128,128]{2,1,0:T(8,128)(2,1)S(1)} %get-tuple-element.34), channel_id=1, source_target_pairs={{0,8},{1,2},{2,1},{3,4},{4,3},{5,6},{6,5},{7,15},{8,0},{9,10},{10,... | collective-permute-start | bytes 196616 | tf_op jit(solution)/shard_map/ppermute | solution.py:462
  11.6 1.4 %collective-permute-start.4 = (bf16[2,128,384]{2,1,0:T(8,128)(2,1)S(1)}, bf16[2,128,384]{2,1,0:T(8,128)(2,1)S(1)}, u32[]{:S(2)}, u32[]{:S(2)}) collective-permute-start(bf16[2,128,384]{2,1,0:T(8,128)(2,1)S(1)} %pad_maximum_fusion.own_ref), channel_id=1, source_target_pairs={{0,1},{1,0},{2,3},{3,2},{4,5},{5,4},{6,7},{7,6},{8,9},{9,8},{10,11... | collective-permute-start | bytes 589832 | tf_op jit(solution)/shard_map/ppermute | solution.py:447
  11.6 5.0 %collective-permute-start.3 = (bf16[2,128,256]{2,1,0:T(8,128)(2,1)S(1)}, bf16[2,128,256]{2,1,0:T(8,128)(2,1)S(1)}, u32[]{:S(2)}, u32[]{:S(2)}) collective-permute-start(bf16[2,128,256]{2,1,0:T(8,128)(2,1)S(1)} %pad_maximum_fusion.1), channel_id=1, source_target_pairs={{0,8},{1,2},{2,1},{3,4},{4,3},{5,6},{6,5},{7,15},{8,0},{9,10},{10,... | collective-permute-start | bytes 393224 | tf_op jit(solution)/shard_map/ppermute | solution.py:462
  14.1 6.1 %collective-permute-start.6 = (bf16[2,4,16,128]{3,2,1,0:T(8,128)(2,1)S(1)}, bf16[2,4,16,128]{3,2,1,0:T(8,128)(2,1)S(1)}, u32[]{:S(2)}, u32[]{:S(2)}) collective-permute-start(bf16[2,4,16,128]{3,2,1,0:T(8,128)(2,1)S(1)} %get-tuple-element.48), channel_id=1, source_target_pairs={{0,4},{1,5},{2,6},{3,7},{4,0},{5,1},{6,2},{7,3},{8,12},{9,13},{10,... | collective-permute-start | bytes 98312 | tf_op jit(solution)/shard_map/ppermute | solution.py:468
  17.2 8.0 %collective-permute-start.5 = (bf16[2,2,4,16,128]{4,3,2,1,0:T(8,128)(2,1)S(1)}, bf16[2,2,4,16,128]{4,3,2,1,0:T(8,128)(2,1)S(1)}, u32[]{:S(2)}, u32[]{:S(2)}) collective-permute-start(bf16[2,2,4,16,128]{4,3,2,1,0:T(8,128)(2,1)S(1)} %get-tuple-element.46), channel_id=1, source_target_pairs={{0,6},{1,7},{2,4},{3,5},{4,2},{5,3},{6,0},{7,1},{8,14},{9,15},{10,... | collective-permute-start | bytes 196616 | tf_op jit(solution)/shard_map/ppermute | solution.py:468
  20.2 5.2 %collective-permute-start.8 = (bf16[2,2,4,16,128]{4,3,2,1,0:T(8,128)(2,1)S(1)}, bf16[2,2,4,16,128]{4,3,2,1,0:T(8,128)(2,1)S(1)}, u32[]{:S(2)}, u32[]{:S(2)}) collective-permute-start(bf16[2,2,4,16,128]{4,3,2,1,0:T(8,128)(2,1)S(1)} %get-tuple-element.50), channel_id=1, source_target_pairs={{0,2},{1,3},{2,0},{3,1},{4,6},{5,7},{6,4},{7,5},{8,10},{9,11},{10,... | collective-permute-start | bytes 196616 | tf_op jit(solution)/shard_map/ppermute | solution.py:468
  20.2 5.2 %collective-permute-start.9 = (bf16[3,4,16,128]{3,2,1,0:T(8,128)(2,1)S(1)}, bf16[3,4,16,128]{3,2,1,0:T(8,128)(2,1)S(1)}, u32[]{:S(2)}, u32[]{:S(2)}) collective-permute-start(bf16[3,4,16,128]{3,2,1,0:T(8,128)(2,1)S(1)} %pack.2), channel_id=1, source_target_pairs={{0,1},{1,0},{2,3},{3,2},{4,5},{5,4},{6,7},{7,6},{8,9},{9,8},{10,11... | collective-permute-start | bytes 147464 | tf_op jit(solution)/shard_map/ppermute | solution.py:447
  20.3 4.9 %collective-permute-start.7 = (bf16[2,4,16,128]{3,2,1,0:T(8,128)(2,1)S(1)}, bf16[2,4,16,128]{3,2,1,0:T(8,128)(2,1)S(1)}, u32[]{:S(2)}, u32[]{:S(2)}) collective-permute-start(bf16[2,4,16,128]{3,2,1,0:T(8,128)(2,1)S(1)} %get-tuple-element.49), channel_id=1, source_target_pairs={{0,4},{1,5},{2,6},{3,7},{4,0},{5,1},{6,2},{7,3},{8,12},{9,13},{10,... | collective-permute-start | bytes 98312 | tf_op jit(solution)/shard_map/ppermute | solution.py:468
  25.4 1.3 %collective-permute-start.10 = (bf16[5,4,16,128]{3,2,1,0:T(8,128)(2,1)S(1)}, bf16[5,4,16,128]{3,2,1,0:T(8,128)(2,1)S(1)}, u32[]{:S(2)}, u32[]{:S(2)}) collective-permute-start(bf16[5,4,16,128]{3,2,1,0:T(8,128)(2,1)S(1)} %pack.3), channel_id=1, source_target_pairs={{0,1},{1,0},{2,3},{3,2},{4,5},{5,4},{6,7},{7,6},{8,9},{9,8},{10,11... | collective-permute-start | bytes 245768 | tf_op jit(solution)/shard_map/ppermute | solution.py:447
